TPU v7x, 32 devices: a whole 2x2x4 slice. The times are simulated.
32 devices in a mesh: section: 4 (over z), dp: 4 (over x, core), mp: 2 (over y).
Axes of the slice: x: 2, y: 2, z: 4, core: 2. Of those that a mesh axis runs over, the one named last changes fastest.
Arguments:
- section_in: bfloat16 [2, 4, 256, 12288], P(None, 'section', 'dp'), may hold values from -6 to 6
- out_grad: bfloat16 [2, 4, 256, 12288], P(None, 'section', 'dp'), may hold values from -1.5 to 1.5
- lengths: int32 [2, 4, 4], P(None, 'section', 'dp'), may hold values from 1 to 64, as said below
- w_in: bfloat16 [4, 2, 192, 128, 128], P('section', None, 'mp'), as said below
- w_out: bfloat16 [4, 2, 192, 128, 128], P('section', None, 'mp'), as said below
- idx_in: int32 [4, 2, 192], P('section', None, 'mp'), may hold values from 0 to 95, as said below
- idx_out: int32 [4, 2, 192], P('section', None, 'mp'), may hold values from 0 to 95, as said below
Outputs:
- passed: bfloat16 [2, 4, 256, 12288], P(None, 'section', ('dp', 'mp'))
- grads: float32 [4, 2, 2, 96, 128, 128], P(None, None, 'mp', 'section', 'dp')
Inputs may be any that keep to these rules, and one draw needn't show every extreme that they name: `lengths`: some micro-batch is full and some has a single live row. w_in[s, 1] equals w_in[3 - s, 0]: copy 1 at section s is the up relay's replica of layer 3 - s. w_out[s, 1] equals w_out[3 - s, 0]. idx_in[s, 1] equals idx_in[3 - s, 0]. idx_out[s, 1] equals idx_out[3 - s, 0].
All inputs are finite; a program needn't handle non-finite values.
Results may differ from a plain program's by a relative error of at most 0.0095.
Values may be sent and summed in bfloat16 or wider, within the bound.
No kernel may reach another device: no remote copies, remote signals or barrier semaphores. Data moves between devices by JAX's collectives and lax.ppermute only.
A program may use at most 128 MiB of HBM per device.

v0:
```python
from functools import partial

import jax
import jax.numpy as jnp
from jax import lax
from jax.sharding import PartitionSpec as P


def from_behind(block, axis, distance):
    devices = range(lax.axis_size(axis))
    route = [(i - distance, i) for i in devices if i - distance in devices]
    return lax.ppermute(block, axis, route)


def gelu_back(pre, upstream):
    return jax.vjp(lambda value: jax.nn.gelu(value, approximate=True), pre)[1](upstream)[0]


def body(section_in, out_grad, lengths, w_in, w_out, idx_in, idx_out):
    inputs = section_in[:, 0]
    rows = inputs.shape[1]
    width = inputs.shape[2]
    block = w_in.shape[-1]
    count = width // block
    live = lax.broadcasted_iota(jnp.int32, (2, rows), 1) < lengths[:, 0, 0][:, None]
    masked = jnp.where(live[:, :, None], out_grad[:, 0], jnp.zeros((), out_grad.dtype))
    weight_in = w_in[0]
    weight_out = w_out[0]
    index_in = idx_in[0]
    index_out = idx_out[0]
    groups = index_in.shape[1]
    select = jax.vmap(partial(jnp.take, axis=1))
    picked = select(inputs.reshape(2, rows, count, block), index_in)
    back = select(masked.reshape(2, rows, count, block), index_out)
    pre = jnp.einsum("prjc,pjcd->prjd", picked, weight_in, preferred_element_type=jnp.float32)
    act = jax.nn.gelu(pre, approximate=True).astype(jnp.bfloat16)
    back_pre = jnp.einsum("prjd,pjcd->prjc", back, weight_out, preferred_element_type=jnp.float32)
    grad_pre = gelu_back(pre, back_pre).astype(jnp.bfloat16)
    terms = jnp.einsum("prjd,pjcd->prjc", grad_pre, weight_in, preferred_element_type=jnp.float32)
    share = rows // lax.axis_size("mp")
    first = lax.axis_index("mp") * share
    same = index_in[:, :, None] == index_in[:, None, :]
    merged = jnp.einsum(
        "prkc,pjk->prjc", terms, same.astype(jnp.float32), precision=lax.Precision.HIGHEST
    )
    order = lax.broadcasted_iota(jnp.int32, (groups, groups), 1) < lax.broadcasted_iota(
        jnp.int32, (groups, groups), 0
    )
    repeated = jnp.any(same & order[None], axis=2)
    keep_first = jnp.where(repeated, 0.0, 1.0).astype(jnp.float32)
    compact = (merged * keep_first[:, None, :, None]).astype(jnp.bfloat16)
    all_index = lax.all_gather(index_in, "mp", axis=1, tiled=True)
    received = lax.all_to_all(compact[:, :, None], "mp", split_axis=1, concat_axis=2, tiled=True)
    received = received.reshape(2, share, all_index.shape[1], block)
    placing = jax.nn.one_hot(all_index, count, dtype=jnp.float32)
    summed = jnp.einsum(
        "psjc,pjb->psbc", received.astype(jnp.float32), placing, precision=lax.Precision.HIGHEST
    ).reshape(2, share, width)
    own_rows = lax.dynamic_slice_in_dim(masked, first, share, 1)
    result = (own_rows.astype(jnp.float32) + summed).astype(jnp.bfloat16)
    from_next = from_behind(result[0], "section", -1)
    from_prev = from_behind(result[1], "section", 1)
    passed = jnp.stack([from_next, from_prev], axis=0)[:, None]
    grad_in = jnp.einsum("prjc,prjd->pjcd", picked, grad_pre, preferred_element_type=jnp.float32)
    grad_out = jnp.einsum("prjc,prjd->pjcd", act, back, preferred_element_type=jnp.float32)
    stacked = jnp.stack([grad_in, grad_out], axis=1)
    reduced = lax.psum_scatter(
        stacked.astype(jnp.bfloat16), "dp", scatter_dimension=3, tiled=True
    ).astype(jnp.float32)
    moved = lax.all_to_all(
        reduced[None].astype(jnp.bfloat16), "section", split_axis=3, concat_axis=0, tiled=True
    ).astype(jnp.float32)
    total = moved[:, 0] + jnp.flip(moved[:, 1], 0)
    return (passed, total[:, :, None])


def solution(mesh):
    placed = (
        P(None, "section", "dp", None),
        P(None, "section", "dp", None),
        P(None, "section", "dp"),
        P("section", None, "mp", None, None),
        P("section", None, "mp", None, None),
        P("section", None, "mp"),
        P("section", None, "mp"),
    )
    return jax.shard_map(
        body,
        mesh=mesh,
        in_specs=placed,
        out_specs=(
            P(None, "section", ("dp", "mp"), None),
            P(None, None, "mp", "section", "dp", None),
        ),
        check_vma=False,
    )
```

profile of v0, /device:TPU:8, one launch (start us, length us, event | category | flops | bytes accessed | tf_op | source)
XLA Modules:
  0.0 273.8 jit_solution(17189582049106624803)
XLA Ops:
  7.2 0.7 bitcast_or_fusion
  8.6 0.7 bitcast_or_fusion.1
  10.0 2.6 copy.32
  12.6 2.9 %copy.23 = bf16[2,64,96,128]{3,1,2,0:T(8,128)(2,1)} copy(bf16[2,64,96,128]{3,2,1,0:T(8,128)(2,1)S(1)} %bitcast.143) | data formatting | bytes 6291456 | tf_op jit(solution)/shard_map/reshape;squeeze | solution.py:33
  15.6 2.3 copy.31
  18.0 4.0 %gather_fusion.1 = bf16[192,64,128]{2,1,0:T(8,128)(2,1)S(1)} fusion(bf16[2,64,96,128]{3,1,2,0:T(8,128)(2,1)} %copy.23, s32[192]{0:T(256)S(1)} %reshape.91), kind=kCustom, calls=%fused_computation.1.clone | custom fusion | bytes 6292992 | tf_op jit(solution)/shard_map/vmap(jit(_take))/gather | solution.py:33
  22.1 4.6 %copy_select_fusion = bf16[2,64,96,128]{3,1,2,0:T(8,128)(2,1)} fusion(bf16[2,64,96,128]{3,2,1,0:T(8,128)(2,1)} %bitcast.142, pred[2,64]{1,0:T(4,128)(4,1)S(1)} %iota_compare_fusion.2), kind=kLoop, calls=%fused_computation.40 | loop fusion | flops 1572864 | bytes 6291584 | tf_op jit(solution)/shard_map/jit(_where)/select_n | solution.py:26
  26.7 5.6 %gather_fusion = bf16[192,64,128]{2,1,0:T(8,128)(2,1)} fusion(bf16[2,64,96,128]{3,1,2,0:T(8,128)(2,1)} %copy_select_fusion, s32[192]{0:T(256)S(1)} %reshape.86), kind=kCustom, calls=%fused_computation.clone | custom fusion | bytes 6292992 | tf_op jit(solution)/shard_map/vmap(jit(_take))/gather | solution.py:34
  32.3 7.3 %fusion.12 = f32[2,96,64,128]{3,2,1,0:T(8,128)} fusion(bf16[1,2,96,128,128]{4,3,2,1,0:T(8,128)(2,1)} %param.12, bf16[2,96,64,128]{3,2,1,0:T(8,128)(2,1)S(1)} %bitcast.139, pred[2,96]{1,0:T(4,128)(4,1)S(1)} %compare_and_fusion.1), kind=kOutput, calls=%fused_computation.19 | convolution fusion | flops 404226048 | bytes 15728832 | tf_op jit(solution)/shard_map/prjc,pjcd->prjd/dot_general | solution.py:35
  39.5 6.9 %convert_bitcast_fusion = bf16[2,1,96,128,128]{4,3,2,0,1:T(8,128)(2,1)S(1)} fusion(f32[2,96,64,128]{3,2,1,0:T(8,128)} %fusion.12, bf16[2,96,64,128]{3,2,1,0:T(8,128)(2,1)} %bitcast.150, pred[2,96]{1,0:T(4,128)(4,1)S(1)} %compare_and_fusion.2), kind=kOutput, calls=%fused_computation.28 | convolution fusion | flops 421527552 | bytes 15728832 | tf_op jit(solution)/shard_map/prjc,prjd->pjcd/dot_general | solution.py:65
  46.5 11.4 %fusion.6 = bf16[2,64,96,128]{3,1,2,0:T(8,128)(2,1)S(1)} fusion(f32[2,96,64,128]{3,2,1,0:T(8,128)} %fusion.12, bf16[1,2,96,128,128]{4,3,2,1,0:T(8,128)(2,1)} %param.13, bf16[2,96,64,128]{3,2,1,0:T(8,128)(2,1)} %bitcast.151, pred[2,96]{1,0:T(4,128)(4,1)S(1)} %compare_and_fusion.2), kind=kOutput, calls=%fused_computation.11 | convolution fusion | flops 435683328 | bytes 18874560 | tf_op jit(solution)/shard_map/prjd,pjcd->prjc/dot_general | solution.py:37
  57.9 2.6 convert_bitcast_fusion.1
  60.5 5.4 %pad_maximum_fusion = bf16[2,2,96,128,128]{4,3,2,0,1:T(8,128)(2,1)} fusion(bf16[2,1,96,128,128]{4,3,2,0,1:T(8,128)(2,1)S(1)} %convert_bitcast_fusion, bf16[2,1,96,128,128]{4,3,2,0,1:T(8,128)(2,1)S(1)} %convert_bitcast_fusion.1), kind=kLoop, calls=%fused_computation.2 | loop fusion | flops 6291456 | bytes 25165824 | tf_op jit(solution)/shard_map/stack | solution.py:66
  66.7 1.0 copy-done.1
  67.7 6.4 %fusion.37 = f32[2,64,96,128]{3,1,2,0:T(8,128)S(1)} fusion(bf16[2,64,96,128]{3,1,2,0:T(8,128)(2,1)S(1)} %copy-done.1, bf16[1,2,96,128,128]{4,3,2,1,0:T(8,128)(2,1)} %param.12), kind=kOutput, calls=%fused_computation.48 | convolution fusion | flops 402653184 | bytes 15728640 | tf_op jit(solution)/shard_map/prjd,pjcd->prjc/dot_general | solution.py:39
  74.1 6.3 %fusion.19 = bf16[2,64,1,96,128]{4,3,1,0,2:T(8,128)(2,1)S(1)} fusion(f32[2,96]{1,0:T(2,128)S(1)} %broadcast_select_fusion.6, f32[2,64,96,128]{3,1,2,0:T(8,128)S(1)} %fusion.37, s32[2,96]{1,0:T(2,128)S(1)} %bitcast.156), kind=kOutput, calls=%fused_computation.31 | convolution fusion | flops 1815103488 | bytes 9438720 | tf_op jit(solution)/shard_map/prkc,pjk->prjc/dot_general | solution.py:43
  80.4 2.4 copy.25
  82.9 4.1 %all-to-all-start = ((bf16[2,64,1,96,128]{4,3,0,2,1:T(8,128)(2,1)}), bf16[2,64,1,96,128]{4,3,0,2,1:T(8,128)(2,1)S(1)}, u32[]{:S(2)}, u32[]{:S(2)}) async-start(bf16[2,64,1,96,128]{4,3,0,2,1:T(8,128)(2,1)} %copy.25), calls=%async_computation | async-start | bytes 6291456 | tf_op jit(solution)/shard_map/all_to_all | solution.py:53
  87.0 37.5 %all-gather = s32[1,2,192]{1,0,2:T(1,128)S(1)} all-gather(s32[1,2,96]{1,0,2:T(1,128)S(1)} %copy.20), channel_id=2, replica_groups=mesh['section'=4,'dp'=4,'mp'=2] {'mp'}, dimensions={2}, use_global_device_ids=true | all-gather | bytes 2304 | tf_op jit(solution)/shard_map/all_gather | solution.py:52
  125.1 2.2 convolution_bitcast_fusion
  127.3 2.8 %reshape.59 = f32[2,32,12288]{2,1,0:T(8,128)S(1)} reshape(f32[2,32,96,128]{3,2,1,0:T(8,128)} %convolution_bitcast_fusion) | data formatting | bytes 6291456 | tf_op jit(solution)/shard_map/reshape | solution.py:58
  130.1 3.0 %add_convert_fusion = bf16[2,32,12288]{2,1,0:T(8,128)(2,1)} fusion(f32[2,32,12288]{2,1,0:T(8,128)S(1)} %reshape.59, bf16[2,64,12288]{2,1,0:T(8,128)(2,1)} %bitcast.146, s32[]{:T(128)S(6)} %select_n.26, pred[2,32]{1,0:T(4,128)(4,1)S(1)} %constant_dynamic-slice_fusion), kind=kLoop, calls=%fused_computation.41 | loop fusion | flops 3145728 | bytes 6291524 | tf_op jit(solution)/shard_map/convert_element_type | solution.py:60
  133.1 33.1 %reduce-scatter.2.cloned.1.call-done = bf16[2,2,96,32,128]{4,3,2,0,1:T(8,128)(2,1)} async-done(((bf16[2,2,96,128,128]{4,3,2,0,1:T(8,128)(2,1)}), bf16[2,2,96,32,128]{4,3,2,0,1:T(8,128)(2,1)}) %reduce-scatter.2.cloned.1.call-update) | async-done | bytes 3145744 | tf_op jit(solution)/shard_map/reduce_scatter | solution.py:67
  166.2 4.6 %copy.27 = bf16[1,2,2,96,32,128]{5,4,1,2,0,3:T(8,128)(2,1)} copy(bf16[1,2,2,96,32,128]{5,4,3,1,2,0:T(8,128)(2,1)} %bitcast.149) | data formatting | bytes 6291456 | tf_op jit(solution)/shard_map/convert_element_type | solution.py:71
  170.8 5.2 %all-to-all-start.1 = ((bf16[1,2,2,96,32,128]{5,4,1,2,0,3:T(8,128)(2,1)}), bf16[1,2,2,96,32,128]{5,4,1,2,0,3:T(8,128)(2,1)S(1)}, u32[]{:S(2)}, u32[]{:S(2)}) async-start(bf16[1,2,2,96,32,128]{5,4,1,2,0,3:T(8,128)(2,1)} %copy.27), calls=%async_computation.2 | async-start | bytes 6291456 | tf_op jit(solution)/shard_map/all_to_all | solution.py:70
  175.9 1.5 slice_bitcast_fusion.3
  177.4 1.9 collective-permute-start
  179.3 3.9 %collective-permute-start.1 = (bf16[32,12288]{1,0:T(8,128)(2,1)S(1)}, bf16[32,12288]{1,0:T(8,128)(2,1)S(1)}, u32[]{:S(2)}, u32[]{:S(2)}) collective-permute-start(bf16[32,12288]{1,0:T(8,128)(2,1)S(1)} %get-tuple-element.4), channel_id=1, source_target_pairs={{0,8},{8,16},{16,24},{1,9},{9,17},{17,25},{2,10},{10,18},{18,26},{... | collective-permute-start | bytes 2359304 | tf_op jit(solution)/shard_map/ppermute | solution.py:12
  183.3 78.7 %collective-permute-done = bf16[32,12288]{1,0:T(8,128)(2,1)S(1)} collective-permute-done((bf16[32,12288]{1,0:T(8,128)(2,1)S(1)}, bf16[32,12288]{1,0:T(8,128)(2,1)S(1)}, u32[]{:S(2)}, u32[]{:S(2)}) %collective-permute-start) | collective-permute-done | bytes 786464 | tf_op jit(solution)/shard_map/ppermute | solution.py:12
  262.0 1.3 maximum_bitcast_fusion
  263.3 0.9 copy_bitcast_fusion
  264.5 2.4 fusion.22
  (27 shorter events, 3.5 us)
Async XLA Ops:
  7.2 159.1 %reduce-scatter.2.cloned.1.call-start = ((), (), s32[]{:S(2)}) async-start(), calls=%async_computation.3 | async-start | bytes 15728640 | tf_op jit(solution)/shard_map/reduce_scatter | solution.py:67
  12.6 3.0 %copy-start.4 = (s32[2,1,1]{0,2,1:T(1,128)S(1)}, s32[2,1,1]{0,2,1:T(1,128)}, u32[]{:S(2)}) copy-start(s32[2,1,1]{0,2,1:T(1,128)} %param.11) | copy-start | bytes 28
  12.6 3.1 %copy-start.2 = (bf16[2,1,64,12288]{3,2,1,0:T(8,128)(2,1)S(1)}, bf16[2,1,64,12288]{3,2,1,0:T(8,128)(2,1)}, u32[]{:S(2)}) copy-start(bf16[2,1,64,12288]{3,2,1,0:T(8,128)(2,1)} %param.10) | copy-start | bytes 9437188
  57.8 2.6 copy-start
  65.8 0.7 copy-start.3
  65.8 1.9 copy-start.1
  82.9 41.8 %all-to-all-start = ((bf16[2,64,1,96,128]{4,3,0,2,1:T(8,128)(2,1)}), bf16[2,64,1,96,128]{4,3,0,2,1:T(8,128)(2,1)S(1)}, u32[]{:S(2)}, u32[]{:S(2)}) async-start(bf16[2,64,1,96,128]{4,3,0,2,1:T(8,128)(2,1)} %copy.25), calls=%async_computation | async-start | bytes 6291456 | tf_op jit(solution)/shard_map/all_to_all | solution.py:53
  170.8 92.5 %all-to-all-start.1 = ((bf16[1,2,2,96,32,128]{5,4,1,2,0,3:T(8,128)(2,1)}), bf16[1,2,2,96,32,128]{5,4,1,2,0,3:T(8,128)(2,1)S(1)}, u32[]{:S(2)}, u32[]{:S(2)}) async-start(bf16[1,2,2,96,32,128]{5,4,1,2,0,3:T(8,128)(2,1)} %copy.27), calls=%async_computation.2 | async-start | bytes 6291456 | tf_op jit(solution)/shard_map/all_to_all | solution.py:70
  177.4 84.6 %collective-permute-start = (bf16[32,12288]{1,0:T(8,128)(2,1)S(1)}, bf16[32,12288]{1,0:T(8,128)(2,1)S(1)}, u32[]{:S(2)}, u32[]{:S(2)}) collective-permute-start(bf16[32,12288]{1,0:T(8,128)(2,1)S(1)} %get-tuple-element.3), channel_id=1, source_target_pairs={{8,0},{16,8},{24,16},{9,1},{17,9},{25,17},{10,2},{18,10},{26,18},{... | collective-permute-start | bytes 2359304 | tf_op jit(solution)/shard_map/ppermute | solution.py:12
  179.3 82.7 %collective-permute-start.1 = (bf16[32,12288]{1,0:T(8,128)(2,1)S(1)}, bf16[32,12288]{1,0:T(8,128)(2,1)S(1)}, u32[]{:S(2)}, u32[]{:S(2)}) collective-permute-start(bf16[32,12288]{1,0:T(8,128)(2,1)S(1)} %get-tuple-element.4), channel_id=1, source_target_pairs={{0,8},{8,16},{16,24},{1,9},{9,17},{17,25},{2,10},{10,18},{18,26},{... | collective-permute-start | bytes 2359304 | tf_op jit(solution)/shard_map/ppermute | solution.py:12
Sparse Core Ops, SparseCore 0:
  66.0 100.2 reduce-scatter.1
where the time goes:
time: 274 us
  waiting for transfers between devices  112 us (41%)
  matrix products  43.1 us (16%)
  blocking collectives  37.5 us (14%)
  local copies, waits for them, and re-layouts  31.4 us (11%)
  other arithmetic  20.6 us (8%)
  starting transfers between devices  15.1 us (6%)
  between operations  14.2 us (5%)
    ppermute x2, waiting for transfers between devices, from_behind(): return lax.ppermute(block, axis, route)  78.7 us
    all_gather x1, blocking collectives, body(): all_index = lax.all_gather(index_in, 'mp', axis=1, tiled=True)  37.5 us
    reduce_scatter x1, waiting for transfers between devices, body(): lax.psum_scatter(stacked.astype(jnp.bfloat16), 'dp', scatter_dimension=3,...  33.1 us
    dot_general x1, matrix products, body(): jnp.einsum('prjd,pjcd->prjc', back, weight_out, preferred_element_type=jn...  11.4 us
    dot_general x1, matrix products, body(): jnp.einsum('prjc,pjcd->prjd', picked, weight_in, preferred_element_type=j...  7.27 us
    dot_general x1, matrix products, body(): jnp.einsum('prjc,prjd->pjcd', act, back, preferred_element_type=jnp.float32)  6.93 us
    unnamed x13, local copies, waits for them, and re-layouts  6.73 us
    dot_general x1, matrix products, body(): jnp.einsum('prjd,pjcd->prjc', grad_pre, weight_in, preferred_element_type...  6.39 us
  transfers between devices with their start and end apart: 5, of which 2 were waited for; matrix products, arithmetic and copies ran while one was open for 10% of the time, Pallas kernels for 0%

commit v1 on v0

v1 whole, which is shorter than its diff:
```python
import functools
import math

import jax
import jax.numpy as jnp
from jax import lax
from jax.experimental import pallas as pl
from jax.experimental.pallas import tpu as pltpu
from jax.sharding import PartitionSpec as P

SCALE = math.sqrt(2.0 / math.pi)
CUBIC = 0.044715


def tick_kernel(relay, per_step, len_ref, idx_in_ref, idx_out_ref, x_ref, g_ref, w_in_ref, w_out_ref,
                keep_in_ref, send_in_ref, keep_out_ref, send_out_ref, share_ref, acc_ref):
    step = pl.program_id(0)
    me = lax.axis_index("dp")
    rows, block = x_ref.shape[0], w_in_ref.shape[-1]
    piece = keep_in_ref.shape[2]
    pieces = block // piece
    live = lax.broadcasted_iota(jnp.int32, (rows, block), 0) < len_ref[relay, 0, 0]

    @pl.when(step == 0)
    def _():
        acc_ref[...] = jnp.zeros_like(acc_ref)

    def put(keep_ref, send_ref, i, value):
        value = value.astype(jnp.bfloat16)
        for q in range(pieces):
            part = value[q * piece:(q + 1) * piece]
            slot = q ^ me

            @pl.when(slot % 2 == 0)
            def _():
                keep_ref[slot // 2, i] = part

            @pl.when(slot % 2 == 1)
            def _():
                send_ref[slot // 2, i] = part

    for i in range(per_step):
        j = step * per_step + i
        from_block = idx_in_ref[0, relay, j]
        to_block = idx_out_ref[0, relay, j]
        picked = x_ref[:, pl.ds(pl.multiple_of(from_block * block, block), block)]
        back = g_ref[:, pl.ds(pl.multiple_of(to_block * block, block), block)]
        back = jnp.where(live, back, jnp.zeros_like(back))
        w_in = w_in_ref[i]
        w_out = w_out_ref[i]
        pre = jnp.dot(picked, w_in, preferred_element_type=jnp.float32)
        back_pre = lax.dot_general(back, w_out, (((1,), (1,)), ((), ())), preferred_element_type=jnp.float32)
        square = pre * pre
        th = jnp.tanh(SCALE * (pre + CUBIC * (square * pre)))
        cdf = 0.5 * (1.0 + th)
        act = (pre * cdf).astype(jnp.bfloat16)
        slope = cdf + (0.5 * pre) * ((1.0 - th) * (1.0 + th)) * (SCALE * (1.0 + (3.0 * CUBIC) * square))
        grad_pre = (back_pre * slope).astype(jnp.bfloat16)
        term = lax.dot_general(grad_pre, w_in, (((1,), (1,)), ((), ())), preferred_element_type=jnp.float32)
        acc_ref[from_block] += term
        over_rows = (((0,), (0,)), ((), ()))
        put(keep_in_ref, send_in_ref, i, lax.dot_general(picked, grad_pre, over_rows, preferred_element_type=jnp.float32))
        put(keep_out_ref, send_out_ref, i, lax.dot_general(act, back, over_rows, preferred_element_type=jnp.float32))

    @pl.when(step == pl.num_programs(0) - 1)
    def _():
        for b in range(acc_ref.shape[0]):
            share_ref[:, b * block:(b + 1) * block] = acc_ref[b].astype(jnp.bfloat16)


def tick(relay, n_dp, lengths, idx_in, idx_out, section_in, out_grad, w_in, w_out):
    rows, width = section_in.shape[2:]
    blocks, block = w_in.shape[2:4]
    per_step = math.gcd(blocks, 8)
    steps = blocks // per_step
    piece = block // n_dp
    whole = pl.BlockSpec((None, None, rows, width), lambda i, *_: (relay, 0, 0, 0))
    weight = pl.BlockSpec((None, None, per_step, block, block), lambda i, *_: (0, relay, i, 0, 0))
    slots = jax.ShapeDtypeStruct((n_dp // 2, blocks, piece, block), jnp.bfloat16)
    slots_spec = pl.BlockSpec((n_dp // 2, per_step, piece, block), lambda i, *_: (0, i, 0, 0))
    return pl.pallas_call(
        functools.partial(tick_kernel, relay, per_step),
        grid_spec=pltpu.PrefetchScalarGridSpec(
            num_scalar_prefetch=3,
            grid=(steps,),
            in_specs=[whole, whole, weight, weight],
            out_specs=[slots_spec] * 4 + [pl.BlockSpec((rows, width), lambda i, *_: (0, 0))],
            scratch_shapes=[pltpu.VMEM((width // block, rows, block), jnp.float32)],
        ),
        out_shape=[slots] * 4 + [jax.ShapeDtypeStruct((rows, width), jnp.bfloat16)],
        compiler_params=pltpu.CompilerParams(
            dimension_semantics=("arbitrary",), vmem_limit_bytes=40 * 1024 * 1024
        ),
        cost_estimate=pl.CostEstimate(
            flops=blocks * 10 * rows * block * block,
            bytes_accessed=blocks * block * block * 8 + rows * width * 6,
            transcendentals=blocks * rows * block,
        ),
        name=f"tick{relay}",
    )(lengths, idx_in, idx_out, section_in, out_grad, w_in, w_out)


def total_kernel(down_in, up_in, down_out, up_out, out):
    out[0] = down_in[...].astype(jnp.float32) + up_in[...].astype(jnp.float32)
    out[1] = down_out[...].astype(jnp.float32) + up_out[...].astype(jnp.float32)


def total_grads(down_in, up_in, down_out, up_out):
    sections, per, piece, block = down_in.shape
    same = pl.BlockSpec((None, per, piece, block), lambda l: (l, 0, 0, 0))
    mirror = pl.BlockSpec((None, per, piece, block), lambda l: (sections - 1 - l, 0, 0, 0))
    return pl.pallas_call(
        total_kernel,
        grid=(sections,),
        in_specs=[same, mirror, same, mirror],
        out_specs=pl.BlockSpec((None, 2, None, per, piece, block), lambda l: (l, 0, 0, 0, 0, 0)),
        out_shape=jax.ShapeDtypeStruct((sections, 2, 1, per, piece, block), jnp.float32),
        name="total",
    )(down_in, up_in, down_out, up_out)


def over_replicas(keep, send, n_dp):
    f32 = jnp.float32
    kept = [keep[k] for k in range(n_dp // 2)]
    got = lax.ppermute(send, "dp", [(d, d ^ 1) for d in range(n_dp)])
    got = [got[k] for k in range(n_dp // 2)]
    sums = [a.astype(f32) + b.astype(f32) for a, b in zip(kept, got)]
    bit = 2
    while bit < n_dp:
        route = [(d, d ^ bit) for d in range(n_dp)]
        odd = jnp.stack([v.astype(jnp.bfloat16) for v in sums[1::2]]) if len(sums) > 2 else sums[1].astype(jnp.bfloat16)
        came = lax.ppermute(odd, "dp", route)
        came = [came[k] for k in range(len(sums) // 2)] if len(sums) > 2 else [came]
        sums = [a + b.astype(f32) for a, b in zip(sums[0::2], came)]
        bit *= 2
    return sums[0].astype(jnp.bfloat16)


def from_behind(value, axis, distance):
    devices = range(lax.axis_size(axis))
    route = [(i - distance, i) for i in devices if i - distance in devices]
    return lax.ppermute(value, axis, route)


def body(section_in, out_grad, lengths, w_in, w_out, idx_in, idx_out):
    n_dp = lax.axis_size("dp")
    n_mp = lax.axis_size("mp")
    sections = lax.axis_size("section")
    rows, width = section_in.shape[2:]
    share_rows = rows // n_mp
    first = lax.axis_index("mp") * share_rows
    moved, passed = [], []
    for relay in range(2):
        keep_in, send_in, keep_out, send_out, share = tick(
            relay, n_dp, lengths, idx_in, idx_out, section_in, out_grad, w_in, w_out
        )
        for keep, send in ((keep_in, send_in), (keep_out, send_out)):
            mine = over_replicas(keep, send, n_dp)
            mine = mine.reshape(sections, -1, *mine.shape[1:])
            moved.append(lax.all_to_all(mine, "section", split_axis=0, concat_axis=0, tiled=True))
        terms = lax.all_to_all(share.reshape(n_mp, share_rows, width), "mp", split_axis=0, concat_axis=0, tiled=True)
        own = lax.dynamic_slice_in_dim(out_grad[relay, 0], first, share_rows, 0)
        live = first + lax.broadcasted_iota(jnp.int32, own.shape, 0) < lengths[relay, 0, 0]
        own = jnp.where(live, own, jnp.zeros_like(own)).astype(jnp.float32)
        dx = (own + jnp.sum(terms.astype(jnp.float32), axis=0)).astype(jnp.bfloat16)
        passed.append(from_behind(dx, "section", 1 if relay else -1))
    grads = total_grads(moved[0], moved[2], moved[1], moved[3])
    return jnp.stack(passed, axis=0)[:, None], grads


def solution(mesh):
    placed = (
        P(None, "section", "dp", None),
        P(None, "section", "dp", None),
        P(None, "section", "dp"),
        P("section", None, "mp", None, None),
        P("section", None, "mp", None, None),
        P("section", None, "mp"),
        P("section", None, "mp"),
    )
    return jax.shard_map(
        body,
        mesh=mesh,
        in_specs=placed,
        out_specs=(
            P(None, "section", ("dp", "mp"), None),
            P(None, None, "mp", "section", "dp", None),
        ),
        check_vma=False,
    )
```

time: 274 us -> 273 us (level)
  the two profiles are of different devices: /device:TPU:8 before, /device:TPU:0 now
where the time goes in v1:
time: 273 us; the launch traced here: 272 us
  Pallas kernels  113 us (41%)
  waiting for transfers between devices  54.2 us (20%)
  starting transfers between devices  51.7 us (19%)
  other arithmetic  32.6 us (12%)
  local copies, waits for them, and re-layouts  19.4 us (7%)
    pallas_call x2, Pallas kernels, tick(): pl.pallas_call(functools.partial(tick_kernel, relay, per_step), grid_spec...  109 us
    all_to_all x4, starting transfers between devices, body(): lax.all_to_all(mine, 'section', split_axis=0, concat_axis=0, tiled=True)  29.2 us
    ppermute x4, waiting for transfers between devices, over_replicas(): came = lax.ppermute(odd, 'dp', route)  25.7 us
    all_to_all x4, waiting for transfers between devices, body(): lax.all_to_all(mine, 'section', split_axis=0, concat_axis=0, tiled=True)  25 us
    unnamed x47, local copies, waits for them, and re-layouts  16.9 us
    convert_element_type x4, other arithmetic, over_replicas(): return sums[0].astype(jnp.bfloat16)  10.2 us
    all_to_all x2, starting transfers between devices, body(): lax.all_to_all(share.reshape(n_mp, share_rows, width), 'mp', split_axis=0...  9.55 us
    convert_element_type x4, other arithmetic, over_replicas(): sums[1].astype(jnp.bfloat16)  8.05 us
  transfers between devices with their start and end apart: 16, of which 7 were waited for; matrix products, arithmetic and copies ran while one was open for 13% of the time, Pallas kernels for 20%

profile of v1, /device:TPU:0, one launch (start us, length us, event | category | flops | bytes accessed | tf_op | source)
XLA Modules:
  0.0 272.1 jit_solution(12988248645659115785)
XLA Ops:
  1.4 1.9 copy-done
  3.3 1.9 copy-done.2
  6.5 54.6 %tick1.1 = (bf16[2,96,32,128]{3,2,1,0:T(8,128)(2,1)S(1)}, bf16[2,96,32,128]{3,2,1,0:T(8,128)(2,1)}, bf16[2,96,32,128]{3,2,1,0:T(8,128)(2,1)S(1)}, bf16[2,96,32,1...) custom-call(s32[2,1,1]{2,1,0:T(1,128)S(1)} %copy.9.len_ref, s32[1,2,96]{2,1,0:T(2,128)S(1)} %copy-done.14, ...), custom_call_target="tpu_custom_call" | custom-call | flops 1006632960 | bytes 17301504 | tf_op jit(solution)/shard_map/tick1/pallas_call | solution.py:81
  66.5 4.9 %all-to-all-start.1 = ((bf16[2,32,12288]{2,1,0:T(8,128)(2,1)}), bf16[2,32,12288]{2,1,0:T(8,128)(2,1)}, u32[]{:S(2)}, u32[]{:S(2)}) async-start(bf16[2,32,12288]{2,1,0:T(8,128)(2,1)} %bitcast.45), calls=%async_computation.1 | async-start | bytes 3145728 | tf_op jit(solution)/shard_map/all_to_all | solution.py:161
  71.6 1.9 copy-done.3
  73.4 54.6 %tick0.1 = (bf16[2,96,32,128]{3,2,1,0:T(8,128)(2,1)S(1)}, bf16[2,96,32,128]{3,2,1,0:T(8,128)(2,1)}, bf16[2,96,32,128]{3,2,1,0:T(8,128)(2,1)S(1)}, bf16[2,96,32,128]{3,2,1,0:T(8,128)(2,1)}, bf16[64,12288]{1,0:T(8,128)(2,1)S(1)}) custom-call(s32[2,1,1]{2,1,0:T(1,128)S(1)} %copy.9.len_ref, s32[1,2,96]{2,1,0:T(2,128)S(1)} %copy-done.15, ...), custom_call_target="tpu_custom_call" | custom-call | flops 1006632960 | bytes 17301504 | tf_op jit(solution)/shard_map/tick0/pallas_call | solution.py:81
  132.4 2.2 fusion.5
  134.7 2.3 collective-permute-start.5
  137.0 4.7 %all-to-all-start = ((bf16[2,32,12288]{2,1,0:T(8,128)(2,1)}), bf16[2,32,12288]{2,1,0:T(8,128)(2,1)}, u32[]{:S(2)}, u32[]{:S(2)}) async-start(bf16[2,32,12288]{2,1,0:T(8,128)(2,1)} %bitcast.44), calls=%async_computation | async-start | bytes 3145728 | tf_op jit(solution)/shard_map/all_to_all | solution.py:161
  143.5 12.0 %collective-permute-done.5 = bf16[96,32,128]{2,1,0:T(8,128)(2,1)} collective-permute-done((bf16[96,32,128]{2,1,0:T(8,128)(2,1)}, bf16[96,32,128]{2,1,0:T(8,128)(2,1)}, u32[]{:S(2)}, u32[]{:S(2)}) %collective-permute-start.5) | collective-permute-done | bytes 786464 | tf_op jit(solution)/shard_map/ppermute | solution.py:132
  155.5 2.8 %fusion.2 = bf16[96,32,128]{2,1,0:T(8,128)(2,1)} fusion(bf16[96,32,128]{2,1,0:T(8,128)(2,1)} %collective-permute-done.5, bf16[2,96,32,128]{3,2,1,0:T(8,128)(2,1)} %collective-permute-done.4, bf16[2,96,32,128]{3,2,1,0:T(8,128)(2,1)} %copy-done.12), kind=kLoop, calls=%fused_computation.8 | loop fusion | flops 2359296 | bytes 3145728 | tf_op jit(solution)/shard_map/convert_element_type | solution.py:136
  158.3 3.5 %all-to-all-done = bf16[2,32,12288]{2,1,0:T(8,128)(2,1)} async-done(((bf16[2,32,12288]{2,1,0:T(8,128)(2,1)}), bf16[2,32,12288]{2,1,0:T(8,128)(2,1)}, u32[]{:S(2)}, u32[]{:S(2)}) %all-to-all-start) | async-done | bytes 1572896 | tf_op jit(solution)/shard_map/all_to_all | solution.py:161
  161.8 4.9 %all-to-all-start.3 = ((bf16[4,24,32,128]{3,2,1,0:T(8,128)(2,1)}), bf16[4,24,32,128]{3,2,1,0:T(8,128)(2,1)}, u32[]{:S(2)}, u32[]{:S(2)}) async-start(bf16[4,24,32,128]{3,2,1,0:T(8,128)(2,1)} %bitcast.14), calls=%async_computation.3 | async-start | bytes 1572864 | tf_op jit(solution)/shard_map/all_to_all | solution.py:160
  170.5 3.1 %convert_reduce_fusion = f32[32,12288]{1,0:T(8,128)} fusion(bf16[2,32,12288]{2,1,0:T(8,128)(2,1)} %all-to-all-done.1), kind=kLoop, calls=%fused_computation | loop fusion | flops 1179648 | bytes 3145728 | tf_op jit(solution)/shard_map/reduce_sum | solution.py:165
  173.6 2.3 fusion.4
  177.3 11.2 %collective-permute-done.9 = bf16[96,32,128]{2,1,0:T(8,128)(2,1)S(1)} collective-permute-done((bf16[96,32,128]{2,1,0:T(8,128)(2,1)S(1)}, bf16[96,32,128]{2,1,0:T(8,128)(2,1)S(1)}, u32[]{:S(2)}, u32[]{:S(2)}) %collective-permute-start.9) | collective-permute-done | bytes 786464 | tf_op jit(solution)/shard_map/ppermute | solution.py:132
  188.5 2.3 fusion
  190.9 5.2 %all-to-all-start.5 = ((bf16[4,24,32,128]{3,2,1,0:T(8,128)(2,1)}), bf16[4,24,32,128]{3,2,1,0:T(8,128)(2,1)}, u32[]{:S(2)}, u32[]{:S(2)}) async-start(bf16[4,24,32,128]{3,2,1,0:T(8,128)(2,1)} %bitcast.46), calls=%async_computation.5 | async-start | bytes 1572864 | tf_op jit(solution)/shard_map/all_to_all | solution.py:160
  196.1 2.3 add_convert_fusion.4
  198.4 5.0 %collective-permute-start.1 = (bf16[32,12288]{1,0:T(8,128)(2,1)}, bf16[32,12288]{1,0:T(8,128)(2,1)}, u32[]{:S(2)}, u32[]{:S(2)}) collective-permute-start(bf16[32,12288]{1,0:T(8,128)(2,1)} %add_convert_fusion.4), channel_id=1, source_target_pairs={{0,8},{8,16},{16,24},{1,9},{9,17},{17,25},{2,10},{10,18},{18,26},{... | collective-permute-start | bytes 2359304 | tf_op jit(solution)/shard_map/ppermute | solution.py:142
  203.4 3.0 %convert_reduce_fusion.1 = f32[32,12288]{1,0:T(8,128)} fusion(bf16[2,32,12288]{2,1,0:T(8,128)(2,1)} %all-to-all-done), kind=kLoop, calls=%fused_computation.1 | loop fusion | flops 1179648 | bytes 3145728 | tf_op jit(solution)/shard_map/reduce_sum | solution.py:165
  206.4 2.2 fusion.6
  209.1 2.5 fusion.3
  212.5 4.9 %all-to-all-start.2 = ((bf16[4,24,32,128]{3,2,1,0:T(8,128)(2,1)}), bf16[4,24,32,128]{3,2,1,0:T(8,128)(2,1)}, u32[]{:S(2)}, u32[]{:S(2)}) async-start(bf16[4,24,32,128]{3,2,1,0:T(8,128)(2,1)} %bitcast.47), calls=%async_computation.2 | async-start | bytes 1572864 | tf_op jit(solution)/shard_map/all_to_all | solution.py:160
  217.4 2.3 add_convert_fusion.5
  221.0 2.6 collective-permute-done.7
  223.6 2.6 fusion.1
  226.1 8.7 %all-to-all-done.2.down_in = bf16[4,24,32,128]{3,2,1,0:T(8,128)(2,1)} async-done(((bf16[4,24,32,128]{3,2,1,0:T(8,128)(2,1)}), bf16[4,24,32,128]{3,2,1,0:T(8,128)(2,1)}, u32[]{:S(2)}, u32[]{:S(2)}) %all-to-all-start.2) | async-done | bytes 786464 | tf_op jit(solution)/shard_map/all_to_all | solution.py:160
  234.8 14.2 %all-to-all-start.4 = ((bf16[4,24,32,128]{3,2,1,0:T(8,128)(2,1)}), bf16[4,24,32,128]{3,2,1,0:T(8,128)(2,1)S(1)}, u32[]{:S(2)}, u32[]{:S(2)}) async-start(bf16[4,24,32,128]{3,2,1,0:T(8,128)(2,1)} %bitcast.17), calls=%async_computation.4 | async-start | bytes 1572864 | tf_op jit(solution)/shard_map/all_to_all | solution.py:160
  249.0 2.4 maximum_bitcast_fusion
  251.4 15.5 %all-to-all-done.4.down_out = bf16[4,24,32,128]{3,2,1,0:T(8,128)(2,1)S(1)} async-done(((bf16[4,24,32,128]{3,2,1,0:T(8,128)(2,1)}), bf16[4,24,32,128]{3,2,1,0:T(8,128)(2,1)S(1)}, u32[]{:S(2)}, u32[]{:S(2)}) %all-to-all-start.4) | async-done | bytes 786464 | tf_op jit(solution)/shard_map/all_to_all | solution.py:160
  267.8 4.3 %total.1 = f32[4,2,1,24,32,128]{5,4,3,2,1,0:T(8,128)} custom-call(bf16[4,24,32,128]{3,2,1,0:T(8,128)(2,1)} %all-to-all-done.2.down_in, bf16[4,24,32,128]{3,2,1,0:T(8,128)(2,1)} %all-to-all-done.3.up_in, bf16[4,24,32,128]{3,2,1,0:T(8,128)(2,1)} %copy-done.21, bf16[4,24,32,128]{3,2,1,0:T(8,128)(2,1)} %all-to-all-done.5.up_out), custom_call_target="tpu_custom_call" | custom-call | tf_op jit(solution)/shard_map/total/pallas_call | solution.py:112
  (67 shorter events, 22.9 us)
Async XLA Ops:
  1.4 1.9 copy-start
  3.3 1.9 copy-start.2
  6.5 65.0 %copy-start.17 = (s32[1,2,96]{2,1,0:T(2,128)S(1)}, s32[1,2,96]{2,1,0:T(2,128)}, u32[]{:S(2)}) copy-start(s32[1,2,96]{2,1,0:T(2,128)} %idx_out_ref.3) | copy-start | bytes 2308
  63.4 1.2 copy-start.12
  65.7 66.7 %collective-permute-start.4 = (bf16[2,96,32,128]{3,2,1,0:T(8,128)(2,1)}, bf16[2,96,32,128]{3,2,1,0:T(8,128)(2,1)}, u32[]{:S(2)}, u32[]{:S(2)}) collective-permute-start(bf16[2,96,32,128]{3,2,1,0:T(8,128)(2,1)} %get-tuple-element.17), channel_id=1, source_target_pairs={{0,2},{2,0},{4,6},{6,4},{1,3},{3,1},{5,7},{7,5},{8,10},{10,8},{12,... | collective-permute-start | bytes 4718600 | tf_op jit(solution)/shard_map/ppermute | solution.py:125
  66.5 5.0 %copy-start.1 = (bf16[2,1,64,12288]{3,2,1,0:T(8,128)(2,1)S(1)}, bf16[2,1,64,12288]{3,2,1,0:T(8,128)(2,1)}, u32[]{:S(2)}) copy-start(bf16[2,1,64,12288]{3,2,1,0:T(8,128)(2,1)} %g_ref.3) | copy-start | bytes 9437188
  66.5 5.0 %copy-start.15 = (s32[1,2,96]{2,1,0:T(2,128)S(1)}, s32[1,2,96]{2,1,0:T(2,128)}, u32[]{:S(2)}) copy-start(s32[1,2,96]{2,1,0:T(2,128)} %idx_in_ref.3) | copy-start | bytes 2308
  66.5 70.4 %all-to-all-start.1 = ((bf16[2,32,12288]{2,1,0:T(8,128)(2,1)}), bf16[2,32,12288]{2,1,0:T(8,128)(2,1)}, u32[]{:S(2)}, u32[]{:S(2)}) async-start(bf16[2,32,12288]{2,1,0:T(8,128)(2,1)} %bitcast.45), calls=%async_computation.1 | async-start | bytes 3145728 | tf_op jit(solution)/shard_map/all_to_all | solution.py:161
  71.4 95.2 %collective-permute-start.8 = (bf16[2,96,32,128]{3,2,1,0:T(8,128)(2,1)}, bf16[2,96,32,128]{3,2,1,0:T(8,128)(2,1)}, u32[]{:S(2)}, u32[]{:S(2)}) collective-permute-start(bf16[2,96,32,128]{3,2,1,0:T(8,128)(2,1)} %copy-done.18), channel_id=1, source_target_pairs={{0,2},{2,0},{4,6},{6,4},{1,3},{3,1},{5,7},{7,5},{8,10},{10,8},{12,... | collective-permute-start | bytes 4718600 | tf_op jit(solution)/shard_map/ppermute | solution.py:125
  71.5 1.9 copy-start.3
  73.4 59.0 %copy-start.13 = (bf16[2,96,32,128]{3,2,1,0:T(8,128)(2,1)S(1)}, bf16[2,96,32,128]{3,2,1,0:T(8,128)(2,1)}, u32[]{:S(2)}) copy-start(bf16[2,96,32,128]{3,2,1,0:T(8,128)(2,1)} %copy-done.12) | copy-start | bytes 4718596
  129.2 1.2 copy-start.6
  130.4 1.2 copy-start.8
  131.5 42.0 %collective-permute-start.2 = (bf16[2,96,32,128]{3,2,1,0:T(8,128)(2,1)}, bf16[2,96,32,128]{3,2,1,0:T(8,128)(2,1)}, u32[]{:S(2)}, u32[]{:S(2)}) collective-permute-start(bf16[2,96,32,128]{3,2,1,0:T(8,128)(2,1)} %get-tuple-element.15), channel_id=1, source_target_pairs={{0,2},{2,0},{4,6},{6,4},{1,3},{3,1},{5,7},{7,5},{8,10},{10,8},{12,... | collective-permute-start | bytes 4718600 | tf_op jit(solution)/shard_map/ppermute | solution.py:125
  132.4 73.9 %collective-permute-start.6 = (bf16[2,96,32,128]{3,2,1,0:T(8,128)(2,1)}, bf16[2,96,32,128]{3,2,1,0:T(8,128)(2,1)}, u32[]{:S(2)}, u32[]{:S(2)}) collective-permute-start(bf16[2,96,32,128]{3,2,1,0:T(8,128)(2,1)} %get-tuple-element.19), channel_id=1, source_target_pairs={{0,2},{2,0},{4,6},{6,4},{1,3},{3,1},{5,7},{7,5},{8,10},{10,8},{12,... | collective-permute-start | bytes 4718600 | tf_op jit(solution)/shard_map/ppermute | solution.py:125
  134.7 20.8 %collective-permute-start.5 = (bf16[96,32,128]{2,1,0:T(8,128)(2,1)}, bf16[96,32,128]{2,1,0:T(8,128)(2,1)}, u32[]{:S(2)}, u32[]{:S(2)}) collective-permute-start(bf16[96,32,128]{2,1,0:T(8,128)(2,1)} %fusion.5), channel_id=1, source_target_pairs={{0,4},{2,6},{4,0},{6,2},{1,5},{3,7},{5,1},{7,3},{8,12},{10,14},{12... | collective-permute-start | bytes 2359304 | tf_op jit(solution)/shard_map/ppermute | solution.py:132
  137.0 24.8 %all-to-all-start = ((bf16[2,32,12288]{2,1,0:T(8,128)(2,1)}), bf16[2,32,12288]{2,1,0:T(8,128)(2,1)}, u32[]{:S(2)}, u32[]{:S(2)}) async-start(bf16[2,32,12288]{2,1,0:T(8,128)(2,1)} %bitcast.44), calls=%async_computation | async-start | bytes 3145728 | tf_op jit(solution)/shard_map/all_to_all | solution.py:161
  158.3 8.4 %copy-start.11 = (bf16[2,96,32,128]{3,2,1,0:T(8,128)(2,1)S(1)}, bf16[2,96,32,128]{3,2,1,0:T(8,128)(2,1)}, u32[]{:S(2)}) copy-start(bf16[2,96,32,128]{3,2,1,0:T(8,128)(2,1)} %copy-done.10) | copy-start | bytes 4718596
  161.8 29.1 %all-to-all-start.3 = ((bf16[4,24,32,128]{3,2,1,0:T(8,128)(2,1)}), bf16[4,24,32,128]{3,2,1,0:T(8,128)(2,1)}, u32[]{:S(2)}, u32[]{:S(2)}) async-start(bf16[4,24,32,128]{3,2,1,0:T(8,128)(2,1)} %bitcast.14), calls=%async_computation.3 | async-start | bytes 1572864 | tf_op jit(solution)/shard_map/all_to_all | solution.py:160
  166.6 2.0 copy-start.22
  168.0 20.5 %collective-permute-start.9 = (bf16[96,32,128]{2,1,0:T(8,128)(2,1)S(1)}, bf16[96,32,128]{2,1,0:T(8,128)(2,1)S(1)}, u32[]{:S(2)}, u32[]{:S(2)}) collective-permute-start(bf16[96,32,128]{2,1,0:T(8,128)(2,1)S(1)} %fusion.7), channel_id=1, source_target_pairs={{0,4},{2,6},{4,0},{6,2},{1,5},{3,7},{5,1},{7,3},{8,12},{10,14},{12... | collective-permute-start | bytes 2359304 | tf_op jit(solution)/shard_map/ppermute | solution.py:132
  170.5 3.1 %copy-start.9 = (bf16[2,96,32,128]{3,2,1,0:T(8,128)(2,1)S(1)}, bf16[2,96,32,128]{3,2,1,0:T(8,128)(2,1)}, u32[]{:S(2)}) copy-start(bf16[2,96,32,128]{3,2,1,0:T(8,128)(2,1)} %copy-done.8) | copy-start | bytes 4718596
  175.9 33.3 %collective-permute-start.3 = (bf16[96,32,128]{2,1,0:T(8,128)(2,1)}, bf16[96,32,128]{2,1,0:T(8,128)(2,1)}, u32[]{:S(2)}, u32[]{:S(2)}) collective-permute-start(bf16[96,32,128]{2,1,0:T(8,128)(2,1)} %fusion.4), channel_id=1, source_target_pairs={{0,4},{2,6},{4,0},{6,2},{1,5},{3,7},{5,1},{7,3},{8,12},{10,14},{12... | collective-permute-start | bytes 2359304 | tf_op jit(solution)/shard_map/ppermute | solution.py:132
  190.9 5.2 %copy-start.20 = (f32[32,12288]{1,0:T(8,128)S(1)}, f32[32,12288]{1,0:T(8,128)}, u32[]{:S(2)}) copy-start(f32[32,12288]{1,0:T(8,128)} %convert_reduce_fusion) | copy-start | bytes 4718596
  190.9 21.6 %all-to-all-start.5 = ((bf16[4,24,32,128]{3,2,1,0:T(8,128)(2,1)}), bf16[4,24,32,128]{3,2,1,0:T(8,128)(2,1)}, u32[]{:S(2)}, u32[]{:S(2)}) async-start(bf16[4,24,32,128]{3,2,1,0:T(8,128)(2,1)} %bitcast.46), calls=%async_computation.5 | async-start | bytes 1572864 | tf_op jit(solution)/shard_map/all_to_all | solution.py:160
  198.4 8.0 %copy-start.7 = (bf16[2,96,32,128]{3,2,1,0:T(8,128)(2,1)S(1)}, bf16[2,96,32,128]{3,2,1,0:T(8,128)(2,1)}, u32[]{:S(2)}) copy-start(bf16[2,96,32,128]{3,2,1,0:T(8,128)(2,1)} %copy-done.6) | copy-start | bytes 4718596
  198.4 50.5 %collective-permute-start.1 = (bf16[32,12288]{1,0:T(8,128)(2,1)}, bf16[32,12288]{1,0:T(8,128)(2,1)}, u32[]{:S(2)}, u32[]{:S(2)}) collective-permute-start(bf16[32,12288]{1,0:T(8,128)(2,1)} %add_convert_fusion.4), channel_id=1, source_target_pairs={{0,8},{8,16},{16,24},{1,9},{9,17},{17,25},{2,10},{10,18},{18,26},{... | collective-permute-start | bytes 2359304 | tf_op jit(solution)/shard_map/ppermute | solution.py:142
  208.6 15.0 %collective-permute-start.7 = (bf16[96,32,128]{2,1,0:T(8,128)(2,1)}, bf16[96,32,128]{2,1,0:T(8,128)(2,1)}, u32[]{:S(2)}, u32[]{:S(2)}) collective-permute-start(bf16[96,32,128]{2,1,0:T(8,128)(2,1)} %fusion.6), channel_id=1, source_target_pairs={{0,4},{2,6},{4,0},{6,2},{1,5},{3,7},{5,1},{7,3},{8,12},{10,14},{12... | collective-permute-start | bytes 2359304 | tf_op jit(solution)/shard_map/ppermute | solution.py:132
  211.7 5.8 %copy-start.19 = (f32[32,12288]{1,0:T(8,128)S(1)}, f32[32,12288]{1,0:T(8,128)}, u32[]{:S(2)}) copy-start(f32[32,12288]{1,0:T(8,128)} %convert_reduce_fusion.1) | copy-start | bytes 4718596
  212.5 22.3 %all-to-all-start.2 = ((bf16[4,24,32,128]{3,2,1,0:T(8,128)(2,1)}), bf16[4,24,32,128]{3,2,1,0:T(8,128)(2,1)}, u32[]{:S(2)}, u32[]{:S(2)}) async-start(bf16[4,24,32,128]{3,2,1,0:T(8,128)(2,1)} %bitcast.47), calls=%async_computation.2 | async-start | bytes 1572864 | tf_op jit(solution)/shard_map/all_to_all | solution.py:160
  219.7 29.3 %collective-permute-start = (bf16[32,12288]{1,0:T(8,128)(2,1)}, bf16[32,12288]{1,0:T(8,128)(2,1)S(1)}, u32[]{:S(2)}, u32[]{:S(2)}) collective-permute-start(bf16[32,12288]{1,0:T(8,128)(2,1)} %add_convert_fusion.5), channel_id=1, source_target_pairs={{8,0},{16,8},{24,16},{9,1},{17,9},{25,17},{10,2},{18,10},{26,18},{... | collective-permute-start | bytes 2359304 | tf_op jit(solution)/shard_map/ppermute | solution.py:142
  234.8 32.0 %all-to-all-start.4 = ((bf16[4,24,32,128]{3,2,1,0:T(8,128)(2,1)}), bf16[4,24,32,128]{3,2,1,0:T(8,128)(2,1)S(1)}, u32[]{:S(2)}, u32[]{:S(2)}) async-start(bf16[4,24,32,128]{3,2,1,0:T(8,128)(2,1)} %bitcast.17), calls=%async_computation.4 | async-start | bytes 1572864 | tf_op jit(solution)/shard_map/all_to_all | solution.py:160
  (7 other events, 6.9 us)

commit v2 on v1

--- a/solution.py
+++ b/solution.py
@@ -10,6 +10,7 @@
 
 SCALE = math.sqrt(2.0 / math.pi)
 CUBIC = 0.044715
+GROUP = 4
 
 
 def tick_kernel(relay, per_step, len_ref, idx_in_ref, idx_out_ref, x_ref, g_ref, w_in_ref, w_out_ref,
@@ -25,42 +26,43 @@
     def _():
         acc_ref[...] = jnp.zeros_like(acc_ref)
 
+    odd = me % 2 == 1
+
     def put(keep_ref, send_ref, i, value):
         value = value.astype(jnp.bfloat16)
-        for q in range(pieces):
-            part = value[q * piece:(q + 1) * piece]
-            slot = q ^ me
+        for k in range(pieces // 2):
+            low = value[2 * k * piece:(2 * k + 1) * piece]
+            high = value[(2 * k + 1) * piece:(2 * k + 2) * piece]
+            keep_ref[k ^ (me // 2), i] = jnp.where(odd, high, low)
+            send_ref[k ^ (me // 2), i] = jnp.where(odd, low, high)
 
-            @pl.when(slot % 2 == 0)
-            def _():
-                keep_ref[slot // 2, i] = part
-
-            @pl.when(slot % 2 == 1)
-            def _():
-                send_ref[slot // 2, i] = part
-
-    for i in range(per_step):
-        j = step * per_step + i
-        from_block = idx_in_ref[0, relay, j]
-        to_block = idx_out_ref[0, relay, j]
-        picked = x_ref[:, pl.ds(pl.multiple_of(from_block * block, block), block)]
-        back = g_ref[:, pl.ds(pl.multiple_of(to_block * block, block), block)]
-        back = jnp.where(live, back, jnp.zeros_like(back))
-        w_in = w_in_ref[i]
-        w_out = w_out_ref[i]
-        pre = jnp.dot(picked, w_in, preferred_element_type=jnp.float32)
-        back_pre = lax.dot_general(back, w_out, (((1,), (1,)), ((), ())), preferred_element_type=jnp.float32)
-        square = pre * pre
-        th = jnp.tanh(SCALE * (pre + CUBIC * (square * pre)))
-        cdf = 0.5 * (1.0 + th)
-        act = (pre * cdf).astype(jnp.bfloat16)
-        slope = cdf + (0.5 * pre) * ((1.0 - th) * (1.0 + th)) * (SCALE * (1.0 + (3.0 * CUBIC) * square))
-        grad_pre = (back_pre * slope).astype(jnp.bfloat16)
-        term = lax.dot_general(grad_pre, w_in, (((1,), (1,)), ((), ())), preferred_element_type=jnp.float32)
-        acc_ref[from_block] += term
-        over_rows = (((0,), (0,)), ((), ()))
-        put(keep_in_ref, send_in_ref, i, lax.dot_general(picked, grad_pre, over_rows, preferred_element_type=jnp.float32))
-        put(keep_out_ref, send_out_ref, i, lax.dot_general(act, back, over_rows, preferred_element_type=jnp.float32))
+    f32 = jnp.float32
+    over_last = (((1,), (1,)), ((), ()))
+    over_rows = (((0,), (0,)), ((), ()))
+    for start in range(0, per_step, GROUP):
+        group = range(start, min(start + GROUP, per_step))
+        sources = [idx_in_ref[0, relay, step * per_step + i] for i in group]
+        targets = [idx_out_ref[0, relay, step * per_step + i] for i in group]
+        picked = [x_ref[:, pl.ds(pl.multiple_of(b * block, block), block)] for b in sources]
+        back = [g_ref[:, pl.ds(pl.multiple_of(b * block, block), block)] for b in targets]
+        back = [jnp.where(live, v, jnp.zeros_like(v)) for v in back]
+        pre = [jnp.dot(v, w_in_ref[i], preferred_element_type=f32) for v, i in zip(picked, group)]
+        back_pre = [lax.dot_general(v, w_out_ref[i], over_last, preferred_element_type=f32) for v, i in zip(back, group)]
+        act, grad_pre = [], []
+        for v, up in zip(pre, back_pre):
+            square = v * v
+            th = jnp.tanh(SCALE * (v + CUBIC * (square * v)))
+            cdf = 0.5 * (1.0 + th)
+            act.append((v * cdf).astype(jnp.bfloat16))
+            slope = cdf + (0.5 * v) * ((1.0 - th) * (1.0 + th)) * (SCALE * (1.0 + (3.0 * CUBIC) * square))
+            grad_pre.append((up * slope).astype(jnp.bfloat16))
+        terms = [lax.dot_general(v, w_in_ref[i], over_last, preferred_element_type=f32) for v, i in zip(grad_pre, group)]
+        grad_in = [lax.dot_general(a, v, over_rows, preferred_element_type=f32) for a, v in zip(picked, grad_pre)]
+        grad_out = [lax.dot_general(a, v, over_rows, preferred_element_type=f32) for a, v in zip(act, back)]
+        for i, b, term, g_in, g_out in zip(group, sources, terms, grad_in, grad_out):
+            acc_ref[b] += term
+            put(keep_in_ref, send_in_ref, i, g_in)
+            put(keep_out_ref, send_out_ref, i, g_out)
 
     @pl.when(step == pl.num_programs(0) - 1)
     def _():
@@ -89,7 +91,7 @@
         ),
         out_shape=[slots] * 4 + [jax.ShapeDtypeStruct((rows, width), jnp.bfloat16)],
         compiler_params=pltpu.CompilerParams(
-            dimension_semantics=("arbitrary",), vmem_limit_bytes=40 * 1024 * 1024
+            dimension_semantics=("arbitrary",), vmem_limit_bytes=56 * 1024 * 1024
         ),
         cost_estimate=pl.CostEstimate(
             flops=blocks * 10 * rows * block * block,
@@ -100,23 +102,19 @@
     )(lengths, idx_in, idx_out, section_in, out_grad, w_in, w_out)
 
 
-def total_kernel(down_in, up_in, down_out, up_out, out):
-    out[0] = down_in[...].astype(jnp.float32) + up_in[...].astype(jnp.float32)
-    out[1] = down_out[...].astype(jnp.float32) + up_out[...].astype(jnp.float32)
+def total_grads(down_in, up_in, down_out, up_out):
+    n = len(down_in)
+    me = lax.axis_index("section")
 
+    def by_section(parts):
+        stacked = jnp.stack(parts)
+        return jnp.stack([lax.dynamic_index_in_dim(stacked, (me - s) % n, 0, keepdims=False) for s in range(n)])
 
-def total_grads(down_in, up_in, down_out, up_out):
-    sections, per, piece, block = down_in.shape
-    same = pl.BlockSpec((None, per, piece, block), lambda l: (l, 0, 0, 0))
-    mirror = pl.BlockSpec((None, per, piece, block), lambda l: (sections - 1 - l, 0, 0, 0))
-    return pl.pallas_call(
-        total_kernel,
-        grid=(sections,),
-        in_specs=[same, mirror, same, mirror],
-        out_specs=pl.BlockSpec((None, 2, None, per, piece, block), lambda l: (l, 0, 0, 0, 0, 0)),
-        out_shape=jax.ShapeDtypeStruct((sections, 2, 1, per, piece, block), jnp.float32),
-        name="total",
-    )(down_in, up_in, down_out, up_out)
+    def both(down, up):
+        down, up = by_section(down), by_section(up)
+        return down.astype(jnp.float32) + jnp.flip(up, 0).astype(jnp.float32)
+
+    return jnp.stack([both(down_in, up_in), both(down_out, up_out)], axis=1)[:, :, None]
 
 
 def over_replicas(keep, send, n_dp):
@@ -134,6 +132,16 @@
         sums = [a + b.astype(f32) for a, b in zip(sums[0::2], came)]
         bit *= 2
     return sums[0].astype(jnp.bfloat16)
+
+
+def exchange(parts, axis):
+    n = lax.axis_size(axis)
+    me = lax.axis_index(axis)
+    got = []
+    for k in range(n):
+        part = lax.dynamic_index_in_dim(parts, (me + k) % n, 0, keepdims=False)
+        got.append(part if k == 0 else lax.ppermute(part, axis, [(i, (i + k) % n) for i in range(n)]))
+    return got
 
 
 def from_behind(value, axis, distance):
@@ -157,12 +165,12 @@
         for keep, send in ((keep_in, send_in), (keep_out, send_out)):
             mine = over_replicas(keep, send, n_dp)
             mine = mine.reshape(sections, -1, *mine.shape[1:])
-            moved.append(lax.all_to_all(mine, "section", split_axis=0, concat_axis=0, tiled=True))
-        terms = lax.all_to_all(share.reshape(n_mp, share_rows, width), "mp", split_axis=0, concat_axis=0, tiled=True)
+            moved.append(exchange(mine, "section"))
+        terms = exchange(share.reshape(n_mp, share_rows, width), "mp")
         own = lax.dynamic_slice_in_dim(out_grad[relay, 0], first, share_rows, 0)
         live = first + lax.broadcasted_iota(jnp.int32, own.shape, 0) < lengths[relay, 0, 0]
         own = jnp.where(live, own, jnp.zeros_like(own)).astype(jnp.float32)
-        dx = (own + jnp.sum(terms.astype(jnp.float32), axis=0)).astype(jnp.bfloat16)
+        dx = functools.reduce(lambda a, b: a + b.astype(jnp.float32), terms, own).astype(jnp.bfloat16)
         passed.append(from_behind(dx, "section", 1 if relay else -1))
     grads = total_grads(moved[0], moved[2], moved[1], moved[3])
     return jnp.stack(passed, axis=0)[:, None], grads

time: 273 us -> 192 us (0.70)
  Pallas kernels: 113 us -> 33.8 us
  waiting for transfers between devices: 54.2 us -> 81.6 us
  other arithmetic: 32.6 us -> 18.2 us
  local copies, waits for them, and re-layouts: 19.4 us -> 7.18 us
    pallas_call x2, Pallas kernels: 109 us -> 33.8 us  [tick(): pl.pallas_call(functools.partial(tick_kernel, relay, per_step), grid_spec...]
    all_to_all x6 -> x0, starting transfers between devices: 38.7 us -> none  [the longest x4 29.2 us: body(): lax.all_to_all(mine, 'section', split_axis=0, concat_axis=0, tiled=True)]
    ppermute x0 -> x14, waiting for transfers between devices: none -> 38.7 us  [exchange(): lax.ppermute(part, axis, [(i, (i + k) % n) for i in range(n)])]
    ppermute x0 -> x14, starting transfers between devices: none -> 38.5 us  [exchange(): lax.ppermute(part, axis, [(i, (i + k) % n) for i in range(n)])]
    all_to_all x6 -> x0, waiting for transfers between devices: 28.4 us -> none  [the longest x4 25 us: body(): lax.all_to_all(mine, 'section', split_axis=0, concat_axis=0, tiled=True)]
    unnamed x47 -> x15, local copies, waits for them, and re-layouts: 16.9 us -> 1.62 us
    ppermute x2, waiting for transfers between devices: 0.01 us -> 9.36 us  [from_behind(): return lax.ppermute(value, axis, route)]
    ppermute x4, waiting for transfers between devices: 25.7 us -> 33.6 us  [over_replicas(): came = lax.ppermute(odd, 'dp', route)]
  transfers between devices with their start and end apart: 16 -> 24, of which waited for: 7 -> 10; matrix products, arithmetic and copies ran while one was open for 13% -> 10% of each run, Pallas kernels for 20% -> 9%
where the time goes in v2:
time: 192 us; the launch traced here: 191 us
  waiting for transfers between devices  81.6 us (42%)
  starting transfers between devices  49.4 us (26%)
  Pallas kernels  33.8 us (18%)
  other arithmetic  18.2 us (9%)
  local copies, waits for them, and re-layouts  7.18 us (4%)
    ppermute x14, waiting for transfers between devices, exchange(): lax.ppermute(part, axis, [(i, (i + k) % n) for i in range(n)])  38.7 us
    ppermute x14, starting transfers between devices, exchange(): lax.ppermute(part, axis, [(i, (i + k) % n) for i in range(n)])  38.5 us
    pallas_call x2, Pallas kernels, tick(): pl.pallas_call(functools.partial(tick_kernel, relay, per_step), grid_spec...  33.8 us
    ppermute x4, waiting for transfers between devices, over_replicas(): came = lax.ppermute(odd, 'dp', route)  33.6 us
    ppermute x2, waiting for transfers between devices, from_behind(): return lax.ppermute(value, axis, route)  9.36 us
    ppermute x4, starting transfers between devices, over_replicas(): came = lax.ppermute(odd, 'dp', route)  5.22 us
    ppermute x2, starting transfers between devices, from_behind(): return lax.ppermute(value, axis, route)  4.93 us
    convert_element_type x4, other arithmetic, over_replicas(): return sums[0].astype(jnp.bfloat16)  4.63 us
  transfers between devices with their start and end apart: 24, of which 10 were waited for; matrix products, arithmetic and copies ran while one was open for 10% of the time, Pallas kernels for 9%

profile of v2, /device:TPU:0, one launch (start us, length us, event | category | flops | bytes accessed | tf_op | source)
XLA Modules:
  0.0 191.4 jit_solution(14443069246737320535)
XLA Ops:
  2.0 16.8 %tick1.1 = (bf16[2,96,32,128]{3,2,1,0:T(8,128)(2,1)}, bf16[2,96,32,128]{3,2,1,0:T(8,128)(2,1)}, bf16[2,96,32,128]{3,2,1,0:T(8,128)(2,1)}, bf16[2,96,32,128]{3,2,1,0:T(8,128)(2,1)}, bf16[64,12288]{1,0:T(8,128)(2,1)}) custom-call(s32[2,1,1]{2,1,0:T(1,128)} %copy.9.len_ref, s32[1,2,96]{2,1,0:T(2,128)} %idx_in_ref.3, s32[1,2,96]{2,1,0:T(2,128)} %idx_out_ref.3, ...), custom_call_target="tpu_custom_call" | custom-call | flops 1006632960 | bytes 17301504 | tf_op jit(solution)/shard_map/tick1/pallas_call | solution.py:83
  18.8 2.1 %dynamic-slice_bitcast_fusion = bf16[32,12288]{1,0:T(8,128)(2,1)} fusion(bf16[2,32,12288]{2,1,0:T(8,128)(2,1)} %bitcast.100, s32[]{:T(128)S(6)} %select_n.165), kind=kLoop, calls=%fused_computation.34 | loop fusion | bytes 1572868 | tf_op jit(solution)/shard_map/jit(dynamic_index_in_dim)/squeeze | solution.py:142
  20.9 3.0 %collective-permute-start.2 = (bf16[32,12288]{1,0:T(8,128)(2,1)}, bf16[32,12288]{1,0:T(8,128)(2,1)}, u32[]{:S(2)}, u32[]{:S(2)}) collective-permute-start(bf16[32,12288]{1,0:T(8,128)(2,1)} %dynamic-slice_bitcast_fusion), channel_id=1, source_target_pairs={{0,1},{1,0},{2,3},{3,2},{4,5},{5,4},{6,7},{7,6},{8,9},{9,8},{10,11... | collective-permute-start | bytes 2359304 | tf_op jit(solution)/shard_map/ppermute | solution.py:143
  24.3 17.0 %tick0.1 = (bf16[2,96,32,128]{3,2,1,0:T(8,128)(2,1)}, bf16[2,96,32,128]{3,2,1,0:T(8,128)(2,1)}, bf16[2,96,32,128]{3,2,1,0:T(8,128)(2,1)}, bf16[2,96,32,128]{3,2,1,0:T(8,128)(2,1)}, bf16[64,12288]{1,0:T(8,128)(2,1)}) custom-call(s32[2,1,1]{2,1,0:T(1,128)} %copy.9.len_ref, s32[1,2,96]{2,1,0:T(2,128)} %idx_in_ref.3, s32[1,2,96]{2,1,0:T(2,128)} %idx_out_ref.3, ...), custom_call_target="tpu_custom_call" | custom-call | flops 1006632960 | bytes 17301504 | tf_op jit(solution)/shard_map/tick0/pallas_call | solution.py:83
  41.4 2.1 %dynamic-slice_bitcast_fusion.1 = bf16[32,12288]{1,0:T(8,128)(2,1)} fusion(bf16[2,32,12288]{2,1,0:T(8,128)(2,1)} %bitcast.102, s32[]{:T(128)S(6)} %select_n.165), kind=kLoop, calls=%fused_computation.35 | loop fusion | bytes 1572868 | tf_op jit(solution)/shard_map/jit(dynamic_index_in_dim)/squeeze | solution.py:142
  46.5 1.9 fusion.1
  48.4 14.9 %collective-permute-done = bf16[32,12288]{1,0:T(8,128)(2,1)} collective-permute-done((bf16[32,12288]{1,0:T(8,128)(2,1)}, bf16[32,12288]{1,0:T(8,128)(2,1)}, u32[]{:S(2)}, u32[]{:S(2)}) %collective-permute-start) | collective-permute-done | bytes 786464 | tf_op jit(solution)/shard_map/ppermute | solution.py:143
  63.2 3.5 %collective-permute-start.3 = (bf16[32,12288]{1,0:T(8,128)(2,1)S(1)}, bf16[32,12288]{1,0:T(8,128)(2,1)S(1)}, u32[]{:S(2)}, u32[]{:S(2)}) collective-permute-start(bf16[32,12288]{1,0:T(8,128)(2,1)S(1)} %fusion.1), channel_id=1, source_target_pairs={{0,8},{8,16},{16,24},{1,9},{9,17},{17,25},{2,10},{10,18},{18,26},{... | collective-permute-start | bytes 2359304 | tf_op jit(solution)/shard_map/ppermute | solution.py:150
  66.8 1.7 fusion.3
  71.3 1.6 collective-permute-start.10
  76.1 1.6 collective-permute-start.5
  77.9 4.9 %collective-permute-done.3 = bf16[32,12288]{1,0:T(8,128)(2,1)S(1)} collective-permute-done((bf16[32,12288]{1,0:T(8,128)(2,1)S(1)}, bf16[32,12288]{1,0:T(8,128)(2,1)S(1)}, u32[]{:S(2)}, u32[]{:S(2)}) %collective-permute-start.3) | collective-permute-done | bytes 786464 | tf_op jit(solution)/shard_map/ppermute | solution.py:150
  82.8 1.5 collective-permute-start.15
  84.3 4.5 %collective-permute-done.1 = bf16[32,12288]{1,0:T(8,128)(2,1)S(1)} collective-permute-done((bf16[32,12288]{1,0:T(8,128)(2,1)S(1)}, bf16[32,12288]{1,0:T(8,128)(2,1)S(1)}, u32[]{:S(2)}, u32[]{:S(2)}) %collective-permute-start.1) | collective-permute-done | bytes 786464 | tf_op jit(solution)/shard_map/ppermute | solution.py:150
  90.1 1.7 collective-permute-done.10
  91.8 1.4 fusion.6
  93.3 4.7 %collective-permute-start.13 = (bf16[24,32,128]{2,1,0:T(8,128)(2,1)S(1)}, bf16[24,32,128]{2,1,0:T(8,128)(2,1)S(1)}, u32[]{:S(2)}, u32[]{:S(2)}) collective-permute-start(bf16[24,32,128]{2,1,0:T(8,128)(2,1)S(1)} %get-tuple-element.29), channel_id=1, source_target_pairs={{0,24},{8,0},{16,8},{24,16},{1,25},{9,1},{17,9},{25,17},{2,26},{10... | collective-permute-start | bytes 589832 | tf_op jit(solution)/shard_map/ppermute | solution.py:143
  98.1 10.6 %collective-permute-done.20 = bf16[96,32,128]{2,1,0:T(8,128)(2,1)S(1)} collective-permute-done((bf16[96,32,128]{2,1,0:T(8,128)(2,1)S(1)}, bf16[96,32,128]{2,1,0:T(8,128)(2,1)S(1)}, u32[]{:S(2)}, u32[]{:S(2)}) %collective-permute-start.20) | collective-permute-done | bytes 786464 | tf_op jit(solution)/shard_map/ppermute | solution.py:130
  108.7 2.6 %collective-permute-start.11 = (bf16[24,32,128]{2,1,0:T(8,128)(2,1)S(1)}, bf16[24,32,128]{2,1,0:T(8,128)(2,1)S(1)}, u32[]{:S(2)}, u32[]{:S(2)}) collective-permute-start(bf16[24,32,128]{2,1,0:T(8,128)(2,1)S(1)} %get-tuple-element.31), channel_id=1, source_target_pairs={{0,8},{8,16},{16,24},{24,0},{1,9},{9,17},{17,25},{25,1},{2,10},{10... | collective-permute-start | bytes 589832 | tf_op jit(solution)/shard_map/ppermute | solution.py:143
  111.3 1.4 fusion.4
  112.8 12.7 %collective-permute-done.5 = bf16[96,32,128]{2,1,0:T(8,128)(2,1)S(1)} collective-permute-done((bf16[96,32,128]{2,1,0:T(8,128)(2,1)S(1)}, bf16[96,32,128]{2,1,0:T(8,128)(2,1)S(1)}, u32[]{:S(2)}, u32[]{:S(2)}) %collective-permute-start.5) | collective-permute-done | bytes 786464 | tf_op jit(solution)/shard_map/ppermute | solution.py:130
  125.5 4.7 %collective-permute-start.23 = (bf16[24,32,128]{2,1,0:T(8,128)(2,1)S(1)}, bf16[24,32,128]{2,1,0:T(8,128)(2,1)S(1)}, u32[]{:S(2)}, u32[]{:S(2)}) collective-permute-start(bf16[24,32,128]{2,1,0:T(8,128)(2,1)S(1)} %get-tuple-element.45), channel_id=1, source_target_pairs={{0,24},{8,0},{16,8},{24,16},{1,25},{9,1},{17,9},{25,17},{2,26},{10... | collective-permute-start | bytes 589832 | tf_op jit(solution)/shard_map/ppermute | solution.py:143
  131.6 8.6 %collective-permute-done.15 = bf16[96,32,128]{2,1,0:T(8,128)(2,1)S(1)} collective-permute-done((bf16[96,32,128]{2,1,0:T(8,128)(2,1)S(1)}, bf16[96,32,128]{2,1,0:T(8,128)(2,1)S(1)}, u32[]{:S(2)}, u32[]{:S(2)}) %collective-permute-start.15) | collective-permute-done | bytes 786464 | tf_op jit(solution)/shard_map/ppermute | solution.py:130
  140.2 3.4 %collective-permute-start.22 = (bf16[24,32,128]{2,1,0:T(8,128)(2,1)S(1)}, bf16[24,32,128]{2,1,0:T(8,128)(2,1)S(1)}, u32[]{:S(2)}, u32[]{:S(2)}) collective-permute-start(bf16[24,32,128]{2,1,0:T(8,128)(2,1)S(1)} %get-tuple-element.46), channel_id=1, source_target_pairs={{0,16},{8,24},{16,0},{24,8},{1,17},{9,25},{17,1},{25,9},{2,18},{10... | collective-permute-start | bytes 589832 | tf_op jit(solution)/shard_map/ppermute | solution.py:143
  144.0 1.7 collective-permute-start.21
  145.7 2.2 %collective-permute-start.8 = (bf16[24,32,128]{2,1,0:T(8,128)(2,1)S(1)}, bf16[24,32,128]{2,1,0:T(8,128)(2,1)S(1)}, u32[]{:S(2)}, u32[]{:S(2)}) collective-permute-start(bf16[24,32,128]{2,1,0:T(8,128)(2,1)S(1)} %get-tuple-element.37), channel_id=1, source_target_pairs={{0,24},{8,0},{16,8},{24,16},{1,25},{9,1},{17,9},{25,17},{2,26},{10... | collective-permute-start | bytes 589832 | tf_op jit(solution)/shard_map/ppermute | solution.py:143
  148.8 9.3 %collective-permute-done.22 = bf16[24,32,128]{2,1,0:T(8,128)(2,1)S(1)} collective-permute-done((bf16[24,32,128]{2,1,0:T(8,128)(2,1)S(1)}, bf16[24,32,128]{2,1,0:T(8,128)(2,1)S(1)}, u32[]{:S(2)}, u32[]{:S(2)}) %collective-permute-start.22) | collective-permute-done | bytes 196640 | tf_op jit(solution)/shard_map/ppermute | solution.py:143
  158.1 3.7 %collective-permute-start.18 = (bf16[24,32,128]{2,1,0:T(8,128)(2,1)S(1)}, bf16[24,32,128]{2,1,0:T(8,128)(2,1)S(1)}, u32[]{:S(2)}, u32[]{:S(2)}) collective-permute-start(bf16[24,32,128]{2,1,0:T(8,128)(2,1)S(1)} %get-tuple-element.53), channel_id=1, source_target_pairs={{0,24},{8,0},{16,8},{24,16},{1,25},{9,1},{17,9},{25,17},{2,26},{10... | collective-permute-start | bytes 589832 | tf_op jit(solution)/shard_map/ppermute | solution.py:143
  161.8 11.7 %collective-permute-start.17 = (bf16[24,32,128]{2,1,0:T(8,128)(2,1)S(1)}, bf16[24,32,128]{2,1,0:T(8,128)(2,1)S(1)}, u32[]{:S(2)}, u32[]{:S(2)}) collective-permute-start(bf16[24,32,128]{2,1,0:T(8,128)(2,1)S(1)} %get-tuple-element.54), channel_id=1, source_target_pairs={{0,16},{8,24},{16,0},{24,8},{1,17},{9,25},{17,1},{25,9},{2,18},{10... | collective-permute-start | bytes 589832 | tf_op jit(solution)/shard_map/ppermute | solution.py:143
  173.8 5.3 %collective-permute-done.7 = bf16[24,32,128]{2,1,0:T(8,128)(2,1)S(1)} collective-permute-done((bf16[24,32,128]{2,1,0:T(8,128)(2,1)S(1)}, bf16[24,32,128]{2,1,0:T(8,128)(2,1)S(1)}, u32[]{:S(2)}, u32[]{:S(2)}) %collective-permute-start.7) | collective-permute-done | bytes 196640 | tf_op jit(solution)/shard_map/ppermute | solution.py:143
  179.3 9.1 %collective-permute-done.17 = bf16[24,32,128]{2,1,0:T(8,128)(2,1)S(1)} collective-permute-done((bf16[24,32,128]{2,1,0:T(8,128)(2,1)S(1)}, bf16[24,32,128]{2,1,0:T(8,128)(2,1)S(1)}, u32[]{:S(2)}, u32[]{:S(2)}) %collective-permute-start.17) | collective-permute-done | bytes 196640 | tf_op jit(solution)/shard_map/ppermute | solution.py:143
  189.4 2.0 %maximum_bitcast_fusion = f32[4,2,1,24,32,128]{5,4,3,2,1,0:T(8,128)} fusion(f32[4,1,24,32,128]{4,3,2,1,0:T(8,128)S(1)} %get-tuple-element.58, f32[4,1,24,32,128]{4,3,2,1,0:T(8,128)S(1)} %get-tuple-element.59), kind=kLoop, calls=%fused_computation | loop fusion | flops 786432 | bytes 6291456 | tf_op jit(solution)/shard_map/broadcast_in_dim | solution.py:117
  (66 shorter events, 16.4 us)
Async XLA Ops:
  20.9 25.3 %collective-permute-start.2 = (bf16[32,12288]{1,0:T(8,128)(2,1)}, bf16[32,12288]{1,0:T(8,128)(2,1)}, u32[]{:S(2)}, u32[]{:S(2)}) collective-permute-start(bf16[32,12288]{1,0:T(8,128)(2,1)} %dynamic-slice_bitcast_fusion), channel_id=1, source_target_pairs={{0,1},{1,0},{2,3},{3,2},{4,5},{5,4},{6,7},{7,6},{8,9},{9,8},{10,11... | collective-permute-start | bytes 2359304 | tf_op jit(solution)/shard_map/ppermute | solution.py:143
  23.8 44.6 %collective-permute-start.9 = (bf16[2,96,32,128]{3,2,1,0:T(8,128)(2,1)}, bf16[2,96,32,128]{3,2,1,0:T(8,128)(2,1)}, u32[]{:S(2)}, u32[]{:S(2)}) collective-permute-start(bf16[2,96,32,128]{3,2,1,0:T(8,128)(2,1)} %get-tuple-element.17), channel_id=1, source_target_pairs={{0,2},{2,0},{4,6},{6,4},{1,3},{3,1},{5,7},{7,5},{8,10},{10,8},{12,... | collective-permute-start | bytes 4718600 | tf_op jit(solution)/shard_map/ppermute | solution.py:123
  23.8 47.4 %collective-permute-start.19 = (bf16[2,96,32,128]{3,2,1,0:T(8,128)(2,1)}, bf16[2,96,32,128]{3,2,1,0:T(8,128)(2,1)}, u32[]{:S(2)}, u32[]{:S(2)}) collective-permute-start(bf16[2,96,32,128]{3,2,1,0:T(8,128)(2,1)} %get-tuple-element.21), channel_id=1, source_target_pairs={{0,2},{2,0},{4,6},{6,4},{1,3},{3,1},{5,7},{7,5},{8,10},{10,8},{12,... | collective-permute-start | bytes 4718600 | tf_op jit(solution)/shard_map/ppermute | solution.py:123
  24.3 19.2 %copy-start = (bf16[2,1,64,12288]{3,2,1,0:T(8,128)(2,1)S(1)}, bf16[2,1,64,12288]{3,2,1,0:T(8,128)(2,1)}, u32[]{:S(2)}) copy-start(bf16[2,1,64,12288]{3,2,1,0:T(8,128)(2,1)} %g_ref.3) | copy-start | bytes 9437188
  43.5 19.8 %collective-permute-start = (bf16[32,12288]{1,0:T(8,128)(2,1)}, bf16[32,12288]{1,0:T(8,128)(2,1)}, u32[]{:S(2)}, u32[]{:S(2)}) collective-permute-start(bf16[32,12288]{1,0:T(8,128)(2,1)} %dynamic-slice_bitcast_fusion.1), channel_id=1, source_target_pairs={{0,1},{1,0},{2,3},{3,2},{4,5},{5,4},{6,7},{7,6},{8,9},{9,8},{10,11... | collective-permute-start | bytes 2359304 | tf_op jit(solution)/shard_map/ppermute | solution.py:143
  43.5 0.7 copy-start.6
  43.5 30.7 %collective-permute-start.4 = (bf16[2,96,32,128]{3,2,1,0:T(8,128)(2,1)}, bf16[2,96,32,128]{3,2,1,0:T(8,128)(2,1)}, u32[]{:S(2)}, u32[]{:S(2)}) collective-permute-start(bf16[2,96,32,128]{3,2,1,0:T(8,128)(2,1)} %get-tuple-element.15), channel_id=1, source_target_pairs={{0,2},{2,0},{4,6},{6,4},{1,3},{3,1},{5,7},{7,5},{8,10},{10,8},{12,... | collective-permute-start | bytes 4718600 | tf_op jit(solution)/shard_map/ppermute | solution.py:123
  46.2 30.0 %collective-permute-start.14 = (bf16[2,96,32,128]{3,2,1,0:T(8,128)(2,1)}, bf16[2,96,32,128]{3,2,1,0:T(8,128)(2,1)S(1)}, u32[]{:S(2)}, u32[]{:S(2)}) collective-permute-start(bf16[2,96,32,128]{3,2,1,0:T(8,128)(2,1)} %get-tuple-element.19), channel_id=1, source_target_pairs={{0,2},{2,0},{4,6},{6,4},{1,3},{3,1},{5,7},{7,5},{8,10},{10,8},{12,... | collective-permute-start | bytes 4718600 | tf_op jit(solution)/shard_map/ppermute | solution.py:123
  46.5 20.3 %copy-start.1 = (bf16[64,12288]{1,0:T(8,128)(2,1)S(1)}, bf16[64,12288]{1,0:T(8,128)(2,1)}, u32[]{:S(2)}) copy-start(bf16[64,12288]{1,0:T(8,128)(2,1)} %get-tuple-element.12) | copy-start | bytes 4718596
  63.2 19.5 %collective-permute-start.3 = (bf16[32,12288]{1,0:T(8,128)(2,1)S(1)}, bf16[32,12288]{1,0:T(8,128)(2,1)S(1)}, u32[]{:S(2)}, u32[]{:S(2)}) collective-permute-start(bf16[32,12288]{1,0:T(8,128)(2,1)S(1)} %fusion.1), channel_id=1, source_target_pairs={{0,8},{8,16},{16,24},{1,9},{9,17},{17,25},{2,10},{10,18},{18,26},{... | collective-permute-start | bytes 2359304 | tf_op jit(solution)/shard_map/ppermute | solution.py:150
  66.8 3.1 %copy-start.5 = (bf16[2,96,32,128]{3,2,1,0:T(8,128)(2,1)S(1)}, bf16[2,96,32,128]{3,2,1,0:T(8,128)(2,1)}, u32[]{:S(2)}) copy-start(bf16[2,96,32,128]{3,2,1,0:T(8,128)(2,1)} %get-tuple-element.16) | copy-start | bytes 4718596
  68.4 4.4 %copy-start.3 = (bf16[2,96,32,128]{3,2,1,0:T(8,128)(2,1)S(1)}, bf16[2,96,32,128]{3,2,1,0:T(8,128)(2,1)}, u32[]{:S(2)}) copy-start(bf16[2,96,32,128]{3,2,1,0:T(8,128)(2,1)} %get-tuple-element.20) | copy-start | bytes 4718596
  68.5 20.3 %collective-permute-start.1 = (bf16[32,12288]{1,0:T(8,128)(2,1)S(1)}, bf16[32,12288]{1,0:T(8,128)(2,1)S(1)}, u32[]{:S(2)}, u32[]{:S(2)}) collective-permute-start(bf16[32,12288]{1,0:T(8,128)(2,1)S(1)} %fusion.3), channel_id=1, source_target_pairs={{8,0},{16,8},{24,16},{9,1},{17,9},{25,17},{10,2},{18,10},{26,18},{... | collective-permute-start | bytes 2359304 | tf_op jit(solution)/shard_map/ppermute | solution.py:150
  71.2 3.5 %copy-start.4 = (bf16[2,96,32,128]{3,2,1,0:T(8,128)(2,1)S(1)}, bf16[2,96,32,128]{3,2,1,0:T(8,128)(2,1)}, u32[]{:S(2)}) copy-start(bf16[2,96,32,128]{3,2,1,0:T(8,128)(2,1)} %get-tuple-element.14) | copy-start | bytes 4718596
  71.3 20.5 %collective-permute-start.10 = (bf16[96,32,128]{2,1,0:T(8,128)(2,1)S(1)}, bf16[96,32,128]{2,1,0:T(8,128)(2,1)S(1)}, u32[]{:S(2)}, u32[]{:S(2)}) collective-permute-start(bf16[96,32,128]{2,1,0:T(8,128)(2,1)S(1)} %fusion.9), channel_id=1, source_target_pairs={{0,4},{2,6},{4,0},{6,2},{1,5},{3,7},{5,1},{7,3},{8,12},{10,14},{12... | collective-permute-start | bytes 2359304 | tf_op jit(solution)/shard_map/ppermute | solution.py:130
  74.2 3.6 %copy-start.2 = (bf16[2,96,32,128]{3,2,1,0:T(8,128)(2,1)S(1)}, bf16[2,96,32,128]{3,2,1,0:T(8,128)(2,1)}, u32[]{:S(2)}) copy-start(bf16[2,96,32,128]{3,2,1,0:T(8,128)(2,1)} %get-tuple-element.18) | copy-start | bytes 4718596
  74.2 34.5 %collective-permute-start.20 = (bf16[96,32,128]{2,1,0:T(8,128)(2,1)S(1)}, bf16[96,32,128]{2,1,0:T(8,128)(2,1)S(1)}, u32[]{:S(2)}, u32[]{:S(2)}) collective-permute-start(bf16[96,32,128]{2,1,0:T(8,128)(2,1)S(1)} %fusion.11), channel_id=1, source_target_pairs={{0,4},{2,6},{4,0},{6,2},{1,5},{3,7},{5,1},{7,3},{8,12},{10,14},{12... | collective-permute-start | bytes 2359304 | tf_op jit(solution)/shard_map/ppermute | solution.py:130
  76.1 49.4 %collective-permute-start.5 = (bf16[96,32,128]{2,1,0:T(8,128)(2,1)S(1)}, bf16[96,32,128]{2,1,0:T(8,128)(2,1)S(1)}, u32[]{:S(2)}, u32[]{:S(2)}) collective-permute-start(bf16[96,32,128]{2,1,0:T(8,128)(2,1)S(1)} %fusion.8), channel_id=1, source_target_pairs={{0,4},{2,6},{4,0},{6,2},{1,5},{3,7},{5,1},{7,3},{8,12},{10,14},{12... | collective-permute-start | bytes 2359304 | tf_op jit(solution)/shard_map/ppermute | solution.py:130
  82.8 57.4 %collective-permute-start.15 = (bf16[96,32,128]{2,1,0:T(8,128)(2,1)S(1)}, bf16[96,32,128]{2,1,0:T(8,128)(2,1)S(1)}, u32[]{:S(2)}, u32[]{:S(2)}) collective-permute-start(bf16[96,32,128]{2,1,0:T(8,128)(2,1)S(1)} %fusion.10), channel_id=1, source_target_pairs={{0,4},{2,6},{4,0},{6,2},{1,5},{3,7},{5,1},{7,3},{8,12},{10,14},{12... | collective-permute-start | bytes 2359304 | tf_op jit(solution)/shard_map/ppermute | solution.py:130
  93.3 50.7 %collective-permute-start.13 = (bf16[24,32,128]{2,1,0:T(8,128)(2,1)S(1)}, bf16[24,32,128]{2,1,0:T(8,128)(2,1)S(1)}, u32[]{:S(2)}, u32[]{:S(2)}) collective-permute-start(bf16[24,32,128]{2,1,0:T(8,128)(2,1)S(1)} %get-tuple-element.29), channel_id=1, source_target_pairs={{0,24},{8,0},{16,8},{24,16},{1,25},{9,1},{17,9},{25,17},{2,26},{10... | collective-permute-start | bytes 589832 | tf_op jit(solution)/shard_map/ppermute | solution.py:143
  98.1 47.6 %collective-permute-start.12 = (bf16[24,32,128]{2,1,0:T(8,128)(2,1)S(1)}, bf16[24,32,128]{2,1,0:T(8,128)(2,1)S(1)}, u32[]{:S(2)}, u32[]{:S(2)}) collective-permute-start(bf16[24,32,128]{2,1,0:T(8,128)(2,1)S(1)} %get-tuple-element.30), channel_id=1, source_target_pairs={{0,16},{8,24},{16,0},{24,8},{1,17},{9,25},{17,1},{25,9},{2,18},{10... | collective-permute-start | bytes 589832 | tf_op jit(solution)/shard_map/ppermute | solution.py:143
  108.7 39.2 %collective-permute-start.11 = (bf16[24,32,128]{2,1,0:T(8,128)(2,1)S(1)}, bf16[24,32,128]{2,1,0:T(8,128)(2,1)S(1)}, u32[]{:S(2)}, u32[]{:S(2)}) collective-permute-start(bf16[24,32,128]{2,1,0:T(8,128)(2,1)S(1)} %get-tuple-element.31), channel_id=1, source_target_pairs={{0,8},{8,16},{16,24},{24,0},{1,9},{9,17},{17,25},{25,1},{2,10},{10... | collective-permute-start | bytes 589832 | tf_op jit(solution)/shard_map/ppermute | solution.py:143
  125.5 22.6 %collective-permute-start.23 = (bf16[24,32,128]{2,1,0:T(8,128)(2,1)S(1)}, bf16[24,32,128]{2,1,0:T(8,128)(2,1)S(1)}, u32[]{:S(2)}, u32[]{:S(2)}) collective-permute-start(bf16[24,32,128]{2,1,0:T(8,128)(2,1)S(1)} %get-tuple-element.45), channel_id=1, source_target_pairs={{0,24},{8,0},{16,8},{24,16},{1,25},{9,1},{17,9},{25,17},{2,26},{10... | collective-permute-start | bytes 589832 | tf_op jit(solution)/shard_map/ppermute | solution.py:143
  140.2 17.9 %collective-permute-start.22 = (bf16[24,32,128]{2,1,0:T(8,128)(2,1)S(1)}, bf16[24,32,128]{2,1,0:T(8,128)(2,1)S(1)}, u32[]{:S(2)}, u32[]{:S(2)}) collective-permute-start(bf16[24,32,128]{2,1,0:T(8,128)(2,1)S(1)} %get-tuple-element.46), channel_id=1, source_target_pairs={{0,16},{8,24},{16,0},{24,8},{1,17},{9,25},{17,1},{25,9},{2,18},{10... | collective-permute-start | bytes 589832 | tf_op jit(solution)/shard_map/ppermute | solution.py:143
  144.0 17.8 %collective-permute-start.21 = (bf16[24,32,128]{2,1,0:T(8,128)(2,1)S(1)}, bf16[24,32,128]{2,1,0:T(8,128)(2,1)S(1)}, u32[]{:S(2)}, u32[]{:S(2)}) collective-permute-start(bf16[24,32,128]{2,1,0:T(8,128)(2,1)S(1)} %get-tuple-element.47), channel_id=1, source_target_pairs={{0,8},{8,16},{16,24},{24,0},{1,9},{9,17},{17,25},{25,1},{2,10},{10... | collective-permute-start | bytes 589832 | tf_op jit(solution)/shard_map/ppermute | solution.py:143
  145.7 28.0 %collective-permute-start.8 = (bf16[24,32,128]{2,1,0:T(8,128)(2,1)S(1)}, bf16[24,32,128]{2,1,0:T(8,128)(2,1)S(1)}, u32[]{:S(2)}, u32[]{:S(2)}) collective-permute-start(bf16[24,32,128]{2,1,0:T(8,128)(2,1)S(1)} %get-tuple-element.37), channel_id=1, source_target_pairs={{0,24},{8,0},{16,8},{24,16},{1,25},{9,1},{17,9},{25,17},{2,26},{10... | collective-permute-start | bytes 589832 | tf_op jit(solution)/shard_map/ppermute | solution.py:143
  147.9 31.2 %collective-permute-start.7 = (bf16[24,32,128]{2,1,0:T(8,128)(2,1)S(1)}, bf16[24,32,128]{2,1,0:T(8,128)(2,1)S(1)}, u32[]{:S(2)}, u32[]{:S(2)}) collective-permute-start(bf16[24,32,128]{2,1,0:T(8,128)(2,1)S(1)} %get-tuple-element.38), channel_id=1, source_target_pairs={{0,16},{8,24},{16,0},{24,8},{1,17},{9,25},{17,1},{25,9},{2,18},{10... | collective-permute-start | bytes 589832 | tf_op jit(solution)/shard_map/ppermute | solution.py:143
  148.1 31.0 %collective-permute-start.6 = (bf16[24,32,128]{2,1,0:T(8,128)(2,1)S(1)}, bf16[24,32,128]{2,1,0:T(8,128)(2,1)S(1)}, u32[]{:S(2)}, u32[]{:S(2)}) collective-permute-start(bf16[24,32,128]{2,1,0:T(8,128)(2,1)S(1)} %get-tuple-element.39), channel_id=1, source_target_pairs={{0,8},{8,16},{16,24},{24,0},{1,9},{9,17},{17,25},{25,1},{2,10},{10... | collective-permute-start | bytes 589832 | tf_op jit(solution)/shard_map/ppermute | solution.py:143
  158.1 21.2 %collective-permute-start.18 = (bf16[24,32,128]{2,1,0:T(8,128)(2,1)S(1)}, bf16[24,32,128]{2,1,0:T(8,128)(2,1)S(1)}, u32[]{:S(2)}, u32[]{:S(2)}) collective-permute-start(bf16[24,32,128]{2,1,0:T(8,128)(2,1)S(1)} %get-tuple-element.53), channel_id=1, source_target_pairs={{0,24},{8,0},{16,8},{24,16},{1,25},{9,1},{17,9},{25,17},{2,26},{10... | collective-permute-start | bytes 589832 | tf_op jit(solution)/shard_map/ppermute | solution.py:143
  161.8 26.6 %collective-permute-start.17 = (bf16[24,32,128]{2,1,0:T(8,128)(2,1)S(1)}, bf16[24,32,128]{2,1,0:T(8,128)(2,1)S(1)}, u32[]{:S(2)}, u32[]{:S(2)}) collective-permute-start(bf16[24,32,128]{2,1,0:T(8,128)(2,1)S(1)} %get-tuple-element.54), channel_id=1, source_target_pairs={{0,16},{8,24},{16,0},{24,8},{1,17},{9,25},{17,1},{25,9},{2,18},{10... | collective-permute-start | bytes 589832 | tf_op jit(solution)/shard_map/ppermute | solution.py:143
  173.7 14.7 %collective-permute-start.16 = (bf16[24,32,128]{2,1,0:T(8,128)(2,1)S(1)}, bf16[24,32,128]{2,1,0:T(8,128)(2,1)S(1)}, u32[]{:S(2)}, u32[]{:S(2)}) collective-permute-start(bf16[24,32,128]{2,1,0:T(8,128)(2,1)S(1)} %get-tuple-element.55), channel_id=1, source_target_pairs={{0,8},{8,16},{16,24},{24,0},{1,9},{9,17},{17,25},{25,1},{2,10},{10... | collective-permute-start | bytes 589832 | tf_op jit(solution)/shard_map/ppermute | solution.py:143

commit v3 on v0

v3 whole, which is shorter than its diff:
```python
import functools
import math

import jax
import jax.numpy as jnp
from jax import lax
from jax.experimental import pallas as pl
from jax.experimental.pallas import tpu as pltpu
from jax.sharding import PartitionSpec as P

SCALE = math.sqrt(2.0 / math.pi)
CUBIC = 0.044715
GROUP = 6
VMEM = 56 * 1024 * 1024
F32 = jnp.float32
BF16 = jnp.bfloat16


def owner(half, turn, sections):
    size = sections // 2
    me = lax.axis_index("section")
    start = jnp.where(half == 1, me, sections - 1 - me)
    base = jnp.where(start < size, 0, size)
    at = start - base + turn
    return base + jnp.where(at < size, at, at - size)


def tick_kernel(relay, first_block, piece_blocks, sections, has_acc, last, n_deps, *refs):
    len_ref, idx_in_ref, idx_out_ref, x_ref, g_ref, w_in_ref, w_out_ref = refs[:7]
    refs = refs[7:]
    if has_acc:
        before_ref, refs = refs[0], refs[1:]
    refs = refs[n_deps:]
    keep_ref, send_ref = refs[:2]
    if last:
        own_ref, other_ref, acc_ref = refs[2:]
    else:
        (acc_ref,) = refs[2:]
    half, turn, part = pl.program_id(0), pl.program_id(1), pl.program_id(2)
    opening = (half == 0) & (turn == 0) & (part == 0)
    closing = (half == 1) & (turn == pl.num_programs(1) - 1) & (part == pl.num_programs(2) - 1)
    me = lax.axis_index("dp")
    per_step, block = w_in_ref.shape[0], w_in_ref.shape[-1]
    rows = x_ref.shape[0]
    piece = keep_ref.shape[3]
    live = lax.broadcasted_iota(jnp.int32, (rows, block), 0) < len_ref[relay, 0, 0]

    @pl.when(opening)
    def _():
        acc_ref[...] = before_ref[...] if has_acc else jnp.zeros_like(acc_ref)

    odd = me % 2 == 1

    def put(kind, i, value):
        value = value.astype(BF16)
        for k in range(block // piece // 2):
            low = value[2 * k * piece:(2 * k + 1) * piece]
            high = value[(2 * k + 1) * piece:(2 * k + 2) * piece]
            keep_ref[k ^ (me // 2), kind, i] = jnp.where(odd, high, low)
            send_ref[k ^ (me // 2), kind, i] = jnp.where(odd, low, high)

    base = owner(half, turn, sections) * piece_blocks + first_block + part * per_step
    over_last = (((1,), (1,)), ((), ()))
    over_rows = (((0,), (0,)), ((), ()))
    for start in range(0, per_step, GROUP):
        group = range(start, min(start + GROUP, per_step))
        sources = [idx_in_ref[0, relay, base + i] for i in group]
        targets = [idx_out_ref[0, relay, base + i] for i in group]
        picked = [x_ref[:, pl.ds(pl.multiple_of(b * block, block), block)] for b in sources]
        back = [g_ref[:, pl.ds(pl.multiple_of(b * block, block), block)] for b in targets]
        back = [jnp.where(live, v, jnp.zeros_like(v)) for v in back]
        pre = [jnp.dot(v, w_in_ref[i], preferred_element_type=F32) for v, i in zip(picked, group)]
        back_pre = [lax.dot_general(v, w_out_ref[i], over_last, preferred_element_type=F32) for v, i in zip(back, group)]
        act, grad_pre = [], []
        for v, up in zip(pre, back_pre):
            square = v * v
            th = jnp.tanh(SCALE * (v + CUBIC * (square * v)))
            cdf = 0.5 * (1.0 + th)
            act.append((v * cdf).astype(BF16))
            slope = cdf + (0.5 * v) * ((1.0 - th) * (1.0 + th)) * (SCALE * (1.0 + (3.0 * CUBIC) * square))
            grad_pre.append((up * slope).astype(BF16))
        terms = [lax.dot_general(v, w_in_ref[i], over_last, preferred_element_type=F32) for v, i in zip(grad_pre, group)]
        grad_in = [lax.dot_general(a, v, over_rows, preferred_element_type=F32) for a, v in zip(picked, grad_pre)]
        grad_out = [lax.dot_general(a, v, over_rows, preferred_element_type=F32) for a, v in zip(act, back)]
        for i, b, term, g_in, g_out in zip(group, sources, terms, grad_in, grad_out):
            acc_ref[b] += term
            put(0, i, g_in)
            put(1, i, g_out)

    if last:
        @pl.when(closing)
        def _():
            at = lax.axis_index("mp")
            share, n_mp = own_ref.shape[0], rows // own_ref.shape[0]
            own_rows = pl.ds(pl.multiple_of(at * share, share), share)
            for b in range(acc_ref.shape[0]):
                columns = slice(b * block, (b + 1) * block)
                held = g_ref[:, columns]
                acc_ref[b] += jnp.where(live & (lax.broadcasted_iota(jnp.int32, (rows, block), 0) // share == at),
                                        held, jnp.zeros_like(held)).astype(F32)
                own_ref[:, columns] = acc_ref[b, own_rows]
                for k in range(1, n_mp):
                    to = lax.rem(at + k, n_mp)
                    there = pl.ds(pl.multiple_of(to * share, share), share)
                    other_ref[k - 1, :, columns] = acc_ref[b, there].astype(BF16)


def tick(relay, lo, hi, before, last, deps, sizes, args):
    sections, n_dp, n_mp = sizes
    lengths, idx_in, idx_out, section_in, out_grad, w_in, w_out = args
    rows, width = section_in.shape[2:]
    blocks, block = w_in.shape[2:4]
    piece_blocks = blocks // sections
    per_step = math.gcd(math.gcd(hi - lo, lo), 6)
    steps = (hi - lo) // per_step
    size = sections // 2
    rows_cut = block // n_dp
    whole = pl.BlockSpec((None, None, rows, width), lambda h, t, i, *_: (relay, 0, 0, 0))
    at_block = lambda h, t, i, *_: (0, relay, (owner(h, t, sections) * piece_blocks + lo) // per_step + i, 0, 0)
    weight = pl.BlockSpec((None, None, per_step, block, block), at_block)
    slots = jax.ShapeDtypeStruct((n_dp // 2, 2, 2, size, hi - lo, rows_cut, block), BF16)
    slots_spec = pl.BlockSpec(
        (n_dp // 2, None, 2, None, per_step, rows_cut, block), lambda h, t, i, *_: (0, h, 0, t, i, 0, 0)
    )
    acc_shape = (width // block, rows, block)
    acc_spec = pl.BlockSpec(acc_shape, lambda h, t, i, *_: (0, 0, 0))
    share = rows // n_mp
    out_specs, out_shape, scratch = [slots_spec] * 2, [slots] * 2, []
    if last:
        out_specs += [
            pl.BlockSpec((share, width), lambda h, t, i, *_: (0, 0)),
            pl.BlockSpec((n_mp - 1, share, width), lambda h, t, i, *_: (0, 0, 0)),
        ]
        out_shape += [jax.ShapeDtypeStruct((share, width), F32), jax.ShapeDtypeStruct((n_mp - 1, share, width), BF16)]
        scratch = [pltpu.VMEM(acc_shape, F32)]
    else:
        out_specs.append(acc_spec)
        out_shape.append(jax.ShapeDtypeStruct(acc_shape, F32))
    held = [] if before is None else [before]
    done = size * 2 * (hi - lo)
    return pl.pallas_call(
        functools.partial(tick_kernel, relay, lo, piece_blocks, sections, bool(held), last, len(deps)),
        grid_spec=pltpu.PrefetchScalarGridSpec(
            num_scalar_prefetch=3,
            grid=(2, size, steps),
            in_specs=[whole, whole, weight, weight] + [acc_spec] * len(held) + [pl.BlockSpec(memory_space=pl.ANY)] * len(deps),
            out_specs=out_specs,
            scratch_shapes=scratch,
        ),
        out_shape=out_shape,
        compiler_params=pltpu.CompilerParams(dimension_semantics=("arbitrary",) * 3, vmem_limit_bytes=VMEM),
        cost_estimate=pl.CostEstimate(
            flops=done * 10 * rows * block * block,
            bytes_accessed=done * block * block * 8 + rows * width * 8,
            transcendentals=done * rows * block,
        ),
        name=f"tick{relay}_{lo}",
    )(lengths, idx_in, idx_out, section_in, out_grad, w_in, w_out, *held, *deps)


def add_kernel(n_terms, apart, n_deps, *refs):
    terms, outs = refs[:n_terms], refs[n_terms + n_deps:]
    for k in range(2):
        total = terms[0][k].astype(F32)
        for term in terms[1:]:
            total += term[k].astype(F32)
        if apart:
            outs[k][...] = total.astype(BF16)
        else:
            outs[0][k] = total.astype(BF16)


def add(terms, apart, name, deps=()):
    shape = terms[0][0].shape[-6:]
    flat = [(a.reshape(-1, math.prod(shape[1:4]), *shape[4:]), k) for a, k in terms]
    count, rows, block = flat[0][0].shape[1:]
    step = math.gcd(count, max(count // 4, 1))
    if apart:
        out_specs = [pl.BlockSpec((step, rows, block), lambda i: (i, 0, 0))] * 2
        out_shape = [jax.ShapeDtypeStruct((count, rows, block), BF16)] * 2
    else:
        out_specs = [pl.BlockSpec((2, step, rows, block), lambda i: (0, i, 0, 0))]
        out_shape = [jax.ShapeDtypeStruct((2, count, rows, block), BF16)]
    outs = pl.pallas_call(
        functools.partial(add_kernel, len(flat), apart, len(deps)),
        grid=(count // step,),
        in_specs=[pl.BlockSpec((2, step, rows, block), lambda i, k=k: (k, i, 0, 0)) for _, k in flat]
        + [pl.BlockSpec(memory_space=pl.ANY)] * len(deps),
        out_specs=out_specs,
        out_shape=out_shape,
        compiler_params=pltpu.CompilerParams(vmem_limit_bytes=VMEM),
        name=name,
    )(*[a for a, _ in flat], *deps)
    return [o.reshape(shape[1:] if apart else shape) for o in outs]


def segments(spans):
    edges = sorted({e for relay in spans for span in relay for e in span})
    found = []
    for a, b in zip(edges, edges[1:]):
        found.append((a - edges[0], b - a, [next((i, a - lo) for i, (lo, hi) in enumerate(relay) if lo <= a < hi) for relay in spans]))
    return found


def mirror_kernel(spans, size, *refs):
    n = [len(relay) for relay in spans]
    own = [refs[:n[0]], refs[n[0]:n[0] + n[1]]]
    far = [refs[sum(n):sum(n) + n[0]], refs[sum(n) + n[0]:2 * sum(n)]]
    outs = refs[2 * sum(n):]
    for start, length, places in segments(spans):
        for r in range(2):
            (i, at), (j, there) = places[r], places[1 - r]
            for turn in range(1, size):
                total = own[r][i][:, turn, at:at + length].astype(F32) + far[1 - r][j][:, turn, there:there + length].astype(F32)
                outs[turn - 1][r, :, start:start + length] = total.astype(BF16)


def mirror_sum(spans, own, far, name):
    _, size, _, rows, block = own[0][0].shape
    long = spans[0][-1][1] - spans[0][0][0]
    flat = own[0] + own[1] + far[0] + far[1]
    return pl.pallas_call(
        functools.partial(mirror_kernel, spans, size),
        out_shape=[jax.ShapeDtypeStruct((2, 2, long, rows, block), BF16)] * (size - 1),
        compiler_params=pltpu.CompilerParams(vmem_limit_bytes=VMEM),
        name=name,
    )(*flat)


def grads_kernel(spans, sections, has_before, *refs):
    size = sections // 2
    n = [len(relay) for relay in spans]
    own = [refs[:n[0]], refs[n[0]:n[0] + n[1]]]
    far = [refs[sum(n):sum(n) + n[0]], refs[sum(n) + n[0]:2 * sum(n)]]
    came = refs[2 * sum(n):2 * sum(n) + size - 1]
    out = refs[-1]
    me = lax.axis_index("section")
    base = jnp.where(me < size, 0, size)
    for start, length, places in segments(spans):
        for r in range(2):
            (i, at), (j, there) = places[r], places[1 - r]
            layer = sections - 1 - me if r else me
            total = own[r][i][:, at:at + length].astype(F32) + far[1 - r][j][:, there:there + length].astype(F32)
            out[layer, :, start:start + length] = total
    for turn in range(1, size):
        at = me - base - turn
        source = base + jnp.where(at < 0, at + size, at)
        for r in range(2):
            out[sections - 1 - source if r else source] = came[turn - 1][r].astype(F32)


def write_grads(spans, own, far, came, before, sections, piece_blocks, name):
    rows, block = own[0][0].shape[3:]
    long = spans[0][-1][1] - spans[0][0][0]
    place = spans[0][0][0] // long
    first = lambda a: pl.BlockSpec((2, None) + a.shape[2:], lambda i: (0, 0, 0, 0, 0))
    flat = own[0] + own[1] + far[0] + far[1]
    held = [] if before is None else [before]
    return pl.pallas_call(
        functools.partial(grads_kernel, spans, sections, bool(held)),
        grid=(1,),
        in_specs=[first(a) for a in flat]
        + [pl.BlockSpec(a.shape, lambda i: (0, 0, 0, 0, 0)) for a in came]
        + [pl.BlockSpec(memory_space=pl.ANY)] * len(held),
        out_specs=pl.BlockSpec((sections, 2, None, long, rows, block), lambda i: (0, 0, 0, place, 0, 0)),
        out_shape=jax.ShapeDtypeStruct((sections, 2, 1, piece_blocks, rows, block), F32),
        input_output_aliases={len(flat) + len(came): 0} if held else {},
        compiler_params=pltpu.CompilerParams(vmem_limit_bytes=VMEM),
        name=name,
    )(*flat, *came, *held)


def from_behind(value, axis, distance):
    devices = range(lax.axis_size(axis))
    route = [(i - distance, i) for i in devices if i - distance in devices]
    return lax.ppermute(value, axis, route)


def flip_bit(value, axis, bit):
    return lax.ppermute(value, axis, [(i, i ^ bit) for i in range(lax.axis_size(axis))])


def turn_half(value, turn):
    size = lax.axis_size("section") // 2
    route = [(h * size + i, h * size + (i + turn) % size) for h in range(2) for i in range(size)]
    return lax.ppermute(value, "section", route)


def body(section_in, out_grad, lengths, w_in, w_out, idx_in, idx_out):
    sections, n_dp, n_mp = (lax.axis_size(a) for a in ("section", "dp", "mp"))
    size = sections // 2
    piece_blocks = w_in.shape[2] // sections
    args = (lengths, idx_in, idx_out, section_in, out_grad, w_in, w_out)
    cuts = [0, piece_blocks // 2, piece_blocks] if piece_blocks % 4 == 0 else [0, piece_blocks]
    fine = sorted(set([0, piece_blocks // 4] + cuts)) if piece_blocks % 4 == 0 else cuts
    chunks = [(0, lo, hi) for lo, hi in zip(fine, fine[1:])] + [(1, lo, hi) for lo, hi in zip(cuts, cuts[1:])]
    mirror = [(i, sections - 1 - i) for i in range(sections)]

    keep, got, sum_a, came, kept, arrived, passed = {}, {}, {}, {}, {}, {}, []
    acc = None

    def stage_a(c):
        deps = [kept[c - 2]] if c - 2 in kept else []
        (sum_a[c],) = add([(keep[c], 1), (got[c], 1)], False, f"core{c}", deps)
        came[c] = flip_bit(sum_a[c], "dp", 2)

    def stage_b(c):
        away, kept[c] = add([(keep[c], 0), (got[c], 0), (came[c], 0)], True, f"pair{c}")
        arrived[c] = lax.ppermute(away, "section", mirror)

    for c, (relay, lo, hi) in enumerate(chunks):
        last = hi == piece_blocks
        deps = [sum_a[c - 2]] if c >= 2 else []
        if c >= 3:
            deps.append(kept[c - 3])
        results = tick(relay, lo, hi, acc, last, deps, (sections, n_dp, n_mp), args)
        keep[c], send = results[:2]
        got[c] = flip_bit(send, "dp", 1)
        acc = None if last else results[2]
        if last:
            dx, others = results[2:]
            for k in range(1, n_mp):
                dx = dx + lax.ppermute(others[k - 1], "mp", [(i, (i + k) % n_mp) for i in range(n_mp)]).astype(F32)
            passed.append(from_behind(dx.astype(BF16), "section", 1 if relay else -1))
        if c >= 1:
            stage_a(c - 1)
        if c >= 2:
            stage_b(c - 2)
    n = len(chunks)
    if n >= 2:
        stage_b(n - 2)
    stage_a(n - 1)
    stage_b(n - 1)

    grads = None
    for lo, hi in zip(cuts, cuts[1:]):
        inside = [[c for c, (r, a, b) in enumerate(chunks) if r == relay and lo <= a < hi] for relay in range(2)]
        spans = [[chunks[c][1:] for c in relay] for relay in inside]
        own = [[kept[c] for c in relay] for relay in inside]
        far = [[arrived[c] for c in relay] for relay in inside]
        to_turn = mirror_sum(spans, own, far, f"mirror_{lo}") if size > 1 else []
        turned = [turn_half(v, turn + 1) for turn, v in enumerate(to_turn)]
        grads = write_grads(spans, own, far, turned, grads, sections, piece_blocks, f"grads_{lo}")
    return jnp.stack(passed, axis=0)[:, None], grads


def solution(mesh):
    placed = (
        P(None, "section", "dp", None),
        P(None, "section", "dp", None),
        P(None, "section", "dp"),
        P("section", None, "mp", None, None),
        P("section", None, "mp", None, None),
        P("section", None, "mp"),
        P("section", None, "mp"),
    )
    return jax.shard_map(
        body,
        mesh=mesh,
        in_specs=placed,
        out_specs=(
            P(None, "section", ("dp", "mp"), None),
            P(None, None, "mp", "section", "dp", None),
        ),
        check_vma=False,
    )
```

time: 274 us -> 221 us (0.81)
  the two profiles are of different devices: /device:TPU:8 before, /device:TPU:0 now
where the time goes in v3:
time: 221 us; the launch traced here: 219 us
  Pallas kernels  100 us (45%)
  starting transfers between devices  78.6 us (36%)
  waiting for transfers between devices  26.4 us (12%)
  local copies, waits for them, and re-layouts  11.2 us (5%)
    pallas_call x5, Pallas kernels, tick(): pl.pallas_call(functools.partial(tick_kernel, relay, lo, piece_blocks, se...  55.8 us
    ppermute x2, starting transfers between devices, turn_half(): return lax.ppermute(value, 'section', route)  47.5 us
    pallas_call x10, Pallas kernels, add(): pl.pallas_call(functools.partial(add_kernel, len(flat), apart, len(deps))...  34.9 us
    ppermute x10, waiting for transfers between devices, flip_bit(): lax.ppermute(value, axis, [(i, i ^ bit) for i in range(lax.axis_size(axis...  17.8 us
    ppermute x5, starting transfers between devices, stage_b(): arrived[c] = lax.ppermute(away, 'section', mirror)  14.4 us
    unnamed x47, local copies, waits for them, and re-layouts  11.2 us
    ppermute x10, starting transfers between devices, flip_bit(): lax.ppermute(value, axis, [(i, i ^ bit) for i in range(lax.axis_size(axis...  8.54 us
    pallas_call x2, Pallas kernels, write_grads(): pl.pallas_call(functools.partial(grads_kernel, spans, sections, bool(held...  5.24 us
  transfers between devices with their start and end apart: 21, of which 7 were waited for; matrix products, arithmetic and copies ran while one was open for 1% of the time, Pallas kernels for 33%

profile of v3, /device:TPU:0, one launch (start us, length us, event | category | flops | bytes accessed | tf_op | source)
XLA Modules:
  0.0 219.1 jit_solution(15124933209280614935)
XLA Ops:
  2.0 8.1 %tick0_0.1 = (bf16[2,2,2,2,6,32,128]{6,5,4,3,2,1,0:T(8,128)(2,1)}, bf16[2,2,2,2,6,32,128]{6,5,4,3,2,1,0:T(8,128)(2,1)}, f32[96,64,128]{2,1,0:T(8,128)}) custom-call(s32[2,1,1]{2,1,0:T(1,128)} %copy.12.refs_0_, s32[1,2,96]{2,1,0:T(2,128)} %refs_1_.9, s32[1,2,96]{2,1,0:T(2,128)} %refs_2_.9, bf16[2,1,64,12288]{3,2,1,0:T(8,128)(2,1)} %refs_3_.9, ...), custom_call_target="tpu_custom_call" | custom-call | flops 251658240 | bytes 9437184 | tf_op jit(solution)/shard_map/tick0_0/pallas_call | solution.py:141
  10.6 9.0 %tick0_6.1 = (bf16[2,2,2,2,6,32,128]{6,5,4,3,2,1,0:T(8,128)(2,1)}, bf16[2,2,2,2,6,32,128]{6,5,4,3,2,1,0:T(8,128)(2,1)}, f32[96,64,128]{2,1,0:T(8,128)}) custom-call(s32[2,1,1]{2,1,0:T(1,128)} %copy.12.refs_0_, s32[1,2,96]{2,1,0:T(2,128)} %refs_1_.9, s32[1,2,96]{2,1,0:T(2,128)} %refs_2_.9, bf16[2,1,64,12288]{3,2,1,0:T(8,128)(2,1)} %refs_3_.9, ...), custom_call_target="tpu_custom_call" | custom-call | flops 251658240 | bytes 9437184 | tf_op jit(solution)/shard_map/tick0_6/pallas_call | solution.py:141
  20.5 3.2 %core0.1 = bf16[2,24,32,128]{3,2,1,0:T(8,128)(2,1)} custom-call(bf16[4,24,32,128]{3,2,1,0:T(8,128)(2,1)} %bitcast.65, bf16[4,24,32,128]{3,2,1,0:T(8,128)(2,1)} %bitcast.67), custom_call_target="tpu_custom_call" | custom-call | tf_op jit(solution)/shard_map/core0/pallas_call | solution.py:184
  23.7 13.5 %tick0_12.1 = (bf16[2,2,2,2,12,32,128]{6,5,4,3,2,1,0:T(8,128)(2,1)}, bf16[2,2,2,2,12,32,128]{6,5,4,3,2,1,0:T(8,128)(2,1)}, f32[32,12288]{1,0:T(8,128)}, bf16[1,32,12288]{2,1,0:T(8,128)(2,1)}) custom-call(s32[2,1,1]{2,1,0:T(1,128)} %copy.12.refs_0_, s32[1,2,96]{2,1,0:T(2,128)} %refs_1_.9, s32[1,2,96]{2,1,0:T(2,128)} %refs_2_.9, ...), custom_call_target="tpu_custom_call" | custom-call | flops 503316480 | bytes 12582912 | tf_op jit(solution)/shard_map/tick0_12/pallas_call | solution.py:141
  37.8 2.7 %collective-permute-start.1 = (bf16[32,12288]{1,0:T(8,128)(2,1)}, bf16[32,12288]{1,0:T(8,128)(2,1)S(1)}, u32[]{:S(2)}, u32[]{:S(2)}) collective-permute-start(bf16[32,12288]{1,0:T(8,128)(2,1)} %bitcast.87), channel_id=1, source_target_pairs={{0,1},{1,0},{2,3},{3,2},{4,5},{5,4},{6,7},{7,6},{8,9},{9,8},{10,11... | collective-permute-start | bytes 2359304 | tf_op jit(solution)/shard_map/ppermute | solution.py:323
  42.8 3.3 %core1.1 = bf16[2,24,32,128]{3,2,1,0:T(8,128)(2,1)} custom-call(bf16[4,24,32,128]{3,2,1,0:T(8,128)(2,1)} %bitcast.63, bf16[4,24,32,128]{3,2,1,0:T(8,128)(2,1)} %bitcast.69), custom_call_target="tpu_custom_call" | custom-call | tf_op jit(solution)/shard_map/core1/pallas_call | solution.py:184
  46.1 2.3 %collective-permute-start.6 = (bf16[2,2,2,6,32,128]{5,4,3,2,1,0:T(8,128)(2,1)}, bf16[2,2,2,6,32,128]{5,4,3,2,1,0:T(8,128)(2,1)S(1)}, u32[]{:S(2)}, u32[]{:S(2)}) collective-permute-start(bf16[2,2,2,6,32,128]{5,4,3,2,1,0:T(8,128)(2,1)} %bitcast.77), channel_id=1, source_target_pairs={{0,4},{2,6},{4,0},{6,2},{1,5},{3,7},{5,1},{7,3},{8,12},{10,14},{12... | collective-permute-start | bytes 1179656 | tf_op jit(solution)/shard_map/ppermute | solution.py:280
  48.4 4.0 %collective-permute-done.4 = bf16[2,2,2,6,32,128]{5,4,3,2,1,0:T(8,128)(2,1)S(1)} collective-permute-done((bf16[2,2,2,6,32,128]{5,4,3,2,1,0:T(8,128)(2,1)S(1)}, bf16[2,2,2,6,32,128]{5,4,3,2,1,0:T(8,128)(2,1)S(1)}, u32[]{:S(2)}, u32[]{:S(2)}) %collective-permute-start.4) | collective-permute-done | bytes 393248 | tf_op jit(solution)/shard_map/ppermute | solution.py:280
  53.2 3.3 %pair0.1 = (bf16[24,32,128]{2,1,0:T(8,128)(2,1)}, bf16[24,32,128]{2,1,0:T(8,128)(2,1)}) custom-call(bf16[4,24,32,128]{3,2,1,0:T(8,128)(2,1)} %bitcast.66, bf16[4,24,32,128]{3,2,1,0:T(8,128)(2,1)} %bitcast.68, bf16[2,24,32,128]{3,2,1,0:T(8,128)(2,1)} %bitcast.85), custom_call_target="tpu_custom_call" | custom-call | tf_op jit(solution)/shard_map/pair0/pallas_call | solution.py:184
  56.5 3.5 %collective-permute-done.6 = bf16[2,2,2,6,32,128]{5,4,3,2,1,0:T(8,128)(2,1)S(1)} collective-permute-done((bf16[2,2,2,6,32,128]{5,4,3,2,1,0:T(8,128)(2,1)}, bf16[2,2,2,6,32,128]{5,4,3,2,1,0:T(8,128)(2,1)S(1)}, u32[]{:S(2)}, u32[]{:S(2)}) %collective-permute-start.6) | collective-permute-done | bytes 393248 | tf_op jit(solution)/shard_map/ppermute | solution.py:280
  60.8 3.3 %pair1.1 = (bf16[24,32,128]{2,1,0:T(8,128)(2,1)}, bf16[24,32,128]{2,1,0:T(8,128)(2,1)}) custom-call(bf16[4,24,32,128]{3,2,1,0:T(8,128)(2,1)} %bitcast.64, bf16[4,24,32,128]{3,2,1,0:T(8,128)(2,1)} %bitcast.70, bf16[2,24,32,128]{3,2,1,0:T(8,128)(2,1)} %bitcast.86), custom_call_target="tpu_custom_call" | custom-call | tf_op jit(solution)/shard_map/pair1/pallas_call | solution.py:184
  64.1 11.7 %tick1_0.1 = (bf16[2,2,2,2,12,32,128]{6,5,4,3,2,1,0:T(8,128)(2,1)}, bf16[2,2,2,2,12,32,128]{6,5,4,3,2,1,0:T(8,128)(2,1)}, f32[96,64,128]{2,1,0:T(8,128)}) custom-call(s32[2,1,1]{2,1,0:T(1,128)} %copy.12.refs_0_, s32[1,2,96]{2,1,0:T(2,128)} %refs_1_.9, s32[1,2,96]{2,1,0:T(2,128)} %refs_2_.9, bf16[2,1,64,12288]{3,2,1,0:T(8,128)(2,1)} %refs_3_.9, ...), custom_call_target="tpu_custom_call" | custom-call | flops 503316480 | bytes 12582912 | tf_op jit(solution)/shard_map/tick1_0/pallas_call | solution.py:141
  77.2 3.5 %core2.1 = bf16[2,48,32,128]{3,2,1,0:T(8,128)(2,1)} custom-call(bf16[4,48,32,128]{3,2,1,0:T(8,128)(2,1)} %bitcast.42, bf16[4,48,32,128]{3,2,1,0:T(8,128)(2,1)} %bitcast.44, bf16[2,2,6,32,128]{4,3,2,1,0:T(8,128)(2,1)} %bitcast.54), custom_call_target="tpu_custom_call" | custom-call | tf_op jit(solution)/shard_map/core2/pallas_call | solution.py:184
  82.2 13.5 %tick1_12.1 = (bf16[2,2,2,2,12,32,128]{6,5,4,3,2,1,0:T(8,128)(2,1)}, bf16[2,2,2,2,12,32,128]{6,5,4,3,2,1,0:T(8,128)(2,1)}, f32[32,12288]{1,0:T(8,128)}, bf16[1,32,12288]{2,1,0:T(8,128)(2,1)}) custom-call(s32[2,1,1]{2,1,0:T(1,128)} %copy.12.refs_0_, s32[1,2,96]{2,1,0:T(2,128)} %refs_1_.9, s32[1,2,96]{2,1,0:T(2,128)} %refs_2_.9, ...), custom_call_target="tpu_custom_call" | custom-call | flops 503316480 | bytes 12582912 | tf_op jit(solution)/shard_map/tick1_12/pallas_call | solution.py:141
  98.9 3.5 %core3.1 = bf16[2,48,32,128]{3,2,1,0:T(8,128)(2,1)} custom-call(bf16[4,48,32,128]{3,2,1,0:T(8,128)(2,1)} %bitcast.46, bf16[4,48,32,128]{3,2,1,0:T(8,128)(2,1)} %bitcast.48, bf16[2,2,6,32,128]{4,3,2,1,0:T(8,128)(2,1)} %bitcast.58), custom_call_target="tpu_custom_call" | custom-call | tf_op jit(solution)/shard_map/core3/pallas_call | solution.py:184
  102.8 3.7 %pair2.1 = (bf16[48,32,128]{2,1,0:T(8,128)(2,1)}, bf16[48,32,128]{2,1,0:T(8,128)(2,1)}) custom-call(bf16[4,48,32,128]{3,2,1,0:T(8,128)(2,1)} %bitcast.43, bf16[4,48,32,128]{3,2,1,0:T(8,128)(2,1)} %bitcast.45, bf16[2,48,32,128]{3,2,1,0:T(8,128)(2,1)} %bitcast.19.refs_2_), custom_call_target="tpu_custom_call" | custom-call | tf_op jit(solution)/shard_map/pair2/pallas_call | solution.py:184
  107.6 3.6 %core4.1 = bf16[2,48,32,128]{3,2,1,0:T(8,128)(2,1)} custom-call(bf16[4,48,32,128]{3,2,1,0:T(8,128)(2,1)} %bitcast.38, bf16[4,48,32,128]{3,2,1,0:T(8,128)(2,1)} %bitcast.40, bf16[2,2,12,32,128]{4,3,2,1,0:T(8,128)(2,1)} %bitcast.50), custom_call_target="tpu_custom_call" | custom-call | tf_op jit(solution)/shard_map/core4/pallas_call | solution.py:184
  112.9 2.7 %collective-permute-done.7 = bf16[32,12288]{1,0:T(8,128)(2,1)S(1)} collective-permute-done((bf16[32,12288]{1,0:T(8,128)(2,1)}, bf16[32,12288]{1,0:T(8,128)(2,1)S(1)}, u32[]{:S(2)}, u32[]{:S(2)}) %collective-permute-start.7) | collective-permute-done | bytes 786464 | tf_op jit(solution)/shard_map/ppermute | solution.py:323
  115.8 3.6 %collective-permute-start.8 = (bf16[32,12288]{1,0:T(8,128)(2,1)S(1)}, bf16[32,12288]{1,0:T(8,128)(2,1)S(1)}, u32[]{:S(2)}, u32[]{:S(2)}) collective-permute-start(bf16[32,12288]{1,0:T(8,128)(2,1)S(1)} %add_convert_fusion), channel_id=1, source_target_pairs={{0,8},{8,16},{16,24},{1,9},{9,17},{17,25},{2,10},{10,18},{18,26},{... | collective-permute-start | bytes 2359304 | tf_op jit(solution)/shard_map/ppermute | solution.py:276
  123.0 4.7 %collective-permute-start.18 = (bf16[2,2,6,32,128]{4,3,2,1,0:T(8,128)(2,1)S(1)}, bf16[2,2,6,32,128]{4,3,2,1,0:T(8,128)(2,1)S(1)}, u32[]{:S(2)}, u32[]{:S(2)}) collective-permute-start(bf16[2,2,6,32,128]{4,3,2,1,0:T(8,128)(2,1)S(1)} %bitcast.93), channel_id=1, source_target_pairs={{0,24},{8,16},{16,8},{24,0},{1,25},{9,17},{17,9},{25,1},{2,26},{10... | collective-permute-start | bytes 589832 | tf_op jit(solution)/shard_map/ppermute | solution.py:309
  127.7 3.7 %pair3.1 = (bf16[48,32,128]{2,1,0:T(8,128)(2,1)}, bf16[48,32,128]{2,1,0:T(8,128)(2,1)}) custom-call(bf16[4,48,32,128]{3,2,1,0:T(8,128)(2,1)} %bitcast.47, bf16[4,48,32,128]{3,2,1,0:T(8,128)(2,1)} %bitcast.49, bf16[2,48,32,128]{3,2,1,0:T(8,128)(2,1)} %bitcast.81), custom_call_target="tpu_custom_call" | custom-call | tf_op jit(solution)/shard_map/pair3/pallas_call | solution.py:184
  131.3 8.1 %collective-permute-done.11 = bf16[2,2,2,12,32,128]{5,4,3,2,1,0:T(8,128)(2,1)S(1)} collective-permute-done((bf16[2,2,2,12,32,128]{5,4,3,2,1,0:T(8,128)(2,1)}, bf16[2,2,2,12,32,128]{5,4,3,2,1,0:T(8,128)(2,1)S(1)}, u32[]{:S(2)}, u32[]{:S(2)}) %collective-permute-start.11) | collective-permute-done | bytes 786464 | tf_op jit(solution)/shard_map/ppermute | solution.py:280
  139.4 4.4 %collective-permute-start.19 = (bf16[2,2,12,32,128]{4,3,2,1,0:T(8,128)(2,1)}, bf16[2,2,12,32,128]{4,3,2,1,0:T(8,128)(2,1)S(1)}, u32[]{:S(2)}, u32[]{:S(2)}) collective-permute-start(bf16[2,2,12,32,128]{4,3,2,1,0:T(8,128)(2,1)} %bitcast.90), channel_id=1, source_target_pairs={{0,24},{8,16},{16,8},{24,0},{1,25},{9,17},{17,9},{25,1},{2,26},{10... | collective-permute-start | bytes 1179656 | tf_op jit(solution)/shard_map/ppermute | solution.py:309
  143.8 3.7 %pair4.1 = (bf16[48,32,128]{2,1,0:T(8,128)(2,1)}, bf16[48,32,128]{2,1,0:T(8,128)(2,1)}) custom-call(bf16[4,48,32,128]{3,2,1,0:T(8,128)(2,1)} %bitcast.39, bf16[4,48,32,128]{3,2,1,0:T(8,128)(2,1)} %bitcast.41, bf16[2,48,32,128]{3,2,1,0:T(8,128)(2,1)} %bitcast.82), custom_call_target="tpu_custom_call" | custom-call | tf_op jit(solution)/shard_map/pair4/pallas_call | solution.py:184
  148.4 3.0 %collective-permute-start.13 = (bf16[2,2,12,32,128]{4,3,2,1,0:T(8,128)(2,1)}, bf16[2,2,12,32,128]{4,3,2,1,0:T(8,128)(2,1)S(1)}, u32[]{:S(2)}, u32[]{:S(2)}) collective-permute-start(bf16[2,2,12,32,128]{4,3,2,1,0:T(8,128)(2,1)} %bitcast.91), channel_id=1, source_target_pairs={{0,24},{8,16},{16,8},{24,0},{1,25},{9,17},{17,9},{25,1},{2,26},{10... | collective-permute-start | bytes 1179656 | tf_op jit(solution)/shard_map/ppermute | solution.py:309
  151.4 2.7 %collective-permute-done.19.refs_5_ = bf16[2,2,12,32,128]{4,3,2,1,0:T(8,128)(2,1)S(1)} collective-permute-done((bf16[2,2,12,32,128]{4,3,2,1,0:T(8,128)(2,1)}, bf16[2,2,12,32,128]{4,3,2,1,0:T(8,128)(2,1)S(1)}, u32[]{:S(2)}, u32[]{:S(2)}) %collective-permute-start.19) | collective-permute-done | bytes 393248 | tf_op jit(solution)/shard_map/ppermute | solution.py:309
  154.8 2.3 %mirror_0.1 = bf16[2,2,12,32,128]{4,3,2,1,0:T(8,128)(2,1)} custom-call(bf16[2,2,6,32,128]{4,3,2,1,0:T(8,128)(2,1)} %bitcast.55, bf16[2,2,6,32,128]{4,3,2,1,0:T(8,128)(2,1)} %bitcast.59, bf16[2,2,12,32,128]{4,3,2,1,0:T(8,128)(2,1)} %bitcast.73, bf16[2,2,6,32,128]{4,3,2,1,0:T(8,128)(2,1)} %copy-done.11, bf16[2,2,6,32,128]{4,3,2,1,0:T(8,128)(2,1)} %copy-done.12, ...), custom_call_target="tpu_custom_call" | custom-call | tf_op jit(solution)/shard_map/mirror_0/pallas_call | solution.py:222
  157.1 35.5 %collective-permute-start.20 = (bf16[2,2,12,32,128]{4,3,2,1,0:T(8,128)(2,1)}, bf16[2,2,12,32,128]{4,3,2,1,0:T(8,128)(2,1)S(1)}, u32[]{:S(2)}, u32[]{:S(2)}) collective-permute-start(bf16[2,2,12,32,128]{4,3,2,1,0:T(8,128)(2,1)} %mirror_0.1), channel_id=1, source_target_pairs={{0,8},{8,0},{16,24},{24,16},{1,9},{9,1},{17,25},{25,17},{2,10},{10... | collective-permute-start | bytes 1179656 | tf_op jit(solution)/shard_map/ppermute | solution.py:286
  195.7 12.0 %collective-permute-start.14 = (bf16[2,2,12,32,128]{4,3,2,1,0:T(8,128)(2,1)}, bf16[2,2,12,32,128]{4,3,2,1,0:T(8,128)(2,1)S(1)}, u32[]{:S(2)}, u32[]{:S(2)}) collective-permute-start(bf16[2,2,12,32,128]{4,3,2,1,0:T(8,128)(2,1)} %mirror_12.1), channel_id=1, source_target_pairs={{0,8},{8,0},{16,24},{24,16},{1,9},{9,1},{17,25},{25,17},{2,10},{10... | collective-permute-start | bytes 1179656 | tf_op jit(solution)/shard_map/ppermute | solution.py:286
  209.8 2.6 %grads_0.1.refs_5_ = f32[4,2,1,24,32,128]{5,4,3,2,1,0:T(8,128)} custom-call(bf16[2,2,6,32,128]{4,3,2,1,0:T(8,128)(2,1)} %bitcast.56, bf16[2,2,6,32,128]{4,3,2,1,0:T(8,128)(2,1)} %bitcast.60, bf16[2,2,12,32,128]{4,3,2,1,0:T(8,128)(2,1)} %bitcast.74, bf16[2,2,6,32,128]{4,3,2,1,0:T(8,128)(2,1)} %copy-done.11, bf16[2,2,6,32,128]{4,3,2,1,0:T(8,128)(2,1)} %copy-done.12, ...), custom_call_target="tpu_custom_call" | custom-call | tf_op jit(solution)/shard_map/grads_0/pallas_call | solution.py:259
  212.4 3.3 %collective-permute-done.14.refs_4_ = bf16[2,2,12,32,128]{4,3,2,1,0:T(8,128)(2,1)S(1)} collective-permute-done((bf16[2,2,12,32,128]{4,3,2,1,0:T(8,128)(2,1)}, bf16[2,2,12,32,128]{4,3,2,1,0:T(8,128)(2,1)S(1)}, u32[]{:S(2)}, u32[]{:S(2)}) %collective-permute-start.14) | collective-permute-done | bytes 393248 | tf_op jit(solution)/shard_map/ppermute | solution.py:286
  216.5 2.6 %grads_12.1 = f32[4,2,1,24,32,128]{5,4,3,2,1,0:T(8,128)} custom-call(bf16[2,2,12,32,128]{4,3,2,1,0:T(8,128)(2,1)} %bitcast.52, bf16[2,2,12,32,128]{4,3,2,1,0:T(8,128)(2,1)} %bitcast.72, bf16[2,2,12,32,128]{4,3,2,1,0:T(8,128)(2,1)} %copy-done.5, bf16[2,2,12,32,128]{4,3,2,1,0:T(8,128)(2,1)} %copy-done.6, ...), custom_call_target="tpu_custom_call", output_to_operand_aliasing={{}: (5, {})} | custom-call | tf_op jit(solution)/shard_map/grads_12/pallas_call | solution.py:259
  (79 shorter events, 27.5 us)
Async XLA Ops:
  10.0 9.5 %collective-permute-start = (bf16[2,2,2,2,6,32,128]{6,5,4,3,2,1,0:T(8,128)(2,1)}, bf16[2,2,2,2,6,32,128]{6,5,4,3,2,1,0:T(8,128)(2,1)S(1)}, u32[]{:S(2)}, u32[]{:S(2)}) collective-permute-start(bf16[2,2,2,2,6,32,128]{6,5,4,3,2,1,0:T(8,128)(2,1)} %get-tuple-element.32), channel_id=1, source_target_pairs={{0,2},{2,0},{4,6},{6,4},{1,3},{3,1},{5,7},{7,5},{8,10},{10,8},{12,... | collective-permute-start | bytes 2359304 | tf_op jit(solution)/shard_map/ppermute | solution.py:280
  23.7 13.6 %copy-start.19 = (bf16[2,2,2,2,6,32,128]{6,5,4,3,2,1,0:T(8,128)(2,1)S(1)}, bf16[2,2,2,2,6,32,128]{6,5,4,3,2,1,0:T(8,128)(2,1)}, u32[]{:S(2)}) copy-start(bf16[2,2,2,2,6,32,128]{6,5,4,3,2,1,0:T(8,128)(2,1)} %get-tuple-element.36) | copy-start | bytes 2359300
  23.7 16.8 %copy-start.10 = (bf16[2,24,32,128]{3,2,1,0:T(8,128)(2,1)S(1)}, bf16[2,24,32,128]{3,2,1,0:T(8,128)(2,1)}, u32[]{:S(2)}) copy-start(bf16[2,24,32,128]{3,2,1,0:T(8,128)(2,1)} %core0.1) | copy-start | bytes 1179652
  37.2 38.8 %collective-permute-start.5 = (bf16[2,2,2,2,12,32,128]{6,5,4,3,2,1,0:T(8,128)(2,1)}, bf16[2,2,2,2,12,32,128]{6,5,4,3,2,1,0:T(8,128)(2,1)S(1)}, u32[]{:S(2)}, u32[]{:S(2)}) collective-permute-start(bf16[2,2,2,2,12,32,128]{6,5,4,3,2,1,0:T(8,128)(2,1)} %get-tuple-element.40), channel_id=1, source_target_pairs={{0,2},{2,0},{4,6},{6,4},{1,3},{3,1},{5,7},{7,5},{8,10},{10,8},{12,... | collective-permute-start | bytes 4718600 | tf_op jit(solution)/shard_map/ppermute | solution.py:280
  37.3 4.6 %collective-permute-start.3 = (bf16[2,2,2,2,6,32,128]{6,5,4,3,2,1,0:T(8,128)(2,1)S(1)}, bf16[2,2,2,2,6,32,128]{6,5,4,3,2,1,0:T(8,128)(2,1)S(1)}, u32[]{:S(2)}, u32[]{:S(2)}) collective-permute-start(bf16[2,2,2,2,6,32,128]{6,5,4,3,2,1,0:T(8,128)(2,1)S(1)} %copy-done.19), channel_id=1, source_target_pairs={{0,2},{2,0},{4,6},{6,4},{1,3},{3,1},{5,7},{7,5},{8,10},{10,8},{12,... | collective-permute-start | bytes 2359304 | tf_op jit(solution)/shard_map/ppermute | solution.py:280
  37.8 58.5 %collective-permute-start.1 = (bf16[32,12288]{1,0:T(8,128)(2,1)}, bf16[32,12288]{1,0:T(8,128)(2,1)S(1)}, u32[]{:S(2)}, u32[]{:S(2)}) collective-permute-start(bf16[32,12288]{1,0:T(8,128)(2,1)} %bitcast.87), channel_id=1, source_target_pairs={{0,1},{1,0},{2,3},{3,2},{4,5},{5,4},{6,7},{7,6},{8,9},{9,8},{10,11... | collective-permute-start | bytes 2359304 | tf_op jit(solution)/shard_map/ppermute | solution.py:323
  40.5 12.0 %collective-permute-start.4 = (bf16[2,2,2,6,32,128]{5,4,3,2,1,0:T(8,128)(2,1)S(1)}, bf16[2,2,2,6,32,128]{5,4,3,2,1,0:T(8,128)(2,1)S(1)}, u32[]{:S(2)}, u32[]{:S(2)}) collective-permute-start(bf16[2,2,2,6,32,128]{5,4,3,2,1,0:T(8,128)(2,1)S(1)} %bitcast.76), channel_id=1, source_target_pairs={{0,4},{2,6},{4,0},{6,2},{1,5},{3,7},{5,1},{7,3},{8,12},{10,14},{12... | collective-permute-start | bytes 1179656 | tf_op jit(solution)/shard_map/ppermute | solution.py:280
  46.1 14.0 %collective-permute-start.6 = (bf16[2,2,2,6,32,128]{5,4,3,2,1,0:T(8,128)(2,1)}, bf16[2,2,2,6,32,128]{5,4,3,2,1,0:T(8,128)(2,1)S(1)}, u32[]{:S(2)}, u32[]{:S(2)}) collective-permute-start(bf16[2,2,2,6,32,128]{5,4,3,2,1,0:T(8,128)(2,1)} %bitcast.77), channel_id=1, source_target_pairs={{0,4},{2,6},{4,0},{6,2},{1,5},{3,7},{5,1},{7,3},{8,12},{10,14},{12... | collective-permute-start | bytes 1179656 | tf_op jit(solution)/shard_map/ppermute | solution.py:280
  75.9 21.9 %collective-permute-start.15 = (bf16[2,2,2,2,12,32,128]{6,5,4,3,2,1,0:T(8,128)(2,1)}, bf16[2,2,2,2,12,32,128]{6,5,4,3,2,1,0:T(8,128)(2,1)S(1)}, u32[]{:S(2)}, u32[]{:S(2)}) collective-permute-start(bf16[2,2,2,2,12,32,128]{6,5,4,3,2,1,0:T(8,128)(2,1)} %get-tuple-element.51), channel_id=1, source_target_pairs={{0,2},{2,0},{4,6},{6,4},{1,3},{3,1},{5,7},{7,5},{8,10},{10,8},{12,... | collective-permute-start | bytes 4718600 | tf_op jit(solution)/shard_map/ppermute | solution.py:280
  80.7 22.1 %collective-permute-start.9 = (bf16[2,2,2,12,32,128]{5,4,3,2,1,0:T(8,128)(2,1)}, bf16[2,2,2,12,32,128]{5,4,3,2,1,0:T(8,128)(2,1)}, u32[]{:S(2)}, u32[]{:S(2)}) collective-permute-start(bf16[2,2,2,12,32,128]{5,4,3,2,1,0:T(8,128)(2,1)} %bitcast.61), channel_id=1, source_target_pairs={{0,4},{2,6},{4,0},{6,2},{1,5},{3,7},{5,1},{7,3},{8,12},{10,14},{12... | collective-permute-start | bytes 2359304 | tf_op jit(solution)/shard_map/ppermute | solution.py:280
  82.2 14.1 %copy-start.7 = (f32[32,12288]{1,0:T(8,128)S(1)}, f32[32,12288]{1,0:T(8,128)}, u32[]{:S(2)}) copy-start(f32[32,12288]{1,0:T(8,128)} %get-tuple-element.33) | copy-start | bytes 4718596
  95.7 19.9 %collective-permute-start.7 = (bf16[32,12288]{1,0:T(8,128)(2,1)}, bf16[32,12288]{1,0:T(8,128)(2,1)S(1)}, u32[]{:S(2)}, u32[]{:S(2)}) collective-permute-start(bf16[32,12288]{1,0:T(8,128)(2,1)} %bitcast.88), channel_id=1, source_target_pairs={{0,1},{1,0},{2,3},{3,2},{4,5},{5,4},{6,7},{7,6},{8,9},{9,8},{10,11... | collective-permute-start | bytes 2359304 | tf_op jit(solution)/shard_map/ppermute | solution.py:323
  96.3 10.2 %collective-permute-start.10 = (bf16[2,2,2,2,12,32,128]{6,5,4,3,2,1,0:T(8,128)(2,1)}, bf16[2,2,2,2,12,32,128]{6,5,4,3,2,1,0:T(8,128)(2,1)S(1)}, u32[]{:S(2)}, u32[]{:S(2)}) collective-permute-start(bf16[2,2,2,2,12,32,128]{6,5,4,3,2,1,0:T(8,128)(2,1)} %get-tuple-element.46), channel_id=1, source_target_pairs={{0,2},{2,0},{4,6},{6,4},{1,3},{3,1},{5,7},{7,5},{8,10},{10,8},{12,... | collective-permute-start | bytes 4718600 | tf_op jit(solution)/shard_map/ppermute | solution.py:280
  96.4 111.3 %collective-permute-start.2 = (bf16[32,12288]{1,0:T(8,128)(2,1)S(1)}, bf16[32,12288]{1,0:T(8,128)(2,1)S(1)}, u32[]{:S(2)}, u32[]{:S(2)}) collective-permute-start(bf16[32,12288]{1,0:T(8,128)(2,1)S(1)} %add_convert_fusion.1), channel_id=1, source_target_pairs={{8,0},{16,8},{24,16},{9,1},{17,9},{25,17},{10,2},{18,10},{26,18},{... | collective-permute-start | bytes 2359304 | tf_op jit(solution)/shard_map/ppermute | solution.py:276
  102.4 20.5 %collective-permute-start.16 = (bf16[2,2,2,12,32,128]{5,4,3,2,1,0:T(8,128)(2,1)}, bf16[2,2,2,12,32,128]{5,4,3,2,1,0:T(8,128)(2,1)S(1)}, u32[]{:S(2)}, u32[]{:S(2)}) collective-permute-start(bf16[2,2,2,12,32,128]{5,4,3,2,1,0:T(8,128)(2,1)} %bitcast.83), channel_id=1, source_target_pairs={{0,4},{2,6},{4,0},{6,2},{1,5},{3,7},{5,1},{7,3},{8,12},{10,14},{12... | collective-permute-start | bytes 2359304 | tf_op jit(solution)/shard_map/ppermute | solution.py:280
  107.6 8.0 %copy-start.8 = (f32[32,12288]{1,0:T(8,128)S(1)}, f32[32,12288]{1,0:T(8,128)}, u32[]{:S(2)}) copy-start(f32[32,12288]{1,0:T(8,128)} %get-tuple-element.42) | copy-start | bytes 4718596
  111.3 28.2 %collective-permute-start.11 = (bf16[2,2,2,12,32,128]{5,4,3,2,1,0:T(8,128)(2,1)}, bf16[2,2,2,12,32,128]{5,4,3,2,1,0:T(8,128)(2,1)S(1)}, u32[]{:S(2)}, u32[]{:S(2)}) collective-permute-start(bf16[2,2,2,12,32,128]{5,4,3,2,1,0:T(8,128)(2,1)} %bitcast.84), channel_id=1, source_target_pairs={{0,4},{2,6},{4,0},{6,2},{1,5},{3,7},{5,1},{7,3},{8,12},{10,14},{12... | collective-permute-start | bytes 2359304 | tf_op jit(solution)/shard_map/ppermute | solution.py:280
  115.6 3.8 %copy-start.21 = (bf16[24,32,128]{2,1,0:T(8,128)(2,1)S(1)}, bf16[24,32,128]{2,1,0:T(8,128)(2,1)}, u32[]{:S(2)}) copy-start(bf16[24,32,128]{2,1,0:T(8,128)(2,1)} %get-tuple-element.53) | copy-start | bytes 589828
  115.6 7.3 %copy-start.22 = (bf16[24,32,128]{2,1,0:T(8,128)(2,1)S(1)}, bf16[24,32,128]{2,1,0:T(8,128)(2,1)}, u32[]{:S(2)}) copy-start(bf16[24,32,128]{2,1,0:T(8,128)(2,1)} %get-tuple-element.54) | copy-start | bytes 589828
  115.8 92.0 %collective-permute-start.8 = (bf16[32,12288]{1,0:T(8,128)(2,1)S(1)}, bf16[32,12288]{1,0:T(8,128)(2,1)S(1)}, u32[]{:S(2)}, u32[]{:S(2)}) collective-permute-start(bf16[32,12288]{1,0:T(8,128)(2,1)S(1)} %add_convert_fusion), channel_id=1, source_target_pairs={{0,8},{8,16},{16,24},{1,9},{9,17},{17,25},{2,10},{10,18},{18,26},{... | collective-permute-start | bytes 2359304 | tf_op jit(solution)/shard_map/ppermute | solution.py:276
  119.4 28.1 %collective-permute-start.17 = (bf16[2,2,6,32,128]{4,3,2,1,0:T(8,128)(2,1)S(1)}, bf16[2,2,6,32,128]{4,3,2,1,0:T(8,128)(2,1)S(1)}, u32[]{:S(2)}, u32[]{:S(2)}) collective-permute-start(bf16[2,2,6,32,128]{4,3,2,1,0:T(8,128)(2,1)S(1)} %bitcast.92), channel_id=1, source_target_pairs={{0,24},{8,16},{16,8},{24,0},{1,25},{9,17},{17,9},{25,1},{2,26},{10... | collective-permute-start | bytes 589832 | tf_op jit(solution)/shard_map/ppermute | solution.py:309
  123.0 4.7 %copy-start.13 = (bf16[2,2,2,12,32,128]{5,4,3,2,1,0:T(8,128)(2,1)}, bf16[2,2,2,12,32,128]{5,4,3,2,1,0:T(8,128)(2,1)S(1)}, u32[]{:S(2)}) copy-start(bf16[2,2,2,12,32,128]{5,4,3,2,1,0:T(8,128)(2,1)S(1)} %collective-permute-done.16) | copy-start | bytes 2359300
  123.0 25.5 %collective-permute-start.18 = (bf16[2,2,6,32,128]{4,3,2,1,0:T(8,128)(2,1)S(1)}, bf16[2,2,6,32,128]{4,3,2,1,0:T(8,128)(2,1)S(1)}, u32[]{:S(2)}, u32[]{:S(2)}) collective-permute-start(bf16[2,2,6,32,128]{4,3,2,1,0:T(8,128)(2,1)S(1)} %bitcast.93), channel_id=1, source_target_pairs={{0,24},{8,16},{16,8},{24,0},{1,25},{9,17},{17,9},{25,1},{2,26},{10... | collective-permute-start | bytes 589832 | tf_op jit(solution)/shard_map/ppermute | solution.py:309
  139.4 4.4 %copy-start.14 = (bf16[2,2,2,12,32,128]{5,4,3,2,1,0:T(8,128)(2,1)}, bf16[2,2,2,12,32,128]{5,4,3,2,1,0:T(8,128)(2,1)S(1)}, u32[]{:S(2)}) copy-start(bf16[2,2,2,12,32,128]{5,4,3,2,1,0:T(8,128)(2,1)S(1)} %collective-permute-done.11) | copy-start | bytes 2359300
  139.4 14.6 %collective-permute-start.19 = (bf16[2,2,12,32,128]{4,3,2,1,0:T(8,128)(2,1)}, bf16[2,2,12,32,128]{4,3,2,1,0:T(8,128)(2,1)S(1)}, u32[]{:S(2)}, u32[]{:S(2)}) collective-permute-start(bf16[2,2,12,32,128]{4,3,2,1,0:T(8,128)(2,1)} %bitcast.90), channel_id=1, source_target_pairs={{0,24},{8,16},{16,8},{24,0},{1,25},{9,17},{17,9},{25,1},{2,26},{10... | collective-permute-start | bytes 1179656 | tf_op jit(solution)/shard_map/ppermute | solution.py:309
  143.8 3.7 %copy-start.20 = (bf16[48,32,128]{2,1,0:T(8,128)(2,1)S(1)}, bf16[48,32,128]{2,1,0:T(8,128)(2,1)}, u32[]{:S(2)}) copy-start(bf16[48,32,128]{2,1,0:T(8,128)(2,1)} %get-tuple-element.48) | copy-start | bytes 1179652
  147.5 6.6 %copy-start.11 = (bf16[2,2,6,32,128]{4,3,2,1,0:T(8,128)(2,1)}, bf16[2,2,6,32,128]{4,3,2,1,0:T(8,128)(2,1)S(1)}, u32[]{:S(2)}) copy-start(bf16[2,2,6,32,128]{4,3,2,1,0:T(8,128)(2,1)S(1)} %collective-permute-done.17.refs_3_) | copy-start | bytes 589828
  147.5 45.1 %collective-permute-start.12 = (bf16[2,2,12,32,128]{4,3,2,1,0:T(8,128)(2,1)S(1)}, bf16[2,2,12,32,128]{4,3,2,1,0:T(8,128)(2,1)S(1)}, u32[]{:S(2)}, u32[]{:S(2)}) collective-permute-start(bf16[2,2,12,32,128]{4,3,2,1,0:T(8,128)(2,1)S(1)} %bitcast.89), channel_id=1, source_target_pairs={{0,24},{8,16},{16,8},{24,0},{1,25},{9,17},{17,9},{25,1},{2,26},{10... | collective-permute-start | bytes 1179656 | tf_op jit(solution)/shard_map/ppermute | solution.py:309
  148.4 5.6 %copy-start.12 = (bf16[2,2,6,32,128]{4,3,2,1,0:T(8,128)(2,1)}, bf16[2,2,6,32,128]{4,3,2,1,0:T(8,128)(2,1)S(1)}, u32[]{:S(2)}) copy-start(bf16[2,2,6,32,128]{4,3,2,1,0:T(8,128)(2,1)S(1)} %collective-permute-done.18.refs_4_) | copy-start | bytes 589828
  148.4 44.2 %collective-permute-start.13 = (bf16[2,2,12,32,128]{4,3,2,1,0:T(8,128)(2,1)}, bf16[2,2,12,32,128]{4,3,2,1,0:T(8,128)(2,1)S(1)}, u32[]{:S(2)}, u32[]{:S(2)}) collective-permute-start(bf16[2,2,12,32,128]{4,3,2,1,0:T(8,128)(2,1)} %bitcast.91), channel_id=1, source_target_pairs={{0,24},{8,16},{16,8},{24,0},{1,25},{9,17},{17,9},{25,1},{2,26},{10... | collective-permute-start | bytes 1179656 | tf_op jit(solution)/shard_map/ppermute | solution.py:309
  157.1 51.9 %collective-permute-start.20 = (bf16[2,2,12,32,128]{4,3,2,1,0:T(8,128)(2,1)}, bf16[2,2,12,32,128]{4,3,2,1,0:T(8,128)(2,1)S(1)}, u32[]{:S(2)}, u32[]{:S(2)}) collective-permute-start(bf16[2,2,12,32,128]{4,3,2,1,0:T(8,128)(2,1)} %mirror_0.1), channel_id=1, source_target_pairs={{0,8},{8,0},{16,24},{24,16},{1,9},{9,1},{17,25},{25,17},{2,10},{10... | collective-permute-start | bytes 1179656 | tf_op jit(solution)/shard_map/ppermute | solution.py:286
  195.7 20.0 %collective-permute-start.14 = (bf16[2,2,12,32,128]{4,3,2,1,0:T(8,128)(2,1)}, bf16[2,2,12,32,128]{4,3,2,1,0:T(8,128)(2,1)S(1)}, u32[]{:S(2)}, u32[]{:S(2)}) collective-permute-start(bf16[2,2,12,32,128]{4,3,2,1,0:T(8,128)(2,1)} %mirror_12.1), channel_id=1, source_target_pairs={{0,8},{8,0},{16,24},{24,16},{1,9},{9,1},{17,25},{25,17},{2,10},{10... | collective-permute-start | bytes 1179656 | tf_op jit(solution)/shard_map/ppermute | solution.py:286
  (12 other events, 10.7 us)

commit v4 on v3

--- a/solution.py
+++ b/solution.py
@@ -12,6 +12,7 @@
 CUBIC = 0.044715
 GROUP = 6
 VMEM = 56 * 1024 * 1024
+SMALL = pl.CostEstimate(flops=1000, bytes_accessed=1000, transcendentals=0)
 F32 = jnp.float32
 BF16 = jnp.bfloat16
 
@@ -25,17 +26,15 @@
     return base + jnp.where(at < size, at, at - size)
 
 
-def tick_kernel(relay, first_block, piece_blocks, sections, has_acc, last, n_deps, *refs):
+def tick_kernel(relay, first_block, piece_blocks, sections, before, last, n_deps, *refs):
     len_ref, idx_in_ref, idx_out_ref, x_ref, g_ref, w_in_ref, w_out_ref = refs[:7]
-    refs = refs[7:]
-    if has_acc:
-        before_ref, refs = refs[0], refs[1:]
-    refs = refs[n_deps:]
+    before_refs = refs[7:7 + len(before)]
+    refs = refs[7 + len(before) + n_deps:]
     keep_ref, send_ref = refs[:2]
     if last:
         own_ref, other_ref, acc_ref = refs[2:]
     else:
-        (acc_ref,) = refs[2:]
+        (terms_ref,) = refs[2:]
     half, turn, part = pl.program_id(0), pl.program_id(1), pl.program_id(2)
     opening = (half == 0) & (turn == 0) & (part == 0)
     closing = (half == 1) & (turn == pl.num_programs(1) - 1) & (part == pl.num_programs(2) - 1)
@@ -45,9 +44,17 @@
     piece = keep_ref.shape[3]
     live = lax.broadcasted_iota(jnp.int32, (rows, block), 0) < len_ref[relay, 0, 0]
 
-    @pl.when(opening)
-    def _():
-        acc_ref[...] = before_ref[...] if has_acc else jnp.zeros_like(acc_ref)
+    if last:
+        @pl.when(opening)
+        def _():
+            acc_ref[...] = jnp.zeros_like(acc_ref)
+            for lo, ref in zip(before, before_refs):
+                size, count = ref.shape[1:3]
+                for h in range(2):
+                    for t in range(size):
+                        at = owner(h, t, sections) * piece_blocks + lo
+                        for i in range(count):
+                            acc_ref[idx_in_ref[0, relay, at + i]] += ref[h, t, i]
 
     odd = me % 2 == 1
 
@@ -83,7 +90,10 @@
         grad_in = [lax.dot_general(a, v, over_rows, preferred_element_type=F32) for a, v in zip(picked, grad_pre)]
         grad_out = [lax.dot_general(a, v, over_rows, preferred_element_type=F32) for a, v in zip(act, back)]
         for i, b, term, g_in, g_out in zip(group, sources, terms, grad_in, grad_out):
-            acc_ref[b] += term
+            if last:
+                acc_ref[b] += term
+            else:
+                terms_ref[i] = term
             put(0, i, g_in)
             put(1, i, g_out)
 
@@ -123,7 +133,6 @@
         (n_dp // 2, None, 2, None, per_step, rows_cut, block), lambda h, t, i, *_: (0, h, 0, t, i, 0, 0)
     )
     acc_shape = (width // block, rows, block)
-    acc_spec = pl.BlockSpec(acc_shape, lambda h, t, i, *_: (0, 0, 0))
     share = rows // n_mp
     out_specs, out_shape, scratch = [slots_spec] * 2, [slots] * 2, []
     if last:
@@ -134,64 +143,24 @@
         out_shape += [jax.ShapeDtypeStruct((share, width), F32), jax.ShapeDtypeStruct((n_mp - 1, share, width), BF16)]
         scratch = [pltpu.VMEM(acc_shape, F32)]
     else:
-        out_specs.append(acc_spec)
-        out_shape.append(jax.ShapeDtypeStruct(acc_shape, F32))
-    held = [] if before is None else [before]
-    done = size * 2 * (hi - lo)
+        out_specs.append(pl.BlockSpec((None, None, per_step, rows, block), lambda h, t, i, *_: (h, t, i, 0, 0)))
+        out_shape.append(jax.ShapeDtypeStruct((2, size, hi - lo, rows, block), F32))
+    held = [a for _, a in before]
+    held_specs = [pl.BlockSpec(a.shape, lambda h, t, i, *_: (0,) * 5) for a in held]
     return pl.pallas_call(
-        functools.partial(tick_kernel, relay, lo, piece_blocks, sections, bool(held), last, len(deps)),
+        functools.partial(tick_kernel, relay, lo, piece_blocks, sections, [at for at, _ in before], last, len(deps)),
         grid_spec=pltpu.PrefetchScalarGridSpec(
             num_scalar_prefetch=3,
             grid=(2, size, steps),
-            in_specs=[whole, whole, weight, weight] + [acc_spec] * len(held) + [pl.BlockSpec(memory_space=pl.ANY)] * len(deps),
+            in_specs=[whole, whole, weight, weight] + held_specs + [pl.BlockSpec(memory_space=pl.ANY)] * len(deps),
             out_specs=out_specs,
             scratch_shapes=scratch,
         ),
         out_shape=out_shape,
         compiler_params=pltpu.CompilerParams(dimension_semantics=("arbitrary",) * 3, vmem_limit_bytes=VMEM),
-        cost_estimate=pl.CostEstimate(
-            flops=done * 10 * rows * block * block,
-            bytes_accessed=done * block * block * 8 + rows * width * 8,
-            transcendentals=done * rows * block,
-        ),
+        cost_estimate=SMALL,
         name=f"tick{relay}_{lo}",
     )(lengths, idx_in, idx_out, section_in, out_grad, w_in, w_out, *held, *deps)
-
-
-def add_kernel(n_terms, apart, n_deps, *refs):
-    terms, outs = refs[:n_terms], refs[n_terms + n_deps:]
-    for k in range(2):
-        total = terms[0][k].astype(F32)
-        for term in terms[1:]:
-            total += term[k].astype(F32)
-        if apart:
-            outs[k][...] = total.astype(BF16)
-        else:
-            outs[0][k] = total.astype(BF16)
-
-
-def add(terms, apart, name, deps=()):
-    shape = terms[0][0].shape[-6:]
-    flat = [(a.reshape(-1, math.prod(shape[1:4]), *shape[4:]), k) for a, k in terms]
-    count, rows, block = flat[0][0].shape[1:]
-    step = math.gcd(count, max(count // 4, 1))
-    if apart:
-        out_specs = [pl.BlockSpec((step, rows, block), lambda i: (i, 0, 0))] * 2
-        out_shape = [jax.ShapeDtypeStruct((count, rows, block), BF16)] * 2
-    else:
-        out_specs = [pl.BlockSpec((2, step, rows, block), lambda i: (0, i, 0, 0))]
-        out_shape = [jax.ShapeDtypeStruct((2, count, rows, block), BF16)]
-    outs = pl.pallas_call(
-        functools.partial(add_kernel, len(flat), apart, len(deps)),
-        grid=(count // step,),
-        in_specs=[pl.BlockSpec((2, step, rows, block), lambda i, k=k: (k, i, 0, 0)) for _, k in flat]
-        + [pl.BlockSpec(memory_space=pl.ANY)] * len(deps),
-        out_specs=out_specs,
-        out_shape=out_shape,
-        compiler_params=pltpu.CompilerParams(vmem_limit_bytes=VMEM),
-        name=name,
-    )(*[a for a, _ in flat], *deps)
-    return [o.reshape(shape[1:] if apart else shape) for o in outs]
 
 
 def segments(spans):
@@ -202,72 +171,95 @@
     return found
 
 
+def layer_parts(spans, refs):
+    own, far = [], []
+    for relay in spans:
+        own.append([refs[4 * i:4 * i + 3] for i in range(len(relay))])
+        far.append([refs[4 * i + 3] for i in range(len(relay))])
+        refs = refs[4 * len(relay):]
+
+    def at(start, length, places, r, index):
+        (i, here), (j, there) = places[r], places[1 - r]
+        parts = [ref[(slice(None),) + index + (slice(here, here + length),)] for ref in own[r][i]]
+        parts.append(far[1 - r][j][(slice(None),) + index + (slice(there, there + length),)])
+        return functools.reduce(lambda a, b: a + b, [p.astype(F32) for p in parts])
+
+    return at, refs
+
+
 def mirror_kernel(spans, size, *refs):
-    n = [len(relay) for relay in spans]
-    own = [refs[:n[0]], refs[n[0]:n[0] + n[1]]]
-    far = [refs[sum(n):sum(n) + n[0]], refs[sum(n) + n[0]:2 * sum(n)]]
-    outs = refs[2 * sum(n):]
+    at, outs = layer_parts(spans, refs)
     for start, length, places in segments(spans):
         for r in range(2):
-            (i, at), (j, there) = places[r], places[1 - r]
             for turn in range(1, size):
-                total = own[r][i][:, turn, at:at + length].astype(F32) + far[1 - r][j][:, turn, there:there + length].astype(F32)
-                outs[turn - 1][r, :, start:start + length] = total.astype(BF16)
-
-
-def mirror_sum(spans, own, far, name):
-    _, size, _, rows, block = own[0][0].shape
+                outs[turn - 1][r, :, start:start + length] = at(start, length, places, r, (turn,)).astype(BF16)
+
+
+def cut_operands(groups, turn):
+    arrays, specs = [], []
+    for relay in groups:
+        for keep, got, came, far in relay:
+            tail = keep.shape[4:]
+            turns = None if turn is not None else keep.shape[3]
+            for a, lead in ((keep, (0, 1)), (got, (0, 1)), (came, (1,)), (far, ())):
+                arrays.append(a)
+                index = lead + (0, turn or 0, 0, 0, 0)
+                specs.append(pl.BlockSpec((None,) * len(lead) + (2, turns) + tail, lambda i, index=index: index))
+    return arrays, specs
+
+
+def mirror_sum(spans, groups, name):
+    arrays, specs = cut_operands(groups, None)
+    size, _, rows, block = arrays[3].shape[1:]
     long = spans[0][-1][1] - spans[0][0][0]
-    flat = own[0] + own[1] + far[0] + far[1]
+    shape = (2, 2, long, rows, block)
     return pl.pallas_call(
         functools.partial(mirror_kernel, spans, size),
-        out_shape=[jax.ShapeDtypeStruct((2, 2, long, rows, block), BF16)] * (size - 1),
+        grid=(1,),
+        in_specs=specs,
+        out_specs=[pl.BlockSpec(shape, lambda i: (0,) * 5)] * (size - 1),
+        out_shape=[jax.ShapeDtypeStruct(shape, BF16)] * (size - 1),
         compiler_params=pltpu.CompilerParams(vmem_limit_bytes=VMEM),
+        cost_estimate=SMALL,
         name=name,
-    )(*flat)
-
-
-def grads_kernel(spans, sections, has_before, *refs):
+    )(*arrays)
+
+
+def grads_kernel(spans, sections, *refs):
     size = sections // 2
-    n = [len(relay) for relay in spans]
-    own = [refs[:n[0]], refs[n[0]:n[0] + n[1]]]
-    far = [refs[sum(n):sum(n) + n[0]], refs[sum(n) + n[0]:2 * sum(n)]]
-    came = refs[2 * sum(n):2 * sum(n) + size - 1]
-    out = refs[-1]
+    at, refs = layer_parts(spans, refs)
+    came, out = refs[:size - 1], refs[-1]
     me = lax.axis_index("section")
     base = jnp.where(me < size, 0, size)
     for start, length, places in segments(spans):
         for r in range(2):
-            (i, at), (j, there) = places[r], places[1 - r]
-            layer = sections - 1 - me if r else me
-            total = own[r][i][:, at:at + length].astype(F32) + far[1 - r][j][:, there:there + length].astype(F32)
-            out[layer, :, start:start + length] = total
+            out[sections - 1 - me if r else me, :, start:start + length] = at(start, length, places, r, ())
     for turn in range(1, size):
-        at = me - base - turn
-        source = base + jnp.where(at < 0, at + size, at)
+        place = me - base - turn
+        source = base + jnp.where(place < 0, place + size, place)
         for r in range(2):
             out[sections - 1 - source if r else source] = came[turn - 1][r].astype(F32)
 
 
-def write_grads(spans, own, far, came, before, sections, piece_blocks, name):
-    rows, block = own[0][0].shape[3:]
+def write_grads(spans, groups, came, before, sections, piece_blocks, name):
+    arrays, specs = cut_operands(groups, 0)
+    rows, block = arrays[3].shape[3:]
     long = spans[0][-1][1] - spans[0][0][0]
     place = spans[0][0][0] // long
-    first = lambda a: pl.BlockSpec((2, None) + a.shape[2:], lambda i: (0, 0, 0, 0, 0))
-    flat = own[0] + own[1] + far[0] + far[1]
     held = [] if before is None else [before]
     return pl.pallas_call(
-        functools.partial(grads_kernel, spans, sections, bool(held)),
+        functools.partial(grads_kernel, spans, sections),
         grid=(1,),
-        in_specs=[first(a) for a in flat]
-        + [pl.BlockSpec(a.shape, lambda i: (0, 0, 0, 0, 0)) for a in came]
+        in_specs=specs
+        + [pl.BlockSpec(a.shape, lambda i: (0,) * 5) for a in came]
         + [pl.BlockSpec(memory_space=pl.ANY)] * len(held),
         out_specs=pl.BlockSpec((sections, 2, None, long, rows, block), lambda i: (0, 0, 0, place, 0, 0)),
         out_shape=jax.ShapeDtypeStruct((sections, 2, 1, piece_blocks, rows, block), F32),
-        input_output_aliases={len(flat) + len(came): 0} if held else {},
+        input_output_aliases={len(arrays) + len(came): 0} if held else {},
         compiler_params=pltpu.CompilerParams(vmem_limit_bytes=VMEM),
+        cost_estimate=SMALL,
         name=name,
-    )(*flat, *came, *held)
+    )(*arrays, *came, *held)
 
 
 def from_behind(value, axis, distance):
@@ -296,27 +288,26 @@
     chunks = [(0, lo, hi) for lo, hi in zip(fine, fine[1:])] + [(1, lo, hi) for lo, hi in zip(cuts, cuts[1:])]
     mirror = [(i, sections - 1 - i) for i in range(sections)]
 
-    keep, got, sum_a, came, kept, arrived, passed = {}, {}, {}, {}, {}, {}, []
-    acc = None
+    keep, got, sum_a, came, away, arrived, passed = {}, {}, {}, {}, {}, {}, []
+    before = []
 
     def stage_a(c):
-        deps = [kept[c - 2]] if c - 2 in kept else []
-        (sum_a[c],) = add([(keep[c], 1), (got[c], 1)], False, f"core{c}", deps)
+        sum_a[c] = (keep[c][1].astype(F32) + got[c][1].astype(F32)).astype(BF16)
         came[c] = flip_bit(sum_a[c], "dp", 2)
 
     def stage_b(c):
-        away, kept[c] = add([(keep[c], 0), (got[c], 0), (came[c], 0)], True, f"pair{c}")
-        arrived[c] = lax.ppermute(away, "section", mirror)
+        away[c] = (keep[c][0, 0].astype(F32) + got[c][0, 0].astype(F32) + came[c][0].astype(F32)).astype(BF16)
+        arrived[c] = lax.ppermute(away[c], "section", mirror)
 
     for c, (relay, lo, hi) in enumerate(chunks):
         last = hi == piece_blocks
         deps = [sum_a[c - 2]] if c >= 2 else []
         if c >= 3:
-            deps.append(kept[c - 3])
-        results = tick(relay, lo, hi, acc, last, deps, (sections, n_dp, n_mp), args)
+            deps.append(away[c - 3])
+        results = tick(relay, lo, hi, before, last, deps, (sections, n_dp, n_mp), args)
         keep[c], send = results[:2]
         got[c] = flip_bit(send, "dp", 1)
-        acc = None if last else results[2]
+        before = [] if last else before + [(lo, results[2])]
         if last:
             dx, others = results[2:]
             for k in range(1, n_mp):
@@ -336,11 +327,10 @@
     for lo, hi in zip(cuts, cuts[1:]):
         inside = [[c for c, (r, a, b) in enumerate(chunks) if r == relay and lo <= a < hi] for relay in range(2)]
         spans = [[chunks[c][1:] for c in relay] for relay in inside]
-        own = [[kept[c] for c in relay] for relay in inside]
-        far = [[arrived[c] for c in relay] for relay in inside]
-        to_turn = mirror_sum(spans, own, far, f"mirror_{lo}") if size > 1 else []
+        groups = [[(keep[c], got[c], came[c], arrived[c]) for c in relay] for relay in inside]
+        to_turn = mirror_sum(spans, groups, f"mirror_{lo}") if size > 1 else []
         turned = [turn_half(v, turn + 1) for turn, v in enumerate(to_turn)]
-        grads = write_grads(spans, own, far, turned, grads, sections, piece_blocks, f"grads_{lo}")
+        grads = write_grads(spans, groups, turned, grads, sections, piece_blocks, f"grads_{lo}")
     return jnp.stack(passed, axis=0)[:, None], grads
 
 

time: 221 us -> 202 us (0.914)
  Pallas kernels: 100 us -> 63.2 us
  waiting for transfers between devices: 26.4 us -> 60.2 us
  starting transfers between devices: 78.6 us -> 61.8 us
  other arithmetic: 1.54 us -> 10 us
  local copies, waits for them, and re-layouts: 11.2 us -> 5.18 us
    pallas_call x14 -> x4, Pallas kernels: 44.6 us -> 11.6 us  [the longest x2 5.94 us: write_grads(): pl.pallas_call(functools.partial(grads_kernel, spans, sections), grid=(1,...]
    ppermute x10, waiting for transfers between devices: 17.8 us -> 39.4 us  [flip_bit(): lax.ppermute(value, axis, [(i, i ^ bit) for i in range(lax.axis_size(axis...]
    ppermute x2, starting transfers between devices: 47.5 us -> 35.3 us  [turn_half(): return lax.ppermute(value, 'section', route)]
    ppermute x2, waiting for transfers between devices: 2.73 us -> 13 us  [body(): lax.ppermute(others[k - 1], 'mp', [(i, (i + k) % n_mp) for i in range(n_m...]
    unnamed x47 -> x55, local copies, waits for them, and re-layouts: 11.2 us -> 5.18 us
    convert_element_type x0 -> x10, other arithmetic: none -> 4.28 us  [the longest x5 2.87 us: stage_a(): sum_a[c] = (keep[c][1].astype(F32) + got[c][1].astype(F32)).astype(BF16)]
    pallas_call x5, Pallas kernels: 55.8 us -> 51.6 us  [tick(): pl.pallas_call(functools.partial(tick_kernel, relay, lo, piece_blocks, se...]
    ppermute x5, waiting for transfers between devices: 2.68 us -> 6.35 us  [stage_b(): arrived[c] = lax.ppermute(away[c], 'section', mirror)]
  transfers between devices with their start and end apart: 21 -> 21, of which waited for: 7 -> 7; matrix products, arithmetic and copies ran while one was open for 1% -> 5% of each run, Pallas kernels for 33% -> 26%
where the time goes in v4:
time: 202 us; the launch traced here: 201 us
  Pallas kernels  63.2 us (31%)
  starting transfers between devices  61.8 us (31%)
  waiting for transfers between devices  60.2 us (30%)
  other arithmetic  10 us (5%)
  local copies, waits for them, and re-layouts  5.18 us (3%)
    pallas_call x5, Pallas kernels, tick(): pl.pallas_call(functools.partial(tick_kernel, relay, lo, piece_blocks, se...  51.6 us
    ppermute x10, waiting for transfers between devices, flip_bit(): lax.ppermute(value, axis, [(i, i ^ bit) for i in range(lax.axis_size(axis...  39.4 us
    ppermute x2, starting transfers between devices, turn_half(): return lax.ppermute(value, 'section', route)  35.3 us
    ppermute x2, waiting for transfers between devices, body(): lax.ppermute(others[k - 1], 'mp', [(i, (i + k) % n_mp) for i in range(n_m...  13 us
    ppermute x5, starting transfers between devices, stage_b(): arrived[c] = lax.ppermute(away[c], 'section', mirror)  11.6 us
    ppermute x10, starting transfers between devices, flip_bit(): lax.ppermute(value, axis, [(i, i ^ bit) for i in range(lax.axis_size(axis...  7.78 us
    ppermute x5, waiting for transfers between devices, stage_b(): arrived[c] = lax.ppermute(away[c], 'section', mirror)  6.35 us
    pallas_call x2, Pallas kernels, write_grads(): pl.pallas_call(functools.partial(grads_kernel, spans, sections), grid=(1,...  5.94 us
  transfers between devices with their start and end apart: 21, of which 7 were waited for; matrix products, arithmetic and copies ran while one was open for 5% of the time, Pallas kernels for 26%

profile of v4, /device:TPU:0, one launch (start us, length us, event | category | flops | bytes accessed | tf_op | source)
XLA Modules:
  0.0 201.2 jit_solution(16657802701004304947)
XLA Ops:
  0.6 1.3 copy.12.refs_0_
  1.9 6.9 %tick0_0.1 = (bf16[2,2,2,2,6,32,128]{6,5,4,3,2,1,0:T(8,128)(2,1)}, bf16[2,2,2,2,6,32,128]{6,5,4,3,2,1,0:T(8,128)(2,1)}, f32[2,2,6,64,128]{4,3,2,1,0:T(8,128)}) custom-call(s32[2,1,1]{2,1,0:T(1,128)} %copy.12.refs_0_, s32[1,2,96]{2,1,0:T(2,128)} %refs_1_.9, s32[1,2,96]{2,1,0:T(2,128)} %refs_2_.9, bf16[2,1,64,12288]{3,2,1,0:T(8,128)(2,1)} %refs_3_.9, ...), custom_call_target="tpu_custom_call" | custom-call | flops 1000 | bytes 1000 | tf_op jit(solution)/shard_map/tick0_0/pallas_call | solution.py:150
  9.3 7.3 %tick0_6.1 = (bf16[2,2,2,2,6,32,128]{6,5,4,3,2,1,0:T(8,128)(2,1)}, bf16[2,2,2,2,6,32,128]{6,5,4,3,2,1,0:T(8,128)(2,1)}, f32[2,2,6,64,128]{4,3,2,1,0:T(8,128)}) custom-call(s32[2,1,1]{2,1,0:T(1,128)} %copy.12.refs_0_, s32[1,2,96]{2,1,0:T(2,128)} %refs_1_.9, s32[1,2,96]{2,1,0:T(2,128)} %refs_2_.9, bf16[2,1,64,12288]{3,2,1,0:T(8,128)(2,1)} %refs_3_.9, ...), custom_call_target="tpu_custom_call" | custom-call | flops 1000 | bytes 1000 | tf_op jit(solution)/shard_map/tick0_6/pallas_call | solution.py:150
  17.7 13.3 %tick0_12.1 = (bf16[2,2,2,2,12,32,128]{6,5,4,3,2,1,0:T(8,128)(2,1)}, bf16[2,2,2,2,12,32,128]{6,5,4,3,2,1,0:T(8,128)(2,1)}, f32[32,12288]{1,0:T(8,128)}, bf16[1,32,12288]{2,1,0:T(8,128)(2,1)}) custom-call(s32[2,1,1]{2,1,0:T(1,128)} %copy.12.refs_0_, s32[1,2,96]{2,1,0:T(2,128)} %refs_1_.9, s32[1,2,96]{2,1,0:T(2,128)} %refs_2_.9, ...), custom_call_target="tpu_custom_call" | custom-call | flops 1000 | bytes 1000 | tf_op jit(solution)/shard_map/tick0_12/pallas_call | solution.py:150
  31.5 2.6 %collective-permute-start.4 = (bf16[2,2,2,6,32,128]{5,4,3,2,1,0:T(8,128)(2,1)S(1)}, bf16[2,2,2,6,32,128]{5,4,3,2,1,0:T(8,128)(2,1)S(1)}, u32[]{:S(2)}, u32[]{:S(2)}) collective-permute-start(bf16[2,2,2,6,32,128]{5,4,3,2,1,0:T(8,128)(2,1)S(1)} %copy-done.19), channel_id=1, source_target_pairs={{0,4},{2,6},{4,0},{6,2},{1,5},{3,7},{5,1},{7,3},{8,12},{10,14},{12... | collective-permute-start | bytes 1179656 | tf_op jit(solution)/shard_map/ppermute | solution.py:272
  34.3 2.1 %collective-permute-start.1 = (bf16[32,12288]{1,0:T(8,128)(2,1)}, bf16[32,12288]{1,0:T(8,128)(2,1)}, u32[]{:S(2)}, u32[]{:S(2)}) collective-permute-start(bf16[32,12288]{1,0:T(8,128)(2,1)} %bitcast.54), channel_id=1, source_target_pairs={{0,1},{1,0},{2,3},{3,2},{4,5},{5,4},{6,7},{7,6},{8,9},{9,8},{10,11... | collective-permute-start | bytes 2359304 | tf_op jit(solution)/shard_map/ppermute | solution.py:314
  36.4 7.6 %collective-permute-done.4.refs_2_ = bf16[2,2,2,6,32,128]{5,4,3,2,1,0:T(8,128)(2,1)S(1)} collective-permute-done((bf16[2,2,2,6,32,128]{5,4,3,2,1,0:T(8,128)(2,1)S(1)}, bf16[2,2,2,6,32,128]{5,4,3,2,1,0:T(8,128)(2,1)S(1)}, u32[]{:S(2)}, u32[]{:S(2)}) %collective-permute-start.4) | collective-permute-done | bytes 393248 | tf_op jit(solution)/shard_map/ppermute | solution.py:272
  44.9 4.1 %collective-permute-start.15 = (bf16[2,2,6,32,128]{4,3,2,1,0:T(8,128)(2,1)}, bf16[2,2,6,32,128]{4,3,2,1,0:T(8,128)(2,1)}, u32[]{:S(2)}, u32[]{:S(2)}) collective-permute-start(bf16[2,2,6,32,128]{4,3,2,1,0:T(8,128)(2,1)} %fusion.9.refs_8_), channel_id=1, source_target_pairs={{0,24},{8,16},{16,8},{24,0},{1,25},{9,17},{17,9},{25,1},{2,26},{10... | collective-permute-start | bytes 589832 | tf_op jit(solution)/shard_map/ppermute | solution.py:300
  49.0 10.8 %tick1_0.1 = (bf16[2,2,2,2,12,32,128]{6,5,4,3,2,1,0:T(8,128)(2,1)}, bf16[2,2,2,2,12,32,128]{6,5,4,3,2,1,0:T(8,128)(2,1)}, f32[2,2,12,64,128]{4,3,2,1,0:T(8,128)}) custom-call(s32[2,1,1]{2,1,0:T(1,128)} %copy.12.refs_0_, s32[1,2,96]{2,1,0:T(2,128)} %refs_1_.9, s32[1,2,96]{2,1,0:T(2,128)} %refs_2_.9, bf16[2,1,64,12288]{3,2,1,0:T(8,128)(2,1)} %refs_3_.9, ...), custom_call_target="tpu_custom_call" | custom-call | flops 1000 | bytes 1000 | tf_op jit(solution)/shard_map/tick1_0/pallas_call | solution.py:150
  60.1 1.3 fusion.refs_8_
  61.4 13.3 %tick1_12.1 = (bf16[2,2,2,2,12,32,128]{6,5,4,3,2,1,0:T(8,128)(2,1)}, bf16[2,2,2,2,12,32,128]{6,5,4,3,2,1,0:T(8,128)(2,1)}, f32[32,12288]{1,0:T(8,128)}, bf16[1,32,12288]{2,1,0:T(8,128)(2,1)}) custom-call(s32[2,1,1]{2,1,0:T(1,128)} %copy.12.refs_0_, s32[1,2,96]{2,1,0:T(2,128)} %refs_1_.9, s32[1,2,96]{2,1,0:T(2,128)} %refs_2_.9, ...), custom_call_target="tpu_custom_call" | custom-call | flops 1000 | bytes 1000 | tf_op jit(solution)/shard_map/tick1_12/pallas_call | solution.py:150
  74.7 2.0 collective-permute-start.7
  76.9 2.3 %add_convert_fusion.4 = bf16[32,12288]{1,0:T(8,128)(2,1)} fusion(f32[32,12288]{1,0:T(8,128)S(1)} %copy-done.17, bf16[32,12288]{1,0:T(8,128)(2,1)} %collective-permute-done.1), kind=kLoop, calls=%fused_computation.5 | loop fusion | flops 1179648 | bytes 3145728 | tf_op jit(solution)/shard_map/convert_element_type | solution.py:315
  79.2 1.6 collective-permute-start.9
  82.1 13.0 %collective-permute-done.7 = bf16[32,12288]{1,0:T(8,128)(2,1)S(1)} collective-permute-done((bf16[32,12288]{1,0:T(8,128)(2,1)}, bf16[32,12288]{1,0:T(8,128)(2,1)S(1)}, u32[]{:S(2)}, u32[]{:S(2)}) %collective-permute-start.7) | collective-permute-done | bytes 786464 | tf_op jit(solution)/shard_map/ppermute | solution.py:314
  95.1 1.5 collective-permute-start.12
  97.7 2.0 %collective-permute-done.9.refs_2_ = bf16[2,2,2,12,32,128]{5,4,3,2,1,0:T(8,128)(2,1)S(1)} collective-permute-done((bf16[2,2,2,12,32,128]{5,4,3,2,1,0:T(8,128)(2,1)S(1)}, bf16[2,2,2,12,32,128]{5,4,3,2,1,0:T(8,128)(2,1)S(1)}, u32[]{:S(2)}, u32[]{:S(2)}) %collective-permute-start.9) | collective-permute-done | bytes 786464 | tf_op jit(solution)/shard_map/ppermute | solution.py:272
  99.7 1.3 collective-permute-start.2
  101.1 15.4 %collective-permute-done.18.refs_10_ = bf16[2,2,2,12,32,128]{5,4,3,2,1,0:T(8,128)(2,1)S(1)} collective-permute-done((bf16[2,2,2,12,32,128]{5,4,3,2,1,0:T(8,128)(2,1)S(1)}, bf16[2,2,2,12,32,128]{5,4,3,2,1,0:T(8,128)(2,1)S(1)}, u32[]{:S(2)}, u32[]{:S(2)}) %collective-permute-start.18) | collective-permute-done | bytes 786464 | tf_op jit(solution)/shard_map/ppermute | solution.py:272
  116.5 1.7 collective-permute-start.8
  118.4 14.3 %collective-permute-done.12.refs_6_ = bf16[2,2,2,12,32,128]{5,4,3,2,1,0:T(8,128)(2,1)S(1)} collective-permute-done((bf16[2,2,2,12,32,128]{5,4,3,2,1,0:T(8,128)(2,1)S(1)}, bf16[2,2,2,12,32,128]{5,4,3,2,1,0:T(8,128)(2,1)S(1)}, u32[]{:S(2)}, u32[]{:S(2)}) %collective-permute-start.12) | collective-permute-done | bytes 786464 | tf_op jit(solution)/shard_map/ppermute | solution.py:272
  132.8 3.5 %collective-permute-start.19 = (bf16[2,2,12,32,128]{4,3,2,1,0:T(8,128)(2,1)S(1)}, bf16[2,2,12,32,128]{4,3,2,1,0:T(8,128)(2,1)S(1)}, u32[]{:S(2)}, u32[]{:S(2)}) collective-permute-start(bf16[2,2,12,32,128]{4,3,2,1,0:T(8,128)(2,1)S(1)} %fusion.3), channel_id=1, source_target_pairs={{0,24},{8,16},{16,8},{24,0},{1,25},{9,17},{17,9},{25,1},{2,26},{10... | collective-permute-start | bytes 1179656 | tf_op jit(solution)/shard_map/ppermute | solution.py:300
  137.1 3.2 %collective-permute-start.13 = (bf16[2,2,12,32,128]{4,3,2,1,0:T(8,128)(2,1)S(1)}, bf16[2,2,12,32,128]{4,3,2,1,0:T(8,128)(2,1)S(1)}, u32[]{:S(2)}, u32[]{:S(2)}) collective-permute-start(bf16[2,2,12,32,128]{4,3,2,1,0:T(8,128)(2,1)S(1)} %fusion.4), channel_id=1, source_target_pairs={{0,24},{8,16},{16,8},{24,0},{1,25},{9,17},{17,9},{25,1},{2,26},{10... | collective-permute-start | bytes 1179656 | tf_op jit(solution)/shard_map/ppermute | solution.py:300
  140.3 6.3 %collective-permute-done.19.refs_11_ = bf16[2,2,12,32,128]{4,3,2,1,0:T(8,128)(2,1)S(1)} collective-permute-done((bf16[2,2,12,32,128]{4,3,2,1,0:T(8,128)(2,1)S(1)}, bf16[2,2,12,32,128]{4,3,2,1,0:T(8,128)(2,1)S(1)}, u32[]{:S(2)}, u32[]{:S(2)}) %collective-permute-start.19) | collective-permute-done | bytes 393248 | tf_op jit(solution)/shard_map/ppermute | solution.py:300
  147.4 2.9 %mirror_0.1 = bf16[2,2,12,32,128]{4,3,2,1,0:T(8,128)(2,1)} custom-call(bf16[2,2,2,2,6,32,128]{6,5,4,3,2,1,0:T(8,128)(2,1)} %get-tuple-element.21.refs_0_, bf16[2,2,2,2,6,32,128]{6,5,4,3,2,1,0:T(8,128)(2,1)} %copy-done.7, bf16[2,2,2,6,32,128]{5,4,3,2,1,0:T(8,128)(2,1)} %copy-done.14, bf16[2,2,6,32,128]{4,3,2,1,0:T(8,128)(2,1)} %collective-permute-done.15.refs_3_, ...), custom_call_target="tpu_custom_call" | custom-call | flops 1000 | bytes 1000 | tf_op jit(solution)/shard_map/mirror_0/pallas_call | solution.py:216
  150.3 24.9 %collective-permute-start.20 = (bf16[2,2,12,32,128]{4,3,2,1,0:T(8,128)(2,1)}, bf16[2,2,12,32,128]{4,3,2,1,0:T(8,128)(2,1)S(1)}, u32[]{:S(2)}, u32[]{:S(2)}) collective-permute-start(bf16[2,2,12,32,128]{4,3,2,1,0:T(8,128)(2,1)} %mirror_0.1), channel_id=1, source_target_pairs={{0,8},{8,0},{16,24},{24,16},{1,9},{9,1},{17,25},{25,17},{2,10},{10... | collective-permute-start | bytes 1179656 | tf_op jit(solution)/shard_map/ppermute | solution.py:278
  176.7 2.8 %mirror_12.1 = bf16[2,2,12,32,128]{4,3,2,1,0:T(8,128)(2,1)} custom-call(bf16[2,2,2,2,12,32,128]{6,5,4,3,2,1,0:T(8,128)(2,1)} %get-tuple-element.28.refs_0_, bf16[2,2,2,2,12,32,128]{6,5,4,3,2,1,0:T(8,128)(2,1)} %copy-done.1, bf16[2,2,2,12,32,128]{5,4,3,2,1,0:T(8,128)(2,1)} %copy-done.11, bf16[2,2,12,32,128]{4,3,2,1,0:T(8,128)(2,1)} %copy-done.21, ...), custom_call_target="tpu_custom_call" | custom-call | flops 1000 | bytes 1000 | tf_op jit(solution)/shard_map/mirror_12/pallas_call | solution.py:216
  179.5 10.4 %collective-permute-start.14 = (bf16[2,2,12,32,128]{4,3,2,1,0:T(8,128)(2,1)}, bf16[2,2,12,32,128]{4,3,2,1,0:T(8,128)(2,1)S(1)}, u32[]{:S(2)}, u32[]{:S(2)}) collective-permute-start(bf16[2,2,12,32,128]{4,3,2,1,0:T(8,128)(2,1)} %mirror_12.1), channel_id=1, source_target_pairs={{0,8},{8,0},{16,24},{24,16},{1,9},{9,1},{17,25},{25,17},{2,10},{10... | collective-permute-start | bytes 1179656 | tf_op jit(solution)/shard_map/ppermute | solution.py:278
  189.9 2.4 %maximum_bitcast_fusion = bf16[2,1,32,12288]{3,2,1,0:T(8,128)(2,1)} fusion(bf16[1,32,12288]{2,1,0:T(8,128)(2,1)S(1)} %bitcast.53, bf16[1,32,12288]{2,1,0:T(8,128)(2,1)} %bitcast.2), kind=kLoop, calls=%fused_computation | loop fusion | flops 786432 | bytes 3145728
  193.1 3.0 %grads_0.1.refs_9_ = f32[4,2,1,24,32,128]{5,4,3,2,1,0:T(8,128)} custom-call(bf16[2,2,2,2,6,32,128]{6,5,4,3,2,1,0:T(8,128)(2,1)} %get-tuple-element.21.refs_0_, bf16[2,2,2,2,6,32,128]{6,5,4,3,2,1,0:T(8,128)(2,1)} %copy-done.7, bf16[2,2,2,6,32,128]{5,4,3,2,1,0:T(8,128)(2,1)} %copy-done.14, bf16[2,2,6,32,128]{4,3,2,1,0:T(8,128)(2,1)} %collective-permute-done.15.refs_3_, ...), custom_call_target="tpu_custom_call" | custom-call | flops 1000 | bytes 1000 | tf_op jit(solution)/shard_map/grads_0/pallas_call | solution.py:250
  196.1 1.4 collective-permute-done.14.refs_8_
  198.2 3.0 %grads_12.1 = f32[4,2,1,24,32,128]{5,4,3,2,1,0:T(8,128)} custom-call(bf16[2,2,2,2,12,32,128]{6,5,4,3,2,1,0:T(8,128)(2,1)} %get-tuple-element.28.refs_0_, bf16[2,2,2,2,12,32,128]{6,5,4,3,2,1,0:T(8,128)(2,1)} %copy-done.1, bf16[2,2,2,12,32,128]{5,4,3,2,1,0:T(8,128)(2,1)} %copy-done.11, ...), custom_call_target="tpu_custom_call", output_to_operand_aliasing={{}: (9, {})} | custom-call | flops 1000 | bytes 1000 | tf_op jit(solution)/shard_map/grads_12/pallas_call | solution.py:250
  (87 shorter events, 10.9 us)
Async XLA Ops:
  8.9 7.8 %collective-permute-start = (bf16[2,2,2,2,6,32,128]{6,5,4,3,2,1,0:T(8,128)(2,1)}, bf16[2,2,2,2,6,32,128]{6,5,4,3,2,1,0:T(8,128)(2,1)S(1)}, u32[]{:S(2)}, u32[]{:S(2)}) collective-permute-start(bf16[2,2,2,2,6,32,128]{6,5,4,3,2,1,0:T(8,128)(2,1)} %get-tuple-element.22), channel_id=1, source_target_pairs={{0,2},{2,0},{4,6},{6,4},{1,3},{3,1},{5,7},{7,5},{8,10},{10,8},{12,... | collective-permute-start | bytes 2359304 | tf_op jit(solution)/shard_map/ppermute | solution.py:272
  16.6 17.4 %collective-permute-start.3 = (bf16[2,2,2,2,6,32,128]{6,5,4,3,2,1,0:T(8,128)(2,1)}, bf16[2,2,2,2,6,32,128]{6,5,4,3,2,1,0:T(8,128)(2,1)S(1)}, u32[]{:S(2)}, u32[]{:S(2)}) collective-permute-start(bf16[2,2,2,2,6,32,128]{6,5,4,3,2,1,0:T(8,128)(2,1)} %get-tuple-element.26), channel_id=1, source_target_pairs={{0,2},{2,0},{4,6},{6,4},{1,3},{3,1},{5,7},{7,5},{8,10},{10,8},{12,... | collective-permute-start | bytes 2359304 | tf_op jit(solution)/shard_map/ppermute | solution.py:272
  16.7 27.3 %copy-start.7 = (bf16[2,2,2,2,6,32,128]{6,5,4,3,2,1,0:T(8,128)(2,1)}, bf16[2,2,2,2,6,32,128]{6,5,4,3,2,1,0:T(8,128)(2,1)S(1)}, u32[]{:S(2)}) copy-start(bf16[2,2,2,2,6,32,128]{6,5,4,3,2,1,0:T(8,128)(2,1)S(1)} %collective-permute-done.refs_1_) | copy-start | bytes 2359300
  17.7 16.4 %copy-start.8 = (bf16[2,2,2,2,6,32,128]{6,5,4,3,2,1,0:T(8,128)(2,1)S(1)}, bf16[2,2,2,2,6,32,128]{6,5,4,3,2,1,0:T(8,128)(2,1)}, u32[]{:S(2)}) copy-start(bf16[2,2,2,2,6,32,128]{6,5,4,3,2,1,0:T(8,128)(2,1)} %get-tuple-element.25.refs_4_) | copy-start | bytes 2359300
  31.0 29.1 %collective-permute-start.5 = (bf16[2,2,2,2,12,32,128]{6,5,4,3,2,1,0:T(8,128)(2,1)}, bf16[2,2,2,2,12,32,128]{6,5,4,3,2,1,0:T(8,128)(2,1)S(1)}, u32[]{:S(2)}, u32[]{:S(2)}) collective-permute-start(bf16[2,2,2,2,12,32,128]{6,5,4,3,2,1,0:T(8,128)(2,1)} %get-tuple-element.29), channel_id=1, source_target_pairs={{0,2},{2,0},{4,6},{6,4},{1,3},{3,1},{5,7},{7,5},{8,10},{10,8},{12,... | collective-permute-start | bytes 4718600 | tf_op jit(solution)/shard_map/ppermute | solution.py:272
  31.5 12.5 %collective-permute-start.4 = (bf16[2,2,2,6,32,128]{5,4,3,2,1,0:T(8,128)(2,1)S(1)}, bf16[2,2,2,6,32,128]{5,4,3,2,1,0:T(8,128)(2,1)S(1)}, u32[]{:S(2)}, u32[]{:S(2)}) collective-permute-start(bf16[2,2,2,6,32,128]{5,4,3,2,1,0:T(8,128)(2,1)S(1)} %copy-done.19), channel_id=1, source_target_pairs={{0,4},{2,6},{4,0},{6,2},{1,5},{3,7},{5,1},{7,3},{8,12},{10,14},{12... | collective-permute-start | bytes 1179656 | tf_op jit(solution)/shard_map/ppermute | solution.py:272
  34.1 25.7 %copy-start.9 = (bf16[2,2,2,2,6,32,128]{6,5,4,3,2,1,0:T(8,128)(2,1)}, bf16[2,2,2,2,6,32,128]{6,5,4,3,2,1,0:T(8,128)(2,1)S(1)}, u32[]{:S(2)}) copy-start(bf16[2,2,2,2,6,32,128]{6,5,4,3,2,1,0:T(8,128)(2,1)S(1)} %collective-permute-done.3.refs_5_) | copy-start | bytes 2359300
  34.2 25.5 %collective-permute-start.6 = (bf16[2,2,2,6,32,128]{5,4,3,2,1,0:T(8,128)(2,1)S(1)}, bf16[2,2,2,6,32,128]{5,4,3,2,1,0:T(8,128)(2,1)S(1)}, u32[]{:S(2)}, u32[]{:S(2)}) collective-permute-start(bf16[2,2,2,6,32,128]{5,4,3,2,1,0:T(8,128)(2,1)S(1)} %fusion.7.refs_7_), channel_id=1, source_target_pairs={{0,4},{2,6},{4,0},{6,2},{1,5},{3,7},{5,1},{7,3},{8,12},{10,14},{12... | collective-permute-start | bytes 1179656 | tf_op jit(solution)/shard_map/ppermute | solution.py:272
  34.3 42.4 %collective-permute-start.1 = (bf16[32,12288]{1,0:T(8,128)(2,1)}, bf16[32,12288]{1,0:T(8,128)(2,1)}, u32[]{:S(2)}, u32[]{:S(2)}) collective-permute-start(bf16[32,12288]{1,0:T(8,128)(2,1)} %bitcast.54), channel_id=1, source_target_pairs={{0,1},{1,0},{2,3},{3,2},{4,5},{5,4},{6,7},{7,6},{8,9},{9,8},{10,11... | collective-permute-start | bytes 2359304 | tf_op jit(solution)/shard_map/ppermute | solution.py:314
  44.1 15.7 %copy-start.14 = (bf16[2,2,2,6,32,128]{5,4,3,2,1,0:T(8,128)(2,1)}, bf16[2,2,2,6,32,128]{5,4,3,2,1,0:T(8,128)(2,1)S(1)}, u32[]{:S(2)}) copy-start(bf16[2,2,2,6,32,128]{5,4,3,2,1,0:T(8,128)(2,1)S(1)} %collective-permute-done.4.refs_2_) | copy-start | bytes 1179652
  44.9 91.5 %collective-permute-start.15 = (bf16[2,2,6,32,128]{4,3,2,1,0:T(8,128)(2,1)}, bf16[2,2,6,32,128]{4,3,2,1,0:T(8,128)(2,1)}, u32[]{:S(2)}, u32[]{:S(2)}) collective-permute-start(bf16[2,2,6,32,128]{4,3,2,1,0:T(8,128)(2,1)} %fusion.9.refs_8_), channel_id=1, source_target_pairs={{0,24},{8,16},{16,8},{24,0},{1,25},{9,17},{17,9},{25,1},{2,26},{10... | collective-permute-start | bytes 589832 | tf_op jit(solution)/shard_map/ppermute | solution.py:300
  59.9 77.3 %collective-permute-start.16 = (bf16[2,2,6,32,128]{4,3,2,1,0:T(8,128)(2,1)S(1)}, bf16[2,2,6,32,128]{4,3,2,1,0:T(8,128)(2,1)S(1)}, u32[]{:S(2)}, u32[]{:S(2)}) collective-permute-start(bf16[2,2,6,32,128]{4,3,2,1,0:T(8,128)(2,1)S(1)} %fusion.8.refs_9_), channel_id=1, source_target_pairs={{0,24},{8,16},{16,8},{24,0},{1,25},{9,17},{17,9},{25,1},{2,26},{10... | collective-permute-start | bytes 589832 | tf_op jit(solution)/shard_map/ppermute | solution.py:300
  60.1 19.2 %collective-permute-start.17 = (bf16[2,2,2,2,12,32,128]{6,5,4,3,2,1,0:T(8,128)(2,1)}, bf16[2,2,2,2,12,32,128]{6,5,4,3,2,1,0:T(8,128)(2,1)S(1)}, u32[]{:S(2)}, u32[]{:S(2)}) collective-permute-start(bf16[2,2,2,2,12,32,128]{6,5,4,3,2,1,0:T(8,128)(2,1)} %get-tuple-element.35), channel_id=1, source_target_pairs={{0,2},{2,0},{4,6},{6,4},{1,3},{3,1},{5,7},{7,5},{8,10},{10,8},{12,... | collective-permute-start | bytes 4718600 | tf_op jit(solution)/shard_map/ppermute | solution.py:272
  60.1 40.9 %copy-start.1 = (bf16[2,2,2,2,12,32,128]{6,5,4,3,2,1,0:T(8,128)(2,1)}, bf16[2,2,2,2,12,32,128]{6,5,4,3,2,1,0:T(8,128)(2,1)S(1)}, u32[]{:S(2)}) copy-start(bf16[2,2,2,2,12,32,128]{6,5,4,3,2,1,0:T(8,128)(2,1)S(1)} %collective-permute-done.5.refs_1_) | copy-start | bytes 4718596
  61.4 15.5 %copy-start.17 = (f32[32,12288]{1,0:T(8,128)S(1)}, f32[32,12288]{1,0:T(8,128)}, u32[]{:S(2)}) copy-start(f32[32,12288]{1,0:T(8,128)} %get-tuple-element.23) | copy-start | bytes 4718596
  74.7 20.4 %collective-permute-start.7 = (bf16[32,12288]{1,0:T(8,128)(2,1)}, bf16[32,12288]{1,0:T(8,128)(2,1)S(1)}, u32[]{:S(2)}, u32[]{:S(2)}) collective-permute-start(bf16[32,12288]{1,0:T(8,128)(2,1)} %bitcast.55), channel_id=1, source_target_pairs={{0,1},{1,0},{2,3},{3,2},{4,5},{5,4},{6,7},{7,6},{8,9},{9,8},{10,11... | collective-permute-start | bytes 2359304 | tf_op jit(solution)/shard_map/ppermute | solution.py:314
  76.7 4.3 %collective-permute-start.11 = (bf16[2,2,2,2,12,32,128]{6,5,4,3,2,1,0:T(8,128)(2,1)}, bf16[2,2,2,2,12,32,128]{6,5,4,3,2,1,0:T(8,128)(2,1)S(1)}, u32[]{:S(2)}, u32[]{:S(2)}) collective-permute-start(bf16[2,2,2,2,12,32,128]{6,5,4,3,2,1,0:T(8,128)(2,1)} %get-tuple-element.33), channel_id=1, source_target_pairs={{0,2},{2,0},{4,6},{6,4},{1,3},{3,1},{5,7},{7,5},{8,10},{10,8},{12,... | collective-permute-start | bytes 4718600 | tf_op jit(solution)/shard_map/ppermute | solution.py:272
  79.2 39.0 %copy-start.4 = (bf16[2,2,2,2,12,32,128]{6,5,4,3,2,1,0:T(8,128)(2,1)}, bf16[2,2,2,2,12,32,128]{6,5,4,3,2,1,0:T(8,128)(2,1)S(1)}, u32[]{:S(2)}) copy-start(bf16[2,2,2,2,12,32,128]{6,5,4,3,2,1,0:T(8,128)(2,1)S(1)} %collective-permute-done.17.refs_9_) | copy-start | bytes 4718596
  79.2 20.4 %collective-permute-start.9 = (bf16[2,2,2,12,32,128]{5,4,3,2,1,0:T(8,128)(2,1)S(1)}, bf16[2,2,2,12,32,128]{5,4,3,2,1,0:T(8,128)(2,1)S(1)}, u32[]{:S(2)}, u32[]{:S(2)}) collective-permute-start(bf16[2,2,2,12,32,128]{5,4,3,2,1,0:T(8,128)(2,1)S(1)} %copy-done.13), channel_id=1, source_target_pairs={{0,4},{2,6},{4,0},{6,2},{1,5},{3,7},{5,1},{7,3},{8,12},{10,14},{12... | collective-permute-start | bytes 2359304 | tf_op jit(solution)/shard_map/ppermute | solution.py:272
  81.0 15.6 %copy-start.18 = (f32[32,12288]{1,0:T(8,128)S(1)}, f32[32,12288]{1,0:T(8,128)}, u32[]{:S(2)}) copy-start(f32[32,12288]{1,0:T(8,128)} %get-tuple-element.30) | copy-start | bytes 4718596
  81.0 55.2 %copy-start.5 = (bf16[2,2,2,2,12,32,128]{6,5,4,3,2,1,0:T(8,128)(2,1)}, bf16[2,2,2,2,12,32,128]{6,5,4,3,2,1,0:T(8,128)(2,1)S(1)}, u32[]{:S(2)}) copy-start(bf16[2,2,2,2,12,32,128]{6,5,4,3,2,1,0:T(8,128)(2,1)S(1)} %collective-permute-done.11.refs_5_) | copy-start | bytes 4718596
  81.0 35.5 %collective-permute-start.18 = (bf16[2,2,2,12,32,128]{5,4,3,2,1,0:T(8,128)(2,1)S(1)}, bf16[2,2,2,12,32,128]{5,4,3,2,1,0:T(8,128)(2,1)S(1)}, u32[]{:S(2)}, u32[]{:S(2)}) collective-permute-start(bf16[2,2,2,12,32,128]{5,4,3,2,1,0:T(8,128)(2,1)S(1)} %fusion.2), channel_id=1, source_target_pairs={{0,4},{2,6},{4,0},{6,2},{1,5},{3,7},{5,1},{7,3},{8,12},{10,14},{12... | collective-permute-start | bytes 2359304 | tf_op jit(solution)/shard_map/ppermute | solution.py:272
  95.1 37.7 %collective-permute-start.12 = (bf16[2,2,2,12,32,128]{5,4,3,2,1,0:T(8,128)(2,1)S(1)}, bf16[2,2,2,12,32,128]{5,4,3,2,1,0:T(8,128)(2,1)S(1)}, u32[]{:S(2)}, u32[]{:S(2)}) collective-permute-start(bf16[2,2,2,12,32,128]{5,4,3,2,1,0:T(8,128)(2,1)S(1)} %fusion.1), channel_id=1, source_target_pairs={{0,4},{2,6},{4,0},{6,2},{1,5},{3,7},{5,1},{7,3},{8,12},{10,14},{12... | collective-permute-start | bytes 2359304 | tf_op jit(solution)/shard_map/ppermute | solution.py:272
  99.7 18.8 %copy-start.11 = (bf16[2,2,2,12,32,128]{5,4,3,2,1,0:T(8,128)(2,1)}, bf16[2,2,2,12,32,128]{5,4,3,2,1,0:T(8,128)(2,1)S(1)}, u32[]{:S(2)}) copy-start(bf16[2,2,2,12,32,128]{5,4,3,2,1,0:T(8,128)(2,1)S(1)} %collective-permute-done.9.refs_2_) | copy-start | bytes 2359300
  99.7 90.2 %collective-permute-start.2 = (bf16[32,12288]{1,0:T(8,128)(2,1)}, bf16[32,12288]{1,0:T(8,128)(2,1)}, u32[]{:S(2)}, u32[]{:S(2)}) collective-permute-start(bf16[32,12288]{1,0:T(8,128)(2,1)} %add_convert_fusion.4), channel_id=1, source_target_pairs={{8,0},{16,8},{24,16},{9,1},{17,9},{25,17},{10,2},{18,10},{26,18},{... | collective-permute-start | bytes 2359304 | tf_op jit(solution)/shard_map/ppermute | solution.py:268
  116.5 19.9 %copy-start.10 = (bf16[2,2,2,12,32,128]{5,4,3,2,1,0:T(8,128)(2,1)}, bf16[2,2,2,12,32,128]{5,4,3,2,1,0:T(8,128)(2,1)S(1)}, u32[]{:S(2)}) copy-start(bf16[2,2,2,12,32,128]{5,4,3,2,1,0:T(8,128)(2,1)S(1)} %collective-permute-done.18.refs_10_) | copy-start | bytes 2359300
  116.5 73.4 %collective-permute-start.8 = (bf16[32,12288]{1,0:T(8,128)(2,1)}, bf16[32,12288]{1,0:T(8,128)(2,1)S(1)}, u32[]{:S(2)}, u32[]{:S(2)}) collective-permute-start(bf16[32,12288]{1,0:T(8,128)(2,1)} %add_convert_fusion.2), channel_id=1, source_target_pairs={{0,8},{8,16},{16,24},{1,9},{9,17},{17,25},{2,10},{10,18},{18,26},{... | collective-permute-start | bytes 2359304 | tf_op jit(solution)/shard_map/ppermute | solution.py:268
  132.8 13.9 %collective-permute-start.19 = (bf16[2,2,12,32,128]{4,3,2,1,0:T(8,128)(2,1)S(1)}, bf16[2,2,12,32,128]{4,3,2,1,0:T(8,128)(2,1)S(1)}, u32[]{:S(2)}, u32[]{:S(2)}) collective-permute-start(bf16[2,2,12,32,128]{4,3,2,1,0:T(8,128)(2,1)S(1)} %fusion.3), channel_id=1, source_target_pairs={{0,24},{8,16},{16,8},{24,0},{1,25},{9,17},{17,9},{25,1},{2,26},{10... | collective-permute-start | bytes 1179656 | tf_op jit(solution)/shard_map/ppermute | solution.py:300
  136.4 38.7 %collective-permute-start.10 = (bf16[2,2,12,32,128]{4,3,2,1,0:T(8,128)(2,1)S(1)}, bf16[2,2,12,32,128]{4,3,2,1,0:T(8,128)(2,1)S(1)}, u32[]{:S(2)}, u32[]{:S(2)}) collective-permute-start(bf16[2,2,12,32,128]{4,3,2,1,0:T(8,128)(2,1)S(1)} %fusion.5), channel_id=1, source_target_pairs={{0,24},{8,16},{16,8},{24,0},{1,25},{9,17},{17,9},{25,1},{2,26},{10... | collective-permute-start | bytes 1179656 | tf_op jit(solution)/shard_map/ppermute | solution.py:300
  137.1 38.0 %collective-permute-start.13 = (bf16[2,2,12,32,128]{4,3,2,1,0:T(8,128)(2,1)S(1)}, bf16[2,2,12,32,128]{4,3,2,1,0:T(8,128)(2,1)S(1)}, u32[]{:S(2)}, u32[]{:S(2)}) collective-permute-start(bf16[2,2,12,32,128]{4,3,2,1,0:T(8,128)(2,1)S(1)} %fusion.4), channel_id=1, source_target_pairs={{0,24},{8,16},{16,8},{24,0},{1,25},{9,17},{17,9},{25,1},{2,26},{10... | collective-permute-start | bytes 1179656 | tf_op jit(solution)/shard_map/ppermute | solution.py:300
  150.3 42.0 %collective-permute-start.20 = (bf16[2,2,12,32,128]{4,3,2,1,0:T(8,128)(2,1)}, bf16[2,2,12,32,128]{4,3,2,1,0:T(8,128)(2,1)S(1)}, u32[]{:S(2)}, u32[]{:S(2)}) collective-permute-start(bf16[2,2,12,32,128]{4,3,2,1,0:T(8,128)(2,1)} %mirror_0.1), channel_id=1, source_target_pairs={{0,8},{8,0},{16,24},{24,16},{1,9},{9,1},{17,25},{25,17},{2,10},{10... | collective-permute-start | bytes 1179656 | tf_op jit(solution)/shard_map/ppermute | solution.py:278
  179.5 18.0 %collective-permute-start.14 = (bf16[2,2,12,32,128]{4,3,2,1,0:T(8,128)(2,1)}, bf16[2,2,12,32,128]{4,3,2,1,0:T(8,128)(2,1)S(1)}, u32[]{:S(2)}, u32[]{:S(2)}) collective-permute-start(bf16[2,2,12,32,128]{4,3,2,1,0:T(8,128)(2,1)} %mirror_12.1), channel_id=1, source_target_pairs={{0,8},{8,0},{16,24},{24,16},{1,9},{9,1},{17,25},{25,17},{2,10},{10... | collective-permute-start | bytes 1179656 | tf_op jit(solution)/shard_map/ppermute | solution.py:278
  (16 other events, 80.2 us)

commit v5 on v4

--- a/solution.py
+++ b/solution.py
@@ -11,8 +11,10 @@
 SCALE = math.sqrt(2.0 / math.pi)
 CUBIC = 0.044715
 GROUP = 6
+DEPTH = 2
 VMEM = 56 * 1024 * 1024
 SMALL = pl.CostEstimate(flops=1000, bytes_accessed=1000, transcendentals=0)
+LARGE = pl.CostEstimate(flops=1000, bytes_accessed=2 * 10**8, transcendentals=0)
 F32 = jnp.float32
 BF16 = jnp.bfloat16
 
@@ -26,13 +28,13 @@
     return base + jnp.where(at < size, at, at - size)
 
 
-def tick_kernel(relay, first_block, piece_blocks, sections, before, last, n_deps, *refs):
+def tick_kernel(relay, first_block, piece_blocks, sections, n_mp, before, last, n_deps, *refs):
     len_ref, idx_in_ref, idx_out_ref, x_ref, g_ref, w_in_ref, w_out_ref = refs[:7]
     before_refs = refs[7:7 + len(before)]
     refs = refs[7 + len(before) + n_deps:]
     keep_ref, send_ref = refs[:2]
     if last:
-        own_ref, other_ref, acc_ref = refs[2:]
+        share_ref, acc_ref = refs[2:]
     else:
         (terms_ref,) = refs[2:]
     half, turn, part = pl.program_id(0), pl.program_id(1), pl.program_id(2)
@@ -42,7 +44,7 @@
     per_step, block = w_in_ref.shape[0], w_in_ref.shape[-1]
     rows = x_ref.shape[0]
     piece = keep_ref.shape[3]
-    live = lax.broadcasted_iota(jnp.int32, (rows, block), 0) < len_ref[relay, 0, 0]
+    live = lax.broadcasted_iota(jnp.int32, (rows, block), 0) < len_ref[relay]
 
     if last:
         @pl.when(opening)
@@ -100,19 +102,13 @@
     if last:
         @pl.when(closing)
         def _():
-            at = lax.axis_index("mp")
-            share, n_mp = own_ref.shape[0], rows // own_ref.shape[0]
-            own_rows = pl.ds(pl.multiple_of(at * share, share), share)
+            share = rows // n_mp
+            owned = lax.broadcasted_iota(jnp.int32, (rows, block), 0) // share == lax.axis_index("mp")
             for b in range(acc_ref.shape[0]):
                 columns = slice(b * block, (b + 1) * block)
                 held = g_ref[:, columns]
-                acc_ref[b] += jnp.where(live & (lax.broadcasted_iota(jnp.int32, (rows, block), 0) // share == at),
-                                        held, jnp.zeros_like(held)).astype(F32)
-                own_ref[:, columns] = acc_ref[b, own_rows]
-                for k in range(1, n_mp):
-                    to = lax.rem(at + k, n_mp)
-                    there = pl.ds(pl.multiple_of(to * share, share), share)
-                    other_ref[k - 1, :, columns] = acc_ref[b, there].astype(BF16)
+                held = jnp.where(live & owned, held, jnp.zeros_like(held)).astype(F32)
+                share_ref[:, columns] = (acc_ref[b] + held).astype(BF16)
 
 
 def tick(relay, lo, hi, before, last, deps, sizes, args):
@@ -133,14 +129,10 @@
         (n_dp // 2, None, 2, None, per_step, rows_cut, block), lambda h, t, i, *_: (0, h, 0, t, i, 0, 0)
     )
     acc_shape = (width // block, rows, block)
-    share = rows // n_mp
     out_specs, out_shape, scratch = [slots_spec] * 2, [slots] * 2, []
     if last:
-        out_specs += [
-            pl.BlockSpec((share, width), lambda h, t, i, *_: (0, 0)),
-            pl.BlockSpec((n_mp - 1, share, width), lambda h, t, i, *_: (0, 0, 0)),
-        ]
-        out_shape += [jax.ShapeDtypeStruct((share, width), F32), jax.ShapeDtypeStruct((n_mp - 1, share, width), BF16)]
+        out_specs.append(pl.BlockSpec((rows, width), lambda h, t, i, *_: (0, 0)))
+        out_shape.append(jax.ShapeDtypeStruct((rows, width), BF16))
         scratch = [pltpu.VMEM(acc_shape, F32)]
     else:
         out_specs.append(pl.BlockSpec((None, None, per_step, rows, block), lambda h, t, i, *_: (h, t, i, 0, 0)))
@@ -148,7 +140,7 @@
     held = [a for _, a in before]
     held_specs = [pl.BlockSpec(a.shape, lambda h, t, i, *_: (0,) * 5) for a in held]
     return pl.pallas_call(
-        functools.partial(tick_kernel, relay, lo, piece_blocks, sections, [at for at, _ in before], last, len(deps)),
+        functools.partial(tick_kernel, relay, lo, piece_blocks, sections, n_mp, [at for at, _ in before], last, len(deps)),
         grid_spec=pltpu.PrefetchScalarGridSpec(
             num_scalar_prefetch=3,
             grid=(2, size, steps),
@@ -158,7 +150,7 @@
         ),
         out_shape=out_shape,
         compiler_params=pltpu.CompilerParams(dimension_semantics=("arbitrary",) * 3, vmem_limit_bytes=VMEM),
-        cost_estimate=SMALL,
+        cost_estimate=LARGE,
         name=f"tick{relay}_{lo}",
     )(lengths, idx_in, idx_out, section_in, out_grad, w_in, w_out, *held, *deps)
 
@@ -262,6 +254,19 @@
     )(*arrays, *came, *held)
 
 
+def tie(value, *deps):
+    any_space = pl.BlockSpec(memory_space=pl.ANY)
+    return pl.pallas_call(
+        lambda *refs: None,
+        in_specs=[any_space] * (1 + len(deps)),
+        out_specs=any_space,
+        out_shape=jax.ShapeDtypeStruct(value.shape, value.dtype),
+        input_output_aliases={0: 0},
+        cost_estimate=SMALL,
+        name="tie",
+    )(value, *deps)
+
+
 def from_behind(value, axis, distance):
     devices = range(lax.axis_size(axis))
     route = [(i - distance, i) for i in devices if i - distance in devices]
@@ -282,38 +287,57 @@
     sections, n_dp, n_mp = (lax.axis_size(a) for a in ("section", "dp", "mp"))
     size = sections // 2
     piece_blocks = w_in.shape[2] // sections
-    args = (lengths, idx_in, idx_out, section_in, out_grad, w_in, w_out)
+    args = (lengths.reshape(2), idx_in, idx_out, section_in, out_grad, w_in, w_out)
     cuts = [0, piece_blocks // 2, piece_blocks] if piece_blocks % 4 == 0 else [0, piece_blocks]
     fine = sorted(set([0, piece_blocks // 4] + cuts)) if piece_blocks % 4 == 0 else cuts
     chunks = [(0, lo, hi) for lo, hi in zip(fine, fine[1:])] + [(1, lo, hi) for lo, hi in zip(cuts, cuts[1:])]
     mirror = [(i, sections - 1 - i) for i in range(sections)]
 
-    keep, got, sum_a, came, away, arrived, passed = {}, {}, {}, {}, {}, {}, []
-    before = []
+    keep, got, sum_a, came, away, arrived, dx, passed = {}, {}, {}, {}, {}, {}, {}, {}
+    before, shares = [], []
+    x_queue, z_queue = [], []
+
+    def queued(queue, operand, move):
+        if len(queue) >= DEPTH:
+            operand = tie(operand, queue[-DEPTH])
+        queue.append(move(operand))
+        return queue[-1]
 
     def stage_a(c):
         sum_a[c] = (keep[c][1].astype(F32) + got[c][1].astype(F32)).astype(BF16)
-        came[c] = flip_bit(sum_a[c], "dp", 2)
+        came[c] = queued(x_queue, sum_a[c], lambda v: flip_bit(v, "dp", 2))
 
     def stage_b(c):
         away[c] = (keep[c][0, 0].astype(F32) + got[c][0, 0].astype(F32) + came[c][0].astype(F32)).astype(BF16)
-        arrived[c] = lax.ppermute(away[c], "section", mirror)
-
+        arrived[c] = queued(z_queue, away[c], lambda v: lax.ppermute(v, "section", mirror))
+        for relay in (r for r in range(2) if dx_after[r] == c):
+            passed[relay] = queued(z_queue, dx[relay], lambda v: from_behind(v, "section", 1 if relay else -1))
+
+    ends = [max(c for c, chunk in enumerate(chunks) if chunk[0] == r) for r in range(2)]
+    dx_after = [2, 3] if len(chunks) > 4 else ends
     for c, (relay, lo, hi) in enumerate(chunks):
         last = hi == piece_blocks
+        if c == 2:
+            stage_a(1)
         deps = [sum_a[c - 2]] if c >= 2 else []
+        if c == 2:
+            deps.append(sum_a[1])
         if c >= 3:
             deps.append(away[c - 3])
+        if c >= 4:
+            deps.append(arrived[c - 4])
         results = tick(relay, lo, hi, before, last, deps, (sections, n_dp, n_mp), args)
         keep[c], send = results[:2]
         got[c] = flip_bit(send, "dp", 1)
         before = [] if last else before + [(lo, results[2])]
         if last:
-            dx, others = results[2:]
-            for k in range(1, n_mp):
-                dx = dx + lax.ppermute(others[k - 1], "mp", [(i, (i + k) % n_mp) for i in range(n_mp)]).astype(F32)
-            passed.append(from_behind(dx.astype(BF16), "section", 1 if relay else -1))
-        if c >= 1:
+            shares.append((relay, results[2]))
+        if c + 1 == len(chunks):
+            for r, share in shares:
+                if r != relay:
+                    share = tie(share, keep[c])
+                dx[r] = lax.psum_scatter(share, "mp", scatter_dimension=0, tiled=True)
+        if c >= 1 and c != 2:
             stage_a(c - 1)
         if c >= 2:
             stage_b(c - 2)
@@ -329,9 +353,9 @@
         spans = [[chunks[c][1:] for c in relay] for relay in inside]
         groups = [[(keep[c], got[c], came[c], arrived[c]) for c in relay] for relay in inside]
         to_turn = mirror_sum(spans, groups, f"mirror_{lo}") if size > 1 else []
-        turned = [turn_half(v, turn + 1) for turn, v in enumerate(to_turn)]
+        turned = [queued(z_queue, v, lambda v, turn=turn: turn_half(v, turn + 1)) for turn, v in enumerate(to_turn)]
         grads = write_grads(spans, groups, turned, grads, sections, piece_blocks, f"grads_{lo}")
-    return jnp.stack(passed, axis=0)[:, None], grads
+    return jnp.stack([passed[0], passed[1]], axis=0)[:, None], grads
 
 
 def solution(mesh):

time: 202 us -> 237 us (1.17)
  waiting for transfers between devices: 60.2 us -> 80.9 us
  between operations: 0.88 us -> 14.2 us
  other arithmetic: 10 us -> 19.6 us
  starting transfers between devices: 61.8 us -> 54 us
    ppermute x10, waiting for transfers between devices: 39.4 us -> 14.2 us  [flip_bit(): lax.ppermute(value, axis, [(i, i ^ bit) for i in range(lax.axis_size(axis...]
    ppermute x7 -> x5, waiting for transfers between devices: 19.4 us -> 40.1 us  [stage_b(): lax.ppermute(v, 'section', mirror)]
    ppermute x2, starting transfers between devices: 35.3 us -> 15.2 us  [turn_half(): return lax.ppermute(value, 'section', route)]
    ppermute x2, starting transfers between devices: 2.99 us -> 19.6 us  [from_behind(): return lax.ppermute(value, axis, route)]
    reduce_scatter x0 -> x2, waiting for transfers between devices: none -> 13.2 us  [body(): dx[r] = lax.psum_scatter(share, 'mp', scatter_dimension=0, tiled=True)]
    ppermute x2, waiting for transfers between devices: 1.42 us -> 12.7 us  [turn_half(): return lax.ppermute(value, 'section', route)]
    convert_element_type x5, other arithmetic: 1.4 us -> 8.09 us  [stage_b(): (keep[c][0, 0].astype(F32) + got[c][0, 0].astype(F32) + came[c][0].astype...]
    convert_element_type x5, other arithmetic: 2.87 us -> 8.89 us  [stage_a(): sum_a[c] = (keep[c][1].astype(F32) + got[c][1].astype(F32)).astype(BF16)]
  transfers between devices with their start and end apart: 21 -> 21, of which waited for: 7 -> 9; matrix products, arithmetic and copies ran while one was open for 5% -> 7% of each run, Pallas kernels for 26% -> 11%
where the time goes in v5:
time: 237 us; the launch traced here: 236 us
  waiting for transfers between devices  80.9 us (34%)
  Pallas kernels  61.4 us (26%)
  starting transfers between devices  54 us (23%)
  other arithmetic  19.6 us (8%)
  between operations  14.2 us (6%)
  local copies, waits for them, and re-layouts  5.39 us (2%)
    pallas_call x5, Pallas kernels, tick(): pl.pallas_call(functools.partial(tick_kernel, relay, lo, piece_blocks, se...  49.8 us
    ppermute x5, waiting for transfers between devices, stage_b(): lax.ppermute(v, 'section', mirror)  40.1 us
    ppermute x2, starting transfers between devices, from_behind(): return lax.ppermute(value, axis, route)  19.6 us
    ppermute x2, starting transfers between devices, turn_half(): return lax.ppermute(value, 'section', route)  15.2 us
    ppermute x10, waiting for transfers between devices, flip_bit(): lax.ppermute(value, axis, [(i, i ^ bit) for i in range(lax.axis_size(axis...  14.2 us
    reduce_scatter x2, waiting for transfers between devices, body(): dx[r] = lax.psum_scatter(share, 'mp', scatter_dimension=0, tiled=True)  13.2 us
    ppermute x2, waiting for transfers between devices, turn_half(): return lax.ppermute(value, 'section', route)  12.7 us
    ppermute x5, starting transfers between devices, stage_b(): lax.ppermute(v, 'section', mirror)  10.2 us
  transfers between devices with their start and end apart: 21, of which 9 were waited for; matrix products, arithmetic and copies ran while one was open for 7% of the time, Pallas kernels for 11%

profile of v5, /device:TPU:0, one launch (start us, length us, event | category | flops | bytes accessed | tf_op | source)
XLA Modules:
  0.0 235.5 jit_solution(8956944909872700557)
XLA Ops:
  7.2 7.0 %tick0_0.1 = (bf16[2,2,2,2,6,32,128]{6,5,4,3,2,1,0:T(8,128)(2,1)}, bf16[2,2,2,2,6,32,128]{6,5,4,3,2,1,0:T(8,128)(2,1)}, f32[2,2,6,64,128]{4,3,2,1,0:T(8,128)}) custom-call(s32[2]{0:T(128)} %bitcast.53, s32[1,2,96]{2,1,0:T(2,128)} %refs_1_.9, s32[1,2,96]{2,1,0:T(2,128)} %refs_2_.9, bf16[2,1,64,12288]{3,2,1,0:T(8,128)(2,1)} %refs_3_.9, ...), custom_call_target="tpu_custom_call" | custom-call | flops 1000 | bytes 200000000 | tf_op jit(solution)/shard_map/tick0_0/pallas_call | solution.py:142
  14.6 7.3 %tick0_6.1 = (bf16[2,2,2,2,6,32,128]{6,5,4,3,2,1,0:T(8,128)(2,1)}, bf16[2,2,2,2,6,32,128]{6,5,4,3,2,1,0:T(8,128)(2,1)}, f32[2,2,6,64,128]{4,3,2,1,0:T(8,128)}) custom-call(s32[2]{0:T(128)} %bitcast.54, s32[1,2,96]{2,1,0:T(2,128)} %refs_1_.9, s32[1,2,96]{2,1,0:T(2,128)} %refs_2_.9, bf16[2,1,64,12288]{3,2,1,0:T(8,128)(2,1)} %refs_3_.9, ...), custom_call_target="tpu_custom_call" | custom-call | flops 1000 | bytes 200000000 | tf_op jit(solution)/shard_map/tick0_6/pallas_call | solution.py:142
  24.4 2.1 fusion.7.refs_10_.refs_7_
  26.5 12.5 %tick0_12.1 = (bf16[2,2,2,2,12,32,128]{6,5,4,3,2,1,0:T(8,128)(2,1)}, bf16[2,2,2,2,12,32,128]{6,5,4,3,2,1,0:T(8,128)(2,1)}, bf16[64,12288]{1,0:T(8,128)(2,1)}) custom-call(s32[2]{0:T(128)} %bitcast.55, s32[1,2,96]{2,1,0:T(2,128)} %refs_1_.9, s32[1,2,96]{2,1,0:T(2,128)} %refs_2_.9, bf16[2,1,64,12288]{3,2,1,0:T(8,128)(2,1)} %refs_3_.9, ...), custom_call_target="tpu_custom_call" | custom-call | flops 1000 | bytes 200000000 | tf_op jit(solution)/shard_map/tick0_12/pallas_call | solution.py:142
  39.2 2.9 %collective-permute-start.2 = (bf16[2,2,2,6,32,128]{5,4,3,2,1,0:T(8,128)(2,1)S(1)}, bf16[2,2,2,6,32,128]{5,4,3,2,1,0:T(8,128)(2,1)S(1)}, u32[]{:S(2)}, u32[]{:S(2)}) collective-permute-start(bf16[2,2,2,6,32,128]{5,4,3,2,1,0:T(8,128)(2,1)S(1)} %copy-done.16), channel_id=1, source_target_pairs={{0,4},{2,6},{4,0},{6,2},{1,5},{3,7},{5,1},{7,3},{8,12},{10,14},{12... | collective-permute-start | bytes 1179656 | tf_op jit(solution)/shard_map/ppermute | solution.py:277
  42.2 9.8 %collective-permute-done.2.refs_1_.refs_2_ = bf16[2,2,2,6,32,128]{5,4,3,2,1,0:T(8,128)(2,1)S(1)} collective-permute-done((bf16[2,2,2,6,32,128]{5,4,3,2,1,0:T(8,128)(2,1)S(1)}, bf16[2,2,2,6,32,128]{5,4,3,2,1,0:T(8,128)(2,1)S(1)}, u32[]{:S(2)}, u32[]{:S(2)}) %collective-permute-start.2) | collective-permute-done | bytes 393248 | tf_op jit(solution)/shard_map/ppermute | solution.py:277
  52.1 4.2 %collective-permute-start.5 = (bf16[2,2,6,32,128]{4,3,2,1,0:T(8,128)(2,1)S(1)}, bf16[2,2,6,32,128]{4,3,2,1,0:T(8,128)(2,1)S(1)}, u32[]{:S(2)}, u32[]{:S(2)}) collective-permute-start(bf16[2,2,6,32,128]{4,3,2,1,0:T(8,128)(2,1)S(1)} %fusion.9.refs_8_), channel_id=1, source_target_pairs={{0,24},{8,16},{16,8},{24,0},{1,25},{9,17},{17,9},{25,1},{2,26},{10... | collective-permute-start | bytes 589832 | tf_op jit(solution)/shard_map/ppermute | solution.py:312
  56.3 10.7 %tick1_0.1 = (bf16[2,2,2,2,12,32,128]{6,5,4,3,2,1,0:T(8,128)(2,1)}, bf16[2,2,2,2,12,32,128]{6,5,4,3,2,1,0:T(8,128)(2,1)}, f32[2,2,12,64,128]{4,3,2,1,0:T(8,128)}) custom-call(s32[2]{0:T(128)} %bitcast.56, s32[1,2,96]{2,1,0:T(2,128)} %refs_1_.9, s32[1,2,96]{2,1,0:T(2,128)} %refs_2_.9, bf16[2,1,64,12288]{3,2,1,0:T(8,128)(2,1)} %refs_3_.9, ...), custom_call_target="tpu_custom_call" | custom-call | flops 1000 | bytes 200000000 | tf_op jit(solution)/shard_map/tick1_0/pallas_call | solution.py:142
  67.1 1.8 fusion.8.refs_9_
  70.9 12.4 %tick1_12.1 = (bf16[2,2,2,2,12,32,128]{6,5,4,3,2,1,0:T(8,128)(2,1)}, bf16[2,2,2,2,12,32,128]{6,5,4,3,2,1,0:T(8,128)(2,1)}, bf16[64,12288]{1,0:T(8,128)(2,1)}) custom-call(s32[2]{0:T(128)} %bitcast.57, s32[1,2,96]{2,1,0:T(2,128)} %refs_1_.9, s32[1,2,96]{2,1,0:T(2,128)} %refs_2_.9, bf16[2,1,64,12288]{3,2,1,0:T(8,128)(2,1)} %refs_3_.9, ...), custom_call_target="tpu_custom_call" | custom-call | flops 1000 | bytes 200000000 | tf_op jit(solution)/shard_map/tick1_12/pallas_call | solution.py:142
  84.6 1.5 collective-permute-start.9
  87.9 2.3 fusion.2.refs_0_
  90.1 1.6 collective-permute-start.14
  91.8 2.9 %collective-permute-done.6.refs_1_.refs_7_ = bf16[2,2,6,32,128]{4,3,2,1,0:T(8,128)(2,1)S(1)} collective-permute-done((bf16[2,2,6,32,128]{4,3,2,1,0:T(8,128)(2,1)S(1)}, bf16[2,2,6,32,128]{4,3,2,1,0:T(8,128)(2,1)S(1)}, u32[]{:S(2)}, u32[]{:S(2)}) %collective-permute-start.6) | collective-permute-done | bytes 196640 | tf_op jit(solution)/shard_map/ppermute | solution.py:312
  94.7 13.2 %reduce-scatter.3.cloned.1.call-done.refs_0_ = bf16[32,12288]{1,0:T(8,128)(2,1)} async-done(((bf16[64,12288]{1,0:T(8,128)(2,1)}), bf16[32,12288]{1,0:T(8,128)(2,1)}) %reduce-scatter.3.cloned.1.call-update) | async-done | bytes 786448 | tf_op jit(solution)/shard_map/reduce_scatter | solution.py:339
  109.2 2.2 fusion.1.refs_0_
  111.4 1.5 collective-permute-start.12
  112.9 2.0 fusion.5.refs_0_
  114.9 5.4 %collective-permute-start.10 = (bf16[2,2,12,32,128]{4,3,2,1,0:T(8,128)(2,1)}, bf16[2,2,12,32,128]{4,3,2,1,0:T(8,128)(2,1)S(1)}, u32[]{:S(2)}, u32[]{:S(2)}) collective-permute-start(bf16[2,2,12,32,128]{4,3,2,1,0:T(8,128)(2,1)} %tie.15), channel_id=1, source_target_pairs={{0,24},{8,16},{16,8},{24,0},{1,25},{9,17},{17,9},{25,1},{2,26},{10... | collective-permute-start | bytes 1179656 | tf_op jit(solution)/shard_map/ppermute | solution.py:312
  120.3 1.9 collective-permute-done.14.refs_10_
  122.2 2.1 fusion.3.refs_0_
  124.3 15.3 %collective-permute-done.10.refs_1_.refs_3_ = bf16[2,2,12,32,128]{4,3,2,1,0:T(8,128)(2,1)S(1)} collective-permute-done((bf16[2,2,12,32,128]{4,3,2,1,0:T(8,128)(2,1)}, bf16[2,2,12,32,128]{4,3,2,1,0:T(8,128)(2,1)S(1)}, u32[]{:S(2)}, u32[]{:S(2)}) %collective-permute-start.10) | collective-permute-done | bytes 393248 | tf_op jit(solution)/shard_map/ppermute | solution.py:312
  140.4 18.3 %collective-permute-start.8 = (bf16[32,12288]{1,0:T(8,128)(2,1)}, bf16[32,12288]{1,0:T(8,128)(2,1)S(1)}, u32[]{:S(2)}, u32[]{:S(2)}) collective-permute-start(bf16[32,12288]{1,0:T(8,128)(2,1)} %tie.13), channel_id=1, source_target_pairs={{0,8},{8,16},{16,24},{1,9},{9,17},{17,25},{2,10},{10,18},{18,26},{... | collective-permute-start | bytes 2359304 | tf_op jit(solution)/shard_map/ppermute | solution.py:273
  158.8 2.0 fusion.4.refs_0_
  161.6 21.9 %collective-permute-done.16.refs_7_.refs_1_ = bf16[2,2,12,32,128]{4,3,2,1,0:T(8,128)(2,1)S(1)} collective-permute-done((bf16[2,2,12,32,128]{4,3,2,1,0:T(8,128)(2,1)}, bf16[2,2,12,32,128]{4,3,2,1,0:T(8,128)(2,1)S(1)}, u32[]{:S(2)}, u32[]{:S(2)}) %collective-permute-start.16) | collective-permute-done | bytes 393248 | tf_op jit(solution)/shard_map/ppermute | solution.py:312
  184.2 2.8 %mirror_12.1.refs_0_ = bf16[2,2,12,32,128]{4,3,2,1,0:T(8,128)(2,1)} custom-call(bf16[2,2,2,2,12,32,128]{6,5,4,3,2,1,0:T(8,128)(2,1)} %get-tuple-element.25.refs_0_, bf16[2,2,2,2,12,32,128]{6,5,4,3,2,1,0:T(8,128)(2,1)} %copy-done.2, bf16[2,2,2,12,32,128]{5,4,3,2,1,0:T(8,128)(2,1)} %collective-permute-done.9.refs_1_.refs_2_, ...), custom_call_target="tpu_custom_call" | custom-call | flops 1000 | bytes 1000 | tf_op jit(solution)/shard_map/mirror_12/pallas_call | solution.py:208
  187.0 2.9 %mirror_0.1.refs_0_ = bf16[2,2,12,32,128]{4,3,2,1,0:T(8,128)(2,1)} custom-call(bf16[2,2,2,2,6,32,128]{6,5,4,3,2,1,0:T(8,128)(2,1)} %get-tuple-element.19.refs_0_, bf16[2,2,2,2,6,32,128]{6,5,4,3,2,1,0:T(8,128)(2,1)} %copy-done.5, bf16[2,2,2,6,32,128]{5,4,3,2,1,0:T(8,128)(2,1)} %copy-done.7, bf16[2,2,6,32,128]{4,3,2,1,0:T(8,128)(2,1)} %copy-done.13, ...), custom_call_target="tpu_custom_call" | custom-call | flops 1000 | bytes 1000 | tf_op jit(solution)/shard_map/mirror_0/pallas_call | solution.py:208
  189.9 15.2 %collective-permute-start.17 = (bf16[2,2,12,32,128]{4,3,2,1,0:T(8,128)(2,1)}, bf16[2,2,12,32,128]{4,3,2,1,0:T(8,128)(2,1)S(1)}, u32[]{:S(2)}, u32[]{:S(2)}) collective-permute-start(bf16[2,2,12,32,128]{4,3,2,1,0:T(8,128)(2,1)} %tie.20), channel_id=1, source_target_pairs={{0,8},{8,0},{16,24},{24,16},{1,9},{9,1},{17,25},{25,17},{2,10},{10... | collective-permute-start | bytes 1179656 | tf_op jit(solution)/shard_map/ppermute | solution.py:283
  205.9 2.7 %maximum_bitcast_fusion = bf16[2,1,32,12288]{3,2,1,0:T(8,128)(2,1)} fusion(bf16[1,32,12288]{2,1,0:T(8,128)(2,1)} %bitcast.52, bf16[1,32,12288]{2,1,0:T(8,128)(2,1)} %bitcast.8), kind=kLoop, calls=%fused_computation | loop fusion | flops 786432 | bytes 3145728
  208.6 12.7 %collective-permute-done.18.refs_12_ = bf16[2,2,12,32,128]{4,3,2,1,0:T(8,128)(2,1)S(1)} collective-permute-done((bf16[2,2,12,32,128]{4,3,2,1,0:T(8,128)(2,1)}, bf16[2,2,12,32,128]{4,3,2,1,0:T(8,128)(2,1)S(1)}, u32[]{:S(2)}, u32[]{:S(2)}) %collective-permute-start.18) | collective-permute-done | bytes 393248 | tf_op jit(solution)/shard_map/ppermute | solution.py:283
  222.0 3.0 %grads_0.1.refs_9_ = f32[4,2,1,24,32,128]{5,4,3,2,1,0:T(8,128)} custom-call(bf16[2,2,2,2,6,32,128]{6,5,4,3,2,1,0:T(8,128)(2,1)} %get-tuple-element.19.refs_0_, bf16[2,2,2,2,6,32,128]{6,5,4,3,2,1,0:T(8,128)(2,1)} %copy-done.5, bf16[2,2,2,6,32,128]{5,4,3,2,1,0:T(8,128)(2,1)} %copy-done.7, bf16[2,2,6,32,128]{4,3,2,1,0:T(8,128)(2,1)} %copy-done.13, ...), custom_call_target="tpu_custom_call" | custom-call | flops 1000 | bytes 1000 | tf_op jit(solution)/shard_map/grads_0/pallas_call | solution.py:242
  225.7 3.0 %grads_12.1 = f32[4,2,1,24,32,128]{5,4,3,2,1,0:T(8,128)} custom-call(bf16[2,2,2,2,12,32,128]{6,5,4,3,2,1,0:T(8,128)(2,1)} %get-tuple-element.25.refs_0_, bf16[2,2,2,2,12,32,128]{6,5,4,3,2,1,0:T(8,128)(2,1)} %copy-done.2, bf16[2,2,2,12,32,128]{5,4,3,2,1,0:T(8,128)(2,1)} %collective-permute-done.9.refs_1_.refs_2_, ...), custom_call_target="tpu_custom_call", output_to_operand_aliasing={{}: (9, {})} | custom-call | flops 1000 | bytes 1000 | tf_op jit(solution)/shard_map/grads_12/pallas_call | solution.py:242
  (85 shorter events, 14.3 us)
Async XLA Ops:
  7.2 100.7 %reduce-scatter.3.cloned.1.call-start = ((), (), s32[]{:S(2)}) async-start(), calls=%async_computation.2 | async-start | bytes 2359296 | tf_op jit(solution)/shard_map/reduce_scatter | solution.py:339
  14.2 7.8 %collective-permute-start = (bf16[2,2,2,2,6,32,128]{6,5,4,3,2,1,0:T(8,128)(2,1)}, bf16[2,2,2,2,6,32,128]{6,5,4,3,2,1,0:T(8,128)(2,1)S(1)}, u32[]{:S(2)}, u32[]{:S(2)}) collective-permute-start(bf16[2,2,2,2,6,32,128]{6,5,4,3,2,1,0:T(8,128)(2,1)} %get-tuple-element.20), channel_id=1, source_target_pairs={{0,2},{2,0},{4,6},{6,4},{1,3},{3,1},{5,7},{7,5},{8,10},{10,8},{12,... | collective-permute-start | bytes 2359304 | tf_op jit(solution)/shard_map/ppermute | solution.py:277
  14.6 7.4 %copy-start.4 = (bf16[2,2,2,2,6,32,128]{6,5,4,3,2,1,0:T(8,128)(2,1)S(1)}, bf16[2,2,2,2,6,32,128]{6,5,4,3,2,1,0:T(8,128)(2,1)}, u32[]{:S(2)}) copy-start(bf16[2,2,2,2,6,32,128]{6,5,4,3,2,1,0:T(8,128)(2,1)} %get-tuple-element.19.refs_0_) | copy-start | bytes 2359300
  21.9 2.5 %collective-permute-start.1 = (bf16[2,2,2,2,6,32,128]{6,5,4,3,2,1,0:T(8,128)(2,1)}, bf16[2,2,2,2,6,32,128]{6,5,4,3,2,1,0:T(8,128)(2,1)S(1)}, u32[]{:S(2)}, u32[]{:S(2)}) collective-permute-start(bf16[2,2,2,2,6,32,128]{6,5,4,3,2,1,0:T(8,128)(2,1)} %get-tuple-element.22), channel_id=1, source_target_pairs={{0,2},{2,0},{4,6},{6,4},{1,3},{3,1},{5,7},{7,5},{8,10},{10,8},{12,... | collective-permute-start | bytes 2359304 | tf_op jit(solution)/shard_map/ppermute | solution.py:277
  22.0 30.0 %copy-start.5 = (bf16[2,2,2,2,6,32,128]{6,5,4,3,2,1,0:T(8,128)(2,1)}, bf16[2,2,2,2,6,32,128]{6,5,4,3,2,1,0:T(8,128)(2,1)S(1)}, u32[]{:S(2)}) copy-start(bf16[2,2,2,2,6,32,128]{6,5,4,3,2,1,0:T(8,128)(2,1)S(1)} %collective-permute-done.refs_1_) | copy-start | bytes 2359300
  24.4 42.6 %copy-start.6 = (bf16[2,2,2,2,6,32,128]{6,5,4,3,2,1,0:T(8,128)(2,1)}, bf16[2,2,2,2,6,32,128]{6,5,4,3,2,1,0:T(8,128)(2,1)S(1)}, u32[]{:S(2)}) copy-start(bf16[2,2,2,2,6,32,128]{6,5,4,3,2,1,0:T(8,128)(2,1)S(1)} %collective-permute-done.1.refs_5_) | copy-start | bytes 2359300
  26.5 12.7 %copy-start.16 = (bf16[2,2,2,6,32,128]{5,4,3,2,1,0:T(8,128)(2,1)S(1)}, bf16[2,2,2,6,32,128]{5,4,3,2,1,0:T(8,128)(2,1)}, u32[]{:S(2)}) copy-start(bf16[2,2,2,6,32,128]{5,4,3,2,1,0:T(8,128)(2,1)} %fusion.6.refs_9_) | copy-start | bytes 1179652
  26.5 15.5 %copy-start.10 = (bf16[2,2,2,6,32,128]{5,4,3,2,1,0:T(8,128)(2,1)S(1)}, bf16[2,2,2,6,32,128]{5,4,3,2,1,0:T(8,128)(2,1)}, u32[]{:S(2)}) copy-start(bf16[2,2,2,6,32,128]{5,4,3,2,1,0:T(8,128)(2,1)} %fusion.7.refs_10_.refs_7_) | copy-start | bytes 1179652
  39.0 29.9 %collective-permute-start.3 = (bf16[2,2,2,2,12,32,128]{6,5,4,3,2,1,0:T(8,128)(2,1)}, bf16[2,2,2,2,12,32,128]{6,5,4,3,2,1,0:T(8,128)(2,1)S(1)}, u32[]{:S(2)}, u32[]{:S(2)}) collective-permute-start(bf16[2,2,2,2,12,32,128]{6,5,4,3,2,1,0:T(8,128)(2,1)} %get-tuple-element.26), channel_id=1, source_target_pairs={{0,2},{2,0},{4,6},{6,4},{1,3},{3,1},{5,7},{7,5},{8,10},{10,8},{12,... | collective-permute-start | bytes 4718600 | tf_op jit(solution)/shard_map/ppermute | solution.py:277
  39.2 12.8 %collective-permute-start.2 = (bf16[2,2,2,6,32,128]{5,4,3,2,1,0:T(8,128)(2,1)S(1)}, bf16[2,2,2,6,32,128]{5,4,3,2,1,0:T(8,128)(2,1)S(1)}, u32[]{:S(2)}, u32[]{:S(2)}) collective-permute-start(bf16[2,2,2,6,32,128]{5,4,3,2,1,0:T(8,128)(2,1)S(1)} %copy-done.16), channel_id=1, source_target_pairs={{0,4},{2,6},{4,0},{6,2},{1,5},{3,7},{5,1},{7,3},{8,12},{10,14},{12... | collective-permute-start | bytes 1179656 | tf_op jit(solution)/shard_map/ppermute | solution.py:277
  42.1 25.0 %collective-permute-start.4 = (bf16[2,2,2,6,32,128]{5,4,3,2,1,0:T(8,128)(2,1)S(1)}, bf16[2,2,2,6,32,128]{5,4,3,2,1,0:T(8,128)(2,1)S(1)}, u32[]{:S(2)}, u32[]{:S(2)}) collective-permute-start(bf16[2,2,2,6,32,128]{5,4,3,2,1,0:T(8,128)(2,1)S(1)} %copy-done.10), channel_id=1, source_target_pairs={{0,4},{2,6},{4,0},{6,2},{1,5},{3,7},{5,1},{7,3},{8,12},{10,14},{12... | collective-permute-start | bytes 1179656 | tf_op jit(solution)/shard_map/ppermute | solution.py:277
  52.0 15.1 %copy-start.7 = (bf16[2,2,2,6,32,128]{5,4,3,2,1,0:T(8,128)(2,1)}, bf16[2,2,2,6,32,128]{5,4,3,2,1,0:T(8,128)(2,1)S(1)}, u32[]{:S(2)}) copy-start(bf16[2,2,2,6,32,128]{5,4,3,2,1,0:T(8,128)(2,1)S(1)} %collective-permute-done.2.refs_1_.refs_2_) | copy-start | bytes 1179652
  52.1 16.8 %copy-start.1 = (bf16[2,2,2,2,12,32,128]{6,5,4,3,2,1,0:T(8,128)(2,1)S(1)}, bf16[2,2,2,2,12,32,128]{6,5,4,3,2,1,0:T(8,128)(2,1)}, u32[]{:S(2)}) copy-start(bf16[2,2,2,2,12,32,128]{6,5,4,3,2,1,0:T(8,128)(2,1)} %get-tuple-element.25.refs_0_) | copy-start | bytes 4718596
  52.1 18.1 %collective-permute-start.5 = (bf16[2,2,6,32,128]{4,3,2,1,0:T(8,128)(2,1)S(1)}, bf16[2,2,6,32,128]{4,3,2,1,0:T(8,128)(2,1)S(1)}, u32[]{:S(2)}, u32[]{:S(2)}) collective-permute-start(bf16[2,2,6,32,128]{4,3,2,1,0:T(8,128)(2,1)S(1)} %fusion.9.refs_8_), channel_id=1, source_target_pairs={{0,24},{8,16},{16,8},{24,0},{1,25},{9,17},{17,9},{25,1},{2,26},{10... | collective-permute-start | bytes 589832 | tf_op jit(solution)/shard_map/ppermute | solution.py:312
  68.9 14.3 %copy-start.2 = (bf16[2,2,2,2,12,32,128]{6,5,4,3,2,1,0:T(8,128)(2,1)}, bf16[2,2,2,2,12,32,128]{6,5,4,3,2,1,0:T(8,128)(2,1)S(1)}, u32[]{:S(2)}) copy-start(bf16[2,2,2,2,12,32,128]{6,5,4,3,2,1,0:T(8,128)(2,1)S(1)} %collective-permute-done.3.refs_1_) | copy-start | bytes 4718596
  83.3 57.1 %reduce-scatter.5.cloned.1.call-start = ((), (), s32[]{:S(2)}) async-start(), calls=%async_computation.3 | async-start | bytes 2359296 | tf_op jit(solution)/shard_map/reduce_scatter | solution.py:339
  83.4 4.5 %copy-start.3 = (bf16[2,2,2,2,12,32,128]{6,5,4,3,2,1,0:T(8,128)(2,1)S(1)}, bf16[2,2,2,2,12,32,128]{6,5,4,3,2,1,0:T(8,128)(2,1)}, u32[]{:S(2)}) copy-start(bf16[2,2,2,2,12,32,128]{6,5,4,3,2,1,0:T(8,128)(2,1)} %get-tuple-element.30.refs_8_) | copy-start | bytes 4718596
  84.1 3.8 %collective-permute-start.13 = (bf16[2,2,2,2,12,32,128]{6,5,4,3,2,1,0:T(8,128)(2,1)}, bf16[2,2,2,2,12,32,128]{6,5,4,3,2,1,0:T(8,128)(2,1)}, u32[]{:S(2)}, u32[]{:S(2)}) collective-permute-start(bf16[2,2,2,2,12,32,128]{6,5,4,3,2,1,0:T(8,128)(2,1)} %get-tuple-element.31), channel_id=1, source_target_pairs={{0,2},{2,0},{4,6},{6,4},{1,3},{3,1},{5,7},{7,5},{8,10},{10,8},{12,... | collective-permute-start | bytes 4718600 | tf_op jit(solution)/shard_map/ppermute | solution.py:277
  84.1 25.0 %collective-permute-start.11 = (bf16[2,2,2,2,12,32,128]{6,5,4,3,2,1,0:T(8,128)(2,1)}, bf16[2,2,2,2,12,32,128]{6,5,4,3,2,1,0:T(8,128)(2,1)}, u32[]{:S(2)}, u32[]{:S(2)}) collective-permute-start(bf16[2,2,2,2,12,32,128]{6,5,4,3,2,1,0:T(8,128)(2,1)} %get-tuple-element.29), channel_id=1, source_target_pairs={{0,2},{2,0},{4,6},{6,4},{1,3},{3,1},{5,7},{7,5},{8,10},{10,8},{12,... | collective-permute-start | bytes 4718600 | tf_op jit(solution)/shard_map/ppermute | solution.py:277
  84.6 26.8 %collective-permute-start.9 = (bf16[2,2,2,12,32,128]{5,4,3,2,1,0:T(8,128)(2,1)}, bf16[2,2,2,12,32,128]{5,4,3,2,1,0:T(8,128)(2,1)}, u32[]{:S(2)}, u32[]{:S(2)}) collective-permute-start(bf16[2,2,2,12,32,128]{5,4,3,2,1,0:T(8,128)(2,1)} %tie.14), channel_id=1, source_target_pairs={{0,4},{2,6},{4,0},{6,2},{1,5},{3,7},{5,1},{7,3},{8,12},{10,14},{12... | collective-permute-start | bytes 2359304 | tf_op jit(solution)/shard_map/ppermute | solution.py:277
  86.2 8.5 %collective-permute-start.6 = (bf16[2,2,6,32,128]{4,3,2,1,0:T(8,128)(2,1)S(1)}, bf16[2,2,6,32,128]{4,3,2,1,0:T(8,128)(2,1)S(1)}, u32[]{:S(2)}, u32[]{:S(2)}) collective-permute-start(bf16[2,2,6,32,128]{4,3,2,1,0:T(8,128)(2,1)S(1)} %copy-done.17), channel_id=1, source_target_pairs={{0,24},{8,16},{16,8},{24,0},{1,25},{9,17},{17,9},{25,1},{2,26},{10... | collective-permute-start | bytes 589832 | tf_op jit(solution)/shard_map/ppermute | solution.py:312
  90.1 19.0 %copy-start = (bf16[2,2,2,2,12,32,128]{6,5,4,3,2,1,0:T(8,128)(2,1)S(1)}, bf16[2,2,2,2,12,32,128]{6,5,4,3,2,1,0:T(8,128)(2,1)}, u32[]{:S(2)}) copy-start(bf16[2,2,2,2,12,32,128]{6,5,4,3,2,1,0:T(8,128)(2,1)} %get-tuple-element.27.refs_1_.refs_4_) | copy-start | bytes 4718596
  90.1 32.1 %collective-permute-start.14 = (bf16[2,2,2,12,32,128]{5,4,3,2,1,0:T(8,128)(2,1)}, bf16[2,2,2,12,32,128]{5,4,3,2,1,0:T(8,128)(2,1)}, u32[]{:S(2)}, u32[]{:S(2)}) collective-permute-start(bf16[2,2,2,12,32,128]{5,4,3,2,1,0:T(8,128)(2,1)} %tie.17), channel_id=1, source_target_pairs={{0,4},{2,6},{4,0},{6,2},{1,5},{3,7},{5,1},{7,3},{8,12},{10,14},{12... | collective-permute-start | bytes 2359304 | tf_op jit(solution)/shard_map/ppermute | solution.py:277
  94.7 13.2 %copy-start.15 = (bf16[2,2,6,32,128]{4,3,2,1,0:T(8,128)(2,1)}, bf16[2,2,6,32,128]{4,3,2,1,0:T(8,128)(2,1)S(1)}, u32[]{:S(2)}) copy-start(bf16[2,2,6,32,128]{4,3,2,1,0:T(8,128)(2,1)S(1)} %collective-permute-done.6.refs_1_.refs_7_) | copy-start | bytes 589828
  107.9 32.5 %collective-permute-start.7 = (bf16[32,12288]{1,0:T(8,128)(2,1)}, bf16[32,12288]{1,0:T(8,128)(2,1)}, u32[]{:S(2)}, u32[]{:S(2)}) collective-permute-start(bf16[32,12288]{1,0:T(8,128)(2,1)} %tie.12), channel_id=1, source_target_pairs={{8,0},{16,8},{24,16},{9,1},{17,9},{25,17},{10,2},{18,10},{26,18},{... | collective-permute-start | bytes 2359304 | tf_op jit(solution)/shard_map/ppermute | solution.py:273
  111.4 47.4 %collective-permute-start.12 = (bf16[2,2,2,12,32,128]{5,4,3,2,1,0:T(8,128)(2,1)}, bf16[2,2,2,12,32,128]{5,4,3,2,1,0:T(8,128)(2,1)}, u32[]{:S(2)}, u32[]{:S(2)}) collective-permute-start(bf16[2,2,2,12,32,128]{5,4,3,2,1,0:T(8,128)(2,1)} %tie.16), channel_id=1, source_target_pairs={{0,4},{2,6},{4,0},{6,2},{1,5},{3,7},{5,1},{7,3},{8,12},{10,14},{12... | collective-permute-start | bytes 2359304 | tf_op jit(solution)/shard_map/ppermute | solution.py:277
  114.9 24.7 %collective-permute-start.10 = (bf16[2,2,12,32,128]{4,3,2,1,0:T(8,128)(2,1)}, bf16[2,2,12,32,128]{4,3,2,1,0:T(8,128)(2,1)S(1)}, u32[]{:S(2)}, u32[]{:S(2)}) collective-permute-start(bf16[2,2,12,32,128]{4,3,2,1,0:T(8,128)(2,1)} %tie.15), channel_id=1, source_target_pairs={{0,24},{8,16},{16,8},{24,0},{1,25},{9,17},{17,9},{25,1},{2,26},{10... | collective-permute-start | bytes 1179656 | tf_op jit(solution)/shard_map/ppermute | solution.py:312
  140.4 20.4 %collective-permute-start.15 = (bf16[2,2,12,32,128]{4,3,2,1,0:T(8,128)(2,1)}, bf16[2,2,12,32,128]{4,3,2,1,0:T(8,128)(2,1)S(1)}, u32[]{:S(2)}, u32[]{:S(2)}) collective-permute-start(bf16[2,2,12,32,128]{4,3,2,1,0:T(8,128)(2,1)} %tie.18), channel_id=1, source_target_pairs={{0,24},{8,16},{16,8},{24,0},{1,25},{9,17},{17,9},{25,1},{2,26},{10... | collective-permute-start | bytes 1179656 | tf_op jit(solution)/shard_map/ppermute | solution.py:312
  140.4 64.6 %collective-permute-start.8 = (bf16[32,12288]{1,0:T(8,128)(2,1)}, bf16[32,12288]{1,0:T(8,128)(2,1)S(1)}, u32[]{:S(2)}, u32[]{:S(2)}) collective-permute-start(bf16[32,12288]{1,0:T(8,128)(2,1)} %tie.13), channel_id=1, source_target_pairs={{0,8},{8,16},{16,24},{1,9},{9,17},{17,25},{2,10},{10,18},{18,26},{... | collective-permute-start | bytes 2359304 | tf_op jit(solution)/shard_map/ppermute | solution.py:273
  161.6 21.9 %collective-permute-start.16 = (bf16[2,2,12,32,128]{4,3,2,1,0:T(8,128)(2,1)}, bf16[2,2,12,32,128]{4,3,2,1,0:T(8,128)(2,1)S(1)}, u32[]{:S(2)}, u32[]{:S(2)}) collective-permute-start(bf16[2,2,12,32,128]{4,3,2,1,0:T(8,128)(2,1)} %tie.19), channel_id=1, source_target_pairs={{0,24},{8,16},{16,8},{24,0},{1,25},{9,17},{17,9},{25,1},{2,26},{10... | collective-permute-start | bytes 1179656 | tf_op jit(solution)/shard_map/ppermute | solution.py:312
  189.9 35.1 %collective-permute-start.17 = (bf16[2,2,12,32,128]{4,3,2,1,0:T(8,128)(2,1)}, bf16[2,2,12,32,128]{4,3,2,1,0:T(8,128)(2,1)S(1)}, u32[]{:S(2)}, u32[]{:S(2)}) collective-permute-start(bf16[2,2,12,32,128]{4,3,2,1,0:T(8,128)(2,1)} %tie.20), channel_id=1, source_target_pairs={{0,8},{8,0},{16,24},{24,16},{1,9},{9,1},{17,25},{25,17},{2,10},{10... | collective-permute-start | bytes 1179656 | tf_op jit(solution)/shard_map/ppermute | solution.py:283
  205.9 15.3 %collective-permute-start.18 = (bf16[2,2,12,32,128]{4,3,2,1,0:T(8,128)(2,1)}, bf16[2,2,12,32,128]{4,3,2,1,0:T(8,128)(2,1)S(1)}, u32[]{:S(2)}, u32[]{:S(2)}) collective-permute-start(bf16[2,2,12,32,128]{4,3,2,1,0:T(8,128)(2,1)} %tie.21), channel_id=1, source_target_pairs={{0,8},{8,0},{16,24},{24,16},{1,9},{9,1},{17,25},{25,17},{2,10},{10... | collective-permute-start | bytes 1179656 | tf_op jit(solution)/shard_map/ppermute | solution.py:283
  (10 other events, 15.5 us)
Sparse Core Ops, SparseCore 0:
  83.4 24.4 reduce-scatter.2
  110.2 26.0 reduce-scatter.4

commit v6 on v2

v6 whole, which is shorter than its diff:
```python
import functools
import math

import jax
import jax.numpy as jnp
from jax import lax
from jax.experimental import pallas as pl
from jax.experimental.pallas import tpu as pltpu
from jax.sharding import PartitionSpec as P

SCALE = math.sqrt(2.0 / math.pi)
CUBIC = 0.044715
GROUP = 4
STEP = 8


def tick_kernel(relay, per_step, n_deps, len_ref, idx_in_ref, idx_out_ref, x_ref, g_ref, w_in_ref, w_out_ref, *refs):
    keep_ref, send_ref, own_ref, other_ref, acc_ref = refs[n_deps:]
    step = pl.program_id(0)
    me = lax.axis_index("dp")
    rows, block = x_ref.shape[0], w_in_ref.shape[-1]
    piece = keep_ref.shape[3]
    pieces = block // piece
    live = lax.broadcasted_iota(jnp.int32, (rows, block), 0) < len_ref[relay]

    @pl.when(step == 0)
    def _():
        acc_ref[...] = jnp.zeros_like(acc_ref)

    odd = me % 2 == 1

    def put(kind, i, value):
        value = value.astype(jnp.bfloat16)
        for k in range(pieces // 2):
            low = value[2 * k * piece:(2 * k + 1) * piece]
            high = value[(2 * k + 1) * piece:(2 * k + 2) * piece]
            keep_ref[k ^ (me // 2), kind, i] = jnp.where(odd, high, low)
            send_ref[k ^ (me // 2), kind, i] = jnp.where(odd, low, high)

    f32 = jnp.float32
    over_last = (((1,), (1,)), ((), ()))
    over_rows = (((0,), (0,)), ((), ()))
    for start in range(0, per_step, GROUP):
        group = range(start, min(start + GROUP, per_step))
        sources = [idx_in_ref[0, relay, step * per_step + i] for i in group]
        targets = [idx_out_ref[0, relay, step * per_step + i] for i in group]
        picked = [x_ref[:, pl.ds(pl.multiple_of(b * block, block), block)] for b in sources]
        back = [g_ref[:, pl.ds(pl.multiple_of(b * block, block), block)] for b in targets]
        back = [jnp.where(live, v, jnp.zeros_like(v)) for v in back]
        pre = [jnp.dot(v, w_in_ref[i], preferred_element_type=f32) for v, i in zip(picked, group)]
        back_pre = [lax.dot_general(v, w_out_ref[i], over_last, preferred_element_type=f32) for v, i in zip(back, group)]
        act, grad_pre = [], []
        for v, up in zip(pre, back_pre):
            square = v * v
            th = jnp.tanh(SCALE * (v + CUBIC * (square * v)))
            cdf = 0.5 * (1.0 + th)
            act.append((v * cdf).astype(jnp.bfloat16))
            slope = cdf + (0.5 * v) * ((1.0 - th) * (1.0 + th)) * (SCALE * (1.0 + (3.0 * CUBIC) * square))
            grad_pre.append((up * slope).astype(jnp.bfloat16))
        terms = [lax.dot_general(v, w_in_ref[i], over_last, preferred_element_type=f32) for v, i in zip(grad_pre, group)]
        grad_in = [lax.dot_general(a, v, over_rows, preferred_element_type=f32) for a, v in zip(picked, grad_pre)]
        grad_out = [lax.dot_general(a, v, over_rows, preferred_element_type=f32) for a, v in zip(act, back)]
        for i, b, term, g_in, g_out in zip(group, sources, terms, grad_in, grad_out):
            acc_ref[b] += term
            put(0, i, g_in)
            put(1, i, g_out)

    @pl.when(step == pl.num_programs(0) - 1)
    def _():
        at = lax.axis_index("mp")
        share, n_mp = own_ref.shape[0], rows // own_ref.shape[0]
        owned = live & (lax.broadcasted_iota(jnp.int32, (rows, block), 0) // share == at)
        for b in range(acc_ref.shape[0]):
            columns = slice(b * block, (b + 1) * block)
            held = g_ref[:, columns]
            acc_ref[b] += jnp.where(owned, held, jnp.zeros_like(held)).astype(jnp.float32)
            own_ref[:, columns] = acc_ref[b, pl.ds(pl.multiple_of(at * share, share), share)]
            for k in range(1, n_mp):
                there = pl.multiple_of(lax.rem(at + k, n_mp) * share, share)
                other_ref[k - 1, :, columns] = acc_ref[b, pl.ds(there, share)].astype(jnp.bfloat16)


def tick(relay, sizes, deps, lengths, idx_in, idx_out, section_in, out_grad, w_in, w_out):
    sections, n_dp, n_mp = sizes
    rows, width = section_in.shape[2:]
    blocks, block = w_in.shape[2:4]
    per = blocks // sections
    per_step = math.gcd(per, STEP)
    turns = per // per_step
    piece, share = block // n_dp, rows // n_mp
    whole = pl.BlockSpec((None, None, rows, width), lambda i, *_: (relay, 0, 0, 0))
    weight = pl.BlockSpec((None, None, per_step, block, block), lambda i, *_: (0, relay, i, 0, 0))
    slots = jax.ShapeDtypeStruct((n_dp // 2, sections, 2, per, piece, block), jnp.bfloat16)
    slots_spec = pl.BlockSpec(
        (n_dp // 2, None, 2, per_step, piece, block), lambda i, *_: (0, i // turns, 0, i % turns, 0, 0)
    )
    return pl.pallas_call(
        functools.partial(tick_kernel, relay, per_step, len(deps)),
        grid_spec=pltpu.PrefetchScalarGridSpec(
            num_scalar_prefetch=3,
            grid=(sections * turns,),
            in_specs=[whole, whole, weight, weight] + [pl.BlockSpec(memory_space=pl.ANY)] * len(deps),
            out_specs=[slots_spec] * 2
            + [pl.BlockSpec((share, width), lambda i, *_: (0, 0)), pl.BlockSpec((n_mp - 1, share, width), lambda i, *_: (0, 0, 0))],
            scratch_shapes=[pltpu.VMEM((width // block, rows, block), jnp.float32)],
        ),
        out_shape=[slots] * 2
        + [jax.ShapeDtypeStruct((share, width), jnp.float32), jax.ShapeDtypeStruct((n_mp - 1, share, width), jnp.bfloat16)],
        compiler_params=pltpu.CompilerParams(
            dimension_semantics=("arbitrary",), vmem_limit_bytes=56 * 1024 * 1024
        ),
        cost_estimate=pl.CostEstimate(
            flops=blocks * 10 * rows * block * block,
            bytes_accessed=blocks * block * block * 8 + rows * width * 6,
            transcendentals=blocks * rows * block,
        ),
        name=f"tick{relay}",
    )(lengths, idx_in, idx_out, section_in, out_grad, w_in, w_out, *deps)


def total(*parts):
    return functools.reduce(lambda a, b: a + b, [p.astype(jnp.float32) for p in parts])


def tie(value, *deps):
    any_space = pl.BlockSpec(memory_space=pl.ANY)
    return pl.pallas_call(
        lambda *refs: None,
        in_specs=[any_space] * (1 + len(deps)),
        out_specs=any_space,
        out_shape=jax.ShapeDtypeStruct(value.shape, value.dtype),
        input_output_aliases={0: 0},
        cost_estimate=pl.CostEstimate(flops=1000, bytes_accessed=1000, transcendentals=0),
        name="tie",
    )(value, *deps)


def flip_bit(value, axis, bit):
    return lax.ppermute(value, axis, [(i, i ^ bit) for i in range(lax.axis_size(axis))])


def from_behind(value, axis, distance):
    devices = range(lax.axis_size(axis))
    route = [(i - distance, i) for i in devices if i - distance in devices]
    return lax.ppermute(value, axis, route)


def body(section_in, out_grad, lengths, w_in, w_out, idx_in, idx_out):
    sections, n_dp, n_mp = sizes = tuple(lax.axis_size(a) for a in ("section", "dp", "mp"))
    per = w_in.shape[2] // sections
    args = (lengths.reshape(2), idx_in, idx_out, section_in, out_grad, w_in, w_out)
    keep, got, own, others = [], [], [], []
    for relay in range(2):
        kept, send, mine, theirs = tick(relay, sizes, keep, *args)
        keep.append(kept)
        got.append(flip_bit(send, "dp", 1))
        own.append(mine)
        others.append([lax.ppermute(theirs[k - 1], "mp", [(i, (i + k) % n_mp) for i in range(n_mp)]) for k in range(1, n_mp)])
    small = per // 3 if per % 3 == 0 else per
    cuts = [(0, small), (small, per)] if small < per else [(0, per)]
    chunks = [(relay, cut) for cut in cuts for relay in range(2)]

    def parts(slot, relay, cut):
        return [v[relay][slot][:, :, cut[0]:cut[1]] for v in (keep, got)]

    sums = [total(*parts(1, *chunk)).astype(jnp.bfloat16) for chunk in chunks]
    came = [flip_bit(tie(v, *sums[:i]) if i > 1 else v, "dp", 2) for i, v in enumerate(sums)]
    passed = []
    for relay in range(2):
        dx = total(tie(own[relay], *sums), *others[relay]).astype(jnp.bfloat16)
        passed.append(from_behind(dx, "section", 1 if relay else -1))
    moved = {}
    for chunk, far in zip(chunks, came):
        mine = total(*parts(0, *chunk), far).astype(jnp.bfloat16)
        moved[chunk] = lax.all_to_all(mine, "section", split_axis=0, concat_axis=0, tiled=True)
    grads = jnp.concatenate([total(moved[0, cut], jnp.flip(moved[1, cut], 0)) for cut in cuts], axis=2)
    return jnp.stack(passed, axis=0)[:, None], grads[:, :, None]


def solution(mesh):
    placed = (
        P(None, "section", "dp", None),
        P(None, "section", "dp", None),
        P(None, "section", "dp"),
        P("section", None, "mp", None, None),
        P("section", None, "mp", None, None),
        P("section", None, "mp"),
        P("section", None, "mp"),
    )
    return jax.shard_map(
        body,
        mesh=mesh,
        in_specs=placed,
        out_specs=(
            P(None, "section", ("dp", "mp"), None),
            P(None, None, "mp", "section", "dp", None),
        ),
        check_vma=False,
    )
```

time: 192 us -> 196 us (1.021)
  starting transfers between devices: 49.4 us -> 32.5 us
  waiting for transfers between devices: 81.6 us -> 94 us
  other arithmetic: 18.2 us -> 24.9 us
  Pallas kernels: 33.8 us -> 36.2 us
    all_to_all x0 -> x4, waiting for transfers between devices: none -> 42.2 us  [body(): lax.all_to_all(mine, 'section', split_axis=0, concat_axis=0, tiled=True)]
    ppermute x22 -> x8, starting transfers between devices: 44.5 us -> 9.11 us  [the longest x6 6.08 us: flip_bit(): lax.ppermute(value, axis, [(i, i ^ bit) for i in range(lax.axis_size(axis...]
    ppermute x22 -> x8, waiting for transfers between devices: 72.3 us -> 42 us  [the longest x6 42 us: flip_bit(): lax.ppermute(value, axis, [(i, i ^ bit) for i in range(lax.axis_size(axis...]
    all_to_all x0 -> x4, starting transfers between devices: none -> 17.4 us  [body(): lax.all_to_all(mine, 'section', split_axis=0, concat_axis=0, tiled=True)]
    convert_element_type x10 -> x9, other arithmetic: 12.4 us -> 17.6 us  [the longest x4 8.82 us: body(): mine = total(*parts(0, *chunk), far).astype(jnp.bfloat16)]
    unnamed x0 -> x2, other arithmetic: none -> 4.57 us
    broadcast_in_dim x2 -> x0, other arithmetic: 3.25 us -> none  [the longest x1 1.97 us: total_grads(): jnp.stack([both(down_in, up_in), both(down_out, up_out)], axis=1)]
    add x0 -> x2, other arithmetic: none -> 2.73 us  [total(): a + b]
  transfers between devices with their start and end apart: 24 -> 14, of which waited for: 10 -> 8; matrix products, arithmetic and copies ran while one was open for 10% -> 13% of each run, Pallas kernels for 9% -> 0%
where the time goes in v6:
time: 196 us; the launch traced here: 195 us
  waiting for transfers between devices  94 us (48%)
  Pallas kernels  36.2 us (18%)
  starting transfers between devices  32.5 us (17%)
  other arithmetic  24.9 us (13%)
  local copies, waits for them, and re-layouts  6.52 us (3%)
    all_to_all x4, waiting for transfers between devices, body(): lax.all_to_all(mine, 'section', split_axis=0, concat_axis=0, tiled=True)  42.2 us
    ppermute x6, waiting for transfers between devices, flip_bit(): lax.ppermute(value, axis, [(i, i ^ bit) for i in range(lax.axis_size(axis...  42 us
    pallas_call x2, Pallas kernels, tick(): pl.pallas_call(functools.partial(tick_kernel, relay, per_step, len(deps))...  36.2 us
    all_to_all x4, starting transfers between devices, body(): lax.all_to_all(mine, 'section', split_axis=0, concat_axis=0, tiled=True)  17.4 us
    ppermute x2, waiting for transfers between devices, from_behind(): return lax.ppermute(value, axis, route)  9.85 us
    convert_element_type x4, other arithmetic, body(): mine = total(*parts(0, *chunk), far).astype(jnp.bfloat16)  8.82 us
    ppermute x6, starting transfers between devices, flip_bit(): lax.ppermute(value, axis, [(i, i ^ bit) for i in range(lax.axis_size(axis...  6.08 us
    ppermute x2, starting transfers between devices, from_behind(): return lax.ppermute(value, axis, route)  6.05 us
  transfers between devices with their start and end apart: 14, of which 8 were waited for; matrix products, arithmetic and copies ran while one was open for 13% of the time, Pallas kernels for 0%

profile of v6, /device:TPU:0, one launch (start us, length us, event | category | flops | bytes accessed | tf_op | source)
XLA Modules:
  0.0 195.1 jit_solution(12178502854875878882)
XLA Ops:
  0.6 18.0 %tick0.1 = (bf16[2,4,2,24,32,128]{5,4,3,2,1,0:T(8,128)(2,1)}, bf16[2,4,2,24,32,128]{5,4,3,2,1,0:T(8,128)(2,1)}, f32[32,12288]{1,0:T(8,128)}, bf16[1,32,12288]{2,1,0:T(8,128)(2,1)}) custom-call(s32[2]{0:T(128)} %bitcast.30, s32[1,2,96]{2,1,0:T(2,128)} %idx_in_ref.3, s32[1,2,96]{2,1,0:T(2,128)} %idx_out_ref.3, bf16[2,1,64,12288]{3,2,1,0:T(8,128)(2,1)} %x_ref.3, ...), custom_call_target="tpu_custom_call" | custom-call | flops 1006632960 | bytes 17301504 | tf_op jit(solution)/shard_map/tick0/pallas_call | solution.py:97
  18.7 18.2 %tick1.1 = (bf16[2,4,2,24,32,128]{5,4,3,2,1,0:T(8,128)(2,1)}, bf16[2,4,2,24,32,128]{5,4,3,2,1,0:T(8,128)(2,1)}, f32[32,12288]{1,0:T(8,128)}, bf16[1,32,12288]{2,1,0:T(8,128)(2,1)}) custom-call(s32[2]{0:T(128)} %bitcast.31, s32[1,2,96]{2,1,0:T(2,128)} %idx_in_ref.3, s32[1,2,96]{2,1,0:T(2,128)} %idx_out_ref.3, bf16[2,1,64,12288]{3,2,1,0:T(8,128)(2,1)} %x_ref.3, ...), custom_call_target="tpu_custom_call" | custom-call | flops 1006632960 | bytes 17301504 | tf_op jit(solution)/shard_map/tick1/pallas_call | solution.py:97
  38.2 1.7 copy-done.17
  39.9 1.7 slice_bitcast_fusion.4
  41.6 1.3 collective-permute-done.1
  42.9 1.7 slice_bitcast_fusion
  44.6 2.8 %collective-permute-done = bf16[2,4,2,24,32,128]{5,4,3,2,1,0:T(8,128)(2,1)S(1)} collective-permute-done((bf16[2,4,2,24,32,128]{5,4,3,2,1,0:T(8,128)(2,1)}, bf16[2,4,2,24,32,128]{5,4,3,2,1,0:T(8,128)(2,1)S(1)}, u32[]{:S(2)}, u32[]{:S(2)}) %collective-permute-start) | collective-permute-done | bytes 3145760 | tf_op jit(solution)/shard_map/ppermute | solution.py:139
  48.4 2.9 %collective-permute-start.6 = (bf16[4,2,8,32,128]{4,3,2,1,0:T(8,128)(2,1)S(1)}, bf16[4,2,8,32,128]{4,3,2,1,0:T(8,128)(2,1)S(1)}, u32[]{:S(2)}, u32[]{:S(2)}) collective-permute-start(bf16[4,2,8,32,128]{4,3,2,1,0:T(8,128)(2,1)S(1)} %get-tuple-element.29.refs_1_), channel_id=1, source_target_pairs={{0,4},{2,6},{4,0},{6,2},{1,5},{3,7},{5,1},{7,3},{8,12},{10,14},{12... | collective-permute-start | bytes 1572872 | tf_op jit(solution)/shard_map/ppermute | solution.py:139
  51.4 1.5 collective-permute-start.4
  53.4 10.7 %collective-permute-done.6 = bf16[4,2,8,32,128]{4,3,2,1,0:T(8,128)(2,1)S(1)} collective-permute-done((bf16[4,2,8,32,128]{4,3,2,1,0:T(8,128)(2,1)S(1)}, bf16[4,2,8,32,128]{4,3,2,1,0:T(8,128)(2,1)S(1)}, u32[]{:S(2)}, u32[]{:S(2)}) %collective-permute-start.6) | collective-permute-done | bytes 524320 | tf_op jit(solution)/shard_map/ppermute | solution.py:139
  65.1 5.4 %all-to-all-start = ((bf16[4,2,8,32,128]{4,3,2,1,0:T(8,128)(2,1)}), bf16[4,2,8,32,128]{4,3,2,1,0:T(8,128)(2,1)}, u32[]{:S(2)}, u32[]{:S(2)}) async-start(bf16[4,2,8,32,128]{4,3,2,1,0:T(8,128)(2,1)} %add_convert_fusion.7), calls=%async_computation | async-start | bytes 1048576 | tf_op jit(solution)/shard_map/all_to_all | solution.py:175
  70.6 2.7 %add_convert_fusion.3.refs_3_.refs_0_ = bf16[4,2,16,32,128]{4,3,2,1,0:T(8,128)(2,1)} fusion(bf16[4,2,24,32,128]{4,3,2,1,0:T(8,128)(2,1)} %copy-done.10, bf16[4,2,24,32,128]{4,3,2,1,0:T(8,128)(2,1)S(1)} %get-tuple-element.25), kind=kLoop, calls=%fused_computation.5 | loop fusion | flops 2097152 | bytes 3145728 | tf_op jit(solution)/shard_map/convert_element_type | solution.py:166
  74.5 1.5 collective-permute-start.2
  76.0 1.5 collective-permute-start.9
  78.0 2.5 %add_convert_fusion.6 = bf16[4,2,8,32,128]{4,3,2,1,0:T(8,128)(2,1)} fusion(bf16[4,2,8,32,128]{4,3,2,1,0:T(8,128)(2,1)} %collective-permute-done.7, bf16[4,2,24,32,128]{4,3,2,1,0:T(8,128)(2,1)} %get-tuple-element.22, bf16[4,2,24,32,128]{4,3,2,1,0:T(8,128)(2,1)} %get-tuple-element.20), kind=kLoop, calls=%fused_computation.18 | loop fusion | flops 1572864 | bytes 2097152 | tf_op jit(solution)/shard_map/convert_element_type | solution.py:174
  80.5 3.4 %all-to-all-done = bf16[4,2,8,32,128]{4,3,2,1,0:T(8,128)(2,1)} async-done(((bf16[4,2,8,32,128]{4,3,2,1,0:T(8,128)(2,1)}), bf16[4,2,8,32,128]{4,3,2,1,0:T(8,128)(2,1)}, u32[]{:S(2)}, u32[]{:S(2)}) %all-to-all-start) | async-done | bytes 524320 | tf_op jit(solution)/shard_map/all_to_all | solution.py:175
  83.9 3.5 %all-to-all-start.1 = ((bf16[4,2,8,32,128]{4,3,2,1,0:T(8,128)(2,1)}), bf16[4,2,8,32,128]{4,3,2,1,0:T(8,128)(2,1)S(1)}, u32[]{:S(2)}, u32[]{:S(2)}) async-start(bf16[4,2,8,32,128]{4,3,2,1,0:T(8,128)(2,1)} %add_convert_fusion.6), calls=%async_computation.1 | async-start | bytes 1048576 | tf_op jit(solution)/shard_map/all_to_all | solution.py:175
  87.4 2.3 %add_convert_fusion.4 = bf16[32,12288]{1,0:T(8,128)(2,1)} fusion(f32[32,12288]{1,0:T(8,128)S(1)} %copy-done.5, bf16[32,12288]{1,0:T(8,128)(2,1)} %collective-permute-done.4), kind=kLoop, calls=%fused_computation.13 | loop fusion | flops 1179648 | bytes 3145728 | tf_op jit(solution)/shard_map/convert_element_type | solution.py:170
  89.8 4.8 %collective-permute-start.5 = (bf16[32,12288]{1,0:T(8,128)(2,1)}, bf16[32,12288]{1,0:T(8,128)(2,1)}, u32[]{:S(2)}, u32[]{:S(2)}) collective-permute-start(bf16[32,12288]{1,0:T(8,128)(2,1)} %add_convert_fusion.4), channel_id=1, source_target_pairs={{0,8},{8,16},{16,24},{1,9},{9,17},{17,25},{2,10},{10,18},{18,26},{... | collective-permute-start | bytes 2359304 | tf_op jit(solution)/shard_map/ppermute | solution.py:145
  94.6 27.1 %collective-permute-done.8 = bf16[4,2,16,32,128]{4,3,2,1,0:T(8,128)(2,1)} collective-permute-done((bf16[4,2,16,32,128]{4,3,2,1,0:T(8,128)(2,1)}, bf16[4,2,16,32,128]{4,3,2,1,0:T(8,128)(2,1)}, u32[]{:S(2)}, u32[]{:S(2)}) %collective-permute-start.8) | collective-permute-done | bytes 1048608 | tf_op jit(solution)/shard_map/ppermute | solution.py:139
  121.7 2.7 %add_convert_fusion.1 = bf16[4,2,16,32,128]{4,3,2,1,0:T(8,128)(2,1)} fusion(bf16[4,2,16,32,128]{4,3,2,1,0:T(8,128)(2,1)} %collective-permute-done.8, bf16[4,2,24,32,128]{4,3,2,1,0:T(8,128)(2,1)S(1)} %copy-done.16, bf16[4,2,24,32,128]{4,3,2,1,0:T(8,128)(2,1)S(1)} %copy-done.14), kind=kLoop, calls=%fused_computation.3 | loop fusion | flops 3145728 | bytes 4194304 | tf_op jit(solution)/shard_map/convert_element_type | solution.py:174
  124.4 5.0 %all-to-all-start.2 = ((bf16[4,2,16,32,128]{4,3,2,1,0:T(8,128)(2,1)}), bf16[4,2,16,32,128]{4,3,2,1,0:T(8,128)(2,1)}, u32[]{:S(2)}, u32[]{:S(2)}) async-start(bf16[4,2,16,32,128]{4,3,2,1,0:T(8,128)(2,1)} %add_convert_fusion.1), calls=%async_computation.2 | async-start | bytes 2097152 | tf_op jit(solution)/shard_map/all_to_all | solution.py:175
  129.4 2.3 %add_convert_fusion.5 = bf16[32,12288]{1,0:T(8,128)(2,1)} fusion(f32[32,12288]{1,0:T(8,128)S(1)} %copy-done.4, bf16[32,12288]{1,0:T(8,128)(2,1)} %collective-permute-done.2), kind=kLoop, calls=%fused_computation.14 | loop fusion | flops 1179648 | bytes 3145728 | tf_op jit(solution)/shard_map/convert_element_type | solution.py:170
  131.7 1.3 collective-permute-start.3
  133.0 2.6 %add_convert_fusion = bf16[4,2,16,32,128]{4,3,2,1,0:T(8,128)(2,1)} fusion(bf16[4,2,16,32,128]{4,3,2,1,0:T(8,128)(2,1)} %collective-permute-done.9, bf16[4,2,24,32,128]{4,3,2,1,0:T(8,128)(2,1)S(1)} %copy-done.12, bf16[4,2,24,32,128]{4,3,2,1,0:T(8,128)(2,1)S(1)} %copy-done.11), kind=kLoop, calls=%fused_computation.2 | loop fusion | flops 3145728 | bytes 4194304 | tf_op jit(solution)/shard_map/convert_element_type | solution.py:174
  135.6 18.3 %all-to-all-done.2 = bf16[4,2,16,32,128]{4,3,2,1,0:T(8,128)(2,1)} async-done(((bf16[4,2,16,32,128]{4,3,2,1,0:T(8,128)(2,1)}), bf16[4,2,16,32,128]{4,3,2,1,0:T(8,128)(2,1)}, u32[]{:S(2)}, u32[]{:S(2)}) %all-to-all-start.2) | async-done | bytes 1048608 | tf_op jit(solution)/shard_map/all_to_all | solution.py:175
  153.9 3.5 %all-to-all-start.3 = ((bf16[4,2,16,32,128]{4,3,2,1,0:T(8,128)(2,1)}), bf16[4,2,16,32,128]{4,3,2,1,0:T(8,128)(2,1)S(1)}, u32[]{:S(2)}, u32[]{:S(2)}) async-start(bf16[4,2,16,32,128]{4,3,2,1,0:T(8,128)(2,1)} %add_convert_fusion), calls=%async_computation.3 | async-start | bytes 2097152 | tf_op jit(solution)/shard_map/all_to_all | solution.py:175
  157.4 9.8 %collective-permute-done.3 = bf16[32,12288]{1,0:T(8,128)(2,1)S(1)} collective-permute-done((bf16[32,12288]{1,0:T(8,128)(2,1)}, bf16[32,12288]{1,0:T(8,128)(2,1)S(1)}, u32[]{:S(2)}, u32[]{:S(2)}) %collective-permute-start.3) | collective-permute-done | bytes 786464 | tf_op jit(solution)/shard_map/ppermute | solution.py:145
  167.3 2.5 %maximum_bitcast_fusion.1 = bf16[2,1,32,12288]{3,2,1,0:T(8,128)(2,1)} fusion(bf16[1,32,12288]{2,1,0:T(8,128)(2,1)} %bitcast.8, bf16[1,32,12288]{2,1,0:T(8,128)(2,1)S(1)} %bitcast.29), kind=kLoop, calls=%fused_computation.10 | loop fusion | flops 786432 | bytes 3145728
  170.9 20.5 %all-to-all-done.3 = bf16[4,2,16,32,128]{4,3,2,1,0:T(8,128)(2,1)S(1)} async-done(((bf16[4,2,16,32,128]{4,3,2,1,0:T(8,128)(2,1)}), bf16[4,2,16,32,128]{4,3,2,1,0:T(8,128)(2,1)S(1)}, u32[]{:S(2)}, u32[]{:S(2)}) %all-to-all-start.3) | async-done | bytes 1048608 | tf_op jit(solution)/shard_map/all_to_all | solution.py:175
  191.4 1.5 convert_add_fusion
  193.0 2.1 %maximum_bitcast_fusion = f32[4,2,1,24,32,128]{5,4,3,2,1,0:T(8,128)} fusion(f32[4,2,16,32,128]{4,3,2,1,0:T(8,128)S(1)} %convert_add_fusion, f32[4,2,8,32,128]{4,3,2,1,0:T(8,128)S(1)} %convert_add_fusion.1), kind=kLoop, calls=%fused_computation | loop fusion | flops 786432 | bytes 6291456
  (59 shorter events, 6.9 us)
Async XLA Ops:
  18.7 18.8 %copy-start.3 = (bf16[2,4,2,24,32,128]{5,4,3,2,1,0:T(8,128)(2,1)S(1)}, bf16[2,4,2,24,32,128]{5,4,3,2,1,0:T(8,128)(2,1)}, u32[]{:S(2)}) copy-start(bf16[2,4,2,24,32,128]{5,4,3,2,1,0:T(8,128)(2,1)} %get-tuple-element.11.refs_0_) | copy-start | bytes 9437188
  36.9 6.0 %collective-permute-start.1 = (bf16[2,4,2,24,32,128]{5,4,3,2,1,0:T(8,128)(2,1)}, bf16[2,4,2,24,32,128]{5,4,3,2,1,0:T(8,128)(2,1)S(1)}, u32[]{:S(2)}, u32[]{:S(2)}) collective-permute-start(bf16[2,4,2,24,32,128]{5,4,3,2,1,0:T(8,128)(2,1)} %get-tuple-element.14), channel_id=1, source_target_pairs={{0,2},{2,0},{4,6},{6,4},{1,3},{3,1},{5,7},{7,5},{8,10},{10,8},{12,... | collective-permute-start | bytes 9437192 | tf_op jit(solution)/shard_map/ppermute | solution.py:139
  37.4 10.0 %collective-permute-start = (bf16[2,4,2,24,32,128]{5,4,3,2,1,0:T(8,128)(2,1)}, bf16[2,4,2,24,32,128]{5,4,3,2,1,0:T(8,128)(2,1)S(1)}, u32[]{:S(2)}, u32[]{:S(2)}) collective-permute-start(bf16[2,4,2,24,32,128]{5,4,3,2,1,0:T(8,128)(2,1)} %get-tuple-element.12), channel_id=1, source_target_pairs={{0,2},{2,0},{4,6},{6,4},{1,3},{3,1},{5,7},{7,5},{8,10},{10,8},{12,... | collective-permute-start | bytes 9437192 | tf_op jit(solution)/shard_map/ppermute | solution.py:139
  38.2 25.9 %copy-start.13 = (bf16[4,2,24,32,128]{4,3,2,1,0:T(8,128)(2,1)}, bf16[4,2,24,32,128]{4,3,2,1,0:T(8,128)(2,1)S(1)}, u32[]{:S(2)}) copy-start(bf16[4,2,24,32,128]{4,3,2,1,0:T(8,128)(2,1)S(1)} %get-tuple-element.24) | copy-start | bytes 4718596
  41.6 6.5 %copy-start.6 = (bf16[4,2,24,32,128]{4,3,2,1,0:T(8,128)(2,1)}, bf16[4,2,24,32,128]{4,3,2,1,0:T(8,128)(2,1)S(1)}, u32[]{:S(2)}) copy-start(bf16[4,2,24,32,128]{4,3,2,1,0:T(8,128)(2,1)S(1)} %get-tuple-element.21) | copy-start | bytes 4718596
  44.6 3.5 %copy-start.8 = (bf16[4,2,24,32,128]{4,3,2,1,0:T(8,128)(2,1)}, bf16[4,2,24,32,128]{4,3,2,1,0:T(8,128)(2,1)S(1)}, u32[]{:S(2)}) copy-start(bf16[4,2,24,32,128]{4,3,2,1,0:T(8,128)(2,1)S(1)} %get-tuple-element.23) | copy-start | bytes 4718596
  48.1 16.0 %copy-start.10 = (bf16[4,2,24,32,128]{4,3,2,1,0:T(8,128)(2,1)}, bf16[4,2,24,32,128]{4,3,2,1,0:T(8,128)(2,1)S(1)}, u32[]{:S(2)}) copy-start(bf16[4,2,24,32,128]{4,3,2,1,0:T(8,128)(2,1)S(1)} %get-tuple-element.27) | copy-start | bytes 4718596
  48.1 16.0 %copy-start.15 = (bf16[4,2,24,32,128]{4,3,2,1,0:T(8,128)(2,1)}, bf16[4,2,24,32,128]{4,3,2,1,0:T(8,128)(2,1)S(1)}, u32[]{:S(2)}) copy-start(bf16[4,2,24,32,128]{4,3,2,1,0:T(8,128)(2,1)S(1)} %get-tuple-element.26) | copy-start | bytes 4718596
  48.4 16.7 %copy-start.1 = (bf16[4,2,8,32,128]{4,3,2,1,0:T(8,128)(2,1)}, bf16[4,2,8,32,128]{4,3,2,1,0:T(8,128)(2,1)S(1)}, u32[]{:S(2)}) copy-start(bf16[4,2,8,32,128]{4,3,2,1,0:T(8,128)(2,1)S(1)} %get-tuple-element.28.refs_2_) | copy-start | bytes 1572868
  48.4 16.7 %copy-start.2 = (bf16[4,2,8,32,128]{4,3,2,1,0:T(8,128)(2,1)}, bf16[4,2,8,32,128]{4,3,2,1,0:T(8,128)(2,1)S(1)}, u32[]{:S(2)}) copy-start(bf16[4,2,8,32,128]{4,3,2,1,0:T(8,128)(2,1)S(1)} %get-tuple-element.29.refs_1_) | copy-start | bytes 1572868
  48.4 15.6 %collective-permute-start.6 = (bf16[4,2,8,32,128]{4,3,2,1,0:T(8,128)(2,1)S(1)}, bf16[4,2,8,32,128]{4,3,2,1,0:T(8,128)(2,1)S(1)}, u32[]{:S(2)}, u32[]{:S(2)}) collective-permute-start(bf16[4,2,8,32,128]{4,3,2,1,0:T(8,128)(2,1)S(1)} %get-tuple-element.29.refs_1_), channel_id=1, source_target_pairs={{0,4},{2,6},{4,0},{6,2},{1,5},{3,7},{5,1},{7,3},{8,12},{10,14},{12... | collective-permute-start | bytes 1572872 | tf_op jit(solution)/shard_map/ppermute | solution.py:139
  51.4 36.0 %collective-permute-start.4 = (bf16[32,12288]{1,0:T(8,128)(2,1)}, bf16[32,12288]{1,0:T(8,128)(2,1)}, u32[]{:S(2)}, u32[]{:S(2)}) collective-permute-start(bf16[32,12288]{1,0:T(8,128)(2,1)} %bitcast.7), channel_id=1, source_target_pairs={{0,1},{1,0},{2,3},{3,2},{4,5},{5,4},{6,7},{7,6},{8,9},{9,8},{10,11... | collective-permute-start | bytes 2359304 | tf_op jit(solution)/shard_map/ppermute | solution.py:158
  52.9 25.2 %collective-permute-start.7 = (bf16[4,2,8,32,128]{4,3,2,1,0:T(8,128)(2,1)S(1)}, bf16[4,2,8,32,128]{4,3,2,1,0:T(8,128)(2,1)}, u32[]{:S(2)}, u32[]{:S(2)}) collective-permute-start(bf16[4,2,8,32,128]{4,3,2,1,0:T(8,128)(2,1)S(1)} %get-tuple-element.28.refs_2_), channel_id=1, source_target_pairs={{0,4},{2,6},{4,0},{6,2},{1,5},{3,7},{5,1},{7,3},{8,12},{10,14},{12... | collective-permute-start | bytes 1572872 | tf_op jit(solution)/shard_map/ppermute | solution.py:139
  65.1 18.8 %all-to-all-start = ((bf16[4,2,8,32,128]{4,3,2,1,0:T(8,128)(2,1)}), bf16[4,2,8,32,128]{4,3,2,1,0:T(8,128)(2,1)}, u32[]{:S(2)}, u32[]{:S(2)}) async-start(bf16[4,2,8,32,128]{4,3,2,1,0:T(8,128)(2,1)} %add_convert_fusion.7), calls=%async_computation | async-start | bytes 1048576 | tf_op jit(solution)/shard_map/all_to_all | solution.py:175
  70.6 2.7 %copy-start.7 = (bf16[4,2,24,32,128]{4,3,2,1,0:T(8,128)(2,1)S(1)}, bf16[4,2,24,32,128]{4,3,2,1,0:T(8,128)(2,1)}, u32[]{:S(2)}) copy-start(bf16[4,2,24,32,128]{4,3,2,1,0:T(8,128)(2,1)} %copy-done.6) | copy-start | bytes 4718596
  70.6 2.7 %copy-start.9 = (bf16[4,2,24,32,128]{4,3,2,1,0:T(8,128)(2,1)S(1)}, bf16[4,2,24,32,128]{4,3,2,1,0:T(8,128)(2,1)}, u32[]{:S(2)}) copy-start(bf16[4,2,24,32,128]{4,3,2,1,0:T(8,128)(2,1)} %copy-done.8) | copy-start | bytes 4718596
  74.5 54.9 %collective-permute-start.2 = (bf16[32,12288]{1,0:T(8,128)(2,1)}, bf16[32,12288]{1,0:T(8,128)(2,1)}, u32[]{:S(2)}, u32[]{:S(2)}) collective-permute-start(bf16[32,12288]{1,0:T(8,128)(2,1)} %bitcast.5), channel_id=1, source_target_pairs={{0,1},{1,0},{2,3},{3,2},{4,5},{5,4},{6,7},{7,6},{8,9},{9,8},{10,11... | collective-permute-start | bytes 2359304 | tf_op jit(solution)/shard_map/ppermute | solution.py:158
  76.0 57.0 %collective-permute-start.9 = (bf16[4,2,16,32,128]{4,3,2,1,0:T(8,128)(2,1)S(1)}, bf16[4,2,16,32,128]{4,3,2,1,0:T(8,128)(2,1)}, u32[]{:S(2)}, u32[]{:S(2)}) collective-permute-start(bf16[4,2,16,32,128]{4,3,2,1,0:T(8,128)(2,1)S(1)} %copy-done), channel_id=1, source_target_pairs={{0,4},{2,6},{4,0},{6,2},{1,5},{3,7},{5,1},{7,3},{8,12},{10,14},{12... | collective-permute-start | bytes 3145736 | tf_op jit(solution)/shard_map/ppermute | solution.py:139
  77.5 44.2 %collective-permute-start.8 = (bf16[4,2,16,32,128]{4,3,2,1,0:T(8,128)(2,1)}, bf16[4,2,16,32,128]{4,3,2,1,0:T(8,128)(2,1)}, u32[]{:S(2)}, u32[]{:S(2)}) collective-permute-start(bf16[4,2,16,32,128]{4,3,2,1,0:T(8,128)(2,1)} %tie.6), channel_id=1, source_target_pairs={{0,4},{2,6},{4,0},{6,2},{1,5},{3,7},{5,1},{7,3},{8,12},{10,14},{12... | collective-permute-start | bytes 3145736 | tf_op jit(solution)/shard_map/ppermute | solution.py:139
  78.0 9.4 %copy-start.5 = (f32[32,12288]{1,0:T(8,128)S(1)}, f32[32,12288]{1,0:T(8,128)}, u32[]{:S(2)}) copy-start(f32[32,12288]{1,0:T(8,128)} %tie.5) | copy-start | bytes 4718596
  83.9 40.5 %all-to-all-start.1 = ((bf16[4,2,8,32,128]{4,3,2,1,0:T(8,128)(2,1)}), bf16[4,2,8,32,128]{4,3,2,1,0:T(8,128)(2,1)S(1)}, u32[]{:S(2)}, u32[]{:S(2)}) async-start(bf16[4,2,8,32,128]{4,3,2,1,0:T(8,128)(2,1)} %add_convert_fusion.6), calls=%async_computation.1 | async-start | bytes 1048576 | tf_op jit(solution)/shard_map/all_to_all | solution.py:175
  87.4 34.3 %copy-start.14 = (bf16[4,2,24,32,128]{4,3,2,1,0:T(8,128)(2,1)S(1)}, bf16[4,2,24,32,128]{4,3,2,1,0:T(8,128)(2,1)}, u32[]{:S(2)}) copy-start(bf16[4,2,24,32,128]{4,3,2,1,0:T(8,128)(2,1)} %copy-done.13) | copy-start | bytes 4718596
  87.4 34.3 %copy-start.16 = (bf16[4,2,24,32,128]{4,3,2,1,0:T(8,128)(2,1)S(1)}, bf16[4,2,24,32,128]{4,3,2,1,0:T(8,128)(2,1)}, u32[]{:S(2)}) copy-start(bf16[4,2,24,32,128]{4,3,2,1,0:T(8,128)(2,1)} %copy-done.15) | copy-start | bytes 4718596
  89.8 67.6 %collective-permute-start.5 = (bf16[32,12288]{1,0:T(8,128)(2,1)}, bf16[32,12288]{1,0:T(8,128)(2,1)}, u32[]{:S(2)}, u32[]{:S(2)}) collective-permute-start(bf16[32,12288]{1,0:T(8,128)(2,1)} %add_convert_fusion.4), channel_id=1, source_target_pairs={{0,8},{8,16},{16,24},{1,9},{9,17},{17,25},{2,10},{10,18},{18,26},{... | collective-permute-start | bytes 2359304 | tf_op jit(solution)/shard_map/ppermute | solution.py:145
  124.4 5.0 %copy-start.4 = (f32[32,12288]{1,0:T(8,128)S(1)}, f32[32,12288]{1,0:T(8,128)}, u32[]{:S(2)}) copy-start(f32[32,12288]{1,0:T(8,128)} %tie.4) | copy-start | bytes 4718596
  124.4 7.3 %copy-start.18 = (bf16[4,2,8,32,128]{4,3,2,1,0:T(8,128)(2,1)}, bf16[4,2,8,32,128]{4,3,2,1,0:T(8,128)(2,1)S(1)}, u32[]{:S(2)}) copy-start(bf16[4,2,8,32,128]{4,3,2,1,0:T(8,128)(2,1)S(1)} %all-to-all-done.1) | copy-start | bytes 1572868
  124.4 29.5 %all-to-all-start.2 = ((bf16[4,2,16,32,128]{4,3,2,1,0:T(8,128)(2,1)}), bf16[4,2,16,32,128]{4,3,2,1,0:T(8,128)(2,1)}, u32[]{:S(2)}, u32[]{:S(2)}) async-start(bf16[4,2,16,32,128]{4,3,2,1,0:T(8,128)(2,1)} %add_convert_fusion.1), calls=%async_computation.2 | async-start | bytes 2097152 | tf_op jit(solution)/shard_map/all_to_all | solution.py:175
  129.4 3.6 %copy-start.11 = (bf16[4,2,24,32,128]{4,3,2,1,0:T(8,128)(2,1)S(1)}, bf16[4,2,24,32,128]{4,3,2,1,0:T(8,128)(2,1)}, u32[]{:S(2)}) copy-start(bf16[4,2,24,32,128]{4,3,2,1,0:T(8,128)(2,1)} %get-tuple-element.20) | copy-start | bytes 4718596
  129.4 3.6 %copy-start.12 = (bf16[4,2,24,32,128]{4,3,2,1,0:T(8,128)(2,1)S(1)}, bf16[4,2,24,32,128]{4,3,2,1,0:T(8,128)(2,1)}, u32[]{:S(2)}) copy-start(bf16[4,2,24,32,128]{4,3,2,1,0:T(8,128)(2,1)} %get-tuple-element.22) | copy-start | bytes 4718596
  131.7 35.6 %collective-permute-start.3 = (bf16[32,12288]{1,0:T(8,128)(2,1)}, bf16[32,12288]{1,0:T(8,128)(2,1)S(1)}, u32[]{:S(2)}, u32[]{:S(2)}) collective-permute-start(bf16[32,12288]{1,0:T(8,128)(2,1)} %add_convert_fusion.5), channel_id=1, source_target_pairs={{8,0},{16,8},{24,16},{9,1},{17,9},{25,17},{10,2},{18,10},{26,18},{... | collective-permute-start | bytes 2359304 | tf_op jit(solution)/shard_map/ppermute | solution.py:145
  153.9 37.6 %all-to-all-start.3 = ((bf16[4,2,16,32,128]{4,3,2,1,0:T(8,128)(2,1)}), bf16[4,2,16,32,128]{4,3,2,1,0:T(8,128)(2,1)S(1)}, u32[]{:S(2)}, u32[]{:S(2)}) async-start(bf16[4,2,16,32,128]{4,3,2,1,0:T(8,128)(2,1)} %add_convert_fusion), calls=%async_computation.3 | async-start | bytes 2097152 | tf_op jit(solution)/shard_map/all_to_all | solution.py:175
  167.3 2.5 %copy-start.19 = (bf16[4,2,8,32,128]{4,3,2,1,0:T(8,128)(2,1)S(1)}, bf16[4,2,8,32,128]{4,3,2,1,0:T(8,128)(2,1)}, u32[]{:S(2)}) copy-start(bf16[4,2,8,32,128]{4,3,2,1,0:T(8,128)(2,1)} %copy-done.18) | copy-start | bytes 1572868
  (2 other events, 3.9 us)

commit v7 on v6

v7 whole, which is shorter than its diff:
```python
import functools
import math

import jax
import jax.numpy as jnp
from jax import lax
from jax.experimental import pallas as pl
from jax.experimental.pallas import tpu as pltpu
from jax.sharding import PartitionSpec as P

SCALE = math.sqrt(2.0 / math.pi)
CUBIC = 0.044715
GROUP = 4


def tick_kernel(relay, per_step, n_mp, n_deps, len_ref, idx_in_ref, idx_out_ref, x_ref, g_ref, w_in_ref, w_out_ref, *refs):
    keep_in_ref, send_in_ref, keep_out_ref, send_out_ref, share_ref, acc_ref = refs[n_deps:]
    step = pl.program_id(0)
    me = lax.axis_index("dp")
    rows, block = x_ref.shape[0], w_in_ref.shape[-1]
    piece = keep_in_ref.shape[2]
    pieces = block // piece
    live = lax.broadcasted_iota(jnp.int32, (rows, block), 0) < len_ref[relay]

    @pl.when(step == 0)
    def _():
        acc_ref[...] = jnp.zeros_like(acc_ref)

    odd = me % 2 == 1

    def put(keep_ref, send_ref, i, value):
        value = value.astype(jnp.bfloat16)
        for k in range(pieces // 2):
            low = value[2 * k * piece:(2 * k + 1) * piece]
            high = value[(2 * k + 1) * piece:(2 * k + 2) * piece]
            keep_ref[k ^ (me // 2), i] = jnp.where(odd, high, low)
            send_ref[k ^ (me // 2), i] = jnp.where(odd, low, high)

    f32 = jnp.float32
    over_last = (((1,), (1,)), ((), ()))
    over_rows = (((0,), (0,)), ((), ()))
    for start in range(0, per_step, GROUP):
        group = range(start, min(start + GROUP, per_step))
        sources = [idx_in_ref[0, relay, step * per_step + i] for i in group]
        targets = [idx_out_ref[0, relay, step * per_step + i] for i in group]
        picked = [x_ref[:, pl.ds(pl.multiple_of(b * block, block), block)] for b in sources]
        back = [g_ref[:, pl.ds(pl.multiple_of(b * block, block), block)] for b in targets]
        back = [jnp.where(live, v, jnp.zeros_like(v)) for v in back]
        pre = [jnp.dot(v, w_in_ref[i], preferred_element_type=f32) for v, i in zip(picked, group)]
        back_pre = [lax.dot_general(v, w_out_ref[i], over_last, preferred_element_type=f32) for v, i in zip(back, group)]
        act, grad_pre = [], []
        for v, up in zip(pre, back_pre):
            square = v * v
            th = jnp.tanh(SCALE * (v + CUBIC * (square * v)))
            cdf = 0.5 * (1.0 + th)
            act.append((v * cdf).astype(jnp.bfloat16))
            slope = cdf + (0.5 * v) * ((1.0 - th) * (1.0 + th)) * (SCALE * (1.0 + (3.0 * CUBIC) * square))
            grad_pre.append((up * slope).astype(jnp.bfloat16))
        terms = [lax.dot_general(v, w_in_ref[i], over_last, preferred_element_type=f32) for v, i in zip(grad_pre, group)]
        grad_in = [lax.dot_general(a, v, over_rows, preferred_element_type=f32) for a, v in zip(picked, grad_pre)]
        grad_out = [lax.dot_general(a, v, over_rows, preferred_element_type=f32) for a, v in zip(act, back)]
        for i, b, term, g_in, g_out in zip(group, sources, terms, grad_in, grad_out):
            acc_ref[b] += term
            put(keep_in_ref, send_in_ref, i, g_in)
            put(keep_out_ref, send_out_ref, i, g_out)

    @pl.when(step == pl.num_programs(0) - 1)
    def _():
        share = rows // n_mp
        owned = live & (lax.broadcasted_iota(jnp.int32, (rows, block), 0) // share == lax.axis_index("mp"))
        for b in range(acc_ref.shape[0]):
            columns = slice(b * block, (b + 1) * block)
            held = g_ref[:, columns]
            held = jnp.where(owned, held, jnp.zeros_like(held)).astype(jnp.float32)
            share_ref[:, columns] = (acc_ref[b] + held).astype(jnp.bfloat16)


def tick(relay, n_dp, n_mp, deps, lengths, idx_in, idx_out, section_in, out_grad, w_in, w_out):
    rows, width = section_in.shape[2:]
    blocks, block = w_in.shape[2:4]
    per_step = math.gcd(blocks, 8)
    steps = blocks // per_step
    piece = block // n_dp
    whole = pl.BlockSpec((None, None, rows, width), lambda i, *_: (relay, 0, 0, 0))
    weight = pl.BlockSpec((None, None, per_step, block, block), lambda i, *_: (0, relay, i, 0, 0))
    slots = jax.ShapeDtypeStruct((n_dp // 2, blocks, piece, block), jnp.bfloat16)
    slots_spec = pl.BlockSpec((n_dp // 2, per_step, piece, block), lambda i, *_: (0, i, 0, 0))
    return pl.pallas_call(
        functools.partial(tick_kernel, relay, per_step, n_mp, len(deps)),
        grid_spec=pltpu.PrefetchScalarGridSpec(
            num_scalar_prefetch=3,
            grid=(steps,),
            in_specs=[whole, whole, weight, weight] + [pl.BlockSpec(memory_space=pl.ANY)] * len(deps),
            out_specs=[slots_spec] * 4 + [pl.BlockSpec((rows, width), lambda i, *_: (0, 0))],
            scratch_shapes=[pltpu.VMEM((width // block, rows, block), jnp.float32)],
        ),
        out_shape=[slots] * 4 + [jax.ShapeDtypeStruct((rows, width), jnp.bfloat16)],
        compiler_params=pltpu.CompilerParams(
            dimension_semantics=("arbitrary",), vmem_limit_bytes=56 * 1024 * 1024
        ),
        cost_estimate=pl.CostEstimate(
            flops=blocks * 10 * rows * block * block,
            bytes_accessed=blocks * block * block * 8 + rows * width * 6,
            transcendentals=blocks * rows * block,
        ),
        name=f"tick{relay}",
    )(lengths, idx_in, idx_out, section_in, out_grad, w_in, w_out, *deps)


def total(*parts):
    return functools.reduce(lambda a, b: a + b, [p.astype(jnp.float32) for p in parts])


def tie(value, *deps):
    any_space = pl.BlockSpec(memory_space=pl.ANY)
    return pl.pallas_call(
        lambda *refs: None,
        in_specs=[any_space] * (1 + len(deps)),
        out_specs=any_space,
        out_shape=jax.ShapeDtypeStruct(value.shape, value.dtype),
        input_output_aliases={0: 0},
        cost_estimate=pl.CostEstimate(flops=1000, bytes_accessed=1000, transcendentals=0),
        name="tie",
    )(value, *deps)


def flip_bit(value, axis, bit):
    return lax.ppermute(value, axis, [(i, i ^ bit) for i in range(lax.axis_size(axis))])


def from_behind(value, axis, distance):
    devices = range(lax.axis_size(axis))
    route = [(i - distance, i) for i in devices if i - distance in devices]
    return lax.ppermute(value, axis, route)


def body(section_in, out_grad, lengths, w_in, w_out, idx_in, idx_out):
    sections, n_dp, n_mp = (lax.axis_size(a) for a in ("section", "dp", "mp"))
    args = (lengths.reshape(2), idx_in, idx_out, section_in, out_grad, w_in, w_out)
    keep, got, dx = [], [], []
    for relay in range(2):
        keep_in, send_in, keep_out, send_out, share = tick(relay, n_dp, n_mp, keep[:1], *args)
        keep += [keep_in, keep_out]
        got += [flip_bit(send_in, "dp", 1), flip_bit(send_out, "dp", 1)]
        dx.append(lax.psum_scatter(share, "mp", scatter_dimension=0, tiled=True))
    sums = [total(k[1], g[1]).astype(jnp.bfloat16) for k, g in zip(keep, got)]
    came = [flip_bit(tie(v, *sums[:i]) if i else v, "dp", 2) for i, v in enumerate(sums)]
    passed = [from_behind(v, "section", distance) for v, distance in zip(dx, (-1, 1))]
    moved = []
    for i, (k, g, far) in enumerate(zip(keep, got, came)):
        mine = total(k[0], g[0], tie(far, *(sums if i == 0 else [mine]))).astype(jnp.bfloat16)
        mine = mine.reshape(sections, -1, *mine.shape[1:])
        moved.append(lax.all_to_all(mine, "section", split_axis=0, concat_axis=0, tiled=True))
    grads = jnp.stack([total(moved[i], jnp.flip(moved[i + 2], 0)) for i in range(2)], axis=1)
    return jnp.stack(passed, axis=0)[:, None], grads[:, :, None]


def solution(mesh):
    placed = (
        P(None, "section", "dp", None),
        P(None, "section", "dp", None),
        P(None, "section", "dp"),
        P("section", None, "mp", None, None),
        P("section", None, "mp", None, None),
        P("section", None, "mp"),
        P("section", None, "mp"),
    )
    return jax.shard_map(
        body,
        mesh=mesh,
        in_specs=placed,
        out_specs=(
            P(None, "section", ("dp", "mp"), None),
            P(None, None, "mp", "section", "dp", None),
        ),
        check_vma=False,
    )
```

time: 196 us -> 188 us (0.959)
  waiting for transfers between devices: 94 us -> 74.9 us
  between operations: 0.87 us -> 14.2 us
  starting transfers between devices: 32.5 us -> 34.7 us
  Pallas kernels: 36.2 us -> 34.1 us
    all_to_all x4, waiting for transfers between devices: 42.2 us -> 14.7 us  [body(): lax.all_to_all(mine, 'section', split_axis=0, concat_axis=0, tiled=True)]
    ppermute x6 -> x8, waiting for transfers between devices: 42 us -> 51.1 us  [flip_bit(): lax.ppermute(value, axis, [(i, i ^ bit) for i in range(lax.axis_size(axis...]
    squeeze x4 -> x0, local copies, waits for them, and re-layouts: 4.76 us -> none  [parts(): return [v[relay][slot][:, :, cut[0]:cut[1]] for v in (keep, got)]]
    unnamed x40 -> x27, local copies, waits for them, and re-layouts: 1.76 us -> 5.79 us
    ppermute x2 -> x0, starting transfers between devices: 3.03 us -> none  [body(): lax.ppermute(theirs[k - 1], 'mp', [(i, (i + k) % n_mp) for i in range(n_m...]
    add x2 -> x0, other arithmetic: 2.73 us -> none  [total(): a + b]
    another operation x0 -> x2, other arithmetic: none -> 2.69 us  [body(): jnp.stack([total(moved[i], jnp.flip(moved[i + 2], 0)) for i in range(2)],...]
    ppermute x6 -> x8, starting transfers between devices: 6.08 us -> 8.72 us  [flip_bit(): lax.ppermute(value, axis, [(i, i ^ bit) for i in range(lax.axis_size(axis...]
  transfers between devices with their start and end apart: 14 -> 16, of which waited for: 8 -> 7; matrix products, arithmetic and copies ran while one was open for 13% -> 12% of each run, Pallas kernels for 0% -> 9%
where the time goes in v7:
time: 188 us; the launch traced here: 187 us
  waiting for transfers between devices  74.9 us (40%)
  starting transfers between devices  34.7 us (18%)
  Pallas kernels  34.1 us (18%)
  other arithmetic  23.4 us (12%)
  between operations  14.2 us (8%)
  local copies, waits for them, and re-layouts  5.79 us (3%)
    ppermute x8, waiting for transfers between devices, flip_bit(): lax.ppermute(value, axis, [(i, i ^ bit) for i in range(lax.axis_size(axis...  51.1 us
    pallas_call x2, Pallas kernels, tick(): pl.pallas_call(functools.partial(tick_kernel, relay, per_step, n_mp, len(...  34.1 us
    all_to_all x4, starting transfers between devices, body(): lax.all_to_all(mine, 'section', split_axis=0, concat_axis=0, tiled=True)  19.1 us
    all_to_all x4, waiting for transfers between devices, body(): lax.all_to_all(mine, 'section', split_axis=0, concat_axis=0, tiled=True)  14.7 us
    convert_element_type x4, other arithmetic, body(): total(k[0], g[0], tie(far, *(sums if i == 0 else [mine])))  10.7 us
    ppermute x2, waiting for transfers between devices, from_behind(): return lax.ppermute(value, axis, route)  9.02 us
    ppermute x8, starting transfers between devices, flip_bit(): lax.ppermute(value, axis, [(i, i ^ bit) for i in range(lax.axis_size(axis...  8.72 us
    convert_element_type x4, other arithmetic, body(): sums = [total(k[1], g[1]).astype(jnp.bfloat16) for k, g in zip(keep, got)]  7.04 us
  transfers between devices with their start and end apart: 16, of which 7 were waited for; matrix products, arithmetic and copies ran while one was open for 12% of the time, Pallas kernels for 9%

profile of v7, /device:TPU:0, one launch (start us, length us, event | category | flops | bytes accessed | tf_op | source)
XLA Modules:
  0.0 187.1 jit_solution(2492294274809366565)
XLA Ops:
  7.2 17.0 %tick0.1 = (bf16[2,96,32,128]{3,2,1,0:T(8,128)(2,1)}, bf16[2,96,32,128]{3,2,1,0:T(8,128)(2,1)}, bf16[2,96,32,128]{3,2,1,0:T(8,128)(2,1)}, bf16[2,96,32,128]{3,2,1,0:T(8,128)(2,1)}, bf16[64,12288]{1,0:T(8,128)(2,1)}) custom-call(s32[2]{0:T(128)} %bitcast.41, s32[1,2,96]{2,1,0:T(2,128)} %idx_in_ref.3, s32[1,2,96]{2,1,0:T(2,128)} %idx_out_ref.3, ...), custom_call_target="tpu_custom_call" | custom-call | flops 1006632960 | bytes 17301504 | tf_op jit(solution)/shard_map/tick0/pallas_call | solution.py:88
  24.9 17.1 %tick1.1 = (bf16[2,96,32,128]{3,2,1,0:T(8,128)(2,1)}, bf16[2,96,32,128]{3,2,1,0:T(8,128)(2,1)}, bf16[2,96,32,128]{3,2,1,0:T(8,128)(2,1)}, bf16[2,96,32,128]{3,2,1,0:T(8,128)(2,1)}, bf16[64,12288]{1,0:T(8,128)(2,1)}) custom-call(s32[2]{0:T(128)} %bitcast.42, s32[1,2,96]{2,1,0:T(2,128)} %idx_in_ref.3, s32[1,2,96]{2,1,0:T(2,128)} %idx_out_ref.3, ...), custom_call_target="tpu_custom_call" | custom-call | flops 1006632960 | bytes 17301504 | tf_op jit(solution)/shard_map/tick1/pallas_call | solution.py:88
  42.7 1.1 copy-done.12
  44.0 3.0 %collective-permute-start.3 = (bf16[96,32,128]{2,1,0:T(8,128)(2,1)S(1)}, bf16[96,32,128]{2,1,0:T(8,128)(2,1)S(1)}, u32[]{:S(2)}, u32[]{:S(2)}) collective-permute-start(bf16[96,32,128]{2,1,0:T(8,128)(2,1)S(1)} %fusion.4.refs_1_), channel_id=1, source_target_pairs={{0,4},{2,6},{4,0},{6,2},{1,5},{3,7},{5,1},{7,3},{8,12},{10,14},{12... | collective-permute-start | bytes 2359304 | tf_op jit(solution)/shard_map/ppermute | solution.py:128
  47.1 2.2 %fusion.5.refs_2_.refs_0_ = bf16[96,32,128]{2,1,0:T(8,128)(2,1)} fusion(bf16[2,96,32,128]{3,2,1,0:T(8,128)(2,1)} %collective-permute-done.4, bf16[2,96,32,128]{3,2,1,0:T(8,128)(2,1)S(1)} %copy-done.10), kind=kLoop, calls=%fused_computation.17 | loop fusion | flops 1572864 | bytes 2359296 | tf_op jit(solution)/shard_map/convert_element_type | solution.py:146
  49.3 2.4 %fusion.6.refs_3_.refs_0_ = bf16[96,32,128]{2,1,0:T(8,128)(2,1)} fusion(bf16[2,96,32,128]{3,2,1,0:T(8,128)(2,1)} %collective-permute-done.5, bf16[2,96,32,128]{3,2,1,0:T(8,128)(2,1)S(1)} %copy-done.9), kind=kLoop, calls=%fused_computation.18 | loop fusion | flops 1572864 | bytes 2359296 | tf_op jit(solution)/shard_map/convert_element_type | solution.py:146
  51.7 2.2 %fusion.7.refs_4_.refs_0_ = bf16[96,32,128]{2,1,0:T(8,128)(2,1)} fusion(bf16[2,96,32,128]{3,2,1,0:T(8,128)(2,1)} %collective-permute-done.6, bf16[2,96,32,128]{3,2,1,0:T(8,128)(2,1)S(1)} %copy-done.8), kind=kLoop, calls=%fused_computation.19 | loop fusion | flops 1572864 | bytes 2359296 | tf_op jit(solution)/shard_map/convert_element_type | solution.py:146
  53.9 10.9 %collective-permute-done.3.refs_0_ = bf16[96,32,128]{2,1,0:T(8,128)(2,1)S(1)} collective-permute-done((bf16[96,32,128]{2,1,0:T(8,128)(2,1)S(1)}, bf16[96,32,128]{2,1,0:T(8,128)(2,1)S(1)}, u32[]{:S(2)}, u32[]{:S(2)}) %collective-permute-start.3) | collective-permute-done | bytes 786464 | tf_op jit(solution)/shard_map/ppermute | solution.py:128
  64.9 0.9 copy-done.4
  65.7 2.6 %fusion.3 = bf16[96,32,128]{2,1,0:T(8,128)(2,1)} fusion(bf16[96,32,128]{2,1,0:T(8,128)(2,1)} %tie.7, bf16[2,96,32,128]{3,2,1,0:T(8,128)(2,1)} %copy-done.12, bf16[2,96,32,128]{3,2,1,0:T(8,128)(2,1)S(1)} %copy-done.3), kind=kLoop, calls=%fused_computation.9 | loop fusion | flops 2359296 | bytes 3145728 | tf_op jit(solution)/shard_map/convert_element_type | solution.py:151
  68.3 5.1 %all-to-all-start = ((bf16[4,24,32,128]{3,2,1,0:T(8,128)(2,1)}), bf16[4,24,32,128]{3,2,1,0:T(8,128)(2,1)S(1)}, u32[]{:S(2)}, u32[]{:S(2)}) async-start(bf16[4,24,32,128]{3,2,1,0:T(8,128)(2,1)} %bitcast.10.refs_1_), calls=%async_computation.2 | async-start | bytes 1572864 | tf_op jit(solution)/shard_map/all_to_all | solution.py:153
  73.4 1.5 collective-permute-start.8
  74.9 17.2 %collective-permute-done.8.refs_0_ = bf16[96,32,128]{2,1,0:T(8,128)(2,1)S(1)} collective-permute-done((bf16[96,32,128]{2,1,0:T(8,128)(2,1)}, bf16[96,32,128]{2,1,0:T(8,128)(2,1)S(1)}, u32[]{:S(2)}, u32[]{:S(2)}) %collective-permute-start.8) | collective-permute-done | bytes 786464 | tf_op jit(solution)/shard_map/ppermute | solution.py:128
  93.1 2.6 %fusion.1 = bf16[96,32,128]{2,1,0:T(8,128)(2,1)} fusion(bf16[96,32,128]{2,1,0:T(8,128)(2,1)} %tie.10, bf16[2,96,32,128]{3,2,1,0:T(8,128)(2,1)} %collective-permute-done.4, bf16[2,96,32,128]{3,2,1,0:T(8,128)(2,1)S(1)} %copy-done.11), kind=kLoop, calls=%fused_computation.5 | loop fusion | flops 2359296 | bytes 3145728 | tf_op jit(solution)/shard_map/convert_element_type | solution.py:151
  95.6 4.9 %all-to-all-start.2 = ((bf16[4,24,32,128]{3,2,1,0:T(8,128)(2,1)}), bf16[4,24,32,128]{3,2,1,0:T(8,128)(2,1)S(1)}, u32[]{:S(2)}, u32[]{:S(2)}) async-start(bf16[4,24,32,128]{3,2,1,0:T(8,128)(2,1)} %bitcast.13.refs_1_), calls=%async_computation.4 | async-start | bytes 1572864 | tf_op jit(solution)/shard_map/all_to_all | solution.py:153
  100.5 1.5 collective-permute-start.7
  102.0 15.5 %collective-permute-done.7.refs_0_ = bf16[96,32,128]{2,1,0:T(8,128)(2,1)S(1)} collective-permute-done((bf16[96,32,128]{2,1,0:T(8,128)(2,1)S(1)}, bf16[96,32,128]{2,1,0:T(8,128)(2,1)S(1)}, u32[]{:S(2)}, u32[]{:S(2)}) %collective-permute-start.7) | collective-permute-done | bytes 786464 | tf_op jit(solution)/shard_map/ppermute | solution.py:128
  118.4 2.8 %fusion.2 = bf16[96,32,128]{2,1,0:T(8,128)(2,1)} fusion(bf16[96,32,128]{2,1,0:T(8,128)(2,1)} %tie.11, bf16[2,96,32,128]{3,2,1,0:T(8,128)(2,1)} %collective-permute-done.5, bf16[2,96,32,128]{3,2,1,0:T(8,128)(2,1)} %get-tuple-element.18), kind=kLoop, calls=%fused_computation.7 | loop fusion | flops 2359296 | bytes 3145728 | tf_op jit(solution)/shard_map/convert_element_type | solution.py:151
  121.2 4.9 %all-to-all-start.1 = ((bf16[4,24,32,128]{3,2,1,0:T(8,128)(2,1)}), bf16[4,24,32,128]{3,2,1,0:T(8,128)(2,1)S(1)}, u32[]{:S(2)}, u32[]{:S(2)}) async-start(bf16[4,24,32,128]{3,2,1,0:T(8,128)(2,1)} %bitcast.14.refs_1_), calls=%async_computation.3 | async-start | bytes 1572864 | tf_op jit(solution)/shard_map/all_to_all | solution.py:153
  126.2 1.5 collective-permute-start.9
  127.7 1.3 collective-permute-start
  129.0 5.5 %collective-permute-start.1 = (bf16[32,12288]{1,0:T(8,128)(2,1)}, bf16[32,12288]{1,0:T(8,128)(2,1)}, u32[]{:S(2)}, u32[]{:S(2)}) collective-permute-start(bf16[32,12288]{1,0:T(8,128)(2,1)} %reduce-scatter.5.cloned.1.call-done), channel_id=1, source_target_pairs={{0,8},{8,16},{16,24},{1,9},{9,17},{17,25},{2,10},{10,18},{18,26},{... | collective-permute-start | bytes 2359304 | tf_op jit(solution)/shard_map/ppermute | solution.py:134
  134.5 7.4 %collective-permute-done.9.refs_0_ = bf16[96,32,128]{2,1,0:T(8,128)(2,1)} collective-permute-done((bf16[96,32,128]{2,1,0:T(8,128)(2,1)S(1)}, bf16[96,32,128]{2,1,0:T(8,128)(2,1)}, u32[]{:S(2)}, u32[]{:S(2)}) %collective-permute-start.9) | collective-permute-done | bytes 786464 | tf_op jit(solution)/shard_map/ppermute | solution.py:128
  141.8 2.8 %fusion = bf16[96,32,128]{2,1,0:T(8,128)(2,1)} fusion(bf16[96,32,128]{2,1,0:T(8,128)(2,1)} %tie.13, bf16[2,96,32,128]{3,2,1,0:T(8,128)(2,1)} %collective-permute-done.6, bf16[2,96,32,128]{3,2,1,0:T(8,128)(2,1)} %get-tuple-element.20), kind=kLoop, calls=%fused_computation.3 | loop fusion | flops 2359296 | bytes 3145728 | tf_op jit(solution)/shard_map/convert_element_type | solution.py:151
  144.7 1.0 all-to-all-done.1
  145.7 4.2 %all-to-all-start.3 = ((bf16[4,24,32,128]{3,2,1,0:T(8,128)(2,1)}), bf16[4,24,32,128]{3,2,1,0:T(8,128)(2,1)}, u32[]{:S(2)}, u32[]{:S(2)}) async-start(bf16[4,24,32,128]{3,2,1,0:T(8,128)(2,1)} %bitcast.17), calls=%async_computation.5 | async-start | bytes 1572864 | tf_op jit(solution)/shard_map/all_to_all | solution.py:153
  149.9 9.0 %collective-permute-done = bf16[32,12288]{1,0:T(8,128)(2,1)} collective-permute-done((bf16[32,12288]{1,0:T(8,128)(2,1)}, bf16[32,12288]{1,0:T(8,128)(2,1)}, u32[]{:S(2)}, u32[]{:S(2)}) %collective-permute-start) | collective-permute-done | bytes 786464 | tf_op jit(solution)/shard_map/ppermute | solution.py:134
  158.9 2.7 %maximum_bitcast_fusion.1 = bf16[2,1,32,12288]{3,2,1,0:T(8,128)(2,1)} fusion(bf16[1,32,12288]{2,1,0:T(8,128)(2,1)} %bitcast.2, bf16[1,32,12288]{2,1,0:T(8,128)(2,1)} %bitcast.1), kind=kLoop, calls=%fused_computation.1 | loop fusion | flops 786432 | bytes 3145728
  161.6 1.3 add_bitcast_fusion.1
  162.9 13.7 %all-to-all-done.3 = bf16[4,24,32,128]{3,2,1,0:T(8,128)(2,1)} async-done(((bf16[4,24,32,128]{3,2,1,0:T(8,128)(2,1)}), bf16[4,24,32,128]{3,2,1,0:T(8,128)(2,1)}, u32[]{:S(2)}, u32[]{:S(2)}) %all-to-all-start.3) | async-done | bytes 786464 | tf_op jit(solution)/shard_map/all_to_all | solution.py:153
  176.6 1.3 add_bitcast_fusion
  178.3 2.0 %copy.17 = f32[4,2,1,24,32,128]{5,4,3,2,1,0:T(8,128)} copy(f32[4,2,1,24,32,128]{5,4,3,0,1,2:T(8,128)S(1)} %maximum_bitcast_fusion) | data formatting | bytes 6291456
  (50 shorter events, 3.6 us)
Async XLA Ops:
  7.2 120.5 %reduce-scatter.3.cloned.1.call-start = ((), (), s32[]{:S(2)}) async-start(), calls=%async_computation.6 | async-start | bytes 2359296 | tf_op jit(solution)/shard_map/reduce_scatter | solution.py:145
  24.3 104.7 %reduce-scatter.5.cloned.1.call-start = ((), (), s32[]{:S(2)}) async-start(), calls=%async_computation.7 | async-start | bytes 2359296 | tf_op jit(solution)/shard_map/reduce_scatter | solution.py:145
  24.3 18.3 %collective-permute-start.2 = (bf16[2,96,32,128]{3,2,1,0:T(8,128)(2,1)}, bf16[2,96,32,128]{3,2,1,0:T(8,128)(2,1)S(1)}, u32[]{:S(2)}, u32[]{:S(2)}) collective-permute-start(bf16[2,96,32,128]{3,2,1,0:T(8,128)(2,1)} %get-tuple-element.15), channel_id=1, source_target_pairs={{0,2},{2,0},{4,6},{6,4},{1,3},{3,1},{5,7},{7,5},{8,10},{10,8},{12,... | collective-permute-start | bytes 4718600 | tf_op jit(solution)/shard_map/ppermute | solution.py:128
  24.9 22.2 %collective-permute-start.4 = (bf16[2,96,32,128]{3,2,1,0:T(8,128)(2,1)}, bf16[2,96,32,128]{3,2,1,0:T(8,128)(2,1)}, u32[]{:S(2)}, u32[]{:S(2)}) collective-permute-start(bf16[2,96,32,128]{3,2,1,0:T(8,128)(2,1)} %get-tuple-element.17), channel_id=1, source_target_pairs={{0,2},{2,0},{4,6},{6,4},{1,3},{3,1},{5,7},{7,5},{8,10},{10,8},{12,... | collective-permute-start | bytes 4718600 | tf_op jit(solution)/shard_map/ppermute | solution.py:128
  42.0 1.8 copy-start.3
  42.0 7.2 %collective-permute-start.5 = (bf16[2,96,32,128]{3,2,1,0:T(8,128)(2,1)}, bf16[2,96,32,128]{3,2,1,0:T(8,128)(2,1)}, u32[]{:S(2)}, u32[]{:S(2)}) collective-permute-start(bf16[2,96,32,128]{3,2,1,0:T(8,128)(2,1)} %get-tuple-element.19), channel_id=1, source_target_pairs={{0,2},{2,0},{4,6},{6,4},{1,3},{3,1},{5,7},{7,5},{8,10},{10,8},{12,... | collective-permute-start | bytes 4718600 | tf_op jit(solution)/shard_map/ppermute | solution.py:128
  42.5 9.1 %collective-permute-start.6 = (bf16[2,96,32,128]{3,2,1,0:T(8,128)(2,1)}, bf16[2,96,32,128]{3,2,1,0:T(8,128)(2,1)}, u32[]{:S(2)}, u32[]{:S(2)}) collective-permute-start(bf16[2,96,32,128]{3,2,1,0:T(8,128)(2,1)} %get-tuple-element.21), channel_id=1, source_target_pairs={{0,2},{2,0},{4,6},{6,4},{1,3},{3,1},{5,7},{7,5},{8,10},{10,8},{12,... | collective-permute-start | bytes 4718600 | tf_op jit(solution)/shard_map/ppermute | solution.py:128
  42.6 4.4 %copy-start.10 = (bf16[2,96,32,128]{3,2,1,0:T(8,128)(2,1)S(1)}, bf16[2,96,32,128]{3,2,1,0:T(8,128)(2,1)}, u32[]{:S(2)}) copy-start(bf16[2,96,32,128]{3,2,1,0:T(8,128)(2,1)} %get-tuple-element.16) | copy-start | bytes 4718596
  42.7 1.1 copy-start.12
  44.0 7.7 %copy-start = (bf16[96,32,128]{2,1,0:T(8,128)(2,1)}, bf16[96,32,128]{2,1,0:T(8,128)(2,1)S(1)}, u32[]{:S(2)}) copy-start(bf16[96,32,128]{2,1,0:T(8,128)(2,1)S(1)} %fusion.4.refs_1_) | copy-start | bytes 2359300
  44.0 5.3 %copy-start.9 = (bf16[2,96,32,128]{3,2,1,0:T(8,128)(2,1)S(1)}, bf16[2,96,32,128]{3,2,1,0:T(8,128)(2,1)}, u32[]{:S(2)}) copy-start(bf16[2,96,32,128]{3,2,1,0:T(8,128)(2,1)} %get-tuple-element.18) | copy-start | bytes 4718596
  44.0 20.8 %collective-permute-start.3 = (bf16[96,32,128]{2,1,0:T(8,128)(2,1)S(1)}, bf16[96,32,128]{2,1,0:T(8,128)(2,1)S(1)}, u32[]{:S(2)}, u32[]{:S(2)}) collective-permute-start(bf16[96,32,128]{2,1,0:T(8,128)(2,1)S(1)} %fusion.4.refs_1_), channel_id=1, source_target_pairs={{0,4},{2,6},{4,0},{6,2},{1,5},{3,7},{5,1},{7,3},{8,12},{10,14},{12... | collective-permute-start | bytes 2359304 | tf_op jit(solution)/shard_map/ppermute | solution.py:128
  49.3 2.4 %copy-start.8 = (bf16[2,96,32,128]{3,2,1,0:T(8,128)(2,1)S(1)}, bf16[2,96,32,128]{3,2,1,0:T(8,128)(2,1)}, u32[]{:S(2)}) copy-start(bf16[2,96,32,128]{3,2,1,0:T(8,128)(2,1)} %get-tuple-element.20) | copy-start | bytes 4718596
  64.9 0.9 copy-start.4
  68.3 27.3 %all-to-all-start = ((bf16[4,24,32,128]{3,2,1,0:T(8,128)(2,1)}), bf16[4,24,32,128]{3,2,1,0:T(8,128)(2,1)S(1)}, u32[]{:S(2)}, u32[]{:S(2)}) async-start(bf16[4,24,32,128]{3,2,1,0:T(8,128)(2,1)} %bitcast.10.refs_1_), calls=%async_computation.2 | async-start | bytes 1572864 | tf_op jit(solution)/shard_map/all_to_all | solution.py:153
  73.4 19.7 %copy-start.11 = (bf16[2,96,32,128]{3,2,1,0:T(8,128)(2,1)S(1)}, bf16[2,96,32,128]{3,2,1,0:T(8,128)(2,1)}, u32[]{:S(2)}) copy-start(bf16[2,96,32,128]{3,2,1,0:T(8,128)(2,1)} %get-tuple-element.16) | copy-start | bytes 4718596
  73.4 18.8 %collective-permute-start.8 = (bf16[96,32,128]{2,1,0:T(8,128)(2,1)}, bf16[96,32,128]{2,1,0:T(8,128)(2,1)S(1)}, u32[]{:S(2)}, u32[]{:S(2)}) collective-permute-start(bf16[96,32,128]{2,1,0:T(8,128)(2,1)} %tie.9), channel_id=1, source_target_pairs={{0,4},{2,6},{4,0},{6,2},{1,5},{3,7},{5,1},{7,3},{8,12},{10,14},{12... | collective-permute-start | bytes 2359304 | tf_op jit(solution)/shard_map/ppermute | solution.py:128
  92.2 0.9 copy-start.6
  95.6 4.9 %copy-start.1 = (bf16[96,32,128]{2,1,0:T(8,128)(2,1)S(1)}, bf16[96,32,128]{2,1,0:T(8,128)(2,1)}, u32[]{:S(2)}) copy-start(bf16[96,32,128]{2,1,0:T(8,128)(2,1)} %tie.8) | copy-start | bytes 2359300
  95.6 25.6 %all-to-all-start.2 = ((bf16[4,24,32,128]{3,2,1,0:T(8,128)(2,1)}), bf16[4,24,32,128]{3,2,1,0:T(8,128)(2,1)S(1)}, u32[]{:S(2)}, u32[]{:S(2)}) async-start(bf16[4,24,32,128]{3,2,1,0:T(8,128)(2,1)} %bitcast.13.refs_1_), calls=%async_computation.4 | async-start | bytes 1572864 | tf_op jit(solution)/shard_map/all_to_all | solution.py:153
  100.5 17.0 %collective-permute-start.7 = (bf16[96,32,128]{2,1,0:T(8,128)(2,1)S(1)}, bf16[96,32,128]{2,1,0:T(8,128)(2,1)S(1)}, u32[]{:S(2)}, u32[]{:S(2)}) collective-permute-start(bf16[96,32,128]{2,1,0:T(8,128)(2,1)S(1)} %copy-done.1), channel_id=1, source_target_pairs={{0,4},{2,6},{4,0},{6,2},{1,5},{3,7},{5,1},{7,3},{8,12},{10,14},{12... | collective-permute-start | bytes 2359304 | tf_op jit(solution)/shard_map/ppermute | solution.py:128
  117.6 0.9 copy-start.7
  121.2 5.0 %copy-start.2 = (bf16[96,32,128]{2,1,0:T(8,128)(2,1)S(1)}, bf16[96,32,128]{2,1,0:T(8,128)(2,1)}, u32[]{:S(2)}) copy-start(bf16[96,32,128]{2,1,0:T(8,128)(2,1)} %tie.12) | copy-start | bytes 2359300
  121.2 24.4 %all-to-all-start.1 = ((bf16[4,24,32,128]{3,2,1,0:T(8,128)(2,1)}), bf16[4,24,32,128]{3,2,1,0:T(8,128)(2,1)S(1)}, u32[]{:S(2)}, u32[]{:S(2)}) async-start(bf16[4,24,32,128]{3,2,1,0:T(8,128)(2,1)} %bitcast.14.refs_1_), calls=%async_computation.3 | async-start | bytes 1572864 | tf_op jit(solution)/shard_map/all_to_all | solution.py:153
  126.2 15.7 %collective-permute-start.9 = (bf16[96,32,128]{2,1,0:T(8,128)(2,1)S(1)}, bf16[96,32,128]{2,1,0:T(8,128)(2,1)}, u32[]{:S(2)}, u32[]{:S(2)}) collective-permute-start(bf16[96,32,128]{2,1,0:T(8,128)(2,1)S(1)} %copy-done.2), channel_id=1, source_target_pairs={{0,4},{2,6},{4,0},{6,2},{1,5},{3,7},{5,1},{7,3},{8,12},{10,14},{12... | collective-permute-start | bytes 2359304 | tf_op jit(solution)/shard_map/ppermute | solution.py:128
  127.7 31.2 %collective-permute-start = (bf16[32,12288]{1,0:T(8,128)(2,1)}, bf16[32,12288]{1,0:T(8,128)(2,1)}, u32[]{:S(2)}, u32[]{:S(2)}) collective-permute-start(bf16[32,12288]{1,0:T(8,128)(2,1)} %reduce-scatter.3.cloned.1.call-done), channel_id=1, source_target_pairs={{8,0},{16,8},{24,16},{9,1},{17,9},{25,17},{10,2},{18,10},{26,18},{... | collective-permute-start | bytes 2359304 | tf_op jit(solution)/shard_map/ppermute | solution.py:134
  129.0 29.9 %collective-permute-start.1 = (bf16[32,12288]{1,0:T(8,128)(2,1)}, bf16[32,12288]{1,0:T(8,128)(2,1)}, u32[]{:S(2)}, u32[]{:S(2)}) collective-permute-start(bf16[32,12288]{1,0:T(8,128)(2,1)} %reduce-scatter.5.cloned.1.call-done), channel_id=1, source_target_pairs={{0,8},{8,16},{16,24},{1,9},{9,17},{17,25},{2,10},{10,18},{18,26},{... | collective-permute-start | bytes 2359304 | tf_op jit(solution)/shard_map/ppermute | solution.py:134
  145.7 13.2 %copy-start.5 = (bf16[4,24,32,128]{3,2,1,0:T(8,128)(2,1)}, bf16[4,24,32,128]{3,2,1,0:T(8,128)(2,1)S(1)}, u32[]{:S(2)}) copy-start(bf16[4,24,32,128]{3,2,1,0:T(8,128)(2,1)S(1)} %all-to-all-done.1) | copy-start | bytes 2359300
  145.7 31.0 %all-to-all-start.3 = ((bf16[4,24,32,128]{3,2,1,0:T(8,128)(2,1)}), bf16[4,24,32,128]{3,2,1,0:T(8,128)(2,1)}, u32[]{:S(2)}, u32[]{:S(2)}) async-start(bf16[4,24,32,128]{3,2,1,0:T(8,128)(2,1)} %bitcast.17), calls=%async_computation.5 | async-start | bytes 1572864 | tf_op jit(solution)/shard_map/all_to_all | solution.py:153
Sparse Core Ops, SparseCore 0:
  24.4 28.7 reduce-scatter.2
  55.5 26.0 reduce-scatter.4

commit v8 on v6

--- a/solution.py
+++ b/solution.py
@@ -11,15 +11,13 @@
 SCALE = math.sqrt(2.0 / math.pi)
 CUBIC = 0.044715
 GROUP = 4
-STEP = 8
 
 
 def tick_kernel(relay, per_step, n_deps, len_ref, idx_in_ref, idx_out_ref, x_ref, g_ref, w_in_ref, w_out_ref, *refs):
-    keep_ref, send_ref, own_ref, other_ref, acc_ref = refs[n_deps:]
+    grad_in_ref, grad_out_ref, own_ref, other_ref, acc_ref = refs[n_deps:]
     step = pl.program_id(0)
-    me = lax.axis_index("dp")
     rows, block = x_ref.shape[0], w_in_ref.shape[-1]
-    piece = keep_ref.shape[3]
+    piece = grad_in_ref.shape[2]
     pieces = block // piece
     live = lax.broadcasted_iota(jnp.int32, (rows, block), 0) < len_ref[relay]
 
@@ -27,15 +25,10 @@
     def _():
         acc_ref[...] = jnp.zeros_like(acc_ref)
 
-    odd = me % 2 == 1
-
-    def put(kind, i, value):
+    def put(ref, i, value):
         value = value.astype(jnp.bfloat16)
-        for k in range(pieces // 2):
-            low = value[2 * k * piece:(2 * k + 1) * piece]
-            high = value[(2 * k + 1) * piece:(2 * k + 2) * piece]
-            keep_ref[k ^ (me // 2), kind, i] = jnp.where(odd, high, low)
-            send_ref[k ^ (me // 2), kind, i] = jnp.where(odd, low, high)
+        for q in range(pieces):
+            ref[q, i] = value[q * piece:(q + 1) * piece]
 
     f32 = jnp.float32
     over_last = (((1,), (1,)), ((), ()))
@@ -62,8 +55,8 @@
         grad_out = [lax.dot_general(a, v, over_rows, preferred_element_type=f32) for a, v in zip(act, back)]
         for i, b, term, g_in, g_out in zip(group, sources, terms, grad_in, grad_out):
             acc_ref[b] += term
-            put(0, i, g_in)
-            put(1, i, g_out)
+            put(grad_in_ref, i, g_in)
+            put(grad_out_ref, i, g_out)
 
     @pl.when(step == pl.num_programs(0) - 1)
     def _():
@@ -80,25 +73,21 @@
                 other_ref[k - 1, :, columns] = acc_ref[b, pl.ds(there, share)].astype(jnp.bfloat16)
 
 
-def tick(relay, sizes, deps, lengths, idx_in, idx_out, section_in, out_grad, w_in, w_out):
-    sections, n_dp, n_mp = sizes
+def tick(relay, n_dp, n_mp, deps, lengths, idx_in, idx_out, section_in, out_grad, w_in, w_out):
     rows, width = section_in.shape[2:]
     blocks, block = w_in.shape[2:4]
-    per = blocks // sections
-    per_step = math.gcd(per, STEP)
-    turns = per // per_step
+    per_step = math.gcd(blocks, 8)
+    steps = blocks // per_step
     piece, share = block // n_dp, rows // n_mp
     whole = pl.BlockSpec((None, None, rows, width), lambda i, *_: (relay, 0, 0, 0))
     weight = pl.BlockSpec((None, None, per_step, block, block), lambda i, *_: (0, relay, i, 0, 0))
-    slots = jax.ShapeDtypeStruct((n_dp // 2, sections, 2, per, piece, block), jnp.bfloat16)
-    slots_spec = pl.BlockSpec(
-        (n_dp // 2, None, 2, per_step, piece, block), lambda i, *_: (0, i // turns, 0, i % turns, 0, 0)
-    )
+    slots = jax.ShapeDtypeStruct((n_dp, blocks, piece, block), jnp.bfloat16)
+    slots_spec = pl.BlockSpec((n_dp, per_step, piece, block), lambda i, *_: (0, i, 0, 0))
     return pl.pallas_call(
         functools.partial(tick_kernel, relay, per_step, len(deps)),
         grid_spec=pltpu.PrefetchScalarGridSpec(
             num_scalar_prefetch=3,
-            grid=(sections * turns,),
+            grid=(steps,),
             in_specs=[whole, whole, weight, weight] + [pl.BlockSpec(memory_space=pl.ANY)] * len(deps),
             out_specs=[slots_spec] * 2
             + [pl.BlockSpec((share, width), lambda i, *_: (0, 0)), pl.BlockSpec((n_mp - 1, share, width), lambda i, *_: (0, 0, 0))],
@@ -122,23 +111,6 @@
     return functools.reduce(lambda a, b: a + b, [p.astype(jnp.float32) for p in parts])
 
 
-def tie(value, *deps):
-    any_space = pl.BlockSpec(memory_space=pl.ANY)
-    return pl.pallas_call(
-        lambda *refs: None,
-        in_specs=[any_space] * (1 + len(deps)),
-        out_specs=any_space,
-        out_shape=jax.ShapeDtypeStruct(value.shape, value.dtype),
-        input_output_aliases={0: 0},
-        cost_estimate=pl.CostEstimate(flops=1000, bytes_accessed=1000, transcendentals=0),
-        name="tie",
-    )(value, *deps)
-
-
-def flip_bit(value, axis, bit):
-    return lax.ppermute(value, axis, [(i, i ^ bit) for i in range(lax.axis_size(axis))])
-
-
 def from_behind(value, axis, distance):
     devices = range(lax.axis_size(axis))
     route = [(i - distance, i) for i in devices if i - distance in devices]
@@ -146,34 +118,23 @@
 
 
 def body(section_in, out_grad, lengths, w_in, w_out, idx_in, idx_out):
-    sections, n_dp, n_mp = sizes = tuple(lax.axis_size(a) for a in ("section", "dp", "mp"))
-    per = w_in.shape[2] // sections
+    sections, n_dp, n_mp = (lax.axis_size(a) for a in ("section", "dp", "mp"))
     args = (lengths.reshape(2), idx_in, idx_out, section_in, out_grad, w_in, w_out)
-    keep, got, own, others = [], [], [], []
+    moved, own, others, done = [], [], [], []
     for relay in range(2):
-        kept, send, mine, theirs = tick(relay, sizes, keep, *args)
-        keep.append(kept)
-        got.append(flip_bit(send, "dp", 1))
+        *partials, mine, theirs = tick(relay, n_dp, n_mp, done, *args)
+        done = partials[:1]
+        for partial in partials:
+            summed = lax.psum_scatter(partial, "dp", scatter_dimension=0, tiled=True)
+            summed = summed.reshape(sections, -1, *summed.shape[2:])
+            moved.append(lax.all_to_all(summed, "section", split_axis=0, concat_axis=0, tiled=True))
         own.append(mine)
         others.append([lax.ppermute(theirs[k - 1], "mp", [(i, (i + k) % n_mp) for i in range(n_mp)]) for k in range(1, n_mp)])
-    small = per // 3 if per % 3 == 0 else per
-    cuts = [(0, small), (small, per)] if small < per else [(0, per)]
-    chunks = [(relay, cut) for cut in cuts for relay in range(2)]
-
-    def parts(slot, relay, cut):
-        return [v[relay][slot][:, :, cut[0]:cut[1]] for v in (keep, got)]
-
-    sums = [total(*parts(1, *chunk)).astype(jnp.bfloat16) for chunk in chunks]
-    came = [flip_bit(tie(v, *sums[:i]) if i > 1 else v, "dp", 2) for i, v in enumerate(sums)]
     passed = []
     for relay in range(2):
-        dx = total(tie(own[relay], *sums), *others[relay]).astype(jnp.bfloat16)
+        dx = total(own[relay], *others[relay]).astype(jnp.bfloat16)
         passed.append(from_behind(dx, "section", 1 if relay else -1))
-    moved = {}
-    for chunk, far in zip(chunks, came):
-        mine = total(*parts(0, *chunk), far).astype(jnp.bfloat16)
-        moved[chunk] = lax.all_to_all(mine, "section", split_axis=0, concat_axis=0, tiled=True)
-    grads = jnp.concatenate([total(moved[0, cut], jnp.flip(moved[1, cut], 0)) for cut in cuts], axis=2)
+    grads = jnp.stack([total(moved[i], jnp.flip(moved[i + 2], 0)) for i in range(2)], axis=1)
     return jnp.stack(passed, axis=0)[:, None], grads[:, :, None]
 
 

time: 196 us -> 224 us (1.14)
  waiting for transfers between devices: 94 us -> 134 us
  other arithmetic: 24.9 us -> 11.9 us
  between operations: 0.87 us -> 13.8 us
  local copies, waits for them, and re-layouts: 6.52 us -> 0.01 us
  starting transfers between devices: 32.5 us -> 26.6 us
    reduce_scatter x0 -> x4, waiting for transfers between devices: none -> 117 us  [body(): summed = lax.psum_scatter(partial, 'dp', scatter_dimension=0, tiled=True)]
    ppermute x6 -> x0, waiting for transfers between devices: 42 us -> none  [flip_bit(): lax.ppermute(value, axis, [(i, i ^ bit) for i in range(lax.axis_size(axis...]
    all_to_all x4, waiting for transfers between devices: 42.2 us -> 16.4 us  [body(): lax.all_to_all(summed, 'section', split_axis=0, concat_axis=0, tiled=True)]
    convert_element_type x9 -> x2, other arithmetic: 17.6 us -> 4.76 us  [body(): dx = total(own[relay], *others[relay]).astype(jnp.bfloat16)]
    ppermute x2, waiting for transfers between devices: 9.85 us -> 0.01 us  [from_behind(): return lax.ppermute(value, axis, route)]
    ppermute x6 -> x0, starting transfers between devices: 6.08 us -> none  [flip_bit(): lax.ppermute(value, axis, [(i, i ^ bit) for i in range(lax.axis_size(axis...]
    squeeze x4 -> x0, local copies, waits for them, and re-layouts: 4.76 us -> none  [parts(): return [v[relay][slot][:, :, cut[0]:cut[1]] for v in (keep, got)]]
    add x2 -> x0, other arithmetic: 2.73 us -> none  [total(): a + b]
  transfers between devices with their start and end apart: 14 -> 12, of which waited for: 8 -> 5; matrix products, arithmetic and copies ran while one was open for 13% -> 4% of each run, Pallas kernels for 0% -> 8%
where the time goes in v8:
time: 224 us; the launch traced here: 222 us
  waiting for transfers between devices  134 us (60%)
  Pallas kernels  35.6 us (16%)
  starting transfers between devices  26.6 us (12%)
  between operations  13.8 us (6%)
  other arithmetic  11.9 us (5%)
    reduce_scatter x4, waiting for transfers between devices, body(): summed = lax.psum_scatter(partial, 'dp', scatter_dimension=0, tiled=True)  117 us
    pallas_call x2, Pallas kernels, tick(): pl.pallas_call(functools.partial(tick_kernel, relay, per_step, len(deps))...  35.6 us
    all_to_all x4, starting transfers between devices, body(): lax.all_to_all(summed, 'section', split_axis=0, concat_axis=0, tiled=True)  18.4 us
    all_to_all x4, waiting for transfers between devices, body(): lax.all_to_all(summed, 'section', split_axis=0, concat_axis=0, tiled=True)  16.4 us
    ppermute x2, starting transfers between devices, from_behind(): return lax.ppermute(value, axis, route)  6.11 us
    convert_element_type x2, other arithmetic, body(): dx = total(own[relay], *others[relay]).astype(jnp.bfloat16)  4.76 us
  transfers between devices with their start and end apart: 12, of which 5 were waited for; matrix products, arithmetic and copies ran while one was open for 4% of the time, Pallas kernels for 8%

profile of v8, /device:TPU:0, one launch (start us, length us, event | category | flops | bytes accessed | tf_op | source)
XLA Modules:
  0.0 222.3 jit_solution(14487755861878959396)
XLA Ops:
  7.2 0.0 reduce-scatter.5.cloned.1.call-start
  7.2 17.7 %tick0.1 = (bf16[4,96,32,128]{3,2,1,0:T(8,128)(2,1)}, bf16[4,96,32,128]{3,2,1,0:T(8,128)(2,1)}, f32[32,12288]{1,0:T(8,128)}, bf16[1,32,12288]{2,1,0:T(8,128)(2,1)}) custom-call(s32[2]{0:T(128)} %bitcast.24, s32[1,2,96]{2,1,0:T(2,128)} %idx_in_ref.3, s32[1,2,96]{2,1,0:T(2,128)} %idx_out_ref.3, bf16[2,1,64,12288]{3,2,1,0:T(8,128)(2,1)} %x_ref.3, ...), custom_call_target="tpu_custom_call" | custom-call | flops 1006632960 | bytes 17301504 | tf_op jit(solution)/shard_map/tick0/pallas_call | solution.py:86
  24.9 0.0 reduce-scatter.5.cloned.1.call-update
  25.0 0.0 reduce-scatter.9.cloned.1.call-start
  25.0 0.7 reduce-scatter.9.cloned.1.call-update
  25.7 0.0 reduce-scatter.11.cloned.1.call-start
  25.8 17.9 %tick1.1 = (bf16[4,96,32,128]{3,2,1,0:T(8,128)(2,1)}, bf16[4,96,32,128]{3,2,1,0:T(8,128)(2,1)}, f32[32,12288]{1,0:T(8,128)}, bf16[1,32,12288]{2,1,0:T(8,128)(2,1)}) custom-call(s32[2]{0:T(128)} %bitcast.25, s32[1,2,96]{2,1,0:T(2,128)} %idx_in_ref.3, s32[1,2,96]{2,1,0:T(2,128)} %idx_out_ref.3, bf16[2,1,64,12288]{3,2,1,0:T(8,128)(2,1)} %x_ref.3, ...), custom_call_target="tpu_custom_call" | custom-call | flops 1006632960 | bytes 17301504 | tf_op jit(solution)/shard_map/tick1/pallas_call | solution.py:86
  43.6 0.0 reduce-scatter.11.cloned.1.call-update
  43.7 22.1 %reduce-scatter.5.cloned.1.call-done = bf16[1,96,32,128]{3,2,1,0:T(8,128)(2,1)} async-done(((bf16[4,96,32,128]{3,2,1,0:T(8,128)(2,1)}), bf16[1,96,32,128]{3,2,1,0:T(8,128)(2,1)}) %reduce-scatter.5.cloned.1.call-update) | async-done | bytes 786448 | tf_op jit(solution)/shard_map/reduce_scatter | solution.py:128
  65.8 4.6 %all-to-all-start = ((bf16[4,24,32,128]{3,2,1,0:T(8,128)(2,1)}), bf16[4,24,32,128]{3,2,1,0:T(8,128)(2,1)S(1)}, u32[]{:S(2)}, u32[]{:S(2)}) async-start(bf16[4,24,32,128]{3,2,1,0:T(8,128)(2,1)} %bitcast.22), calls=%async_computation.1 | async-start | bytes 1572864 | tf_op jit(solution)/shard_map/all_to_all | solution.py:130
  70.4 1.5 collective-permute-start
  71.9 0.6 collective-permute-start.2
  72.5 0.0 reduce-scatter.7.cloned.1.call-update
  72.5 0.0 copy-start.1
  72.5 34.0 %reduce-scatter.9.cloned.1.call-done = bf16[1,96,32,128]{3,2,1,0:T(8,128)(2,1)} async-done(((bf16[4,96,32,128]{3,2,1,0:T(8,128)(2,1)}), bf16[1,96,32,128]{3,2,1,0:T(8,128)(2,1)}) %reduce-scatter.9.cloned.1.call-update) | async-done | bytes 786448 | tf_op jit(solution)/shard_map/reduce_scatter | solution.py:128
  106.5 0.0 all-to-all-done
  106.5 4.6 %all-to-all-start.2 = ((bf16[4,24,32,128]{3,2,1,0:T(8,128)(2,1)}), bf16[4,24,32,128]{3,2,1,0:T(8,128)(2,1)S(1)}, u32[]{:S(2)}, u32[]{:S(2)}) async-start(bf16[4,24,32,128]{3,2,1,0:T(8,128)(2,1)} %bitcast.21), calls=%async_computation.5 | async-start | bytes 1572864 | tf_op jit(solution)/shard_map/all_to_all | solution.py:130
  111.1 0.0 collective-permute-done
  111.1 2.1 add_convert_fusion.1
  113.3 1.3 collective-permute-start.1
  114.5 32.5 %reduce-scatter.11.cloned.1.call-done = bf16[1,96,32,128]{3,2,1,0:T(8,128)(2,1)} async-done(((bf16[4,96,32,128]{3,2,1,0:T(8,128)(2,1)}), bf16[1,96,32,128]{3,2,1,0:T(8,128)(2,1)}) %reduce-scatter.11.cloned.1.call-update) | async-done | bytes 786448 | tf_op jit(solution)/shard_map/reduce_scatter | solution.py:128
  147.0 4.6 %all-to-all-start.3 = ((bf16[4,24,32,128]{3,2,1,0:T(8,128)(2,1)}), bf16[4,24,32,128]{3,2,1,0:T(8,128)(2,1)S(1)}, u32[]{:S(2)}, u32[]{:S(2)}) async-start(bf16[4,24,32,128]{3,2,1,0:T(8,128)(2,1)} %bitcast.19), calls=%async_computation.7 | async-start | bytes 1572864 | tf_op jit(solution)/shard_map/all_to_all | solution.py:130
  151.6 0.0 collective-permute-done.2
  151.6 2.6 %add_convert_fusion = bf16[32,12288]{1,0:T(8,128)(2,1)} fusion(f32[32,12288]{1,0:T(8,128)} %get-tuple-element.13, bf16[32,12288]{1,0:T(8,128)(2,1)} %collective-permute-done.2), kind=kLoop, calls=%fused_computation.4 | loop fusion | flops 1179648 | bytes 3145728 | tf_op jit(solution)/shard_map/convert_element_type | solution.py:135
  154.2 4.8 %collective-permute-start.3 = (bf16[32,12288]{1,0:T(8,128)(2,1)}, bf16[32,12288]{1,0:T(8,128)(2,1)}, u32[]{:S(2)}, u32[]{:S(2)}) collective-permute-start(bf16[32,12288]{1,0:T(8,128)(2,1)} %add_convert_fusion), channel_id=1, source_target_pairs={{0,8},{8,16},{16,24},{1,9},{9,17},{17,25},{2,10},{10,18},{18,26},{... | collective-permute-start | bytes 2359304 | tf_op jit(solution)/shard_map/ppermute | solution.py:117
  159.1 28.5 %reduce-scatter.7.cloned.1.call-done = bf16[1,96,32,128]{3,2,1,0:T(8,128)(2,1)} async-done(((bf16[4,96,32,128]{3,2,1,0:T(8,128)(2,1)}), bf16[1,96,32,128]{3,2,1,0:T(8,128)(2,1)}) %reduce-scatter.7.cloned.1.call-update) | async-done | bytes 786448 | tf_op jit(solution)/shard_map/reduce_scatter | solution.py:128
  187.6 4.6 %all-to-all-start.1 = ((bf16[4,24,32,128]{3,2,1,0:T(8,128)(2,1)}), bf16[4,24,32,128]{3,2,1,0:T(8,128)(2,1)}, u32[]{:S(2)}, u32[]{:S(2)}) async-start(bf16[4,24,32,128]{3,2,1,0:T(8,128)(2,1)} %bitcast.20), calls=%async_computation.3 | async-start | bytes 1572864 | tf_op jit(solution)/shard_map/all_to_all | solution.py:130
  192.2 2.4 %maximum_bitcast_fusion.1 = bf16[2,1,32,12288]{3,2,1,0:T(8,128)(2,1)} fusion(bf16[1,32,12288]{2,1,0:T(8,128)(2,1)} %bitcast.4, bf16[1,32,12288]{2,1,0:T(8,128)(2,1)S(1)} %bitcast.23), kind=kLoop, calls=%fused_computation.1 | loop fusion | flops 786432 | bytes 3145728
  194.6 1.3 add_bitcast_fusion
  196.0 16.4 %all-to-all-done.1 = bf16[4,24,32,128]{3,2,1,0:T(8,128)(2,1)} async-done(((bf16[4,24,32,128]{3,2,1,0:T(8,128)(2,1)}), bf16[4,24,32,128]{3,2,1,0:T(8,128)(2,1)}, u32[]{:S(2)}, u32[]{:S(2)}) %all-to-all-start.1) | async-done | bytes 786464 | tf_op jit(solution)/shard_map/all_to_all | solution.py:130
  212.4 1.3 add_bitcast_fusion.1
  213.7 2.0 maximum_bitcast_fusion
  (8 shorter events, 0.0 us)
Async XLA Ops:
  7.2 58.7 %reduce-scatter.5.cloned.1.call-start = ((), (), s32[]{:S(2)}) async-start(), calls=%async_computation.8 | async-start | bytes 3932160 | tf_op jit(solution)/shard_map/reduce_scatter | solution.py:128
  25.0 81.5 %reduce-scatter.9.cloned.1.call-start = ((), (), s32[]{:S(2)}) async-start(), calls=%async_computation.10 | async-start | bytes 3932160 | tf_op jit(solution)/shard_map/reduce_scatter | solution.py:128
  25.7 121.3 %reduce-scatter.11.cloned.1.call-start = ((), (), s32[]{:S(2)}) async-start(), calls=%async_computation.11 | async-start | bytes 3932160 | tf_op jit(solution)/shard_map/reduce_scatter | solution.py:128
  65.8 40.7 %all-to-all-start = ((bf16[4,24,32,128]{3,2,1,0:T(8,128)(2,1)}), bf16[4,24,32,128]{3,2,1,0:T(8,128)(2,1)S(1)}, u32[]{:S(2)}, u32[]{:S(2)}) async-start(bf16[4,24,32,128]{3,2,1,0:T(8,128)(2,1)} %bitcast.22), calls=%async_computation.1 | async-start | bytes 1572864 | tf_op jit(solution)/shard_map/all_to_all | solution.py:130
  70.4 117.1 %reduce-scatter.7.cloned.1.call-start = ((), (), s32[]{:S(2)}) async-start(), calls=%async_computation.9 | async-start | bytes 3932160 | tf_op jit(solution)/shard_map/reduce_scatter | solution.py:128
  70.4 40.7 %collective-permute-start = (bf16[32,12288]{1,0:T(8,128)(2,1)}, bf16[32,12288]{1,0:T(8,128)(2,1)}, u32[]{:S(2)}, u32[]{:S(2)}) collective-permute-start(bf16[32,12288]{1,0:T(8,128)(2,1)} %bitcast.1), channel_id=1, source_target_pairs={{0,1},{1,0},{2,3},{3,2},{4,5},{5,4},{6,7},{7,6},{8,9},{9,8},{10,11... | collective-permute-start | bytes 2359304 | tf_op jit(solution)/shard_map/ppermute | solution.py:132
  71.9 79.7 %collective-permute-start.2 = (bf16[32,12288]{1,0:T(8,128)(2,1)}, bf16[32,12288]{1,0:T(8,128)(2,1)}, u32[]{:S(2)}, u32[]{:S(2)}) collective-permute-start(bf16[32,12288]{1,0:T(8,128)(2,1)} %bitcast.3), channel_id=1, source_target_pairs={{0,1},{1,0},{2,3},{3,2},{4,5},{5,4},{6,7},{7,6},{8,9},{9,8},{10,11... | collective-permute-start | bytes 2359304 | tf_op jit(solution)/shard_map/ppermute | solution.py:132
  72.5 38.6 %copy-start.1 = (f32[32,12288]{1,0:T(8,128)S(1)}, f32[32,12288]{1,0:T(8,128)}, u32[]{:S(2)}) copy-start(f32[32,12288]{1,0:T(8,128)} %get-tuple-element.10) | copy-start | bytes 4718596
  106.5 40.5 %all-to-all-start.2 = ((bf16[4,24,32,128]{3,2,1,0:T(8,128)(2,1)}), bf16[4,24,32,128]{3,2,1,0:T(8,128)(2,1)S(1)}, u32[]{:S(2)}, u32[]{:S(2)}) async-start(bf16[4,24,32,128]{3,2,1,0:T(8,128)(2,1)} %bitcast.21), calls=%async_computation.5 | async-start | bytes 1572864 | tf_op jit(solution)/shard_map/all_to_all | solution.py:130
  113.3 78.9 %collective-permute-start.1 = (bf16[32,12288]{1,0:T(8,128)(2,1)}, bf16[32,12288]{1,0:T(8,128)(2,1)S(1)}, u32[]{:S(2)}, u32[]{:S(2)}) collective-permute-start(bf16[32,12288]{1,0:T(8,128)(2,1)} %add_convert_fusion.1), channel_id=1, source_target_pairs={{8,0},{16,8},{24,16},{9,1},{17,9},{25,17},{10,2},{18,10},{26,18},{... | collective-permute-start | bytes 2359304 | tf_op jit(solution)/shard_map/ppermute | solution.py:117
  147.0 40.5 %all-to-all-start.3 = ((bf16[4,24,32,128]{3,2,1,0:T(8,128)(2,1)}), bf16[4,24,32,128]{3,2,1,0:T(8,128)(2,1)S(1)}, u32[]{:S(2)}, u32[]{:S(2)}) async-start(bf16[4,24,32,128]{3,2,1,0:T(8,128)(2,1)} %bitcast.19), calls=%async_computation.7 | async-start | bytes 1572864 | tf_op jit(solution)/shard_map/all_to_all | solution.py:130
  154.2 37.9 %collective-permute-start.3 = (bf16[32,12288]{1,0:T(8,128)(2,1)}, bf16[32,12288]{1,0:T(8,128)(2,1)}, u32[]{:S(2)}, u32[]{:S(2)}) collective-permute-start(bf16[32,12288]{1,0:T(8,128)(2,1)} %add_convert_fusion), channel_id=1, source_target_pairs={{0,8},{8,16},{16,24},{1,9},{9,17},{17,25},{2,10},{10,18},{18,26},{... | collective-permute-start | bytes 2359304 | tf_op jit(solution)/shard_map/ppermute | solution.py:117
  187.6 4.6 %copy-start = (bf16[4,24,32,128]{3,2,1,0:T(8,128)(2,1)}, bf16[4,24,32,128]{3,2,1,0:T(8,128)(2,1)S(1)}, u32[]{:S(2)}) copy-start(bf16[4,24,32,128]{3,2,1,0:T(8,128)(2,1)S(1)} %all-to-all-done.3) | copy-start | bytes 2359300
  187.6 24.8 %all-to-all-start.1 = ((bf16[4,24,32,128]{3,2,1,0:T(8,128)(2,1)}), bf16[4,24,32,128]{3,2,1,0:T(8,128)(2,1)}, u32[]{:S(2)}, u32[]{:S(2)}) async-start(bf16[4,24,32,128]{3,2,1,0:T(8,128)(2,1)} %bitcast.20), calls=%async_computation.3 | async-start | bytes 1572864 | tf_op jit(solution)/shard_map/all_to_all | solution.py:130
Sparse Core Ops, SparseCore 0:
  25.1 40.6 reduce-scatter.4
  68.5 37.9 reduce-scatter.8
  109.0 37.9 reduce-scatter.10
  149.6 37.9 reduce-scatter.6

commit v9 on v7

--- a/solution.py
+++ b/solution.py
@@ -14,27 +14,27 @@
 
 
 def tick_kernel(relay, per_step, n_mp, n_deps, len_ref, idx_in_ref, idx_out_ref, x_ref, g_ref, w_in_ref, w_out_ref, *refs):
-    keep_in_ref, send_in_ref, keep_out_ref, send_out_ref, share_ref, acc_ref = refs[n_deps:]
+    *slot_refs, share_ref, acc_ref = refs[n_deps:]
     step = pl.program_id(0)
     me = lax.axis_index("dp")
     rows, block = x_ref.shape[0], w_in_ref.shape[-1]
-    piece = keep_in_ref.shape[2]
-    pieces = block // piece
+    piece = slot_refs[0].shape[2]
     live = lax.broadcasted_iota(jnp.int32, (rows, block), 0) < len_ref[relay]
 
     @pl.when(step == 0)
     def _():
         acc_ref[...] = jnp.zeros_like(acc_ref)
 
-    odd = me % 2 == 1
+    odd, high = me % 2 == 1, me // 2 == 1
 
-    def put(keep_ref, send_ref, i, value):
+    def put(kind, i, value):
         value = value.astype(jnp.bfloat16)
-        for k in range(pieces // 2):
-            low = value[2 * k * piece:(2 * k + 1) * piece]
-            high = value[(2 * k + 1) * piece:(2 * k + 2) * piece]
-            keep_ref[k ^ (me // 2), i] = jnp.where(odd, high, low)
-            send_ref[k ^ (me // 2), i] = jnp.where(odd, low, high)
+        p = [value[q * piece:(q + 1) * piece] for q in range(4)]
+        even = [jnp.where(odd, p[k + 1], p[k]) for k in (0, 2)]
+        other = [jnp.where(odd, p[k], p[k + 1]) for k in (0, 2)]
+        for slot, pair in ((0, even), (1, other)):
+            slot_refs[slot][kind, i] = jnp.where(high, pair[1], pair[0])
+            slot_refs[slot + 2][kind, i] = jnp.where(high, pair[0], pair[1])
 
     f32 = jnp.float32
     over_last = (((1,), (1,)), ((), ()))
@@ -61,8 +61,8 @@
         grad_out = [lax.dot_general(a, v, over_rows, preferred_element_type=f32) for a, v in zip(act, back)]
         for i, b, term, g_in, g_out in zip(group, sources, terms, grad_in, grad_out):
             acc_ref[b] += term
-            put(keep_in_ref, send_in_ref, i, g_in)
-            put(keep_out_ref, send_out_ref, i, g_out)
+            put(0, i, g_in)
+            put(1, i, g_out)
 
     @pl.when(step == pl.num_programs(0) - 1)
     def _():
@@ -75,21 +75,22 @@
             share_ref[:, columns] = (acc_ref[b] + held).astype(jnp.bfloat16)
 
 
-def tick(relay, n_dp, n_mp, deps, lengths, idx_in, idx_out, section_in, out_grad, w_in, w_out):
+def tick(relay, sections, n_dp, n_mp, deps, lengths, idx_in, idx_out, section_in, out_grad, w_in, w_out):
     rows, width = section_in.shape[2:]
     blocks, block = w_in.shape[2:4]
-    per_step = math.gcd(blocks, 8)
-    steps = blocks // per_step
+    per = blocks // sections
+    per_step = math.gcd(per, 8)
+    turns = per // per_step
     piece = block // n_dp
     whole = pl.BlockSpec((None, None, rows, width), lambda i, *_: (relay, 0, 0, 0))
     weight = pl.BlockSpec((None, None, per_step, block, block), lambda i, *_: (0, relay, i, 0, 0))
-    slots = jax.ShapeDtypeStruct((n_dp // 2, blocks, piece, block), jnp.bfloat16)
-    slots_spec = pl.BlockSpec((n_dp // 2, per_step, piece, block), lambda i, *_: (0, i, 0, 0))
+    slots = jax.ShapeDtypeStruct((sections, 2, per, piece, block), jnp.bfloat16)
+    slots_spec = pl.BlockSpec((None, 2, per_step, piece, block), lambda i, *_: (i // turns, 0, i % turns, 0, 0))
     return pl.pallas_call(
         functools.partial(tick_kernel, relay, per_step, n_mp, len(deps)),
         grid_spec=pltpu.PrefetchScalarGridSpec(
             num_scalar_prefetch=3,
-            grid=(steps,),
+            grid=(sections * turns,),
             in_specs=[whole, whole, weight, weight] + [pl.BlockSpec(memory_space=pl.ANY)] * len(deps),
             out_specs=[slots_spec] * 4 + [pl.BlockSpec((rows, width), lambda i, *_: (0, 0))],
             scratch_shapes=[pltpu.VMEM((width // block, rows, block), jnp.float32)],
@@ -134,25 +135,46 @@
     return lax.ppermute(value, axis, route)
 
 
+def rotate(parts, axis):
+    n = lax.axis_size(axis)
+    me = lax.axis_index(axis)
+    got = []
+    for k in range(n):
+        part = lax.dynamic_index_in_dim(parts, lax.rem(me + k, n), 0, keepdims=False)
+        got.append(part if k == 0 else lax.ppermute(part, axis, [(i, (i + k) % n) for i in range(n)]))
+    return got
+
+
+def by_source(parts, axis):
+    n = len(parts)
+    me = lax.axis_index(axis)
+    stacked = jnp.stack(parts)
+    return jnp.stack([lax.dynamic_index_in_dim(stacked, lax.rem(me - k + n, n), 0, keepdims=False) for k in range(n)])
+
+
 def body(section_in, out_grad, lengths, w_in, w_out, idx_in, idx_out):
     sections, n_dp, n_mp = (lax.axis_size(a) for a in ("section", "dp", "mp"))
     args = (lengths.reshape(2), idx_in, idx_out, section_in, out_grad, w_in, w_out)
-    keep, got, dx = [], [], []
-    for relay in range(2):
-        keep_in, send_in, keep_out, send_out, share = tick(relay, n_dp, n_mp, keep[:1], *args)
-        keep += [keep_in, keep_out]
-        got += [flip_bit(send_in, "dp", 1), flip_bit(send_out, "dp", 1)]
-        dx.append(lax.psum_scatter(share, "mp", scatter_dimension=0, tiled=True))
-    sums = [total(k[1], g[1]).astype(jnp.bfloat16) for k, g in zip(keep, got)]
-    came = [flip_bit(tie(v, *sums[:i]) if i else v, "dp", 2) for i, v in enumerate(sums)]
-    passed = [from_behind(v, "section", distance) for v, distance in zip(dx, (-1, 1))]
-    moved = []
-    for i, (k, g, far) in enumerate(zip(keep, got, came)):
-        mine = total(k[0], g[0], tie(far, *(sums if i == 0 else [mine]))).astype(jnp.bfloat16)
-        mine = mine.reshape(sections, -1, *mine.shape[1:])
-        moved.append(lax.all_to_all(mine, "section", split_axis=0, concat_axis=0, tiled=True))
-    grads = jnp.stack([total(moved[i], jnp.flip(moved[i + 2], 0)) for i in range(2)], axis=1)
-    return jnp.stack(passed, axis=0)[:, None], grads[:, :, None]
+
+    def scatter(share):
+        return lax.psum_scatter(share, "mp", scatter_dimension=0, tiled=True)
+
+    a0, s0, a2, s2, share0 = tick(0, sections, n_dp, n_mp, [], *args)
+    got0, got2 = flip_bit(s0, "dp", 1), flip_bit(s2, "dp", 1)
+    sum0 = total(a2, got2).astype(jnp.bfloat16)
+    came0 = flip_bit(sum0, "dp", 2)
+    b0, t0, b2, t2, share1 = tick(1, sections, n_dp, n_mp, [sum0], *args)
+    hot0, hot2 = flip_bit(t0, "dp", 1), flip_bit(t2, "dp", 1)
+    dx0 = scatter(share0)
+    sum1 = total(tie(b2, came0), hot2).astype(jnp.bfloat16)
+    came1 = flip_bit(sum1, "dp", 2)
+    dx1 = scatter(tie(share1, came0))
+    moved0 = rotate(total(a0, got0, came0).astype(jnp.bfloat16), "section")
+    passed0 = from_behind(dx0, "section", -1)
+    passed1 = from_behind(dx1, "section", 1)
+    moved1 = rotate(total(b0, hot0, came1).astype(jnp.bfloat16), "section")
+    grads = total(by_source(moved0, "section"), jnp.flip(by_source(moved1, "section"), 0))
+    return jnp.stack([passed0, passed1], axis=0)[:, None], grads[:, :, None]
 
 
 def solution(mesh):

time: 188 us -> 174 us (0.926)
  the two profiles are of different devices: /device:TPU:0 before, /device:TPU:16 now
where the time goes in v9:
time: 174 us; the launch traced here: 173 us
  waiting for transfers between devices  87 us (50%)
  Pallas kernels  34.9 us (20%)
  starting transfers between devices  17.6 us (10%)
  other arithmetic  15 us (9%)
  between operations  14.2 us (8%)
  local copies, waits for them, and re-layouts  4.09 us (2%)
    ppermute x6, waiting for transfers between devices, flip_bit(): lax.ppermute(value, axis, [(i, i ^ bit) for i in range(lax.axis_size(axis...  49.5 us
    pallas_call x2, Pallas kernels, tick(): pl.pallas_call(functools.partial(tick_kernel, relay, per_step, n_mp, len(...  34.9 us
    ppermute x6, waiting for transfers between devices, rotate(): lax.ppermute(part, axis, [(i, (i + k) % n) for i in range(n)])  25.7 us
    ppermute x2, waiting for transfers between devices, from_behind(): return lax.ppermute(value, axis, route)  11.7 us
    ppermute x6, starting transfers between devices, rotate(): lax.ppermute(part, axis, [(i, (i + k) % n) for i in range(n)])  7.92 us
    ppermute x2, starting transfers between devices, from_behind(): return lax.ppermute(value, axis, route)  5.89 us
    ppermute x6, starting transfers between devices, flip_bit(): lax.ppermute(value, axis, [(i, i ^ bit) for i in range(lax.axis_size(axis...  3.76 us
    convert_element_type x1, other arithmetic, body(): sum1 = total(tie(b2, came0), hot2).astype(jnp.bfloat16)  3.66 us
  transfers between devices with their start and end apart: 16, of which 8 were waited for; matrix products, arithmetic and copies ran while one was open for 9% of the time, Pallas kernels for 10%

profile of v9, /device:TPU:16, one launch (start us, length us, event | category | flops | bytes accessed | tf_op | source)
XLA Modules:
  0.0 172.9 jit_solution(5009399977386551796)
XLA Ops:
  7.2 17.2 %tick0.1 = (bf16[4,2,24,32,128]{4,3,2,1,0:T(8,128)(2,1)}, bf16[4,2,24,32,128]{4,3,2,1,0:T(8,128)(2,1)}, bf16[4,2,24,32,128]{4,3,2,1,0:T(8,128)(2,1)}, bf16[4,2,2...) custom-call(s32[2]{0:T(128)} %bitcast.34, s32[1,2,96]{2,1,0:T(2,128)} %idx_in_ref.3, s32[1,2,96]{2,1,0:T(2,128)} %idx_out_ref.3, ...), custom_call_target="tpu_custom_call" | custom-call | flops 1006632960 | bytes 17301504 | tf_op jit(solution)/shard_map/tick0/pallas_call | solution.py:89
  24.6 3.5 %collective-permute-done.1 = bf16[4,2,24,32,128]{4,3,2,1,0:T(8,128)(2,1)S(1)} collective-permute-done((bf16[4,2,24,32,128]{4,3,2,1,0:T(8,128)(2,1)}, bf16[4,2,24,32,128]{4,3,2,1,0:T(8,128)(2,1)S(1)}, u32[]{:S(2)}, u32[]{:S(2)}) %collective-permute-start.1) | collective-permute-done | bytes 1572896 | tf_op jit(solution)/shard_map/ppermute | solution.py:129
  28.1 0.4 add_convert_fusion.3.refs_0_
  28.6 1.6 collective-permute-start.2
  30.1 17.7 %tick1.1 = (bf16[4,2,24,32,128]{4,3,2,1,0:T(8,128)(2,1)}, bf16[4,2,24,32,128]{4,3,2,1,0:T(8,128)(2,1)}, bf16[4,2,24,32,128]{4,3,2,1,0:T(8,128)(2,1)}, bf16[4,2,2...) custom-call(s32[2]{0:T(128)} %bitcast.35, s32[1,2,96]{2,1,0:T(2,128)} %idx_in_ref.3, s32[1,2,96]{2,1,0:T(2,128)} %idx_out_ref.3, ...), custom_call_target="tpu_custom_call" | custom-call | flops 1006632960 | bytes 17301504 | tf_op jit(solution)/shard_map/tick1/pallas_call | solution.py:89
  47.9 17.1 %collective-permute-done.2.refs_1_ = bf16[4,2,24,32,128]{4,3,2,1,0:T(8,128)(2,1)S(1)} collective-permute-done((bf16[4,2,24,32,128]{4,3,2,1,0:T(8,128)(2,1)S(1)}, bf16[4,2,24,32,128]{4,3,2,1,0:T(8,128)(2,1)S(1)}, u32[]{:S(2)}, u32[]{:S(2)}) %collective-permute-start.2) | collective-permute-done | bytes 1572896 | tf_op jit(solution)/shard_map/ppermute | solution.py:129
  65.1 1.2 copy-done
  66.4 0.5 collective-permute-start.8
  66.9 3.7 %add_convert_fusion.1 = bf16[4,2,24,32,128]{4,3,2,1,0:T(8,128)(2,1)} fusion(bf16[4,2,24,32,128]{4,3,2,1,0:T(8,128)(2,1)} %collective-permute-done.9, bf16[4,2,24,32,128]{4,3,2,1,0:T(8,128)(2,1)} %tie.3), kind=kLoop, calls=%fused_computation.2 | loop fusion | flops 3145728 | bytes 4718592 | tf_op jit(solution)/shard_map/convert_element_type | solution.py:169
  70.6 1.5 collective-permute-start.10
  72.1 2.0 %add_convert_fusion.2 = bf16[4,2,24,32,128]{4,3,2,1,0:T(8,128)(2,1)S(1)} fusion(bf16[4,2,24,32,128]{4,3,2,1,0:T(8,128)(2,1)S(1)} %copy-done.1, bf16[4,2,24,32,128]{4,3,2,1,0:T(8,128)(2,1)} %collective-permute-done.4, bf16[4,2,24,32,128]{4,3,2,1,0:T(8,128)(2,1)S(1)} %copy-done.3), kind=kLoop, calls=%fused_computation.3 | loop fusion | flops 4718592 | bytes 6291456 | tf_op jit(solution)/shard_map/convert_element_type | solution.py:172
  74.4 0.5 collective-permute-start.7
  74.9 3.5 %collective-permute-start.6 = (bf16[2,24,32,128]{3,2,1,0:T(8,128)(2,1)S(1)}, bf16[2,24,32,128]{3,2,1,0:T(8,128)(2,1)S(1)}, u32[]{:S(2)}, u32[]{:S(2)}) collective-permute-start(bf16[2,24,32,128]{3,2,1,0:T(8,128)(2,1)S(1)} %get-tuple-element.38), channel_id=1, source_target_pairs={{0,16},{8,24},{16,0},{24,8},{1,17},{9,25},{17,1},{25,9},{2,18},{10... | collective-permute-start | bytes 1179656 | tf_op jit(solution)/shard_map/ppermute | solution.py:144
  78.4 28.9 %collective-permute-done.10 = bf16[4,2,24,32,128]{4,3,2,1,0:T(8,128)(2,1)} collective-permute-done((bf16[4,2,24,32,128]{4,3,2,1,0:T(8,128)(2,1)}, bf16[4,2,24,32,128]{4,3,2,1,0:T(8,128)(2,1)}, u32[]{:S(2)}, u32[]{:S(2)}) %collective-permute-start.10) | collective-permute-done | bytes 1572896 | tf_op jit(solution)/shard_map/ppermute | solution.py:129
  107.3 2.5 %add_convert_fusion = bf16[4,2,24,32,128]{4,3,2,1,0:T(8,128)(2,1)S(1)} fusion(bf16[4,2,24,32,128]{4,3,2,1,0:T(8,128)(2,1)} %collective-permute-done.10, bf16[4,2,24,32,128]{4,3,2,1,0:T(8,128)(2,1)} %collective-permute-done.8, bf16[4,2,24,32,128]{4,3,2,1,0:T(8,128)(2,1)S(1)} %copy-done.4), kind=kLoop, calls=%fused_computation.1 | loop fusion | flops 4718592 | bytes 6291456 | tf_op jit(solution)/shard_map/convert_element_type | solution.py:175
  109.8 1.1 constant_dynamic-slice_fusion.4
  110.9 0.4 collective-permute-start.13
  111.4 3.5 %collective-permute-start.12 = (bf16[2,24,32,128]{3,2,1,0:T(8,128)(2,1)}, bf16[2,24,32,128]{3,2,1,0:T(8,128)(2,1)}, u32[]{:S(2)}, u32[]{:S(2)}) collective-permute-start(bf16[2,24,32,128]{3,2,1,0:T(8,128)(2,1)} %get-tuple-element.30), channel_id=1, source_target_pairs={{0,16},{8,24},{16,0},{24,8},{1,17},{9,25},{17,1},{25,9},{2,18},{10... | collective-permute-start | bytes 1179656 | tf_op jit(solution)/shard_map/ppermute | solution.py:144
  114.9 3.9 %collective-permute-start = (bf16[32,12288]{1,0:T(8,128)(2,1)}, bf16[32,12288]{1,0:T(8,128)(2,1)S(1)}, u32[]{:S(2)}, u32[]{:S(2)}) collective-permute-start(bf16[32,12288]{1,0:T(8,128)(2,1)} %reduce-scatter.3.cloned.1.call-done), channel_id=1, source_target_pairs={{8,0},{16,8},{24,16},{9,1},{17,9},{25,17},{10,2},{18,10},{26,18},{... | collective-permute-start | bytes 2359304 | tf_op jit(solution)/shard_map/ppermute | solution.py:135
  118.8 0.7 copy-done.7
  119.6 1.3 pad_maximum_fusion
  120.9 2.0 %collective-permute-start.3 = (bf16[32,12288]{1,0:T(8,128)(2,1)}, bf16[32,12288]{1,0:T(8,128)(2,1)S(1)}, u32[]{:S(2)}, u32[]{:S(2)}) collective-permute-start(bf16[32,12288]{1,0:T(8,128)(2,1)} %reduce-scatter.5.cloned.1.call-done), channel_id=1, source_target_pairs={{0,8},{8,16},{16,24},{1,9},{9,17},{17,25},{2,10},{10,18},{18,26},{... | collective-permute-start | bytes 2359304 | tf_op jit(solution)/shard_map/ppermute | solution.py:135
  122.9 0.4 constant_dynamic-slice_fusion.8
  123.3 13.3 %collective-permute-done.13 = bf16[2,24,32,128]{3,2,1,0:T(8,128)(2,1)} collective-permute-done((bf16[2,24,32,128]{3,2,1,0:T(8,128)(2,1)}, bf16[2,24,32,128]{3,2,1,0:T(8,128)(2,1)}, u32[]{:S(2)}, u32[]{:S(2)}) %collective-permute-start.13) | collective-permute-done | bytes 393248 | tf_op jit(solution)/shard_map/ppermute | solution.py:144
  136.6 10.0 %collective-permute-done.12 = bf16[2,24,32,128]{3,2,1,0:T(8,128)(2,1)} collective-permute-done((bf16[2,24,32,128]{3,2,1,0:T(8,128)(2,1)}, bf16[2,24,32,128]{3,2,1,0:T(8,128)(2,1)}, u32[]{:S(2)}, u32[]{:S(2)}) %collective-permute-start.12) | collective-permute-done | bytes 393248 | tf_op jit(solution)/shard_map/ppermute | solution.py:144
  146.6 2.3 %collective-permute-done.11 = bf16[2,24,32,128]{3,2,1,0:T(8,128)(2,1)} collective-permute-done((bf16[2,24,32,128]{3,2,1,0:T(8,128)(2,1)}, bf16[2,24,32,128]{3,2,1,0:T(8,128)(2,1)}, u32[]{:S(2)}, u32[]{:S(2)}) %collective-permute-start.11) | collective-permute-done | bytes 393248 | tf_op jit(solution)/shard_map/ppermute | solution.py:144
  148.9 1.4 pad_maximum_fusion.1
  150.4 0.3 constant_dynamic-slice_fusion.3
  150.9 2.2 %add_bitcast_fusion = f32[4,2,1,24,32,128]{5,4,3,2,1,0:T(8,128)} fusion(bf16[1,2,24,32,128]{4,3,2,1,0:T(8,128)(2,1)S(1)} %get-tuple-element.33, bf16[1,2,24,32,128]{4,3,2,1,0:T(8,128)(2,1)S(1)} %get-tuple-element.34, bf16[1,2,24,32,128]{4,3,2,1,0:T(8,128)(2,1)S(1)} %get-tuple-element.35, bf16[1,2,24,32,128]{4,3,2,1,0:T(8,128)(2,1)S(1)} %get-tuple-element.32, ...), kind=kLoop, calls=%fused_computation | loop fusion | flops 7864320 | bytes 6291456
  153.1 8.6 %collective-permute-done = bf16[32,12288]{1,0:T(8,128)(2,1)S(1)} collective-permute-done((bf16[32,12288]{1,0:T(8,128)(2,1)}, bf16[32,12288]{1,0:T(8,128)(2,1)S(1)}, u32[]{:S(2)}, u32[]{:S(2)}) %collective-permute-start) | collective-permute-done | bytes 786464 | tf_op jit(solution)/shard_map/ppermute | solution.py:135
  161.6 3.2 %collective-permute-done.3 = bf16[32,12288]{1,0:T(8,128)(2,1)S(1)} collective-permute-done((bf16[32,12288]{1,0:T(8,128)(2,1)}, bf16[32,12288]{1,0:T(8,128)(2,1)S(1)}, u32[]{:S(2)}, u32[]{:S(2)}) %collective-permute-start.3) | collective-permute-done | bytes 786464 | tf_op jit(solution)/shard_map/ppermute | solution.py:135
  164.8 1.3 maximum_bitcast_fusion
  (35 shorter events, 0.9 us)
Async XLA Ops:
  7.2 107.7 %reduce-scatter.3.cloned.1.call-start = ((), (), s32[]{:S(2)}) async-start(), calls=%async_computation.2 | async-start | bytes 2359296 | tf_op jit(solution)/shard_map/reduce_scatter | solution.py:160
  24.4 3.7 %copy-start.5 = (bf16[4,2,24,32,128]{4,3,2,1,0:T(8,128)(2,1)S(1)}, bf16[4,2,24,32,128]{4,3,2,1,0:T(8,128)(2,1)}, u32[]{:S(2)}) copy-start(bf16[4,2,24,32,128]{4,3,2,1,0:T(8,128)(2,1)} %get-tuple-element.13) | copy-start | bytes 4718596
  24.4 3.7 %collective-permute-start.1 = (bf16[4,2,24,32,128]{4,3,2,1,0:T(8,128)(2,1)}, bf16[4,2,24,32,128]{4,3,2,1,0:T(8,128)(2,1)S(1)}, u32[]{:S(2)}, u32[]{:S(2)}) collective-permute-start(bf16[4,2,24,32,128]{4,3,2,1,0:T(8,128)(2,1)} %get-tuple-element.14), channel_id=1, source_target_pairs={{0,2},{2,0},{4,6},{6,4},{1,3},{3,1},{5,7},{7,5},{8,10},{10,8},{12,... | collective-permute-start | bytes 4718600 | tf_op jit(solution)/shard_map/ppermute | solution.py:129
  24.5 96.4 %reduce-scatter.5.cloned.1.call-start = ((), (), s32[]{:S(2)}) async-start(), calls=%async_computation.3 | async-start | bytes 2359296 | tf_op jit(solution)/shard_map/reduce_scatter | solution.py:160
  28.5 1.6 copy-start.2
  28.6 36.5 %collective-permute-start.2 = (bf16[4,2,24,32,128]{4,3,2,1,0:T(8,128)(2,1)S(1)}, bf16[4,2,24,32,128]{4,3,2,1,0:T(8,128)(2,1)S(1)}, u32[]{:S(2)}, u32[]{:S(2)}) collective-permute-start(bf16[4,2,24,32,128]{4,3,2,1,0:T(8,128)(2,1)S(1)} %add_convert_fusion.3.refs_0_), channel_id=1, source_target_pairs={{0,4},{2,6},{4,0},{6,2},{1,5},{3,7},{5,1},{7,3},{8,12},{10,14},{12... | collective-permute-start | bytes 4718600 | tf_op jit(solution)/shard_map/ppermute | solution.py:129
  47.8 19.1 %collective-permute-start.9 = (bf16[4,2,24,32,128]{4,3,2,1,0:T(8,128)(2,1)}, bf16[4,2,24,32,128]{4,3,2,1,0:T(8,128)(2,1)}, u32[]{:S(2)}, u32[]{:S(2)}) collective-permute-start(bf16[4,2,24,32,128]{4,3,2,1,0:T(8,128)(2,1)} %get-tuple-element.21), channel_id=1, source_target_pairs={{0,2},{2,0},{4,6},{6,4},{1,3},{3,1},{5,7},{7,5},{8,10},{10,8},{12,... | collective-permute-start | bytes 4718600 | tf_op jit(solution)/shard_map/ppermute | solution.py:129
  65.1 1.3 copy-start
  66.3 5.7 %collective-permute-start.4 = (bf16[4,2,24,32,128]{4,3,2,1,0:T(8,128)(2,1)}, bf16[4,2,24,32,128]{4,3,2,1,0:T(8,128)(2,1)}, u32[]{:S(2)}, u32[]{:S(2)}) collective-permute-start(bf16[4,2,24,32,128]{4,3,2,1,0:T(8,128)(2,1)} %get-tuple-element.17), channel_id=1, source_target_pairs={{0,2},{2,0},{4,6},{6,4},{1,3},{3,1},{5,7},{7,5},{8,10},{10,8},{12,... | collective-permute-start | bytes 4718600 | tf_op jit(solution)/shard_map/ppermute | solution.py:129
  66.4 12.0 %collective-permute-start.8 = (bf16[4,2,24,32,128]{4,3,2,1,0:T(8,128)(2,1)}, bf16[4,2,24,32,128]{4,3,2,1,0:T(8,128)(2,1)}, u32[]{:S(2)}, u32[]{:S(2)}) collective-permute-start(bf16[4,2,24,32,128]{4,3,2,1,0:T(8,128)(2,1)} %get-tuple-element.19), channel_id=1, source_target_pairs={{0,2},{2,0},{4,6},{6,4},{1,3},{3,1},{5,7},{7,5},{8,10},{10,8},{12,... | collective-permute-start | bytes 4718600 | tf_op jit(solution)/shard_map/ppermute | solution.py:129
  66.9 5.2 %copy-start.1 = (bf16[4,2,24,32,128]{4,3,2,1,0:T(8,128)(2,1)S(1)}, bf16[4,2,24,32,128]{4,3,2,1,0:T(8,128)(2,1)}, u32[]{:S(2)}) copy-start(bf16[4,2,24,32,128]{4,3,2,1,0:T(8,128)(2,1)} %copy-done) | copy-start | bytes 4718596
  66.9 5.2 %copy-start.3 = (bf16[4,2,24,32,128]{4,3,2,1,0:T(8,128)(2,1)S(1)}, bf16[4,2,24,32,128]{4,3,2,1,0:T(8,128)(2,1)}, u32[]{:S(2)}) copy-start(bf16[4,2,24,32,128]{4,3,2,1,0:T(8,128)(2,1)} %get-tuple-element.16) | copy-start | bytes 4718596
  70.6 36.7 %collective-permute-start.10 = (bf16[4,2,24,32,128]{4,3,2,1,0:T(8,128)(2,1)}, bf16[4,2,24,32,128]{4,3,2,1,0:T(8,128)(2,1)}, u32[]{:S(2)}, u32[]{:S(2)}) collective-permute-start(bf16[4,2,24,32,128]{4,3,2,1,0:T(8,128)(2,1)} %add_convert_fusion.1), channel_id=1, source_target_pairs={{0,4},{2,6},{4,0},{6,2},{1,5},{3,7},{5,1},{7,3},{8,12},{10,14},{12... | collective-permute-start | bytes 4718600 | tf_op jit(solution)/shard_map/ppermute | solution.py:129
  74.1 33.2 %copy-start.4 = (bf16[4,2,24,32,128]{4,3,2,1,0:T(8,128)(2,1)S(1)}, bf16[4,2,24,32,128]{4,3,2,1,0:T(8,128)(2,1)}, u32[]{:S(2)}) copy-start(bf16[4,2,24,32,128]{4,3,2,1,0:T(8,128)(2,1)} %get-tuple-element.18) | copy-start | bytes 4718596
  74.4 40.4 %collective-permute-start.7 = (bf16[2,24,32,128]{3,2,1,0:T(8,128)(2,1)S(1)}, bf16[2,24,32,128]{3,2,1,0:T(8,128)(2,1)S(1)}, u32[]{:S(2)}, u32[]{:S(2)}) collective-permute-start(bf16[2,24,32,128]{3,2,1,0:T(8,128)(2,1)S(1)} %get-tuple-element.37), channel_id=1, source_target_pairs={{0,24},{8,0},{16,8},{24,16},{1,25},{9,1},{17,9},{25,17},{2,26},{10... | collective-permute-start | bytes 1179656 | tf_op jit(solution)/shard_map/ppermute | solution.py:144
  74.9 39.9 %collective-permute-start.6 = (bf16[2,24,32,128]{3,2,1,0:T(8,128)(2,1)S(1)}, bf16[2,24,32,128]{3,2,1,0:T(8,128)(2,1)S(1)}, u32[]{:S(2)}, u32[]{:S(2)}) collective-permute-start(bf16[2,24,32,128]{3,2,1,0:T(8,128)(2,1)S(1)} %get-tuple-element.38), channel_id=1, source_target_pairs={{0,16},{8,24},{16,0},{24,8},{1,17},{9,25},{17,1},{25,9},{2,18},{10... | collective-permute-start | bytes 1179656 | tf_op jit(solution)/shard_map/ppermute | solution.py:144
  78.4 40.4 %collective-permute-start.5 = (bf16[2,24,32,128]{3,2,1,0:T(8,128)(2,1)S(1)}, bf16[2,24,32,128]{3,2,1,0:T(8,128)(2,1)S(1)}, u32[]{:S(2)}, u32[]{:S(2)}) collective-permute-start(bf16[2,24,32,128]{3,2,1,0:T(8,128)(2,1)S(1)} %get-tuple-element.39), channel_id=1, source_target_pairs={{0,8},{8,16},{16,24},{24,0},{1,9},{9,17},{17,25},{25,1},{2,10},{10... | collective-permute-start | bytes 1179656 | tf_op jit(solution)/shard_map/ppermute | solution.py:144
  110.9 25.7 %collective-permute-start.13 = (bf16[2,24,32,128]{3,2,1,0:T(8,128)(2,1)}, bf16[2,24,32,128]{3,2,1,0:T(8,128)(2,1)}, u32[]{:S(2)}, u32[]{:S(2)}) collective-permute-start(bf16[2,24,32,128]{3,2,1,0:T(8,128)(2,1)} %get-tuple-element.29), channel_id=1, source_target_pairs={{0,24},{8,0},{16,8},{24,16},{1,25},{9,1},{17,9},{25,17},{2,26},{10... | collective-permute-start | bytes 1179656 | tf_op jit(solution)/shard_map/ppermute | solution.py:144
  111.4 35.2 %collective-permute-start.12 = (bf16[2,24,32,128]{3,2,1,0:T(8,128)(2,1)}, bf16[2,24,32,128]{3,2,1,0:T(8,128)(2,1)}, u32[]{:S(2)}, u32[]{:S(2)}) collective-permute-start(bf16[2,24,32,128]{3,2,1,0:T(8,128)(2,1)} %get-tuple-element.30), channel_id=1, source_target_pairs={{0,16},{8,24},{16,0},{24,8},{1,17},{9,25},{17,1},{25,9},{2,18},{10... | collective-permute-start | bytes 1179656 | tf_op jit(solution)/shard_map/ppermute | solution.py:144
  114.9 34.1 %collective-permute-start.11 = (bf16[2,24,32,128]{3,2,1,0:T(8,128)(2,1)}, bf16[2,24,32,128]{3,2,1,0:T(8,128)(2,1)}, u32[]{:S(2)}, u32[]{:S(2)}) collective-permute-start(bf16[2,24,32,128]{3,2,1,0:T(8,128)(2,1)} %get-tuple-element.31), channel_id=1, source_target_pairs={{0,8},{8,16},{16,24},{24,0},{1,9},{9,17},{17,25},{25,1},{2,10},{10... | collective-permute-start | bytes 1179656 | tf_op jit(solution)/shard_map/ppermute | solution.py:144
  114.9 3.9 %copy-start.6 = (bf16[2,24,32,128]{3,2,1,0:T(8,128)(2,1)}, bf16[2,24,32,128]{3,2,1,0:T(8,128)(2,1)S(1)}, u32[]{:S(2)}) copy-start(bf16[2,24,32,128]{3,2,1,0:T(8,128)(2,1)S(1)} %collective-permute-done.6) | copy-start | bytes 1179652
  114.9 46.8 %collective-permute-start = (bf16[32,12288]{1,0:T(8,128)(2,1)}, bf16[32,12288]{1,0:T(8,128)(2,1)S(1)}, u32[]{:S(2)}, u32[]{:S(2)}) collective-permute-start(bf16[32,12288]{1,0:T(8,128)(2,1)} %reduce-scatter.3.cloned.1.call-done), channel_id=1, source_target_pairs={{8,0},{16,8},{24,16},{9,1},{17,9},{25,17},{10,2},{18,10},{26,18},{... | collective-permute-start | bytes 2359304 | tf_op jit(solution)/shard_map/ppermute | solution.py:135
  118.8 0.7 copy-start.7
  120.9 43.9 %collective-permute-start.3 = (bf16[32,12288]{1,0:T(8,128)(2,1)}, bf16[32,12288]{1,0:T(8,128)(2,1)S(1)}, u32[]{:S(2)}, u32[]{:S(2)}) collective-permute-start(bf16[32,12288]{1,0:T(8,128)(2,1)} %reduce-scatter.5.cloned.1.call-done), channel_id=1, source_target_pairs={{0,8},{8,16},{16,24},{1,9},{9,17},{17,25},{2,10},{10,18},{18,26},{... | collective-permute-start | bytes 2359304 | tf_op jit(solution)/shard_map/ppermute | solution.py:135
Sparse Core Ops, SparseCore 0:
  24.6 27.2 reduce-scatter.2
  66.5 27.1 reduce-scatter.4

commit v10 on v9

--- a/solution.py
+++ b/solution.py
@@ -13,12 +13,12 @@
 GROUP = 4
 
 
-def tick_kernel(relay, per_step, n_mp, n_deps, len_ref, idx_in_ref, idx_out_ref, x_ref, g_ref, w_in_ref, w_out_ref, *refs):
+def tick_kernel(relay, per_step, n_mp, apart, n_deps, len_ref, idx_in_ref, idx_out_ref, x_ref, g_ref, w_in_ref, w_out_ref, *refs):
     *slot_refs, share_ref, acc_ref = refs[n_deps:]
     step = pl.program_id(0)
     me = lax.axis_index("dp")
     rows, block = x_ref.shape[0], w_in_ref.shape[-1]
-    piece = slot_refs[0].shape[2]
+    piece = slot_refs[0].shape[-2]
     live = lax.broadcasted_iota(jnp.int32, (rows, block), 0) < len_ref[relay]
 
     @pl.when(step == 0)
@@ -33,8 +33,11 @@
         even = [jnp.where(odd, p[k + 1], p[k]) for k in (0, 2)]
         other = [jnp.where(odd, p[k], p[k + 1]) for k in (0, 2)]
         for slot, pair in ((0, even), (1, other)):
-            slot_refs[slot][kind, i] = jnp.where(high, pair[1], pair[0])
-            slot_refs[slot + 2][kind, i] = jnp.where(high, pair[0], pair[1])
+            for at, v in ((slot, jnp.where(high, pair[1], pair[0])), (slot + 2, jnp.where(high, pair[0], pair[1]))):
+                if apart:
+                    slot_refs[2 * at + kind][i] = v
+                else:
+                    slot_refs[at][kind, i] = v
 
     f32 = jnp.float32
     over_last = (((1,), (1,)), ((), ()))
@@ -75,7 +78,7 @@
             share_ref[:, columns] = (acc_ref[b] + held).astype(jnp.bfloat16)
 
 
-def tick(relay, sections, n_dp, n_mp, deps, lengths, idx_in, idx_out, section_in, out_grad, w_in, w_out):
+def tick(relay, sections, n_dp, n_mp, apart, deps, lengths, idx_in, idx_out, section_in, out_grad, w_in, w_out):
     rows, width = section_in.shape[2:]
     blocks, block = w_in.shape[2:4]
     per = blocks // sections
@@ -84,18 +87,22 @@
     piece = block // n_dp
     whole = pl.BlockSpec((None, None, rows, width), lambda i, *_: (relay, 0, 0, 0))
     weight = pl.BlockSpec((None, None, per_step, block, block), lambda i, *_: (0, relay, i, 0, 0))
-    slots = jax.ShapeDtypeStruct((sections, 2, per, piece, block), jnp.bfloat16)
-    slots_spec = pl.BlockSpec((None, 2, per_step, piece, block), lambda i, *_: (i // turns, 0, i % turns, 0, 0))
+    if apart:
+        slots = [jax.ShapeDtypeStruct((sections, per, piece, block), jnp.bfloat16)] * 8
+        slots_spec = [pl.BlockSpec((None, per_step, piece, block), lambda i, *_: (i // turns, i % turns, 0, 0))] * 8
+    else:
+        slots = [jax.ShapeDtypeStruct((sections, 2, per, piece, block), jnp.bfloat16)] * 4
+        slots_spec = [pl.BlockSpec((None, 2, per_step, piece, block), lambda i, *_: (i // turns, 0, i % turns, 0, 0))] * 4
     return pl.pallas_call(
-        functools.partial(tick_kernel, relay, per_step, n_mp, len(deps)),
+        functools.partial(tick_kernel, relay, per_step, n_mp, apart, len(deps)),
         grid_spec=pltpu.PrefetchScalarGridSpec(
             num_scalar_prefetch=3,
             grid=(sections * turns,),
             in_specs=[whole, whole, weight, weight] + [pl.BlockSpec(memory_space=pl.ANY)] * len(deps),
-            out_specs=[slots_spec] * 4 + [pl.BlockSpec((rows, width), lambda i, *_: (0, 0))],
+            out_specs=slots_spec + [pl.BlockSpec((rows, width), lambda i, *_: (0, 0))],
             scratch_shapes=[pltpu.VMEM((width // block, rows, block), jnp.float32)],
         ),
-        out_shape=[slots] * 4 + [jax.ShapeDtypeStruct((rows, width), jnp.bfloat16)],
+        out_shape=slots + [jax.ShapeDtypeStruct((rows, width), jnp.bfloat16)],
         compiler_params=pltpu.CompilerParams(
             dimension_semantics=("arbitrary",), vmem_limit_bytes=56 * 1024 * 1024
         ),
@@ -159,20 +166,24 @@
     def scatter(share):
         return lax.psum_scatter(share, "mp", scatter_dimension=0, tiled=True)
 
-    a0, s0, a2, s2, share0 = tick(0, sections, n_dp, n_mp, [], *args)
+    a0, s0, a2, s2, share0 = tick(0, sections, n_dp, n_mp, False, [], *args)
     got0, got2 = flip_bit(s0, "dp", 1), flip_bit(s2, "dp", 1)
     sum0 = total(a2, got2).astype(jnp.bfloat16)
     came0 = flip_bit(sum0, "dp", 2)
-    b0, t0, b2, t2, share1 = tick(1, sections, n_dp, n_mp, [sum0], *args)
-    hot0, hot2 = flip_bit(t0, "dp", 1), flip_bit(t2, "dp", 1)
-    dx0 = scatter(share0)
-    sum1 = total(tie(b2, came0), hot2).astype(jnp.bfloat16)
-    came1 = flip_bit(sum1, "dp", 2)
-    dx1 = scatter(tie(share1, came0))
+    *slots, share1 = tick(1, sections, n_dp, n_mp, True, [sum0], *args)
+    b0, t0, b2, t2 = (slots[2 * k:2 * k + 2] for k in range(4))
+    hot0, hot2 = [flip_bit(v, "dp", 1) for v in t0], [flip_bit(v, "dp", 1) for v in t2]
+    passed0 = from_behind(tie(scatter(share0), b0[0]), "section", -1)
+    came1 = []
+    for kept, hot in zip(b2, hot2):
+        came1.append(flip_bit(total(tie(kept, came0, passed0, *hot0), hot).astype(jnp.bfloat16), "dp", 2))
+    passed1 = from_behind(scatter(tie(share1, came0)), "section", 1)
     moved0 = rotate(total(a0, got0, came0).astype(jnp.bfloat16), "section")
-    passed0 = from_behind(dx0, "section", -1)
-    passed1 = from_behind(dx1, "section", 1)
-    moved1 = rotate(total(b0, hot0, came1).astype(jnp.bfloat16), "section")
+    moved1 = []
+    for kind in range(2):
+        came = tie(came1[kind], passed1) if kind else came1[kind]
+        moved1.append(rotate(total(b0[kind], hot0[kind], came).astype(jnp.bfloat16), "section"))
+    moved1 = [jnp.stack(pair) for pair in zip(*moved1)]
     grads = total(by_source(moved0, "section"), jnp.flip(by_source(moved1, "section"), 0))
     return jnp.stack([passed0, passed1], axis=0)[:, None], grads[:, :, None]
 

time: 174 us -> 198 us (1.14)
  the two profiles are of different devices: /device:TPU:16 before, /device:TPU:0 now
where the time goes in v10:
time: 198 us; the launch traced here: 197 us
  starting transfers between devices  61.7 us (31%)
  waiting for transfers between devices  58.9 us (30%)
  Pallas kernels  34.9 us (18%)
  other arithmetic  20.3 us (10%)
  between operations  14.3 us (7%)
  local copies, waits for them, and re-layouts  7.35 us (4%)
    pallas_call x2, Pallas kernels, tick(): pl.pallas_call(functools.partial(tick_kernel, relay, per_step, n_mp, apar...  34.9 us
    ppermute x9, starting transfers between devices, rotate(): lax.ppermute(part, axis, [(i, (i + k) % n) for i in range(n)])  32.3 us
    ppermute x2, starting transfers between devices, from_behind(): return lax.ppermute(value, axis, route)  22.4 us
    ppermute x9, waiting for transfers between devices, flip_bit(): lax.ppermute(value, axis, [(i, i ^ bit) for i in range(lax.axis_size(axis...  21.6 us
    ppermute x9, waiting for transfers between devices, rotate(): lax.ppermute(part, axis, [(i, (i + k) % n) for i in range(n)])  21.3 us
    ppermute x2, waiting for transfers between devices, from_behind(): return lax.ppermute(value, axis, route)  16 us
    ppermute x9, starting transfers between devices, flip_bit(): lax.ppermute(value, axis, [(i, i ^ bit) for i in range(lax.axis_size(axis...  6.91 us
    convert_element_type x2, other arithmetic, body(): total(tie(kept, came0, passed0, *hot0), hot).astype(jnp.bfloat16)  5.13 us
  transfers between devices with their start and end apart: 22, of which 8 were waited for; matrix products, arithmetic and copies ran while one was open for 10% of the time, Pallas kernels for 9%

profile of v10, /device:TPU:0, one launch (start us, length us, event | category | flops | bytes accessed | tf_op | source)
XLA Modules:
  0.0 197.4 jit_solution(2129782100788830306)
XLA Ops:
  7.2 17.2 %tick0.1 = (bf16[4,2,24,32,128]{4,3,2,1,0:T(8,128)(2,1)}, bf16[4,2,24,32,128]{4,3,2,1,0:T(8,128)(2,1)}, bf16[4,2,24,32,128]{4,3,2,1,0:T(8,128)(2,1)}, bf16[4,2,2...) custom-call(s32[2]{0:T(128)} %bitcast.53, s32[1,2,96]{2,1,0:T(2,128)} %idx_in_ref.3, s32[1,2,96]{2,1,0:T(2,128)} %idx_out_ref.3, ...), custom_call_target="tpu_custom_call" | custom-call | flops 1006632960 | bytes 17301504 | tf_op jit(solution)/shard_map/tick0/pallas_call | solution.py:96
  25.0 3.2 %collective-permute-done = bf16[4,2,24,32,128]{4,3,2,1,0:T(8,128)(2,1)S(1)} collective-permute-done((bf16[4,2,24,32,128]{4,3,2,1,0:T(8,128)(2,1)}, bf16[4,2,24,32,128]{4,3,2,1,0:T(8,128)(2,1)S(1)}, u32[]{:S(2)}, u32[]{:S(2)}) %collective-permute-start) | collective-permute-done | bytes 1572896 | tf_op jit(solution)/shard_map/ppermute | solution.py:136
  28.7 2.9 %collective-permute-start.2 = (bf16[4,2,24,32,128]{4,3,2,1,0:T(8,128)(2,1)S(1)}, bf16[4,2,24,32,128]{4,3,2,1,0:T(8,128)(2,1)S(1)}, u32[]{:S(2)}, u32[]{:S(2)}) collective-permute-start(bf16[4,2,24,32,128]{4,3,2,1,0:T(8,128)(2,1)S(1)} %add_convert_fusion.1.refs_0_), channel_id=1, source_target_pairs={{0,4},{2,6},{4,0},{6,2},{1,5},{3,7},{5,1},{7,3},{8,12},{10,14},{12... | collective-permute-start | bytes 4718600 | tf_op jit(solution)/shard_map/ppermute | solution.py:136
  31.6 17.7 %tick1.1 = (bf16[4,24,32,128]{3,2,1,0:T(8,128)(2,1)}, bf16[4,24,32,128]{3,2,1,0:T(8,128)(2,1)}, bf16[4,24,32,128]{3,2,1,0:T(8,128)(2,1)}, bf16[4,24,32,128]{3,2,...) custom-call(s32[2]{0:T(128)} %bitcast.54, ...), custom_call_target="tpu_custom_call" | custom-call | flops 1006632960 | bytes 17301504 | tf_op jit(solution)/shard_map/tick1/pallas_call | solution.py:96
  49.3 17.0 %collective-permute-done.2.refs_1_ = bf16[4,2,24,32,128]{4,3,2,1,0:T(8,128)(2,1)S(1)} collective-permute-done((bf16[4,2,24,32,128]{4,3,2,1,0:T(8,128)(2,1)S(1)}, bf16[4,2,24,32,128]{4,3,2,1,0:T(8,128)(2,1)S(1)}, u32[]{:S(2)}, u32[]{:S(2)}) %collective-permute-start.2) | collective-permute-done | bytes 1572896 | tf_op jit(solution)/shard_map/ppermute | solution.py:136
  66.3 1.2 copy-done
  68.1 1.3 collective-permute-start.1
  69.9 1.4 collective-permute-done.4
  71.4 3.6 %add_convert_fusion = bf16[4,2,24,32,128]{4,3,2,1,0:T(8,128)(2,1)} fusion(bf16[4,2,24,32,128]{4,3,2,1,0:T(8,128)(2,1)S(1)} %copy-done.1, bf16[4,2,24,32,128]{4,3,2,1,0:T(8,128)(2,1)} %collective-permute-done.4, bf16[4,2,24,32,128]{4,3,2,1,0:T(8,128)(2,1)} %get-tuple-element.21), kind=kLoop, calls=%fused_computation.1 | loop fusion | flops 4718592 | bytes 6291456 | tf_op jit(solution)/shard_map/convert_element_type | solution.py:181
  75.1 15.1 %collective-permute-done.1.refs_2_ = bf16[32,12288]{1,0:T(8,128)(2,1)S(1)} collective-permute-done((bf16[32,12288]{1,0:T(8,128)(2,1)}, bf16[32,12288]{1,0:T(8,128)(2,1)S(1)}, u32[]{:S(2)}, u32[]{:S(2)}) %collective-permute-start.1) | collective-permute-done | bytes 786464 | tf_op jit(solution)/shard_map/ppermute | solution.py:142
  91.1 2.7 %add_convert_fusion.5 = bf16[4,24,32,128]{3,2,1,0:T(8,128)(2,1)} fusion(bf16[4,24,32,128]{3,2,1,0:T(8,128)(2,1)} %collective-permute-done.10, bf16[4,24,32,128]{3,2,1,0:T(8,128)(2,1)} %tie.7), kind=kLoop, calls=%fused_computation.10 | loop fusion | flops 1572864 | bytes 2359296 | tf_op jit(solution)/shard_map/convert_element_type | solution.py:179
  93.8 1.6 collective-permute-start.11
  95.4 1.2 constant_dynamic-slice_fusion.10
  96.6 1.7 collective-permute-start.7
  98.3 1.4 collective-permute-start.6
  99.7 1.6 collective-permute-start.5
  101.3 2.5 %add_convert_fusion.3 = bf16[4,24,32,128]{3,2,1,0:T(8,128)(2,1)} fusion(bf16[4,24,32,128]{3,2,1,0:T(8,128)(2,1)} %collective-permute-done.12, bf16[4,24,32,128]{3,2,1,0:T(8,128)(2,1)} %tie.8), kind=kLoop, calls=%fused_computation.8 | loop fusion | flops 1572864 | bytes 2359296 | tf_op jit(solution)/shard_map/convert_element_type | solution.py:179
  104.3 3.7 %collective-permute-done.7 = bf16[2,24,32,128]{3,2,1,0:T(8,128)(2,1)S(1)} collective-permute-done((bf16[2,24,32,128]{3,2,1,0:T(8,128)(2,1)S(1)}, bf16[2,24,32,128]{3,2,1,0:T(8,128)(2,1)S(1)}, u32[]{:S(2)}, u32[]{:S(2)}) %collective-permute-start.7) | collective-permute-done | bytes 393248 | tf_op jit(solution)/shard_map/ppermute | solution.py:151
  108.0 21.1 %collective-permute-start.3 = (bf16[32,12288]{1,0:T(8,128)(2,1)}, bf16[32,12288]{1,0:T(8,128)(2,1)S(1)}, u32[]{:S(2)}, u32[]{:S(2)}) collective-permute-start(bf16[32,12288]{1,0:T(8,128)(2,1)} %reduce-scatter.5.cloned.1.call-done), channel_id=1, source_target_pairs={{0,8},{8,16},{16,24},{1,9},{9,17},{17,25},{2,10},{10,18},{18,26},{... | collective-permute-start | bytes 2359304 | tf_op jit(solution)/shard_map/ppermute | solution.py:142
  129.1 4.4 %collective-permute-done.6 = bf16[2,24,32,128]{3,2,1,0:T(8,128)(2,1)S(1)} collective-permute-done((bf16[2,24,32,128]{3,2,1,0:T(8,128)(2,1)}, bf16[2,24,32,128]{3,2,1,0:T(8,128)(2,1)S(1)}, u32[]{:S(2)}, u32[]{:S(2)}) %collective-permute-start.6) | collective-permute-done | bytes 393248 | tf_op jit(solution)/shard_map/ppermute | solution.py:151
  133.5 1.2 pad_maximum_fusion
  134.7 1.1 constant_dynamic-slice_fusion.9
  135.8 1.4 add_convert_fusion.4
  138.1 1.7 collective-permute-start.16
  139.9 2.0 %collective-permute-start.14 = (bf16[24,32,128]{2,1,0:T(8,128)(2,1)}, bf16[24,32,128]{2,1,0:T(8,128)(2,1)}, u32[]{:S(2)}, u32[]{:S(2)}) collective-permute-start(bf16[24,32,128]{2,1,0:T(8,128)(2,1)} %get-tuple-element.47), channel_id=1, source_target_pairs={{0,8},{8,16},{16,24},{24,0},{1,9},{9,17},{17,25},{25,1},{2,10},{10... | collective-permute-start | bytes 589832 | tf_op jit(solution)/shard_map/ppermute | solution.py:151
  143.7 1.7 add_convert_fusion.2
  145.4 5.7 %collective-permute-start.19 = (bf16[24,32,128]{2,1,0:T(8,128)(2,1)S(1)}, bf16[24,32,128]{2,1,0:T(8,128)(2,1)S(1)}, u32[]{:S(2)}, u32[]{:S(2)}) collective-permute-start(bf16[24,32,128]{2,1,0:T(8,128)(2,1)S(1)} %get-tuple-element.49), channel_id=1, source_target_pairs={{0,24},{8,0},{16,8},{24,16},{1,25},{9,1},{17,9},{25,17},{2,26},{10... | collective-permute-start | bytes 589832 | tf_op jit(solution)/shard_map/ppermute | solution.py:151
  151.2 16.2 %collective-permute-start.17 = (bf16[24,32,128]{2,1,0:T(8,128)(2,1)S(1)}, bf16[24,32,128]{2,1,0:T(8,128)(2,1)S(1)}, u32[]{:S(2)}, u32[]{:S(2)}) collective-permute-start(bf16[24,32,128]{2,1,0:T(8,128)(2,1)S(1)} %get-tuple-element.50), channel_id=1, source_target_pairs={{0,16},{8,24},{16,0},{24,8},{1,17},{9,25},{17,1},{25,9},{2,18},{10... | collective-permute-start | bytes 589832 | tf_op jit(solution)/shard_map/ppermute | solution.py:151
  167.4 1.3 maximum_bitcast_fusion
  168.7 2.0 %collective-permute-start.15 = (bf16[24,32,128]{2,1,0:T(8,128)(2,1)S(1)}, bf16[24,32,128]{2,1,0:T(8,128)(2,1)S(1)}, u32[]{:S(2)}, u32[]{:S(2)}) collective-permute-start(bf16[24,32,128]{2,1,0:T(8,128)(2,1)S(1)} %get-tuple-element.51), channel_id=1, source_target_pairs={{0,8},{8,16},{16,24},{24,0},{1,9},{9,17},{17,25},{25,1},{2,10},{10... | collective-permute-start | bytes 589832 | tf_op jit(solution)/shard_map/ppermute | solution.py:151
  171.7 13.2 %collective-permute-done.17 = bf16[24,32,128]{2,1,0:T(8,128)(2,1)S(1)} collective-permute-done((bf16[24,32,128]{2,1,0:T(8,128)(2,1)S(1)}, bf16[24,32,128]{2,1,0:T(8,128)(2,1)S(1)}, u32[]{:S(2)}, u32[]{:S(2)}) %collective-permute-start.17) | collective-permute-done | bytes 196640 | tf_op jit(solution)/shard_map/ppermute | solution.py:151
  188.4 2.2 %add_bitcast_fusion = f32[4,2,1,24,32,128]{5,4,3,2,1,0:T(8,128)} fusion(bf16[1,2,24,32,128]{4,3,2,1,0:T(8,128)(2,1)S(1)} %get-tuple-element.37, bf16[1,2,24,32,128]{4,3,2,1,0:T(8,128)(2,1)S(1)} %get-tuple-element.38, bf16[1,2,24,32,128]{4,3,2,1,0:T(8,128)(2,1)S(1)} %copy-done.13, bf16[1,2,24,32,128]{4,3,2,1,0:T(8,128)(2,1)S(1)} %get-tuple-element.36, ...), kind=kLoop, calls=%fused_computation | loop fusion | flops 7864320 | bytes 6291456
  (71 shorter events, 11.0 us)
Async XLA Ops:
  7.2 61.0 %reduce-scatter.3.cloned.1.call-start = ((), (), s32[]{:S(2)}) async-start(), calls=%async_computation.2 | async-start | bytes 2359296 | tf_op jit(solution)/shard_map/reduce_scatter | solution.py:167
  24.4 3.8 %copy-start.12 = (bf16[4,2,24,32,128]{4,3,2,1,0:T(8,128)(2,1)S(1)}, bf16[4,2,24,32,128]{4,3,2,1,0:T(8,128)(2,1)}, u32[]{:S(2)}) copy-start(bf16[4,2,24,32,128]{4,3,2,1,0:T(8,128)(2,1)} %get-tuple-element.17) | copy-start | bytes 4718596
  24.4 3.8 %collective-permute-start = (bf16[4,2,24,32,128]{4,3,2,1,0:T(8,128)(2,1)}, bf16[4,2,24,32,128]{4,3,2,1,0:T(8,128)(2,1)S(1)}, u32[]{:S(2)}, u32[]{:S(2)}) collective-permute-start(bf16[4,2,24,32,128]{4,3,2,1,0:T(8,128)(2,1)} %get-tuple-element.18), channel_id=1, source_target_pairs={{0,2},{2,0},{4,6},{6,4},{1,3},{3,1},{5,7},{7,5},{8,10},{10,8},{12,... | collective-permute-start | bytes 4718600 | tf_op jit(solution)/shard_map/ppermute | solution.py:136
  25.0 83.0 %reduce-scatter.5.cloned.1.call-start = ((), (), s32[]{:S(2)}) async-start(), calls=%async_computation.3 | async-start | bytes 2359296 | tf_op jit(solution)/shard_map/reduce_scatter | solution.py:167
  28.7 2.9 %copy-start.6 = (bf16[4,2,24,32,128]{4,3,2,1,0:T(8,128)(2,1)}, bf16[4,2,24,32,128]{4,3,2,1,0:T(8,128)(2,1)S(1)}, u32[]{:S(2)}) copy-start(bf16[4,2,24,32,128]{4,3,2,1,0:T(8,128)(2,1)S(1)} %add_convert_fusion.1.refs_0_) | copy-start | bytes 4718596
  28.7 37.6 %collective-permute-start.2 = (bf16[4,2,24,32,128]{4,3,2,1,0:T(8,128)(2,1)S(1)}, bf16[4,2,24,32,128]{4,3,2,1,0:T(8,128)(2,1)S(1)}, u32[]{:S(2)}, u32[]{:S(2)}) collective-permute-start(bf16[4,2,24,32,128]{4,3,2,1,0:T(8,128)(2,1)S(1)} %add_convert_fusion.1.refs_0_), channel_id=1, source_target_pairs={{0,4},{2,6},{4,0},{6,2},{1,5},{3,7},{5,1},{7,3},{8,12},{10,14},{12... | collective-permute-start | bytes 4718600 | tf_op jit(solution)/shard_map/ppermute | solution.py:136
  66.3 1.2 copy-start
  67.5 4.0 %copy-start.1 = (bf16[4,2,24,32,128]{4,3,2,1,0:T(8,128)(2,1)S(1)}, bf16[4,2,24,32,128]{4,3,2,1,0:T(8,128)(2,1)}, u32[]{:S(2)}) copy-start(bf16[4,2,24,32,128]{4,3,2,1,0:T(8,128)(2,1)} %copy-done) | copy-start | bytes 4718596
  67.5 3.8 %collective-permute-start.4 = (bf16[4,2,24,32,128]{4,3,2,1,0:T(8,128)(2,1)}, bf16[4,2,24,32,128]{4,3,2,1,0:T(8,128)(2,1)}, u32[]{:S(2)}, u32[]{:S(2)}) collective-permute-start(bf16[4,2,24,32,128]{4,3,2,1,0:T(8,128)(2,1)} %get-tuple-element.22), channel_id=1, source_target_pairs={{0,2},{2,0},{4,6},{6,4},{1,3},{3,1},{5,7},{7,5},{8,10},{10,8},{12,... | collective-permute-start | bytes 4718600 | tf_op jit(solution)/shard_map/ppermute | solution.py:136
  67.6 7.5 %collective-permute-start.8 = (bf16[4,24,32,128]{3,2,1,0:T(8,128)(2,1)}, bf16[4,24,32,128]{3,2,1,0:T(8,128)(2,1)}, u32[]{:S(2)}, u32[]{:S(2)}) collective-permute-start(bf16[4,24,32,128]{3,2,1,0:T(8,128)(2,1)} %get-tuple-element.23), channel_id=1, source_target_pairs={{0,2},{2,0},{4,6},{6,4},{1,3},{3,1},{5,7},{7,5},{8,10},{10,8},{12,... | collective-permute-start | bytes 2359304 | tf_op jit(solution)/shard_map/ppermute | solution.py:136
  68.1 7.0 %collective-permute-start.9 = (bf16[4,24,32,128]{3,2,1,0:T(8,128)(2,1)}, bf16[4,24,32,128]{3,2,1,0:T(8,128)(2,1)S(1)}, u32[]{:S(2)}, u32[]{:S(2)}) collective-permute-start(bf16[4,24,32,128]{3,2,1,0:T(8,128)(2,1)} %get-tuple-element.25), channel_id=1, source_target_pairs={{0,2},{2,0},{4,6},{6,4},{1,3},{3,1},{5,7},{7,5},{8,10},{10,8},{12,... | collective-permute-start | bytes 2359304 | tf_op jit(solution)/shard_map/ppermute | solution.py:136
  68.1 22.1 %collective-permute-start.1 = (bf16[32,12288]{1,0:T(8,128)(2,1)}, bf16[32,12288]{1,0:T(8,128)(2,1)S(1)}, u32[]{:S(2)}, u32[]{:S(2)}) collective-permute-start(bf16[32,12288]{1,0:T(8,128)(2,1)} %tie.5), channel_id=1, source_target_pairs={{8,0},{16,8},{24,16},{9,1},{17,9},{25,17},{10,2},{18,10},{26,18},{... | collective-permute-start | bytes 2359304 | tf_op jit(solution)/shard_map/ppermute | solution.py:142
  69.4 21.7 %collective-permute-start.10 = (bf16[4,24,32,128]{3,2,1,0:T(8,128)(2,1)}, bf16[4,24,32,128]{3,2,1,0:T(8,128)(2,1)}, u32[]{:S(2)}, u32[]{:S(2)}) collective-permute-start(bf16[4,24,32,128]{3,2,1,0:T(8,128)(2,1)} %get-tuple-element.26), channel_id=1, source_target_pairs={{0,2},{2,0},{4,6},{6,4},{1,3},{3,1},{5,7},{7,5},{8,10},{10,8},{12,... | collective-permute-start | bytes 2359304 | tf_op jit(solution)/shard_map/ppermute | solution.py:136
  71.3 29.9 %collective-permute-start.12 = (bf16[4,24,32,128]{3,2,1,0:T(8,128)(2,1)}, bf16[4,24,32,128]{3,2,1,0:T(8,128)(2,1)}, u32[]{:S(2)}, u32[]{:S(2)}) collective-permute-start(bf16[4,24,32,128]{3,2,1,0:T(8,128)(2,1)} %get-tuple-element.29), channel_id=1, source_target_pairs={{0,2},{2,0},{4,6},{6,4},{1,3},{3,1},{5,7},{7,5},{8,10},{10,8},{12,... | collective-permute-start | bytes 2359304 | tf_op jit(solution)/shard_map/ppermute | solution.py:136
  75.1 15.1 %copy-start.4 = (bf16[4,24,32,128]{3,2,1,0:T(8,128)(2,1)}, bf16[4,24,32,128]{3,2,1,0:T(8,128)(2,1)S(1)}, u32[]{:S(2)}) copy-start(bf16[4,24,32,128]{3,2,1,0:T(8,128)(2,1)S(1)} %collective-permute-done.9.refs_4_) | copy-start | bytes 2359300
  91.1 4.3 %copy-start.7 = (bf16[4,2,24,32,128]{4,3,2,1,0:T(8,128)(2,1)S(1)}, bf16[4,2,24,32,128]{4,3,2,1,0:T(8,128)(2,1)}, u32[]{:S(2)}) copy-start(bf16[4,2,24,32,128]{4,3,2,1,0:T(8,128)(2,1)} %add_convert_fusion) | copy-start | bytes 4718596
  93.8 42.0 %collective-permute-start.11 = (bf16[4,24,32,128]{3,2,1,0:T(8,128)(2,1)}, bf16[4,24,32,128]{3,2,1,0:T(8,128)(2,1)S(1)}, u32[]{:S(2)}, u32[]{:S(2)}) collective-permute-start(bf16[4,24,32,128]{3,2,1,0:T(8,128)(2,1)} %add_convert_fusion.5), channel_id=1, source_target_pairs={{0,4},{2,6},{4,0},{6,2},{1,5},{3,7},{5,1},{7,3},{8,12},{10,14},{12... | collective-permute-start | bytes 2359304 | tf_op jit(solution)/shard_map/ppermute | solution.py:136
  96.6 11.3 %collective-permute-start.7 = (bf16[2,24,32,128]{3,2,1,0:T(8,128)(2,1)S(1)}, bf16[2,24,32,128]{3,2,1,0:T(8,128)(2,1)S(1)}, u32[]{:S(2)}, u32[]{:S(2)}) collective-permute-start(bf16[2,24,32,128]{3,2,1,0:T(8,128)(2,1)S(1)} %get-tuple-element.41), channel_id=1, source_target_pairs={{0,24},{8,0},{16,8},{24,16},{1,25},{9,1},{17,9},{25,17},{2,26},{10... | collective-permute-start | bytes 1179656 | tf_op jit(solution)/shard_map/ppermute | solution.py:151
  98.3 35.1 %collective-permute-start.6 = (bf16[2,24,32,128]{3,2,1,0:T(8,128)(2,1)}, bf16[2,24,32,128]{3,2,1,0:T(8,128)(2,1)S(1)}, u32[]{:S(2)}, u32[]{:S(2)}) collective-permute-start(bf16[2,24,32,128]{3,2,1,0:T(8,128)(2,1)} %get-tuple-element.42), channel_id=1, source_target_pairs={{0,16},{8,24},{16,0},{24,8},{1,17},{9,25},{17,1},{25,9},{2,18},{10... | collective-permute-start | bytes 1179656 | tf_op jit(solution)/shard_map/ppermute | solution.py:151
  99.7 33.8 %collective-permute-start.5 = (bf16[2,24,32,128]{3,2,1,0:T(8,128)(2,1)}, bf16[2,24,32,128]{3,2,1,0:T(8,128)(2,1)}, u32[]{:S(2)}, u32[]{:S(2)}) collective-permute-start(bf16[2,24,32,128]{3,2,1,0:T(8,128)(2,1)} %get-tuple-element.43), channel_id=1, source_target_pairs={{0,8},{8,16},{16,24},{24,0},{1,9},{9,17},{17,25},{25,1},{2,10},{10... | collective-permute-start | bytes 1179656 | tf_op jit(solution)/shard_map/ppermute | solution.py:151
  103.7 38.2 %collective-permute-start.13 = (bf16[4,24,32,128]{3,2,1,0:T(8,128)(2,1)}, bf16[4,24,32,128]{3,2,1,0:T(8,128)(2,1)S(1)}, u32[]{:S(2)}, u32[]{:S(2)}) collective-permute-start(bf16[4,24,32,128]{3,2,1,0:T(8,128)(2,1)} %add_convert_fusion.3), channel_id=1, source_target_pairs={{0,4},{2,6},{4,0},{6,2},{1,5},{3,7},{5,1},{7,3},{8,12},{10,14},{12... | collective-permute-start | bytes 2359304 | tf_op jit(solution)/shard_map/ppermute | solution.py:136
  108.0 34.8 %collective-permute-start.3 = (bf16[32,12288]{1,0:T(8,128)(2,1)}, bf16[32,12288]{1,0:T(8,128)(2,1)S(1)}, u32[]{:S(2)}, u32[]{:S(2)}) collective-permute-start(bf16[32,12288]{1,0:T(8,128)(2,1)} %reduce-scatter.5.cloned.1.call-done), channel_id=1, source_target_pairs={{0,8},{8,16},{16,24},{1,9},{9,17},{17,25},{2,10},{10,18},{18,26},{... | collective-permute-start | bytes 2359304 | tf_op jit(solution)/shard_map/ppermute | solution.py:142
  138.1 5.5 %copy-start.5 = (bf16[4,24,32,128]{3,2,1,0:T(8,128)(2,1)S(1)}, bf16[4,24,32,128]{3,2,1,0:T(8,128)(2,1)}, u32[]{:S(2)}) copy-start(bf16[4,24,32,128]{3,2,1,0:T(8,128)(2,1)} %copy-done.4) | copy-start | bytes 2359300
  138.1 30.5 %collective-permute-start.18 = (bf16[24,32,128]{2,1,0:T(8,128)(2,1)}, bf16[24,32,128]{2,1,0:T(8,128)(2,1)}, u32[]{:S(2)}, u32[]{:S(2)}) collective-permute-start(bf16[24,32,128]{2,1,0:T(8,128)(2,1)} %get-tuple-element.45), channel_id=1, source_target_pairs={{0,24},{8,0},{16,8},{24,16},{1,25},{9,1},{17,9},{25,17},{2,26},{10... | collective-permute-start | bytes 589832 | tf_op jit(solution)/shard_map/ppermute | solution.py:151
  138.1 33.5 %collective-permute-start.16 = (bf16[24,32,128]{2,1,0:T(8,128)(2,1)}, bf16[24,32,128]{2,1,0:T(8,128)(2,1)}, u32[]{:S(2)}, u32[]{:S(2)}) collective-permute-start(bf16[24,32,128]{2,1,0:T(8,128)(2,1)} %get-tuple-element.46), channel_id=1, source_target_pairs={{0,16},{8,24},{16,0},{24,8},{1,17},{9,25},{17,1},{25,9},{2,18},{10... | collective-permute-start | bytes 589832 | tf_op jit(solution)/shard_map/ppermute | solution.py:151
  139.9 46.0 %collective-permute-start.14 = (bf16[24,32,128]{2,1,0:T(8,128)(2,1)}, bf16[24,32,128]{2,1,0:T(8,128)(2,1)}, u32[]{:S(2)}, u32[]{:S(2)}) collective-permute-start(bf16[24,32,128]{2,1,0:T(8,128)(2,1)} %get-tuple-element.47), channel_id=1, source_target_pairs={{0,8},{8,16},{16,24},{24,0},{1,9},{9,17},{17,25},{25,1},{2,10},{10... | collective-permute-start | bytes 589832 | tf_op jit(solution)/shard_map/ppermute | solution.py:151
  145.3 22.0 %copy-start.3 = (bf16[32,12288]{1,0:T(8,128)(2,1)S(1)}, bf16[32,12288]{1,0:T(8,128)(2,1)}, u32[]{:S(2)}) copy-start(bf16[32,12288]{1,0:T(8,128)(2,1)} %copy-done.2) | copy-start | bytes 2359300
  145.3 22.0 %copy-start.10 = (bf16[32,12288]{1,0:T(8,128)(2,1)S(1)}, bf16[32,12288]{1,0:T(8,128)(2,1)}, u32[]{:S(2)}) copy-start(bf16[32,12288]{1,0:T(8,128)(2,1)} %copy-done.9) | copy-start | bytes 2359300
  145.4 25.3 %collective-permute-start.19 = (bf16[24,32,128]{2,1,0:T(8,128)(2,1)S(1)}, bf16[24,32,128]{2,1,0:T(8,128)(2,1)S(1)}, u32[]{:S(2)}, u32[]{:S(2)}) collective-permute-start(bf16[24,32,128]{2,1,0:T(8,128)(2,1)S(1)} %get-tuple-element.49), channel_id=1, source_target_pairs={{0,24},{8,0},{16,8},{24,16},{1,25},{9,1},{17,9},{25,17},{2,26},{10... | collective-permute-start | bytes 589832 | tf_op jit(solution)/shard_map/ppermute | solution.py:151
  151.2 33.7 %collective-permute-start.17 = (bf16[24,32,128]{2,1,0:T(8,128)(2,1)S(1)}, bf16[24,32,128]{2,1,0:T(8,128)(2,1)S(1)}, u32[]{:S(2)}, u32[]{:S(2)}) collective-permute-start(bf16[24,32,128]{2,1,0:T(8,128)(2,1)S(1)} %get-tuple-element.50), channel_id=1, source_target_pairs={{0,16},{8,24},{16,0},{24,8},{1,17},{9,25},{17,1},{25,9},{2,18},{10... | collective-permute-start | bytes 589832 | tf_op jit(solution)/shard_map/ppermute | solution.py:151
  167.4 1.3 copy-start.14
  168.7 17.2 %collective-permute-start.15 = (bf16[24,32,128]{2,1,0:T(8,128)(2,1)S(1)}, bf16[24,32,128]{2,1,0:T(8,128)(2,1)S(1)}, u32[]{:S(2)}, u32[]{:S(2)}) collective-permute-start(bf16[24,32,128]{2,1,0:T(8,128)(2,1)S(1)} %get-tuple-element.51), channel_id=1, source_target_pairs={{0,8},{8,16},{16,24},{24,0},{1,9},{9,17},{17,25},{25,1},{2,10},{10... | collective-permute-start | bytes 589832 | tf_op jit(solution)/shard_map/ppermute | solution.py:151
  (5 other events, 4.8 us)
Sparse Core Ops, SparseCore 0:
  25.1 28.4 reduce-scatter.2
  67.6 27.5 reduce-scatter.4

commit v11 on v10

--- a/solution.py
+++ b/solution.py
@@ -166,24 +166,29 @@
     def scatter(share):
         return lax.psum_scatter(share, "mp", scatter_dimension=0, tiled=True)
 
-    a0, s0, a2, s2, share0 = tick(0, sections, n_dp, n_mp, False, [], *args)
-    got0, got2 = flip_bit(s0, "dp", 1), flip_bit(s2, "dp", 1)
-    sum0 = total(a2, got2).astype(jnp.bfloat16)
-    came0 = flip_bit(sum0, "dp", 2)
-    *slots, share1 = tick(1, sections, n_dp, n_mp, True, [sum0], *args)
-    b0, t0, b2, t2 = (slots[2 * k:2 * k + 2] for k in range(4))
-    hot0, hot2 = [flip_bit(v, "dp", 1) for v in t0], [flip_bit(v, "dp", 1) for v in t2]
-    passed0 = from_behind(tie(scatter(share0), b0[0]), "section", -1)
-    came1 = []
-    for kept, hot in zip(b2, hot2):
-        came1.append(flip_bit(total(tie(kept, came0, passed0, *hot0), hot).astype(jnp.bfloat16), "dp", 2))
-    passed1 = from_behind(scatter(tie(share1, came0)), "section", 1)
-    moved0 = rotate(total(a0, got0, came0).astype(jnp.bfloat16), "section")
-    moved1 = []
-    for kind in range(2):
-        came = tie(came1[kind], passed1) if kind else came1[kind]
-        moved1.append(rotate(total(b0[kind], hot0[kind], came).astype(jnp.bfloat16), "section"))
-    moved1 = [jnp.stack(pair) for pair in zip(*moved1)]
+    def core_pair(slots):
+        keep0, send0, keep2, send2 = (slots[2 * k:2 * k + 2] for k in range(4))
+        got0, got2 = [flip_bit(v, "dp", 1) for v in send0], [flip_bit(v, "dp", 1) for v in send2]
+        return keep0, got0, keep2, got2
+
+    def on_section(kept, got, came):
+        return rotate(total(kept, got, came).astype(jnp.bfloat16), "section")
+
+    *slots, share0 = tick(0, sections, n_dp, n_mp, True, [], *args)
+    a0, got0, a2, got2 = core_pair(slots)
+    sums = [total(tie(k, *got0), g).astype(jnp.bfloat16) for k, g in zip(a2, got2)]
+    came0 = [flip_bit(v, "dp", 2) for v in sums]
+    *slots, share1 = tick(1, sections, n_dp, n_mp, True, sums, *args)
+    b0, hot0, b2, hot2 = core_pair(slots)
+    first = on_section(a0[0], got0[0], came0[0])
+    deps = [came0[1], *first[1:], *hot0]
+    came1 = [flip_bit(total(tie(k, *deps), g).astype(jnp.bfloat16), "dp", 2) for k, g in zip(b2, hot2)]
+    second = on_section(a0[1], got0[1], came0[1])
+    passed0 = from_behind(scatter(share0), "section", -1)
+    passed1 = from_behind(scatter(tie(share1, *first[1:])), "section", 1)
+    third = on_section(b0[0], hot0[0], tie(came1[0], passed0))
+    fourth = on_section(b0[1], hot0[1], tie(came1[1], passed1))
+    moved0, moved1 = ([jnp.stack(pair) for pair in zip(*pairs)] for pairs in ((first, second), (third, fourth)))
     grads = total(by_source(moved0, "section"), jnp.flip(by_source(moved1, "section"), 0))
     return jnp.stack([passed0, passed1], axis=0)[:, None], grads[:, :, None]
 

time: 198 us -> 187 us (0.944)
  starting transfers between devices: 61.7 us -> 35.6 us
  waiting for transfers between devices: 58.9 us -> 66.6 us
  other arithmetic: 20.3 us -> 24.4 us
  local copies, waits for them, and re-layouts: 7.35 us -> 10.6 us
    ppermute x2, starting transfers between devices: 22.4 us -> 2.75 us  [from_behind(): return lax.ppermute(value, axis, route)]
    ppermute x9 -> x12, waiting for transfers between devices: 21.6 us -> 38.3 us  [flip_bit(): lax.ppermute(value, axis, [(i, i ^ bit) for i in range(lax.axis_size(axis...]
    ppermute x2, waiting for transfers between devices: 16 us -> 4.96 us  [from_behind(): return lax.ppermute(value, axis, route)]
    ppermute x9 -> x12, starting transfers between devices: 32.3 us -> 24.2 us  [rotate(): lax.ppermute(part, axis, [(i, (i + k) % n) for i in range(n)])]
    unnamed x30 -> x62, local copies, waits for them, and re-layouts: 3.79 us -> 6.6 us
    another operation x6 -> x10, other arithmetic: 4.32 us -> 6.91 us  [by_source(): stacked = jnp.stack(parts)]
    ppermute x9 -> x12, waiting for transfers between devices: 21.3 us -> 23.3 us  [rotate(): lax.ppermute(part, axis, [(i, (i + k) % n) for i in range(n)])]
    ppermute x9 -> x12, starting transfers between devices: 6.91 us -> 8.57 us  [flip_bit(): lax.ppermute(value, axis, [(i, i ^ bit) for i in range(lax.axis_size(axis...]
  transfers between devices with their start and end apart: 22 -> 28, of which waited for: 8 -> 9; matrix products, arithmetic and copies ran while one was open for 10% -> 13% of each run, Pallas kernels for 9% -> 9%
where the time goes in v11:
time: 187 us; the launch traced here: 186 us
  waiting for transfers between devices  66.6 us (36%)
  starting transfers between devices  35.6 us (19%)
  Pallas kernels  34.3 us (18%)
  other arithmetic  24.4 us (13%)
  between operations  14.4 us (8%)
  local copies, waits for them, and re-layouts  10.6 us (6%)
    ppermute x12, waiting for transfers between devices, flip_bit(): lax.ppermute(value, axis, [(i, i ^ bit) for i in range(lax.axis_size(axis...  38.3 us
    pallas_call x2, Pallas kernels, tick(): pl.pallas_call(functools.partial(tick_kernel, relay, per_step, n_mp, apar...  34.3 us
    ppermute x12, starting transfers between devices, rotate(): lax.ppermute(part, axis, [(i, (i + k) % n) for i in range(n)])  24.2 us
    ppermute x12, waiting for transfers between devices, rotate(): lax.ppermute(part, axis, [(i, (i + k) % n) for i in range(n)])  23.3 us
    ppermute x12, starting transfers between devices, flip_bit(): lax.ppermute(value, axis, [(i, i ^ bit) for i in range(lax.axis_size(axis...  8.57 us
    another operation x10, other arithmetic, by_source(): stacked = jnp.stack(parts)  6.91 us
    unnamed x62, local copies, waits for them, and re-layouts  6.6 us
    convert_element_type x4, other arithmetic, on_section(): return rotate(total(kept, got, came).astype(jnp.bfloat16), 'section')  6.31 us
  transfers between devices with their start and end apart: 28, of which 9 were waited for; matrix products, arithmetic and copies ran while one was open for 13% of the time, Pallas kernels for 9%

profile of v11, /device:TPU:0, one launch (start us, length us, event | category | flops | bytes accessed | tf_op | source)
XLA Modules:
  0.0 185.9 jit_solution(16037516729968149468)
XLA Ops:
  7.2 17.2 %tick0.1 = (bf16[4,24,32,128]{3,2,1,0:T(8,128)(2,1)}, bf16[4,24,32,128]{3,2,1,0:T(8,128)(2,1)}, bf16[4,24,32,128]{3,2,1,0:T(8,128)(2,1)}, bf16[4,24,32,128]{3,2,...) custom-call(s32[2]{0:T(128)} %bitcast.73, ...), custom_call_target="tpu_custom_call" | custom-call | flops 1006632960 | bytes 17301504 | tf_op jit(solution)/shard_map/tick0/pallas_call | solution.py:96
  27.1 2.2 %collective-permute-done.2.refs_2_ = bf16[4,24,32,128]{3,2,1,0:T(8,128)(2,1)S(1)} collective-permute-done((bf16[4,24,32,128]{3,2,1,0:T(8,128)(2,1)}, bf16[4,24,32,128]{3,2,1,0:T(8,128)(2,1)S(1)}, u32[]{:S(2)}, u32[]{:S(2)}) %collective-permute-start.2) | collective-permute-done | bytes 786464 | tf_op jit(solution)/shard_map/ppermute | solution.py:136
  30.3 1.3 add_convert_fusion.7.refs_0_
  31.6 2.9 %collective-permute-start.5 = (bf16[4,24,32,128]{3,2,1,0:T(8,128)(2,1)S(1)}, bf16[4,24,32,128]{3,2,1,0:T(8,128)(2,1)}, u32[]{:S(2)}, u32[]{:S(2)}) collective-permute-start(bf16[4,24,32,128]{3,2,1,0:T(8,128)(2,1)S(1)} %add_convert_fusion.7.refs_0_), channel_id=1, source_target_pairs={{0,4},{2,6},{4,0},{6,2},{1,5},{3,7},{5,1},{7,3},{8,12},{10,14},{12... | collective-permute-start | bytes 2359304 | tf_op jit(solution)/shard_map/ppermute | solution.py:136
  34.6 17.9 %collective-permute-done.5 = bf16[4,24,32,128]{3,2,1,0:T(8,128)(2,1)} collective-permute-done((bf16[4,24,32,128]{3,2,1,0:T(8,128)(2,1)S(1)}, bf16[4,24,32,128]{3,2,1,0:T(8,128)(2,1)}, u32[]{:S(2)}, u32[]{:S(2)}) %collective-permute-start.5) | collective-permute-done | bytes 786464 | tf_op jit(solution)/shard_map/ppermute | solution.py:136
  52.5 1.5 add_convert_fusion.5
  54.7 3.8 %collective-permute-start.8 = (bf16[24,32,128]{2,1,0:T(8,128)(2,1)S(1)}, bf16[24,32,128]{2,1,0:T(8,128)(2,1)S(1)}, u32[]{:S(2)}, u32[]{:S(2)}) collective-permute-start(bf16[24,32,128]{2,1,0:T(8,128)(2,1)S(1)} %get-tuple-element.57), channel_id=1, source_target_pairs={{0,24},{8,0},{16,8},{24,16},{1,25},{9,1},{17,9},{25,17},{2,26},{10... | collective-permute-start | bytes 589832 | tf_op jit(solution)/shard_map/ppermute | solution.py:151
  60.6 17.1 %tick1.1 = (bf16[4,24,32,128]{3,2,1,0:T(8,128)(2,1)}, bf16[4,24,32,128]{3,2,1,0:T(8,128)(2,1)}, bf16[4,24,32,128]{3,2,1,0:T(8,128)(2,1)}, bf16[4,24,32,128]{3,2,...) custom-call(s32[2]{0:T(128)} %bitcast.74, ...), custom_call_target="tpu_custom_call" | custom-call | flops 1006632960 | bytes 17301504 | tf_op jit(solution)/shard_map/tick1/pallas_call | solution.py:96
  78.7 1.5 collective-permute-start.10
  81.3 15.6 %collective-permute-done.10.refs_1_ = bf16[4,24,32,128]{3,2,1,0:T(8,128)(2,1)S(1)} collective-permute-done((bf16[4,24,32,128]{3,2,1,0:T(8,128)(2,1)}, bf16[4,24,32,128]{3,2,1,0:T(8,128)(2,1)S(1)}, u32[]{:S(2)}, u32[]{:S(2)}) %collective-permute-start.10) | collective-permute-done | bytes 786464 | tf_op jit(solution)/shard_map/ppermute | solution.py:136
  96.9 1.7 add_convert_fusion.4
  99.4 3.1 %collective-permute-start.13 = (bf16[24,32,128]{2,1,0:T(8,128)(2,1)S(1)}, bf16[24,32,128]{2,1,0:T(8,128)(2,1)S(1)}, u32[]{:S(2)}, u32[]{:S(2)}) collective-permute-start(bf16[24,32,128]{2,1,0:T(8,128)(2,1)S(1)} %get-tuple-element.61), channel_id=1, source_target_pairs={{0,24},{8,0},{16,8},{24,16},{1,25},{9,1},{17,9},{25,17},{2,26},{10... | collective-permute-start | bytes 589832 | tf_op jit(solution)/shard_map/ppermute | solution.py:151
  104.3 2.6 %add_convert_fusion.3 = bf16[4,24,32,128]{3,2,1,0:T(8,128)(2,1)} fusion(bf16[4,24,32,128]{3,2,1,0:T(8,128)(2,1)} %collective-permute-done.16, bf16[4,24,32,128]{3,2,1,0:T(8,128)(2,1)} %tie.10), kind=kLoop, calls=%fused_computation.8 | loop fusion | flops 1572864 | bytes 2359296 | tf_op jit(solution)/shard_map/convert_element_type | solution.py:185
  106.9 1.5 collective-permute-start.17
  108.5 1.4 collective-permute-start
  109.9 2.5 %add_convert_fusion.1 = bf16[4,24,32,128]{3,2,1,0:T(8,128)(2,1)} fusion(bf16[4,24,32,128]{3,2,1,0:T(8,128)(2,1)} %collective-permute-done.18, bf16[4,24,32,128]{3,2,1,0:T(8,128)(2,1)} %tie.12), kind=kLoop, calls=%fused_computation.6 | loop fusion | flops 1572864 | bytes 2359296 | tf_op jit(solution)/shard_map/convert_element_type | solution.py:185
  113.7 7.0 %collective-permute-done.12 = bf16[24,32,128]{2,1,0:T(8,128)(2,1)} collective-permute-done((bf16[24,32,128]{2,1,0:T(8,128)(2,1)S(1)}, bf16[24,32,128]{2,1,0:T(8,128)(2,1)}, u32[]{:S(2)}, u32[]{:S(2)}) %collective-permute-start.12) | collective-permute-done | bytes 196640 | tf_op jit(solution)/shard_map/ppermute | solution.py:151
  120.7 1.7 maximum_bitcast_fusion.3
  122.4 1.3 collective-permute-start.9
  123.8 1.2 pad_maximum_fusion
  125.0 1.3 constant_dynamic-slice_fusion.9
  126.4 1.4 collective-permute-done.17.refs_0_
  127.7 5.0 %collective-permute-done.refs_1_ = bf16[32,12288]{1,0:T(8,128)(2,1)S(1)} collective-permute-done((bf16[32,12288]{1,0:T(8,128)(2,1)}, bf16[32,12288]{1,0:T(8,128)(2,1)S(1)}, u32[]{:S(2)}, u32[]{:S(2)}) %collective-permute-start) | collective-permute-done | bytes 786464 | tf_op jit(solution)/shard_map/ppermute | solution.py:142
  133.6 1.7 add_convert_fusion.2
  136.1 4.6 %collective-permute-start.22 = (bf16[24,32,128]{2,1,0:T(8,128)(2,1)}, bf16[24,32,128]{2,1,0:T(8,128)(2,1)}, u32[]{:S(2)}, u32[]{:S(2)}) collective-permute-start(bf16[24,32,128]{2,1,0:T(8,128)(2,1)} %get-tuple-element.50), channel_id=1, source_target_pairs={{0,16},{8,24},{16,0},{24,8},{1,17},{9,25},{17,1},{25,9},{2,18},{10... | collective-permute-start | bytes 589832 | tf_op jit(solution)/shard_map/ppermute | solution.py:151
  142.5 1.4 add_convert_fusion
  144.0 3.9 %collective-permute-start.25 = (bf16[24,32,128]{2,1,0:T(8,128)(2,1)S(1)}, bf16[24,32,128]{2,1,0:T(8,128)(2,1)S(1)}, u32[]{:S(2)}, u32[]{:S(2)}) collective-permute-start(bf16[24,32,128]{2,1,0:T(8,128)(2,1)S(1)} %get-tuple-element.53), channel_id=1, source_target_pairs={{0,24},{8,0},{16,8},{24,16},{1,25},{9,1},{17,9},{25,17},{2,26},{10... | collective-permute-start | bytes 589832 | tf_op jit(solution)/shard_map/ppermute | solution.py:151
  147.9 1.3 maximum_bitcast_fusion
  149.3 6.6 %collective-permute-start.21 = (bf16[24,32,128]{2,1,0:T(8,128)(2,1)S(1)}, bf16[24,32,128]{2,1,0:T(8,128)(2,1)S(1)}, u32[]{:S(2)}, u32[]{:S(2)}) collective-permute-start(bf16[24,32,128]{2,1,0:T(8,128)(2,1)S(1)} %get-tuple-element.55), channel_id=1, source_target_pairs={{0,8},{8,16},{16,24},{24,0},{1,9},{9,17},{17,25},{25,1},{2,10},{10... | collective-permute-start | bytes 589832 | tf_op jit(solution)/shard_map/ppermute | solution.py:151
  156.8 9.6 %collective-permute-done.22 = bf16[24,32,128]{2,1,0:T(8,128)(2,1)} collective-permute-done((bf16[24,32,128]{2,1,0:T(8,128)(2,1)}, bf16[24,32,128]{2,1,0:T(8,128)(2,1)}, u32[]{:S(2)}, u32[]{:S(2)}) %collective-permute-start.22) | collective-permute-done | bytes 196640 | tf_op jit(solution)/shard_map/ppermute | solution.py:151
  166.5 6.6 %collective-permute-done.23 = bf16[24,32,128]{2,1,0:T(8,128)(2,1)S(1)} collective-permute-done((bf16[24,32,128]{2,1,0:T(8,128)(2,1)S(1)}, bf16[24,32,128]{2,1,0:T(8,128)(2,1)S(1)}, u32[]{:S(2)}, u32[]{:S(2)}) %collective-permute-start.23) | collective-permute-done | bytes 196640 | tf_op jit(solution)/shard_map/ppermute | solution.py:151
  176.9 2.2 %add_bitcast_fusion = f32[4,2,1,24,32,128]{5,4,3,2,1,0:T(8,128)} fusion(bf16[1,2,24,32,128]{4,3,2,1,0:T(8,128)(2,1)S(1)} %copy-done.24, bf16[1,2,24,32,128]{4,3,2,1,0:T(8,128)(2,1)S(1)} %copy-done.25, bf16[1,2,24,32,128]{4,3,2,1,0:T(8,128)(2,1)S(1)} %copy-done.26, bf16[1,2,24,32,128]{4,3,2,1,0:T(8,128)(2,1)S(1)} %copy-done.23, ...), kind=kLoop, calls=%fused_computation | loop fusion | flops 7864320 | bytes 6291456
  (124 shorter events, 20.7 us)
Async XLA Ops:
  7.2 101.3 %reduce-scatter.3.cloned.1.call-start = ((), (), s32[]{:S(2)}) async-start(), calls=%async_computation.2 | async-start | bytes 2359296 | tf_op jit(solution)/shard_map/reduce_scatter | solution.py:167
  24.4 98.0 %reduce-scatter.5.cloned.1.call-start = ((), (), s32[]{:S(2)}) async-start(), calls=%async_computation.3 | async-start | bytes 2359296 | tf_op jit(solution)/shard_map/reduce_scatter | solution.py:167
  24.5 2.6 %collective-permute-start.1 = (bf16[4,24,32,128]{3,2,1,0:T(8,128)(2,1)}, bf16[4,24,32,128]{3,2,1,0:T(8,128)(2,1)S(1)}, u32[]{:S(2)}, u32[]{:S(2)}) collective-permute-start(bf16[4,24,32,128]{3,2,1,0:T(8,128)(2,1)} %get-tuple-element.22), channel_id=1, source_target_pairs={{0,2},{2,0},{4,6},{6,4},{1,3},{3,1},{5,7},{7,5},{8,10},{10,8},{12,... | collective-permute-start | bytes 2359304 | tf_op jit(solution)/shard_map/ppermute | solution.py:136
  25.0 4.4 %collective-permute-start.2 = (bf16[4,24,32,128]{3,2,1,0:T(8,128)(2,1)}, bf16[4,24,32,128]{3,2,1,0:T(8,128)(2,1)S(1)}, u32[]{:S(2)}, u32[]{:S(2)}) collective-permute-start(bf16[4,24,32,128]{3,2,1,0:T(8,128)(2,1)} %get-tuple-element.23), channel_id=1, source_target_pairs={{0,2},{2,0},{4,6},{6,4},{1,3},{3,1},{5,7},{7,5},{8,10},{10,8},{12,... | collective-permute-start | bytes 2359304 | tf_op jit(solution)/shard_map/ppermute | solution.py:136
  25.5 4.7 %collective-permute-start.3 = (bf16[4,24,32,128]{3,2,1,0:T(8,128)(2,1)S(1)}, bf16[4,24,32,128]{3,2,1,0:T(8,128)(2,1)S(1)}, u32[]{:S(2)}, u32[]{:S(2)}) collective-permute-start(bf16[4,24,32,128]{3,2,1,0:T(8,128)(2,1)S(1)} %copy-done.30), channel_id=1, source_target_pairs={{0,2},{2,0},{4,6},{6,4},{1,3},{3,1},{5,7},{7,5},{8,10},{10,8},{12,... | collective-permute-start | bytes 2359304 | tf_op jit(solution)/shard_map/ppermute | solution.py:136
  31.6 20.9 %collective-permute-start.5 = (bf16[4,24,32,128]{3,2,1,0:T(8,128)(2,1)S(1)}, bf16[4,24,32,128]{3,2,1,0:T(8,128)(2,1)}, u32[]{:S(2)}, u32[]{:S(2)}) collective-permute-start(bf16[4,24,32,128]{3,2,1,0:T(8,128)(2,1)S(1)} %add_convert_fusion.7.refs_0_), channel_id=1, source_target_pairs={{0,4},{2,6},{4,0},{6,2},{1,5},{3,7},{5,1},{7,3},{8,12},{10,14},{12... | collective-permute-start | bytes 2359304 | tf_op jit(solution)/shard_map/ppermute | solution.py:136
  34.5 25.0 %collective-permute-start.4 = (bf16[4,24,32,128]{3,2,1,0:T(8,128)(2,1)}, bf16[4,24,32,128]{3,2,1,0:T(8,128)(2,1)S(1)}, u32[]{:S(2)}, u32[]{:S(2)}) collective-permute-start(bf16[4,24,32,128]{3,2,1,0:T(8,128)(2,1)} %get-tuple-element.26), channel_id=1, source_target_pairs={{0,2},{2,0},{4,6},{6,4},{1,3},{3,1},{5,7},{7,5},{8,10},{10,8},{12,... | collective-permute-start | bytes 2359304 | tf_op jit(solution)/shard_map/ppermute | solution.py:136
  34.5 17.9 %copy-start.3 = (bf16[4,24,32,128]{3,2,1,0:T(8,128)(2,1)S(1)}, bf16[4,24,32,128]{3,2,1,0:T(8,128)(2,1)}, u32[]{:S(2)}) copy-start(bf16[4,24,32,128]{3,2,1,0:T(8,128)(2,1)} %copy-done.2) | copy-start | bytes 2359300
  34.5 17.9 %copy-start.29 = (bf16[4,24,32,128]{3,2,1,0:T(8,128)(2,1)S(1)}, bf16[4,24,32,128]{3,2,1,0:T(8,128)(2,1)}, u32[]{:S(2)}) copy-start(bf16[4,24,32,128]{3,2,1,0:T(8,128)(2,1)} %get-tuple-element.28) | copy-start | bytes 2359300
  54.7 23.1 %collective-permute-start.8 = (bf16[24,32,128]{2,1,0:T(8,128)(2,1)S(1)}, bf16[24,32,128]{2,1,0:T(8,128)(2,1)S(1)}, u32[]{:S(2)}, u32[]{:S(2)}) collective-permute-start(bf16[24,32,128]{2,1,0:T(8,128)(2,1)S(1)} %get-tuple-element.57), channel_id=1, source_target_pairs={{0,24},{8,0},{16,8},{24,16},{1,25},{9,1},{17,9},{25,17},{2,26},{10... | collective-permute-start | bytes 589832 | tf_op jit(solution)/shard_map/ppermute | solution.py:151
  58.5 19.3 %collective-permute-start.7 = (bf16[24,32,128]{2,1,0:T(8,128)(2,1)S(1)}, bf16[24,32,128]{2,1,0:T(8,128)(2,1)S(1)}, u32[]{:S(2)}, u32[]{:S(2)}) collective-permute-start(bf16[24,32,128]{2,1,0:T(8,128)(2,1)S(1)} %get-tuple-element.58), channel_id=1, source_target_pairs={{0,16},{8,24},{16,0},{24,8},{1,17},{9,25},{17,1},{25,9},{2,18},{10... | collective-permute-start | bytes 589832 | tf_op jit(solution)/shard_map/ppermute | solution.py:151
  58.6 19.3 %collective-permute-start.6 = (bf16[24,32,128]{2,1,0:T(8,128)(2,1)S(1)}, bf16[24,32,128]{2,1,0:T(8,128)(2,1)S(1)}, u32[]{:S(2)}, u32[]{:S(2)}) collective-permute-start(bf16[24,32,128]{2,1,0:T(8,128)(2,1)S(1)} %get-tuple-element.59), channel_id=1, source_target_pairs={{0,8},{8,16},{16,24},{24,0},{1,9},{9,17},{17,25},{25,1},{2,10},{10... | collective-permute-start | bytes 589832 | tf_op jit(solution)/shard_map/ppermute | solution.py:151
  78.7 18.2 %copy-start.1 = (bf16[4,24,32,128]{3,2,1,0:T(8,128)(2,1)S(1)}, bf16[4,24,32,128]{3,2,1,0:T(8,128)(2,1)}, u32[]{:S(2)}) copy-start(bf16[4,24,32,128]{3,2,1,0:T(8,128)(2,1)} %copy-done) | copy-start | bytes 2359300
  78.7 18.2 %collective-permute-start.10 = (bf16[4,24,32,128]{3,2,1,0:T(8,128)(2,1)}, bf16[4,24,32,128]{3,2,1,0:T(8,128)(2,1)S(1)}, u32[]{:S(2)}, u32[]{:S(2)}) collective-permute-start(bf16[4,24,32,128]{3,2,1,0:T(8,128)(2,1)} %add_convert_fusion.6.refs_1_), channel_id=1, source_target_pairs={{0,4},{2,6},{4,0},{6,2},{1,5},{3,7},{5,1},{7,3},{8,12},{10,14},{12... | collective-permute-start | bytes 2359304 | tf_op jit(solution)/shard_map/ppermute | solution.py:136
  80.2 22.3 %collective-permute-start.14 = (bf16[4,24,32,128]{3,2,1,0:T(8,128)(2,1)}, bf16[4,24,32,128]{3,2,1,0:T(8,128)(2,1)S(1)}, u32[]{:S(2)}, u32[]{:S(2)}) collective-permute-start(bf16[4,24,32,128]{3,2,1,0:T(8,128)(2,1)} %get-tuple-element.31), channel_id=1, source_target_pairs={{0,2},{2,0},{4,6},{6,4},{1,3},{3,1},{5,7},{7,5},{8,10},{10,8},{12,... | collective-permute-start | bytes 2359304 | tf_op jit(solution)/shard_map/ppermute | solution.py:136
  80.2 23.2 %collective-permute-start.15 = (bf16[4,24,32,128]{3,2,1,0:T(8,128)(2,1)}, bf16[4,24,32,128]{3,2,1,0:T(8,128)(2,1)S(1)}, u32[]{:S(2)}, u32[]{:S(2)}) collective-permute-start(bf16[4,24,32,128]{3,2,1,0:T(8,128)(2,1)} %get-tuple-element.33), channel_id=1, source_target_pairs={{0,2},{2,0},{4,6},{6,4},{1,3},{3,1},{5,7},{7,5},{8,10},{10,8},{12,... | collective-permute-start | bytes 2359304 | tf_op jit(solution)/shard_map/ppermute | solution.py:136
  80.7 23.6 %collective-permute-start.16 = (bf16[4,24,32,128]{3,2,1,0:T(8,128)(2,1)}, bf16[4,24,32,128]{3,2,1,0:T(8,128)(2,1)}, u32[]{:S(2)}, u32[]{:S(2)}) collective-permute-start(bf16[4,24,32,128]{3,2,1,0:T(8,128)(2,1)} %get-tuple-element.34), channel_id=1, source_target_pairs={{0,2},{2,0},{4,6},{6,4},{1,3},{3,1},{5,7},{7,5},{8,10},{10,8},{12,... | collective-permute-start | bytes 2359304 | tf_op jit(solution)/shard_map/ppermute | solution.py:136
  80.8 27.7 %collective-permute-start.18 = (bf16[4,24,32,128]{3,2,1,0:T(8,128)(2,1)}, bf16[4,24,32,128]{3,2,1,0:T(8,128)(2,1)}, u32[]{:S(2)}, u32[]{:S(2)}) collective-permute-start(bf16[4,24,32,128]{3,2,1,0:T(8,128)(2,1)} %get-tuple-element.37), channel_id=1, source_target_pairs={{0,2},{2,0},{4,6},{6,4},{1,3},{3,1},{5,7},{7,5},{8,10},{10,8},{12,... | collective-permute-start | bytes 2359304 | tf_op jit(solution)/shard_map/ppermute | solution.py:136
  99.4 13.0 %collective-permute-start.13 = (bf16[24,32,128]{2,1,0:T(8,128)(2,1)S(1)}, bf16[24,32,128]{2,1,0:T(8,128)(2,1)S(1)}, u32[]{:S(2)}, u32[]{:S(2)}) collective-permute-start(bf16[24,32,128]{2,1,0:T(8,128)(2,1)S(1)} %get-tuple-element.61), channel_id=1, source_target_pairs={{0,24},{8,0},{16,8},{24,16},{1,25},{9,1},{17,9},{25,17},{2,26},{10... | collective-permute-start | bytes 589832 | tf_op jit(solution)/shard_map/ppermute | solution.py:151
  102.5 18.2 %collective-permute-start.12 = (bf16[24,32,128]{2,1,0:T(8,128)(2,1)S(1)}, bf16[24,32,128]{2,1,0:T(8,128)(2,1)}, u32[]{:S(2)}, u32[]{:S(2)}) collective-permute-start(bf16[24,32,128]{2,1,0:T(8,128)(2,1)S(1)} %get-tuple-element.62), channel_id=1, source_target_pairs={{0,16},{8,24},{16,0},{24,8},{1,17},{9,25},{17,1},{25,9},{2,18},{10... | collective-permute-start | bytes 589832 | tf_op jit(solution)/shard_map/ppermute | solution.py:151
  103.4 20.3 %collective-permute-start.11 = (bf16[24,32,128]{2,1,0:T(8,128)(2,1)}, bf16[24,32,128]{2,1,0:T(8,128)(2,1)S(1)}, u32[]{:S(2)}, u32[]{:S(2)}) collective-permute-start(bf16[24,32,128]{2,1,0:T(8,128)(2,1)} %get-tuple-element.63), channel_id=1, source_target_pairs={{0,8},{8,16},{16,24},{24,0},{1,9},{9,17},{17,25},{25,1},{2,10},{10... | collective-permute-start | bytes 589832 | tf_op jit(solution)/shard_map/ppermute | solution.py:151
  106.9 20.8 %collective-permute-start.17 = (bf16[4,24,32,128]{3,2,1,0:T(8,128)(2,1)}, bf16[4,24,32,128]{3,2,1,0:T(8,128)(2,1)}, u32[]{:S(2)}, u32[]{:S(2)}) collective-permute-start(bf16[4,24,32,128]{3,2,1,0:T(8,128)(2,1)} %add_convert_fusion.3), channel_id=1, source_target_pairs={{0,4},{2,6},{4,0},{6,2},{1,5},{3,7},{5,1},{7,3},{8,12},{10,14},{12... | collective-permute-start | bytes 2359304 | tf_op jit(solution)/shard_map/ppermute | solution.py:136
  108.4 15.4 %copy-start.10 = (bf16[24,32,128]{2,1,0:T(8,128)(2,1)S(1)}, bf16[24,32,128]{2,1,0:T(8,128)(2,1)}, u32[]{:S(2)}) copy-start(bf16[24,32,128]{2,1,0:T(8,128)(2,1)} %copy-done.9) | copy-start | bytes 589828
  108.5 24.2 %collective-permute-start = (bf16[32,12288]{1,0:T(8,128)(2,1)}, bf16[32,12288]{1,0:T(8,128)(2,1)S(1)}, u32[]{:S(2)}, u32[]{:S(2)}) collective-permute-start(bf16[32,12288]{1,0:T(8,128)(2,1)} %reduce-scatter.3.cloned.1.call-done), channel_id=1, source_target_pairs={{8,0},{16,8},{24,16},{9,1},{17,9},{25,17},{10,2},{18,10},{26,18},{... | collective-permute-start | bytes 2359304 | tf_op jit(solution)/shard_map/ppermute | solution.py:142
  112.4 28.3 %collective-permute-start.19 = (bf16[4,24,32,128]{3,2,1,0:T(8,128)(2,1)}, bf16[4,24,32,128]{3,2,1,0:T(8,128)(2,1)S(1)}, u32[]{:S(2)}, u32[]{:S(2)}) collective-permute-start(bf16[4,24,32,128]{3,2,1,0:T(8,128)(2,1)} %add_convert_fusion.1), channel_id=1, source_target_pairs={{0,4},{2,6},{4,0},{6,2},{1,5},{3,7},{5,1},{7,3},{8,12},{10,14},{12... | collective-permute-start | bytes 2359304 | tf_op jit(solution)/shard_map/ppermute | solution.py:136
  122.4 18.3 %collective-permute-start.9 = (bf16[32,12288]{1,0:T(8,128)(2,1)}, bf16[32,12288]{1,0:T(8,128)(2,1)S(1)}, u32[]{:S(2)}, u32[]{:S(2)}) collective-permute-start(bf16[32,12288]{1,0:T(8,128)(2,1)} %reduce-scatter.5.cloned.1.call-done), channel_id=1, source_target_pairs={{0,8},{8,16},{16,24},{1,9},{9,17},{17,25},{2,10},{10,18},{18,26},{... | collective-permute-start | bytes 2359304 | tf_op jit(solution)/shard_map/ppermute | solution.py:142
  136.1 13.2 %collective-permute-start.24 = (bf16[24,32,128]{2,1,0:T(8,128)(2,1)}, bf16[24,32,128]{2,1,0:T(8,128)(2,1)}, u32[]{:S(2)}, u32[]{:S(2)}) collective-permute-start(bf16[24,32,128]{2,1,0:T(8,128)(2,1)} %get-tuple-element.49), channel_id=1, source_target_pairs={{0,24},{8,0},{16,8},{24,16},{1,25},{9,1},{17,9},{25,17},{2,26},{10... | collective-permute-start | bytes 589832 | tf_op jit(solution)/shard_map/ppermute | solution.py:151
  136.1 30.4 %collective-permute-start.22 = (bf16[24,32,128]{2,1,0:T(8,128)(2,1)}, bf16[24,32,128]{2,1,0:T(8,128)(2,1)}, u32[]{:S(2)}, u32[]{:S(2)}) collective-permute-start(bf16[24,32,128]{2,1,0:T(8,128)(2,1)} %get-tuple-element.50), channel_id=1, source_target_pairs={{0,16},{8,24},{16,0},{24,8},{1,17},{9,25},{17,1},{25,9},{2,18},{10... | collective-permute-start | bytes 589832 | tf_op jit(solution)/shard_map/ppermute | solution.py:151
  140.7 33.4 %collective-permute-start.20 = (bf16[24,32,128]{2,1,0:T(8,128)(2,1)}, bf16[24,32,128]{2,1,0:T(8,128)(2,1)}, u32[]{:S(2)}, u32[]{:S(2)}) collective-permute-start(bf16[24,32,128]{2,1,0:T(8,128)(2,1)} %get-tuple-element.51), channel_id=1, source_target_pairs={{0,8},{8,16},{16,24},{24,0},{1,9},{9,17},{17,25},{25,1},{2,10},{10... | collective-permute-start | bytes 589832 | tf_op jit(solution)/shard_map/ppermute | solution.py:151
  144.0 11.8 %collective-permute-start.25 = (bf16[24,32,128]{2,1,0:T(8,128)(2,1)S(1)}, bf16[24,32,128]{2,1,0:T(8,128)(2,1)S(1)}, u32[]{:S(2)}, u32[]{:S(2)}) collective-permute-start(bf16[24,32,128]{2,1,0:T(8,128)(2,1)S(1)} %get-tuple-element.53), channel_id=1, source_target_pairs={{0,24},{8,0},{16,8},{24,16},{1,25},{9,1},{17,9},{25,17},{2,26},{10... | collective-permute-start | bytes 589832 | tf_op jit(solution)/shard_map/ppermute | solution.py:151
  147.9 25.2 %collective-permute-start.23 = (bf16[24,32,128]{2,1,0:T(8,128)(2,1)S(1)}, bf16[24,32,128]{2,1,0:T(8,128)(2,1)S(1)}, u32[]{:S(2)}, u32[]{:S(2)}) collective-permute-start(bf16[24,32,128]{2,1,0:T(8,128)(2,1)S(1)} %get-tuple-element.54), channel_id=1, source_target_pairs={{0,16},{8,24},{16,0},{24,8},{1,17},{9,25},{17,1},{25,9},{2,18},{10... | collective-permute-start | bytes 589832 | tf_op jit(solution)/shard_map/ppermute | solution.py:151
  149.3 24.8 %collective-permute-start.21 = (bf16[24,32,128]{2,1,0:T(8,128)(2,1)S(1)}, bf16[24,32,128]{2,1,0:T(8,128)(2,1)S(1)}, u32[]{:S(2)}, u32[]{:S(2)}) collective-permute-start(bf16[24,32,128]{2,1,0:T(8,128)(2,1)S(1)} %get-tuple-element.55), channel_id=1, source_target_pairs={{0,8},{8,16},{16,24},{24,0},{1,9},{9,17},{17,25},{25,1},{2,10},{10... | collective-permute-start | bytes 589832 | tf_op jit(solution)/shard_map/ppermute | solution.py:151
  (27 other events, 85.0 us)
Sparse Core Ops, SparseCore 0:
  24.5 28.7 reduce-scatter.2
  78.8 26.5 reduce-scatter.4

commit v12 on v11

--- a/solution.py
+++ b/solution.py
@@ -180,10 +180,10 @@
     came0 = [flip_bit(v, "dp", 2) for v in sums]
     *slots, share1 = tick(1, sections, n_dp, n_mp, True, sums, *args)
     b0, hot0, b2, hot2 = core_pair(slots)
-    first = on_section(a0[0], got0[0], came0[0])
-    deps = [came0[1], *first[1:], *hot0]
+    first = on_section(a0[0], got0[0], tie(came0[0], sums[1]))
+    deps = [came0[1], *first[1:]]
     came1 = [flip_bit(total(tie(k, *deps), g).astype(jnp.bfloat16), "dp", 2) for k, g in zip(b2, hot2)]
-    second = on_section(a0[1], got0[1], came0[1])
+    second = on_section(tie(a0[1], *hot0), got0[1], came0[1])
     passed0 = from_behind(scatter(share0), "section", -1)
     passed1 = from_behind(scatter(tie(share1, *first[1:])), "section", 1)
     third = on_section(b0[0], hot0[0], tie(came1[0], passed0))

time: 187 us -> 188 us (level)
  other arithmetic: 24.4 us -> 26.4 us
    ppermute x12, waiting for transfers between devices: 38.3 us -> 34.3 us  [flip_bit(): lax.ppermute(value, axis, [(i, i ^ bit) for i in range(lax.axis_size(axis...]
    ppermute x12, waiting for transfers between devices: 23.3 us -> 25.4 us  [rotate(): lax.ppermute(part, axis, [(i, (i + k) % n) for i in range(n)])]
    unnamed x62 -> x60, local copies, waits for them, and re-layouts: 6.6 us -> 8.15 us
  transfers between devices with their start and end apart: 28 -> 28, of which waited for: 9 -> 10; matrix products, arithmetic and copies ran while one was open for 13% -> 14% of each run, Pallas kernels for 9% -> 9%
where the time goes in v12:
time: 188 us; the launch traced here: 187 us
  waiting for transfers between devices  65.6 us (35%)
  starting transfers between devices  35.3 us (19%)
  Pallas kernels  34.3 us (18%)
  other arithmetic  26.4 us (14%)
  between operations  14.4 us (8%)
  local copies, waits for them, and re-layouts  10.8 us (6%)
    pallas_call x2, Pallas kernels, tick(): pl.pallas_call(functools.partial(tick_kernel, relay, per_step, n_mp, apar...  34.3 us
    ppermute x12, waiting for transfers between devices, flip_bit(): lax.ppermute(value, axis, [(i, i ^ bit) for i in range(lax.axis_size(axis...  34.3 us
    ppermute x12, waiting for transfers between devices, rotate(): lax.ppermute(part, axis, [(i, (i + k) % n) for i in range(n)])  25.4 us
    ppermute x12, starting transfers between devices, rotate(): lax.ppermute(part, axis, [(i, (i + k) % n) for i in range(n)])  23.8 us
    ppermute x12, starting transfers between devices, flip_bit(): lax.ppermute(value, axis, [(i, i ^ bit) for i in range(lax.axis_size(axis...  8.61 us
    unnamed x60, local copies, waits for them, and re-layouts  8.15 us
    another operation x10, other arithmetic, by_source(): stacked = jnp.stack(parts)  7.87 us
    convert_element_type x4, other arithmetic, on_section(): return rotate(total(kept, got, came).astype(jnp.bfloat16), 'section')  6.31 us
  transfers between devices with their start and end apart: 28, of which 10 were waited for; matrix products, arithmetic and copies ran while one was open for 14% of the time, Pallas kernels for 9%

profile of v12, /device:TPU:0, one launch (start us, length us, event | category | flops | bytes accessed | tf_op | source)
XLA Modules:
  0.0 186.8 jit_solution(15757528302516691332)
XLA Ops:
  7.2 17.2 %tick0.1 = (bf16[4,24,32,128]{3,2,1,0:T(8,128)(2,1)}, bf16[4,24,32,128]{3,2,1,0:T(8,128)(2,1)}, bf16[4,24,32,128]{3,2,1,0:T(8,128)(2,1)}, bf16[4,24,32,128]{3,2,...) custom-call(s32[2]{0:T(128)} %bitcast.72, ...), custom_call_target="tpu_custom_call" | custom-call | flops 1006632960 | bytes 17301504 | tf_op jit(solution)/shard_map/tick0/pallas_call | solution.py:96
  25.6 1.5 collective-permute-done.1.refs_1_
  29.3 1.3 add_convert_fusion.7.refs_0_
  30.7 2.9 %collective-permute-start.5 = (bf16[4,24,32,128]{3,2,1,0:T(8,128)(2,1)S(1)}, bf16[4,24,32,128]{3,2,1,0:T(8,128)(2,1)S(1)}, u32[]{:S(2)}, u32[]{:S(2)}) collective-permute-start(bf16[4,24,32,128]{3,2,1,0:T(8,128)(2,1)S(1)} %add_convert_fusion.7.refs_0_), channel_id=1, source_target_pairs={{0,4},{2,6},{4,0},{6,2},{1,5},{3,7},{5,1},{7,3},{8,12},{10,14},{12... | collective-permute-start | bytes 2359304 | tf_op jit(solution)/shard_map/ppermute | solution.py:136
  33.6 2.2 %add_convert_fusion.6.refs_1_ = bf16[4,24,32,128]{3,2,1,0:T(8,128)(2,1)} fusion(bf16[4,24,32,128]{3,2,1,0:T(8,128)(2,1)S(1)} %collective-permute-done.4, bf16[4,24,32,128]{3,2,1,0:T(8,128)(2,1)} %tie.10), kind=kLoop, calls=%fused_computation.11 | loop fusion | flops 1572864 | bytes 2359296 | tf_op jit(solution)/shard_map/convert_element_type | solution.py:179
  35.9 15.6 %collective-permute-done.5.refs_0_ = bf16[4,24,32,128]{3,2,1,0:T(8,128)(2,1)S(1)} collective-permute-done((bf16[4,24,32,128]{3,2,1,0:T(8,128)(2,1)S(1)}, bf16[4,24,32,128]{3,2,1,0:T(8,128)(2,1)S(1)}, u32[]{:S(2)}, u32[]{:S(2)}) %collective-permute-start.5) | collective-permute-done | bytes 786464 | tf_op jit(solution)/shard_map/ppermute | solution.py:136
  52.4 1.5 add_convert_fusion.5
  53.9 3.9 %collective-permute-start.8 = (bf16[24,32,128]{2,1,0:T(8,128)(2,1)S(1)}, bf16[24,32,128]{2,1,0:T(8,128)(2,1)S(1)}, u32[]{:S(2)}, u32[]{:S(2)}) collective-permute-start(bf16[24,32,128]{2,1,0:T(8,128)(2,1)S(1)} %get-tuple-element.57), channel_id=1, source_target_pairs={{0,24},{8,0},{16,8},{24,16},{1,25},{9,1},{17,9},{25,17},{2,26},{10... | collective-permute-start | bytes 589832 | tf_op jit(solution)/shard_map/ppermute | solution.py:151
  58.8 17.1 %tick1.1 = (bf16[4,24,32,128]{3,2,1,0:T(8,128)(2,1)}, bf16[4,24,32,128]{3,2,1,0:T(8,128)(2,1)}, bf16[4,24,32,128]{3,2,1,0:T(8,128)(2,1)}, bf16[4,24,32,128]{3,2,...) custom-call(s32[2]{0:T(128)} %bitcast.73, ...), custom_call_target="tpu_custom_call" | custom-call | flops 1006632960 | bytes 17301504 | tf_op jit(solution)/shard_map/tick1/pallas_call | solution.py:96
  78.0 1.5 collective-permute-start.12
  81.8 15.2 %collective-permute-done.12.refs_1_ = bf16[4,24,32,128]{3,2,1,0:T(8,128)(2,1)S(1)} collective-permute-done((bf16[4,24,32,128]{3,2,1,0:T(8,128)(2,1)S(1)}, bf16[4,24,32,128]{3,2,1,0:T(8,128)(2,1)S(1)}, u32[]{:S(2)}, u32[]{:S(2)}) %collective-permute-start.12) | collective-permute-done | bytes 786464 | tf_op jit(solution)/shard_map/ppermute | solution.py:136
  97.0 1.7 add_convert_fusion.4
  98.8 2.9 %collective-permute-start.15 = (bf16[24,32,128]{2,1,0:T(8,128)(2,1)S(1)}, bf16[24,32,128]{2,1,0:T(8,128)(2,1)S(1)}, u32[]{:S(2)}, u32[]{:S(2)}) collective-permute-start(bf16[24,32,128]{2,1,0:T(8,128)(2,1)S(1)} %get-tuple-element.61), channel_id=1, source_target_pairs={{0,24},{8,0},{16,8},{24,16},{1,25},{9,1},{17,9},{25,17},{2,26},{10... | collective-permute-start | bytes 589832 | tf_op jit(solution)/shard_map/ppermute | solution.py:151
  102.8 2.5 %add_convert_fusion.3 = bf16[4,24,32,128]{3,2,1,0:T(8,128)(2,1)} fusion(bf16[4,24,32,128]{3,2,1,0:T(8,128)(2,1)} %collective-permute-done.16, bf16[4,24,32,128]{3,2,1,0:T(8,128)(2,1)} %tie.14), kind=kLoop, calls=%fused_computation.8 | loop fusion | flops 1572864 | bytes 2359296 | tf_op jit(solution)/shard_map/convert_element_type | solution.py:185
  105.4 1.5 collective-permute-start.17
  106.9 1.4 collective-permute-start
  108.3 2.5 %add_convert_fusion.1 = bf16[4,24,32,128]{3,2,1,0:T(8,128)(2,1)} fusion(bf16[4,24,32,128]{3,2,1,0:T(8,128)(2,1)} %collective-permute-done.18, bf16[4,24,32,128]{3,2,1,0:T(8,128)(2,1)} %tie.16), kind=kLoop, calls=%fused_computation.6 | loop fusion | flops 1572864 | bytes 2359296 | tf_op jit(solution)/shard_map/convert_element_type | solution.py:185
  112.2 8.7 %collective-permute-done.14 = bf16[24,32,128]{2,1,0:T(8,128)(2,1)} collective-permute-done((bf16[24,32,128]{2,1,0:T(8,128)(2,1)S(1)}, bf16[24,32,128]{2,1,0:T(8,128)(2,1)}, u32[]{:S(2)}, u32[]{:S(2)}) %collective-permute-start.14) | collective-permute-done | bytes 196640 | tf_op jit(solution)/shard_map/ppermute | solution.py:151
  120.9 1.7 maximum_bitcast_fusion.3
  122.6 1.3 collective-permute-start.9
  125.0 1.2 pad_maximum_fusion
  126.2 1.3 constant_dynamic-slice_fusion.9
  127.5 5.9 %collective-permute-done.refs_1_ = bf16[32,12288]{1,0:T(8,128)(2,1)S(1)} collective-permute-done((bf16[32,12288]{1,0:T(8,128)(2,1)}, bf16[32,12288]{1,0:T(8,128)(2,1)S(1)}, u32[]{:S(2)}, u32[]{:S(2)}) %collective-permute-start) | collective-permute-done | bytes 786464 | tf_op jit(solution)/shard_map/ppermute | solution.py:142
  134.3 1.7 add_convert_fusion.2
  136.9 4.4 %collective-permute-start.22 = (bf16[24,32,128]{2,1,0:T(8,128)(2,1)}, bf16[24,32,128]{2,1,0:T(8,128)(2,1)}, u32[]{:S(2)}, u32[]{:S(2)}) collective-permute-start(bf16[24,32,128]{2,1,0:T(8,128)(2,1)} %get-tuple-element.50), channel_id=1, source_target_pairs={{0,16},{8,24},{16,0},{24,8},{1,17},{9,25},{17,1},{25,9},{2,18},{10... | collective-permute-start | bytes 589832 | tf_op jit(solution)/shard_map/ppermute | solution.py:151
  143.0 1.4 add_convert_fusion
  144.6 3.9 %collective-permute-start.25 = (bf16[24,32,128]{2,1,0:T(8,128)(2,1)S(1)}, bf16[24,32,128]{2,1,0:T(8,128)(2,1)S(1)}, u32[]{:S(2)}, u32[]{:S(2)}) collective-permute-start(bf16[24,32,128]{2,1,0:T(8,128)(2,1)S(1)} %get-tuple-element.53), channel_id=1, source_target_pairs={{0,24},{8,0},{16,8},{24,16},{1,25},{9,1},{17,9},{25,17},{2,26},{10... | collective-permute-start | bytes 589832 | tf_op jit(solution)/shard_map/ppermute | solution.py:151
  148.5 1.3 maximum_bitcast_fusion
  149.8 6.6 %collective-permute-start.21 = (bf16[24,32,128]{2,1,0:T(8,128)(2,1)S(1)}, bf16[24,32,128]{2,1,0:T(8,128)(2,1)S(1)}, u32[]{:S(2)}, u32[]{:S(2)}) collective-permute-start(bf16[24,32,128]{2,1,0:T(8,128)(2,1)S(1)} %get-tuple-element.55), channel_id=1, source_target_pairs={{0,8},{8,16},{16,24},{24,0},{1,9},{9,17},{17,25},{25,1},{2,10},{10... | collective-permute-start | bytes 589832 | tf_op jit(solution)/shard_map/ppermute | solution.py:151
  157.4 10.0 %collective-permute-done.22 = bf16[24,32,128]{2,1,0:T(8,128)(2,1)} collective-permute-done((bf16[24,32,128]{2,1,0:T(8,128)(2,1)}, bf16[24,32,128]{2,1,0:T(8,128)(2,1)}, u32[]{:S(2)}, u32[]{:S(2)}) %collective-permute-start.22) | collective-permute-done | bytes 196640 | tf_op jit(solution)/shard_map/ppermute | solution.py:151
  167.3 6.6 %collective-permute-done.23 = bf16[24,32,128]{2,1,0:T(8,128)(2,1)S(1)} collective-permute-done((bf16[24,32,128]{2,1,0:T(8,128)(2,1)S(1)}, bf16[24,32,128]{2,1,0:T(8,128)(2,1)S(1)}, u32[]{:S(2)}, u32[]{:S(2)}) %collective-permute-start.23) | collective-permute-done | bytes 196640 | tf_op jit(solution)/shard_map/ppermute | solution.py:151
  177.8 2.2 %add_bitcast_fusion = f32[4,2,1,24,32,128]{5,4,3,2,1,0:T(8,128)} fusion(bf16[1,2,24,32,128]{4,3,2,1,0:T(8,128)(2,1)S(1)} %copy-done.25, bf16[1,2,24,32,128]{4,3,2,1,0:T(8,128)(2,1)S(1)} %copy-done.26, bf16[1,2,24,32,128]{4,3,2,1,0:T(8,128)(2,1)S(1)} %copy-done.27, bf16[1,2,24,32,128]{4,3,2,1,0:T(8,128)(2,1)S(1)} %copy-done.24, ...), kind=kLoop, calls=%fused_computation | loop fusion | flops 7864320 | bytes 6291456
  (124 shorter events, 21.6 us)
Async XLA Ops:
  7.2 99.7 %reduce-scatter.3.cloned.1.call-start = ((), (), s32[]{:S(2)}) async-start(), calls=%async_computation.2 | async-start | bytes 2359296 | tf_op jit(solution)/shard_map/reduce_scatter | solution.py:167
  24.4 98.2 %reduce-scatter.5.cloned.1.call-start = ((), (), s32[]{:S(2)}) async-start(), calls=%async_computation.3 | async-start | bytes 2359296 | tf_op jit(solution)/shard_map/reduce_scatter | solution.py:167
  24.4 2.6 %collective-permute-start.1 = (bf16[4,24,32,128]{3,2,1,0:T(8,128)(2,1)}, bf16[4,24,32,128]{3,2,1,0:T(8,128)(2,1)S(1)}, u32[]{:S(2)}, u32[]{:S(2)}) collective-permute-start(bf16[4,24,32,128]{3,2,1,0:T(8,128)(2,1)} %get-tuple-element.22), channel_id=1, source_target_pairs={{0,2},{2,0},{4,6},{6,4},{1,3},{3,1},{5,7},{7,5},{8,10},{10,8},{12,... | collective-permute-start | bytes 2359304 | tf_op jit(solution)/shard_map/ppermute | solution.py:136
  25.0 3.2 %collective-permute-start.2 = (bf16[4,24,32,128]{3,2,1,0:T(8,128)(2,1)}, bf16[4,24,32,128]{3,2,1,0:T(8,128)(2,1)S(1)}, u32[]{:S(2)}, u32[]{:S(2)}) collective-permute-start(bf16[4,24,32,128]{3,2,1,0:T(8,128)(2,1)} %get-tuple-element.23), channel_id=1, source_target_pairs={{0,2},{2,0},{4,6},{6,4},{1,3},{3,1},{5,7},{7,5},{8,10},{10,8},{12,... | collective-permute-start | bytes 2359304 | tf_op jit(solution)/shard_map/ppermute | solution.py:136
  25.0 4.3 %collective-permute-start.3 = (bf16[4,24,32,128]{3,2,1,0:T(8,128)(2,1)}, bf16[4,24,32,128]{3,2,1,0:T(8,128)(2,1)S(1)}, u32[]{:S(2)}, u32[]{:S(2)}) collective-permute-start(bf16[4,24,32,128]{3,2,1,0:T(8,128)(2,1)} %get-tuple-element.24), channel_id=1, source_target_pairs={{0,2},{2,0},{4,6},{6,4},{1,3},{3,1},{5,7},{7,5},{8,10},{10,8},{12,... | collective-permute-start | bytes 2359304 | tf_op jit(solution)/shard_map/ppermute | solution.py:136
  25.5 8.1 %collective-permute-start.4 = (bf16[4,24,32,128]{3,2,1,0:T(8,128)(2,1)}, bf16[4,24,32,128]{3,2,1,0:T(8,128)(2,1)S(1)}, u32[]{:S(2)}, u32[]{:S(2)}) collective-permute-start(bf16[4,24,32,128]{3,2,1,0:T(8,128)(2,1)} %get-tuple-element.26), channel_id=1, source_target_pairs={{0,2},{2,0},{4,6},{6,4},{1,3},{3,1},{5,7},{7,5},{8,10},{10,8},{12,... | collective-permute-start | bytes 2359304 | tf_op jit(solution)/shard_map/ppermute | solution.py:136
  30.7 20.8 %collective-permute-start.5 = (bf16[4,24,32,128]{3,2,1,0:T(8,128)(2,1)S(1)}, bf16[4,24,32,128]{3,2,1,0:T(8,128)(2,1)S(1)}, u32[]{:S(2)}, u32[]{:S(2)}) collective-permute-start(bf16[4,24,32,128]{3,2,1,0:T(8,128)(2,1)S(1)} %add_convert_fusion.7.refs_0_), channel_id=1, source_target_pairs={{0,4},{2,6},{4,0},{6,2},{1,5},{3,7},{5,1},{7,3},{8,12},{10,14},{12... | collective-permute-start | bytes 2359304 | tf_op jit(solution)/shard_map/ppermute | solution.py:136
  35.9 16.5 %copy-start.4 = (bf16[4,24,32,128]{3,2,1,0:T(8,128)(2,1)S(1)}, bf16[4,24,32,128]{3,2,1,0:T(8,128)(2,1)}, u32[]{:S(2)}) copy-start(bf16[4,24,32,128]{3,2,1,0:T(8,128)(2,1)} %copy-done.3) | copy-start | bytes 2359300
  35.9 16.5 %copy-start.29 = (bf16[4,24,32,128]{3,2,1,0:T(8,128)(2,1)S(1)}, bf16[4,24,32,128]{3,2,1,0:T(8,128)(2,1)}, u32[]{:S(2)}) copy-start(bf16[4,24,32,128]{3,2,1,0:T(8,128)(2,1)} %get-tuple-element.28) | copy-start | bytes 2359300
  53.9 22.1 %collective-permute-start.8 = (bf16[24,32,128]{2,1,0:T(8,128)(2,1)S(1)}, bf16[24,32,128]{2,1,0:T(8,128)(2,1)S(1)}, u32[]{:S(2)}, u32[]{:S(2)}) collective-permute-start(bf16[24,32,128]{2,1,0:T(8,128)(2,1)S(1)} %get-tuple-element.57), channel_id=1, source_target_pairs={{0,24},{8,0},{16,8},{24,16},{1,25},{9,1},{17,9},{25,17},{2,26},{10... | collective-permute-start | bytes 589832 | tf_op jit(solution)/shard_map/ppermute | solution.py:151
  57.8 18.2 %collective-permute-start.7 = (bf16[24,32,128]{2,1,0:T(8,128)(2,1)S(1)}, bf16[24,32,128]{2,1,0:T(8,128)(2,1)S(1)}, u32[]{:S(2)}, u32[]{:S(2)}) collective-permute-start(bf16[24,32,128]{2,1,0:T(8,128)(2,1)S(1)} %get-tuple-element.58), channel_id=1, source_target_pairs={{0,16},{8,24},{16,0},{24,8},{1,17},{9,25},{17,1},{25,9},{2,18},{10... | collective-permute-start | bytes 589832 | tf_op jit(solution)/shard_map/ppermute | solution.py:151
  57.8 18.2 %collective-permute-start.6 = (bf16[24,32,128]{2,1,0:T(8,128)(2,1)S(1)}, bf16[24,32,128]{2,1,0:T(8,128)(2,1)S(1)}, u32[]{:S(2)}, u32[]{:S(2)}) collective-permute-start(bf16[24,32,128]{2,1,0:T(8,128)(2,1)S(1)} %get-tuple-element.59), channel_id=1, source_target_pairs={{0,8},{8,16},{16,24},{24,0},{1,9},{9,17},{17,25},{25,1},{2,10},{10... | collective-permute-start | bytes 589832 | tf_op jit(solution)/shard_map/ppermute | solution.py:151
  76.9 3.1 %collective-permute-start.10 = (bf16[4,24,32,128]{3,2,1,0:T(8,128)(2,1)}, bf16[4,24,32,128]{3,2,1,0:T(8,128)(2,1)S(1)}, u32[]{:S(2)}, u32[]{:S(2)}) collective-permute-start(bf16[4,24,32,128]{3,2,1,0:T(8,128)(2,1)} %get-tuple-element.30), channel_id=1, source_target_pairs={{0,2},{2,0},{4,6},{6,4},{1,3},{3,1},{5,7},{7,5},{8,10},{10,8},{12,... | collective-permute-start | bytes 2359304 | tf_op jit(solution)/shard_map/ppermute | solution.py:136
  76.9 3.6 %collective-permute-start.11 = (bf16[4,24,32,128]{3,2,1,0:T(8,128)(2,1)}, bf16[4,24,32,128]{3,2,1,0:T(8,128)(2,1)S(1)}, u32[]{:S(2)}, u32[]{:S(2)}) collective-permute-start(bf16[4,24,32,128]{3,2,1,0:T(8,128)(2,1)} %get-tuple-element.31), channel_id=1, source_target_pairs={{0,2},{2,0},{4,6},{6,4},{1,3},{3,1},{5,7},{7,5},{8,10},{10,8},{12,... | collective-permute-start | bytes 2359304 | tf_op jit(solution)/shard_map/ppermute | solution.py:136
  78.0 19.0 %collective-permute-start.12 = (bf16[4,24,32,128]{3,2,1,0:T(8,128)(2,1)S(1)}, bf16[4,24,32,128]{3,2,1,0:T(8,128)(2,1)S(1)}, u32[]{:S(2)}, u32[]{:S(2)}) collective-permute-start(bf16[4,24,32,128]{3,2,1,0:T(8,128)(2,1)S(1)} %copy-done), channel_id=1, source_target_pairs={{0,4},{2,6},{4,0},{6,2},{1,5},{3,7},{5,1},{7,3},{8,12},{10,14},{12... | collective-permute-start | bytes 2359304 | tf_op jit(solution)/shard_map/ppermute | solution.py:136
  79.4 23.4 %collective-permute-start.16 = (bf16[4,24,32,128]{3,2,1,0:T(8,128)(2,1)}, bf16[4,24,32,128]{3,2,1,0:T(8,128)(2,1)}, u32[]{:S(2)}, u32[]{:S(2)}) collective-permute-start(bf16[4,24,32,128]{3,2,1,0:T(8,128)(2,1)} %get-tuple-element.34), channel_id=1, source_target_pairs={{0,2},{2,0},{4,6},{6,4},{1,3},{3,1},{5,7},{7,5},{8,10},{10,8},{12,... | collective-permute-start | bytes 2359304 | tf_op jit(solution)/shard_map/ppermute | solution.py:136
  79.5 27.4 %collective-permute-start.18 = (bf16[4,24,32,128]{3,2,1,0:T(8,128)(2,1)}, bf16[4,24,32,128]{3,2,1,0:T(8,128)(2,1)}, u32[]{:S(2)}, u32[]{:S(2)}) collective-permute-start(bf16[4,24,32,128]{3,2,1,0:T(8,128)(2,1)} %get-tuple-element.37), channel_id=1, source_target_pairs={{0,2},{2,0},{4,6},{6,4},{1,3},{3,1},{5,7},{7,5},{8,10},{10,8},{12,... | collective-permute-start | bytes 2359304 | tf_op jit(solution)/shard_map/ppermute | solution.py:136
  81.8 15.2 %copy-start.2 = (bf16[4,24,32,128]{3,2,1,0:T(8,128)(2,1)S(1)}, bf16[4,24,32,128]{3,2,1,0:T(8,128)(2,1)}, u32[]{:S(2)}) copy-start(bf16[4,24,32,128]{3,2,1,0:T(8,128)(2,1)} %copy-done.1) | copy-start | bytes 2359300
  98.8 12.0 %collective-permute-start.15 = (bf16[24,32,128]{2,1,0:T(8,128)(2,1)S(1)}, bf16[24,32,128]{2,1,0:T(8,128)(2,1)S(1)}, u32[]{:S(2)}, u32[]{:S(2)}) collective-permute-start(bf16[24,32,128]{2,1,0:T(8,128)(2,1)S(1)} %get-tuple-element.61), channel_id=1, source_target_pairs={{0,24},{8,0},{16,8},{24,16},{1,25},{9,1},{17,9},{25,17},{2,26},{10... | collective-permute-start | bytes 589832 | tf_op jit(solution)/shard_map/ppermute | solution.py:151
  101.6 19.3 %collective-permute-start.14 = (bf16[24,32,128]{2,1,0:T(8,128)(2,1)S(1)}, bf16[24,32,128]{2,1,0:T(8,128)(2,1)}, u32[]{:S(2)}, u32[]{:S(2)}) collective-permute-start(bf16[24,32,128]{2,1,0:T(8,128)(2,1)S(1)} %get-tuple-element.62), channel_id=1, source_target_pairs={{0,16},{8,24},{16,0},{24,8},{1,17},{9,25},{17,1},{25,9},{2,18},{10... | collective-permute-start | bytes 589832 | tf_op jit(solution)/shard_map/ppermute | solution.py:151
  102.8 21.2 %collective-permute-start.13 = (bf16[24,32,128]{2,1,0:T(8,128)(2,1)S(1)}, bf16[24,32,128]{2,1,0:T(8,128)(2,1)}, u32[]{:S(2)}, u32[]{:S(2)}) collective-permute-start(bf16[24,32,128]{2,1,0:T(8,128)(2,1)S(1)} %get-tuple-element.63), channel_id=1, source_target_pairs={{0,8},{8,16},{16,24},{24,0},{1,9},{9,17},{17,25},{25,1},{2,10},{10... | collective-permute-start | bytes 589832 | tf_op jit(solution)/shard_map/ppermute | solution.py:151
  105.4 22.1 %collective-permute-start.17 = (bf16[4,24,32,128]{3,2,1,0:T(8,128)(2,1)}, bf16[4,24,32,128]{3,2,1,0:T(8,128)(2,1)}, u32[]{:S(2)}, u32[]{:S(2)}) collective-permute-start(bf16[4,24,32,128]{3,2,1,0:T(8,128)(2,1)} %add_convert_fusion.3), channel_id=1, source_target_pairs={{0,4},{2,6},{4,0},{6,2},{1,5},{3,7},{5,1},{7,3},{8,12},{10,14},{12... | collective-permute-start | bytes 2359304 | tf_op jit(solution)/shard_map/ppermute | solution.py:136
  106.9 17.1 %copy-start.8 = (bf16[24,32,128]{2,1,0:T(8,128)(2,1)S(1)}, bf16[24,32,128]{2,1,0:T(8,128)(2,1)}, u32[]{:S(2)}) copy-start(bf16[24,32,128]{2,1,0:T(8,128)(2,1)} %copy-done.7) | copy-start | bytes 589828
  106.9 26.5 %collective-permute-start = (bf16[32,12288]{1,0:T(8,128)(2,1)}, bf16[32,12288]{1,0:T(8,128)(2,1)S(1)}, u32[]{:S(2)}, u32[]{:S(2)}) collective-permute-start(bf16[32,12288]{1,0:T(8,128)(2,1)} %reduce-scatter.3.cloned.1.call-done), channel_id=1, source_target_pairs={{8,0},{16,8},{24,16},{9,1},{17,9},{25,17},{10,2},{18,10},{26,18},{... | collective-permute-start | bytes 2359304 | tf_op jit(solution)/shard_map/ppermute | solution.py:142
  110.8 30.4 %collective-permute-start.19 = (bf16[4,24,32,128]{3,2,1,0:T(8,128)(2,1)}, bf16[4,24,32,128]{3,2,1,0:T(8,128)(2,1)S(1)}, u32[]{:S(2)}, u32[]{:S(2)}) collective-permute-start(bf16[4,24,32,128]{3,2,1,0:T(8,128)(2,1)} %add_convert_fusion.1), channel_id=1, source_target_pairs={{0,4},{2,6},{4,0},{6,2},{1,5},{3,7},{5,1},{7,3},{8,12},{10,14},{12... | collective-permute-start | bytes 2359304 | tf_op jit(solution)/shard_map/ppermute | solution.py:136
  122.6 18.6 %collective-permute-start.9 = (bf16[32,12288]{1,0:T(8,128)(2,1)}, bf16[32,12288]{1,0:T(8,128)(2,1)S(1)}, u32[]{:S(2)}, u32[]{:S(2)}) collective-permute-start(bf16[32,12288]{1,0:T(8,128)(2,1)} %reduce-scatter.5.cloned.1.call-done), channel_id=1, source_target_pairs={{0,8},{8,16},{16,24},{1,9},{9,17},{17,25},{2,10},{10,18},{18,26},{... | collective-permute-start | bytes 2359304 | tf_op jit(solution)/shard_map/ppermute | solution.py:142
  136.9 12.9 %collective-permute-start.24 = (bf16[24,32,128]{2,1,0:T(8,128)(2,1)}, bf16[24,32,128]{2,1,0:T(8,128)(2,1)}, u32[]{:S(2)}, u32[]{:S(2)}) collective-permute-start(bf16[24,32,128]{2,1,0:T(8,128)(2,1)} %get-tuple-element.49), channel_id=1, source_target_pairs={{0,24},{8,0},{16,8},{24,16},{1,25},{9,1},{17,9},{25,17},{2,26},{10... | collective-permute-start | bytes 589832 | tf_op jit(solution)/shard_map/ppermute | solution.py:151
  136.9 30.5 %collective-permute-start.22 = (bf16[24,32,128]{2,1,0:T(8,128)(2,1)}, bf16[24,32,128]{2,1,0:T(8,128)(2,1)}, u32[]{:S(2)}, u32[]{:S(2)}) collective-permute-start(bf16[24,32,128]{2,1,0:T(8,128)(2,1)} %get-tuple-element.50), channel_id=1, source_target_pairs={{0,16},{8,24},{16,0},{24,8},{1,17},{9,25},{17,1},{25,9},{2,18},{10... | collective-permute-start | bytes 589832 | tf_op jit(solution)/shard_map/ppermute | solution.py:151
  141.2 33.7 %collective-permute-start.20 = (bf16[24,32,128]{2,1,0:T(8,128)(2,1)}, bf16[24,32,128]{2,1,0:T(8,128)(2,1)}, u32[]{:S(2)}, u32[]{:S(2)}) collective-permute-start(bf16[24,32,128]{2,1,0:T(8,128)(2,1)} %get-tuple-element.51), channel_id=1, source_target_pairs={{0,8},{8,16},{16,24},{24,0},{1,9},{9,17},{17,25},{25,1},{2,10},{10... | collective-permute-start | bytes 589832 | tf_op jit(solution)/shard_map/ppermute | solution.py:151
  144.6 11.8 %collective-permute-start.25 = (bf16[24,32,128]{2,1,0:T(8,128)(2,1)S(1)}, bf16[24,32,128]{2,1,0:T(8,128)(2,1)S(1)}, u32[]{:S(2)}, u32[]{:S(2)}) collective-permute-start(bf16[24,32,128]{2,1,0:T(8,128)(2,1)S(1)} %get-tuple-element.53), channel_id=1, source_target_pairs={{0,24},{8,0},{16,8},{24,16},{1,25},{9,1},{17,9},{25,17},{2,26},{10... | collective-permute-start | bytes 589832 | tf_op jit(solution)/shard_map/ppermute | solution.py:151
  148.4 25.5 %collective-permute-start.23 = (bf16[24,32,128]{2,1,0:T(8,128)(2,1)S(1)}, bf16[24,32,128]{2,1,0:T(8,128)(2,1)S(1)}, u32[]{:S(2)}, u32[]{:S(2)}) collective-permute-start(bf16[24,32,128]{2,1,0:T(8,128)(2,1)S(1)} %get-tuple-element.54), channel_id=1, source_target_pairs={{0,16},{8,24},{16,0},{24,8},{1,17},{9,25},{17,1},{25,9},{2,18},{10... | collective-permute-start | bytes 589832 | tf_op jit(solution)/shard_map/ppermute | solution.py:151
  149.8 25.2 %collective-permute-start.21 = (bf16[24,32,128]{2,1,0:T(8,128)(2,1)S(1)}, bf16[24,32,128]{2,1,0:T(8,128)(2,1)S(1)}, u32[]{:S(2)}, u32[]{:S(2)}) collective-permute-start(bf16[24,32,128]{2,1,0:T(8,128)(2,1)S(1)} %get-tuple-element.55), channel_id=1, source_target_pairs={{0,8},{8,16},{16,24},{24,0},{1,9},{9,17},{17,25},{25,1},{2,10},{10... | collective-permute-start | bytes 589832 | tf_op jit(solution)/shard_map/ppermute | solution.py:151
  (26 other events, 78.5 us)
Sparse Core Ops, SparseCore 0:
  24.5 28.7 reduce-scatter.2
  77.0 26.4 reduce-scatter.4

commit v13 on v9

--- a/solution.py
+++ b/solution.py
@@ -14,16 +14,22 @@
 
 
 def tick_kernel(relay, per_step, n_mp, n_deps, len_ref, idx_in_ref, idx_out_ref, x_ref, g_ref, w_in_ref, w_out_ref, *refs):
-    *slot_refs, share_ref, acc_ref = refs[n_deps:]
+    if relay:
+        g0_ref, w0_ref, gp0_ref = refs[:3]
+        *slot_refs, share0_ref, share_ref, acc0_ref, acc_ref = refs[3 + n_deps:]
+    else:
+        *slot_refs, gp_ref = refs[n_deps:]
     step = pl.program_id(0)
     me = lax.axis_index("dp")
     rows, block = x_ref.shape[0], w_in_ref.shape[-1]
     piece = slot_refs[0].shape[2]
     live = lax.broadcasted_iota(jnp.int32, (rows, block), 0) < len_ref[relay]
 
-    @pl.when(step == 0)
-    def _():
-        acc_ref[...] = jnp.zeros_like(acc_ref)
+    if relay:
+        @pl.when(step == 0)
+        def _():
+            acc_ref[...] = jnp.zeros_like(acc_ref)
+            acc0_ref[...] = jnp.zeros_like(acc0_ref)
 
     odd, high = me % 2 == 1, me // 2 == 1
 
@@ -56,26 +62,40 @@
             act.append((v * cdf).astype(jnp.bfloat16))
             slope = cdf + (0.5 * v) * ((1.0 - th) * (1.0 + th)) * (SCALE * (1.0 + (3.0 * CUBIC) * square))
             grad_pre.append((up * slope).astype(jnp.bfloat16))
-        terms = [lax.dot_general(v, w_in_ref[i], over_last, preferred_element_type=f32) for v, i in zip(grad_pre, group)]
+        if relay:
+            terms = [lax.dot_general(v, w_in_ref[i], over_last, preferred_element_type=f32) for v, i in zip(grad_pre, group)]
+            sources0 = [idx_in_ref[0, 0, step * per_step + i] for i in group]
+            terms0 = [lax.dot_general(gp0_ref[i], w0_ref[i], over_last, preferred_element_type=f32) for i in group]
         grad_in = [lax.dot_general(a, v, over_rows, preferred_element_type=f32) for a, v in zip(picked, grad_pre)]
         grad_out = [lax.dot_general(a, v, over_rows, preferred_element_type=f32) for a, v in zip(act, back)]
-        for i, b, term, g_in, g_out in zip(group, sources, terms, grad_in, grad_out):
-            acc_ref[b] += term
+        if relay:
+            for b, term, b0, term0 in zip(sources, terms, sources0, terms0):
+                acc_ref[b] += term
+                acc0_ref[b0] += term0
+        else:
+            for i, v in zip(group, grad_pre):
+                gp_ref[i] = v
+        for i, g_in, g_out in zip(group, grad_in, grad_out):
             put(0, i, g_in)
             put(1, i, g_out)
+
+    if not relay:
+        return
 
     @pl.when(step == pl.num_programs(0) - 1)
     def _():
         share = rows // n_mp
-        owned = live & (lax.broadcasted_iota(jnp.int32, (rows, block), 0) // share == lax.axis_index("mp"))
-        for b in range(acc_ref.shape[0]):
-            columns = slice(b * block, (b + 1) * block)
-            held = g_ref[:, columns]
-            held = jnp.where(owned, held, jnp.zeros_like(held)).astype(jnp.float32)
-            share_ref[:, columns] = (acc_ref[b] + held).astype(jnp.bfloat16)
-
-
-def tick(relay, sections, n_dp, n_mp, deps, lengths, idx_in, idx_out, section_in, out_grad, w_in, w_out):
+        owned = (lax.broadcasted_iota(jnp.int32, (rows, block), 0) // share == lax.axis_index("mp"))
+        live0 = lax.broadcasted_iota(jnp.int32, (rows, block), 0) < len_ref[0]
+        for rows_live, held_ref, sum_ref, out_ref in ((live0, g0_ref, acc0_ref, share0_ref), (live, g_ref, acc_ref, share_ref)):
+            for b in range(acc_ref.shape[0]):
+                columns = slice(b * block, (b + 1) * block)
+                held = held_ref[:, columns]
+                held = jnp.where(rows_live & owned, held, jnp.zeros_like(held)).astype(jnp.float32)
+                out_ref[:, columns] = (sum_ref[b] + held).astype(jnp.bfloat16)
+
+
+def tick(relay, sections, n_dp, n_mp, deps, gp0, lengths, idx_in, idx_out, section_in, out_grad, w_in, w_out):
     rows, width = section_in.shape[2:]
     blocks, block = w_in.shape[2:4]
     per = blocks // sections
@@ -86,18 +106,31 @@
     weight = pl.BlockSpec((None, None, per_step, block, block), lambda i, *_: (0, relay, i, 0, 0))
     slots = jax.ShapeDtypeStruct((sections, 2, per, piece, block), jnp.bfloat16)
     slots_spec = pl.BlockSpec((None, 2, per_step, piece, block), lambda i, *_: (i // turns, 0, i % turns, 0, 0))
+    terms_spec = pl.BlockSpec((per_step, rows, block), lambda i, *_: (i, 0, 0))
+    acc = pltpu.VMEM((width // block, rows, block), jnp.float32)
+    share_spec = pl.BlockSpec((rows, width), lambda i, *_: (0, 0))
+    share = jax.ShapeDtypeStruct((rows, width), jnp.bfloat16)
+    extra_specs, extra = [], []
+    if relay:
+        extra_specs = [
+            pl.BlockSpec((None, None, rows, width), lambda i, *_: (0, 0, 0, 0)),
+            pl.BlockSpec((None, None, per_step, block, block), lambda i, *_: (0, 0, i, 0, 0)),
+            terms_spec,
+        ]
+        extra = [out_grad, w_in, gp0]
     return pl.pallas_call(
         functools.partial(tick_kernel, relay, per_step, n_mp, len(deps)),
         grid_spec=pltpu.PrefetchScalarGridSpec(
             num_scalar_prefetch=3,
             grid=(sections * turns,),
-            in_specs=[whole, whole, weight, weight] + [pl.BlockSpec(memory_space=pl.ANY)] * len(deps),
-            out_specs=[slots_spec] * 4 + [pl.BlockSpec((rows, width), lambda i, *_: (0, 0))],
-            scratch_shapes=[pltpu.VMEM((width // block, rows, block), jnp.float32)],
-        ),
-        out_shape=[slots] * 4 + [jax.ShapeDtypeStruct((rows, width), jnp.bfloat16)],
+            in_specs=[whole, whole, weight, weight] + extra_specs + [pl.BlockSpec(memory_space=pl.ANY)] * len(deps),
+            out_specs=[slots_spec] * 4 + ([share_spec] * 2 if relay else [terms_spec]),
+            scratch_shapes=[acc] * 2 if relay else [],
+        ),
+        out_shape=[slots] * 4
+        + ([share] * 2 if relay else [jax.ShapeDtypeStruct((blocks, rows, block), jnp.bfloat16)]),
         compiler_params=pltpu.CompilerParams(
-            dimension_semantics=("arbitrary",), vmem_limit_bytes=56 * 1024 * 1024
+            dimension_semantics=("arbitrary",), vmem_limit_bytes=58 * 1024 * 1024
         ),
         cost_estimate=pl.CostEstimate(
             flops=blocks * 10 * rows * block * block,
@@ -105,7 +138,7 @@
             transcendentals=blocks * rows * block,
         ),
         name=f"tick{relay}",
-    )(lengths, idx_in, idx_out, section_in, out_grad, w_in, w_out, *deps)
+    )(lengths, idx_in, idx_out, section_in, out_grad, w_in, w_out, *extra, *deps)
 
 
 def total(*parts):
@@ -159,11 +192,11 @@
     def scatter(share):
         return lax.psum_scatter(share, "mp", scatter_dimension=0, tiled=True)
 
-    a0, s0, a2, s2, share0 = tick(0, sections, n_dp, n_mp, [], *args)
+    a0, s0, a2, s2, gp0 = tick(0, sections, n_dp, n_mp, [], None, *args)
     got0, got2 = flip_bit(s0, "dp", 1), flip_bit(s2, "dp", 1)
     sum0 = total(a2, got2).astype(jnp.bfloat16)
     came0 = flip_bit(sum0, "dp", 2)
-    b0, t0, b2, t2, share1 = tick(1, sections, n_dp, n_mp, [sum0], *args)
+    b0, t0, b2, t2, share0, share1 = tick(1, sections, n_dp, n_mp, [sum0], gp0, *args)
     hot0, hot2 = flip_bit(t0, "dp", 1), flip_bit(t2, "dp", 1)
     dx0 = scatter(share0)
     sum1 = total(tie(b2, came0), hot2).astype(jnp.bfloat16)

time: 174 us -> 197 us (1.13)
  the two profiles are of different devices: /device:TPU:16 before, /device:TPU:20 now
where the time goes in v13:
time: 197 us; the launch traced here: 196 us
  waiting for transfers between devices  106 us (54%)
  Pallas kernels  36.6 us (19%)
  starting transfers between devices  17.5 us (9%)
  other arithmetic  17.4 us (9%)
  between operations  14.2 us (7%)
  local copies, waits for them, and re-layouts  4.56 us (2%)
    ppermute x6, waiting for transfers between devices, flip_bit(): lax.ppermute(value, axis, [(i, i ^ bit) for i in range(lax.axis_size(axis...  67.4 us
    pallas_call x2, Pallas kernels, tick(): pl.pallas_call(functools.partial(tick_kernel, relay, per_step, n_mp, len(...  36.6 us
    ppermute x6, waiting for transfers between devices, rotate(): lax.ppermute(part, axis, [(i, (i + k) % n) for i in range(n)])  26.4 us
    ppermute x2, waiting for transfers between devices, from_behind(): return lax.ppermute(value, axis, route)  11.9 us
    ppermute x6, starting transfers between devices, rotate(): lax.ppermute(part, axis, [(i, (i + k) % n) for i in range(n)])  7.97 us
    ppermute x2, starting transfers between devices, from_behind(): return lax.ppermute(value, axis, route)  5.89 us
  transfers between devices with their start and end apart: 16, of which 8 were waited for; matrix products, arithmetic and copies ran while one was open for 8% of the time, Pallas kernels for 0%

profile of v13, /device:TPU:20, one launch (start us, length us, event | category | flops | bytes accessed | tf_op | source)
XLA Modules:
  0.0 196.0 jit_solution(16141474673292463208)
XLA Ops:
  7.2 15.7 %tick0.1 = (bf16[4,2,24,32,128]{4,3,2,1,0:T(8,128)(2,1)}, bf16[4,2,24,32,128]{4,3,2,1,0:T(8,128)(2,1)}, bf16[4,2,24,32,128]{4,3,2,1,0:T(8,128)(2,1)}, bf16[4,2,2...) custom-call(s32[2]{0:T(128)} %bitcast.34, s32[1,2,96]{2,1,0:T(2,128)} %idx_in_ref.3, s32[1,2,96]{2,1,0:T(2,128)} %idx_out_ref.3, ...), custom_call_target="tpu_custom_call" | custom-call | flops 1006632960 | bytes 17301504 | tf_op jit(solution)/shard_map/tick0/pallas_call | solution.py:121
  23.0 3.6 %collective-permute-done = bf16[4,2,24,32,128]{4,3,2,1,0:T(8,128)(2,1)S(1)} collective-permute-done((bf16[4,2,24,32,128]{4,3,2,1,0:T(8,128)(2,1)}, bf16[4,2,24,32,128]{4,3,2,1,0:T(8,128)(2,1)S(1)}, u32[]{:S(2)}, u32[]{:S(2)}) %collective-permute-start) | collective-permute-done | bytes 1572896 | tf_op jit(solution)/shard_map/ppermute | solution.py:162
  26.6 3.0 %add_convert_fusion.3.refs_3_ = bf16[4,2,24,32,128]{4,3,2,1,0:T(8,128)(2,1)} fusion(bf16[4,2,24,32,128]{4,3,2,1,0:T(8,128)(2,1)S(1)} %collective-permute-done, bf16[4,2,24,32,128]{4,3,2,1,0:T(8,128)(2,1)} %get-tuple-element.14), kind=kLoop, calls=%fused_computation.4 | loop fusion | flops 3145728 | bytes 4718592 | tf_op jit(solution)/shard_map/convert_element_type | solution.py:197
  29.6 20.8 %tick1.1 = (bf16[4,2,24,32,128]{4,3,2,1,0:T(8,128)(2,1)}, bf16[4,2,24,32,128]{4,3,2,1,0:T(8,128)(2,1)}, bf16[4,2,24,32,128]{4,3,2,1,0:T(8,128)(2,1)}, bf16[4,2,2...) custom-call(s32[2]{0:T(128)} %bitcast.35, s32[1,2,96]{2,1,0:T(2,128)} %idx_in_ref.3, ...), custom_call_target="tpu_custom_call" | custom-call | flops 1006632960 | bytes 17301504 | tf_op jit(solution)/shard_map/tick1/pallas_call | solution.py:121
  50.5 1.3 copy-done.2
  51.8 1.5 collective-permute-start.2
  53.3 34.9 %collective-permute-done.2.refs_1_ = bf16[4,2,24,32,128]{4,3,2,1,0:T(8,128)(2,1)S(1)} collective-permute-done((bf16[4,2,24,32,128]{4,3,2,1,0:T(8,128)(2,1)S(1)}, bf16[4,2,24,32,128]{4,3,2,1,0:T(8,128)(2,1)S(1)}, u32[]{:S(2)}, u32[]{:S(2)}) %collective-permute-start.2) | collective-permute-done | bytes 1572896 | tf_op jit(solution)/shard_map/ppermute | solution.py:162
  88.3 1.1 copy-done
  89.5 0.5 collective-permute-start.8
  90.0 3.7 %add_convert_fusion.1 = bf16[4,2,24,32,128]{4,3,2,1,0:T(8,128)(2,1)} fusion(bf16[4,2,24,32,128]{4,3,2,1,0:T(8,128)(2,1)} %collective-permute-done.9, bf16[4,2,24,32,128]{4,3,2,1,0:T(8,128)(2,1)} %tie.3), kind=kLoop, calls=%fused_computation.2 | loop fusion | flops 3145728 | bytes 4718592 | tf_op jit(solution)/shard_map/convert_element_type | solution.py:202
  93.7 1.5 collective-permute-start.10
  95.2 2.0 %add_convert_fusion.2 = bf16[4,2,24,32,128]{4,3,2,1,0:T(8,128)(2,1)S(1)} fusion(bf16[4,2,24,32,128]{4,3,2,1,0:T(8,128)(2,1)S(1)} %copy-done.1, bf16[4,2,24,32,128]{4,3,2,1,0:T(8,128)(2,1)} %collective-permute-done.4, bf16[4,2,24,32,128]{4,3,2,1,0:T(8,128)(2,1)S(1)} %copy-done.4), kind=kLoop, calls=%fused_computation.3 | loop fusion | flops 4718592 | bytes 6291456 | tf_op jit(solution)/shard_map/convert_element_type | solution.py:205
  97.5 0.5 collective-permute-start.7
  98.0 3.5 %collective-permute-start.6 = (bf16[2,24,32,128]{3,2,1,0:T(8,128)(2,1)S(1)}, bf16[2,24,32,128]{3,2,1,0:T(8,128)(2,1)}, u32[]{:S(2)}, u32[]{:S(2)}) collective-permute-start(bf16[2,24,32,128]{3,2,1,0:T(8,128)(2,1)S(1)} %get-tuple-element.40), channel_id=1, source_target_pairs={{0,16},{8,24},{16,0},{24,8},{1,17},{9,25},{17,1},{25,9},{2,18},{10... | collective-permute-start | bytes 1179656 | tf_op jit(solution)/shard_map/ppermute | solution.py:177
  101.5 28.9 %collective-permute-done.10 = bf16[4,2,24,32,128]{4,3,2,1,0:T(8,128)(2,1)} collective-permute-done((bf16[4,2,24,32,128]{4,3,2,1,0:T(8,128)(2,1)}, bf16[4,2,24,32,128]{4,3,2,1,0:T(8,128)(2,1)}, u32[]{:S(2)}, u32[]{:S(2)}) %collective-permute-start.10) | collective-permute-done | bytes 1572896 | tf_op jit(solution)/shard_map/ppermute | solution.py:162
  130.4 2.5 %add_convert_fusion = bf16[4,2,24,32,128]{4,3,2,1,0:T(8,128)(2,1)S(1)} fusion(bf16[4,2,24,32,128]{4,3,2,1,0:T(8,128)(2,1)} %collective-permute-done.10, bf16[4,2,24,32,128]{4,3,2,1,0:T(8,128)(2,1)} %collective-permute-done.8, bf16[4,2,24,32,128]{4,3,2,1,0:T(8,128)(2,1)S(1)} %copy-done.3), kind=kLoop, calls=%fused_computation.1 | loop fusion | flops 4718592 | bytes 6291456 | tf_op jit(solution)/shard_map/convert_element_type | solution.py:208
  132.9 1.1 constant_dynamic-slice_fusion.4
  134.0 0.4 collective-permute-start.13
  134.5 3.5 %collective-permute-start.12 = (bf16[2,24,32,128]{3,2,1,0:T(8,128)(2,1)}, bf16[2,24,32,128]{3,2,1,0:T(8,128)(2,1)S(1)}, u32[]{:S(2)}, u32[]{:S(2)}) collective-permute-start(bf16[2,24,32,128]{3,2,1,0:T(8,128)(2,1)} %get-tuple-element.32), channel_id=1, source_target_pairs={{0,16},{8,24},{16,0},{24,8},{1,17},{9,25},{17,1},{25,9},{2,18},{10... | collective-permute-start | bytes 1179656 | tf_op jit(solution)/shard_map/ppermute | solution.py:177
  138.0 1.3 pad_maximum_fusion
  139.3 3.9 %collective-permute-start.1 = (bf16[32,12288]{1,0:T(8,128)(2,1)}, bf16[32,12288]{1,0:T(8,128)(2,1)S(1)}, u32[]{:S(2)}, u32[]{:S(2)}) collective-permute-start(bf16[32,12288]{1,0:T(8,128)(2,1)} %reduce-scatter.3.cloned.1.call-done), channel_id=1, source_target_pairs={{8,0},{16,8},{24,16},{9,1},{17,9},{25,17},{10,2},{18,10},{26,18},{... | collective-permute-start | bytes 2359304 | tf_op jit(solution)/shard_map/ppermute | solution.py:168
  143.3 2.0 %collective-permute-start.3 = (bf16[32,12288]{1,0:T(8,128)(2,1)}, bf16[32,12288]{1,0:T(8,128)(2,1)S(1)}, u32[]{:S(2)}, u32[]{:S(2)}) collective-permute-start(bf16[32,12288]{1,0:T(8,128)(2,1)} %reduce-scatter.5.cloned.1.call-done), channel_id=1, source_target_pairs={{0,8},{8,16},{16,24},{1,9},{9,17},{17,25},{2,10},{10,18},{18,26},{... | collective-permute-start | bytes 2359304 | tf_op jit(solution)/shard_map/ppermute | solution.py:168
  145.3 0.4 constant_dynamic-slice_fusion.8
  145.6 14.0 %collective-permute-done.13 = bf16[2,24,32,128]{3,2,1,0:T(8,128)(2,1)S(1)} collective-permute-done((bf16[2,24,32,128]{3,2,1,0:T(8,128)(2,1)}, bf16[2,24,32,128]{3,2,1,0:T(8,128)(2,1)S(1)}, u32[]{:S(2)}, u32[]{:S(2)}) %collective-permute-start.13) | collective-permute-done | bytes 393248 | tf_op jit(solution)/shard_map/ppermute | solution.py:177
  159.7 10.0 %collective-permute-done.12 = bf16[2,24,32,128]{3,2,1,0:T(8,128)(2,1)S(1)} collective-permute-done((bf16[2,24,32,128]{3,2,1,0:T(8,128)(2,1)}, bf16[2,24,32,128]{3,2,1,0:T(8,128)(2,1)S(1)}, u32[]{:S(2)}, u32[]{:S(2)}) %collective-permute-start.12) | collective-permute-done | bytes 393248 | tf_op jit(solution)/shard_map/ppermute | solution.py:177
  169.7 2.4 %collective-permute-done.11 = bf16[2,24,32,128]{3,2,1,0:T(8,128)(2,1)} collective-permute-done((bf16[2,24,32,128]{3,2,1,0:T(8,128)(2,1)}, bf16[2,24,32,128]{3,2,1,0:T(8,128)(2,1)}, u32[]{:S(2)}, u32[]{:S(2)}) %collective-permute-start.11) | collective-permute-done | bytes 393248 | tf_op jit(solution)/shard_map/ppermute | solution.py:177
  172.0 1.2 pad_maximum_fusion.1
  173.2 0.3 constant_dynamic-slice_fusion.3
  173.7 2.2 %add_bitcast_fusion = f32[4,2,1,24,32,128]{5,4,3,2,1,0:T(8,128)} fusion(bf16[1,2,24,32,128]{4,3,2,1,0:T(8,128)(2,1)S(1)} %get-tuple-element.35, bf16[1,2,24,32,128]{4,3,2,1,0:T(8,128)(2,1)S(1)} %get-tuple-element.36, bf16[1,2,24,32,128]{4,3,2,1,0:T(8,128)(2,1)S(1)} %get-tuple-element.37, bf16[1,2,24,32,128]{4,3,2,1,0:T(8,128)(2,1)S(1)} %get-tuple-element.34, ...), kind=kLoop, calls=%fused_computation | loop fusion | flops 7864320 | bytes 6291456
  175.9 8.8 %collective-permute-done.1 = bf16[32,12288]{1,0:T(8,128)(2,1)S(1)} collective-permute-done((bf16[32,12288]{1,0:T(8,128)(2,1)}, bf16[32,12288]{1,0:T(8,128)(2,1)S(1)}, u32[]{:S(2)}, u32[]{:S(2)}) %collective-permute-start.1) | collective-permute-done | bytes 786464 | tf_op jit(solution)/shard_map/ppermute | solution.py:168
  184.7 3.2 %collective-permute-done.3 = bf16[32,12288]{1,0:T(8,128)(2,1)S(1)} collective-permute-done((bf16[32,12288]{1,0:T(8,128)(2,1)}, bf16[32,12288]{1,0:T(8,128)(2,1)S(1)}, u32[]{:S(2)}, u32[]{:S(2)}) %collective-permute-start.3) | collective-permute-done | bytes 786464 | tf_op jit(solution)/shard_map/ppermute | solution.py:168
  187.9 1.3 maximum_bitcast_fusion
  (29 shorter events, 0.8 us)
Async XLA Ops:
  7.2 132.2 %reduce-scatter.3.cloned.1.call-start = ((), (), s32[]{:S(2)}) async-start(), calls=%async_computation.2 | async-start | bytes 2359296 | tf_op jit(solution)/shard_map/reduce_scatter | solution.py:193
  23.0 3.6 %collective-permute-start = (bf16[4,2,24,32,128]{4,3,2,1,0:T(8,128)(2,1)}, bf16[4,2,24,32,128]{4,3,2,1,0:T(8,128)(2,1)S(1)}, u32[]{:S(2)}, u32[]{:S(2)}) collective-permute-start(bf16[4,2,24,32,128]{4,3,2,1,0:T(8,128)(2,1)} %get-tuple-element.15), channel_id=1, source_target_pairs={{0,2},{2,0},{4,6},{6,4},{1,3},{3,1},{5,7},{7,5},{8,10},{10,8},{12,... | collective-permute-start | bytes 4718600 | tf_op jit(solution)/shard_map/ppermute | solution.py:162
  50.4 1.4 copy-start.2
  50.4 92.8 %reduce-scatter.5.cloned.1.call-start = ((), (), s32[]{:S(2)}) async-start(), calls=%async_computation.3 | async-start | bytes 2359296 | tf_op jit(solution)/shard_map/reduce_scatter | solution.py:193
  51.8 36.4 %collective-permute-start.2 = (bf16[4,2,24,32,128]{4,3,2,1,0:T(8,128)(2,1)S(1)}, bf16[4,2,24,32,128]{4,3,2,1,0:T(8,128)(2,1)S(1)}, u32[]{:S(2)}, u32[]{:S(2)}) collective-permute-start(bf16[4,2,24,32,128]{4,3,2,1,0:T(8,128)(2,1)S(1)} %copy-done.2), channel_id=1, source_target_pairs={{0,4},{2,6},{4,0},{6,2},{1,5},{3,7},{5,1},{7,3},{8,12},{10,14},{12... | collective-permute-start | bytes 4718600 | tf_op jit(solution)/shard_map/ppermute | solution.py:162
  53.3 36.7 %collective-permute-start.9 = (bf16[4,2,24,32,128]{4,3,2,1,0:T(8,128)(2,1)}, bf16[4,2,24,32,128]{4,3,2,1,0:T(8,128)(2,1)}, u32[]{:S(2)}, u32[]{:S(2)}) collective-permute-start(bf16[4,2,24,32,128]{4,3,2,1,0:T(8,128)(2,1)} %get-tuple-element.23), channel_id=1, source_target_pairs={{0,2},{2,0},{4,6},{6,4},{1,3},{3,1},{5,7},{7,5},{8,10},{10,8},{12,... | collective-permute-start | bytes 4718600 | tf_op jit(solution)/shard_map/ppermute | solution.py:162
  88.3 1.1 copy-start
  89.4 5.7 %collective-permute-start.4 = (bf16[4,2,24,32,128]{4,3,2,1,0:T(8,128)(2,1)}, bf16[4,2,24,32,128]{4,3,2,1,0:T(8,128)(2,1)}, u32[]{:S(2)}, u32[]{:S(2)}) collective-permute-start(bf16[4,2,24,32,128]{4,3,2,1,0:T(8,128)(2,1)} %get-tuple-element.19), channel_id=1, source_target_pairs={{0,2},{2,0},{4,6},{6,4},{1,3},{3,1},{5,7},{7,5},{8,10},{10,8},{12,... | collective-permute-start | bytes 4718600 | tf_op jit(solution)/shard_map/ppermute | solution.py:162
  89.5 12.0 %collective-permute-start.8 = (bf16[4,2,24,32,128]{4,3,2,1,0:T(8,128)(2,1)}, bf16[4,2,24,32,128]{4,3,2,1,0:T(8,128)(2,1)}, u32[]{:S(2)}, u32[]{:S(2)}) collective-permute-start(bf16[4,2,24,32,128]{4,3,2,1,0:T(8,128)(2,1)} %get-tuple-element.21), channel_id=1, source_target_pairs={{0,2},{2,0},{4,6},{6,4},{1,3},{3,1},{5,7},{7,5},{8,10},{10,8},{12,... | collective-permute-start | bytes 4718600 | tf_op jit(solution)/shard_map/ppermute | solution.py:162
  90.0 5.2 %copy-start.1 = (bf16[4,2,24,32,128]{4,3,2,1,0:T(8,128)(2,1)S(1)}, bf16[4,2,24,32,128]{4,3,2,1,0:T(8,128)(2,1)}, u32[]{:S(2)}) copy-start(bf16[4,2,24,32,128]{4,3,2,1,0:T(8,128)(2,1)} %copy-done) | copy-start | bytes 4718596
  90.0 5.2 %copy-start.4 = (bf16[4,2,24,32,128]{4,3,2,1,0:T(8,128)(2,1)S(1)}, bf16[4,2,24,32,128]{4,3,2,1,0:T(8,128)(2,1)}, u32[]{:S(2)}) copy-start(bf16[4,2,24,32,128]{4,3,2,1,0:T(8,128)(2,1)} %get-tuple-element.18) | copy-start | bytes 4718596
  93.7 36.7 %collective-permute-start.10 = (bf16[4,2,24,32,128]{4,3,2,1,0:T(8,128)(2,1)}, bf16[4,2,24,32,128]{4,3,2,1,0:T(8,128)(2,1)}, u32[]{:S(2)}, u32[]{:S(2)}) collective-permute-start(bf16[4,2,24,32,128]{4,3,2,1,0:T(8,128)(2,1)} %add_convert_fusion.1), channel_id=1, source_target_pairs={{0,4},{2,6},{4,0},{6,2},{1,5},{3,7},{5,1},{7,3},{8,12},{10,14},{12... | collective-permute-start | bytes 4718600 | tf_op jit(solution)/shard_map/ppermute | solution.py:162
  97.2 33.2 %copy-start.3 = (bf16[4,2,24,32,128]{4,3,2,1,0:T(8,128)(2,1)S(1)}, bf16[4,2,24,32,128]{4,3,2,1,0:T(8,128)(2,1)}, u32[]{:S(2)}) copy-start(bf16[4,2,24,32,128]{4,3,2,1,0:T(8,128)(2,1)} %get-tuple-element.20) | copy-start | bytes 4718596
  97.5 40.5 %collective-permute-start.7 = (bf16[2,24,32,128]{3,2,1,0:T(8,128)(2,1)S(1)}, bf16[2,24,32,128]{3,2,1,0:T(8,128)(2,1)S(1)}, u32[]{:S(2)}, u32[]{:S(2)}) collective-permute-start(bf16[2,24,32,128]{3,2,1,0:T(8,128)(2,1)S(1)} %get-tuple-element.39), channel_id=1, source_target_pairs={{0,24},{8,0},{16,8},{24,16},{1,25},{9,1},{17,9},{25,17},{2,26},{10... | collective-permute-start | bytes 1179656 | tf_op jit(solution)/shard_map/ppermute | solution.py:177
  98.0 40.0 %collective-permute-start.6 = (bf16[2,24,32,128]{3,2,1,0:T(8,128)(2,1)S(1)}, bf16[2,24,32,128]{3,2,1,0:T(8,128)(2,1)}, u32[]{:S(2)}, u32[]{:S(2)}) collective-permute-start(bf16[2,24,32,128]{3,2,1,0:T(8,128)(2,1)S(1)} %get-tuple-element.40), channel_id=1, source_target_pairs={{0,16},{8,24},{16,0},{24,8},{1,17},{9,25},{17,1},{25,9},{2,18},{10... | collective-permute-start | bytes 1179656 | tf_op jit(solution)/shard_map/ppermute | solution.py:177
  101.5 36.5 %collective-permute-start.5 = (bf16[2,24,32,128]{3,2,1,0:T(8,128)(2,1)S(1)}, bf16[2,24,32,128]{3,2,1,0:T(8,128)(2,1)}, u32[]{:S(2)}, u32[]{:S(2)}) collective-permute-start(bf16[2,24,32,128]{3,2,1,0:T(8,128)(2,1)S(1)} %get-tuple-element.41), channel_id=1, source_target_pairs={{0,8},{8,16},{16,24},{24,0},{1,9},{9,17},{17,25},{25,1},{2,10},{10... | collective-permute-start | bytes 1179656 | tf_op jit(solution)/shard_map/ppermute | solution.py:177
  134.0 25.7 %collective-permute-start.13 = (bf16[2,24,32,128]{3,2,1,0:T(8,128)(2,1)}, bf16[2,24,32,128]{3,2,1,0:T(8,128)(2,1)S(1)}, u32[]{:S(2)}, u32[]{:S(2)}) collective-permute-start(bf16[2,24,32,128]{3,2,1,0:T(8,128)(2,1)} %get-tuple-element.31), channel_id=1, source_target_pairs={{0,24},{8,0},{16,8},{24,16},{1,25},{9,1},{17,9},{25,17},{2,26},{10... | collective-permute-start | bytes 1179656 | tf_op jit(solution)/shard_map/ppermute | solution.py:177
  134.5 35.2 %collective-permute-start.12 = (bf16[2,24,32,128]{3,2,1,0:T(8,128)(2,1)}, bf16[2,24,32,128]{3,2,1,0:T(8,128)(2,1)S(1)}, u32[]{:S(2)}, u32[]{:S(2)}) collective-permute-start(bf16[2,24,32,128]{3,2,1,0:T(8,128)(2,1)} %get-tuple-element.32), channel_id=1, source_target_pairs={{0,16},{8,24},{16,0},{24,8},{1,17},{9,25},{17,1},{25,9},{2,18},{10... | collective-permute-start | bytes 1179656 | tf_op jit(solution)/shard_map/ppermute | solution.py:177
  138.0 34.1 %collective-permute-start.11 = (bf16[2,24,32,128]{3,2,1,0:T(8,128)(2,1)}, bf16[2,24,32,128]{3,2,1,0:T(8,128)(2,1)}, u32[]{:S(2)}, u32[]{:S(2)}) collective-permute-start(bf16[2,24,32,128]{3,2,1,0:T(8,128)(2,1)} %get-tuple-element.33), channel_id=1, source_target_pairs={{0,8},{8,16},{16,24},{24,0},{1,9},{9,17},{17,25},{25,1},{2,10},{10... | collective-permute-start | bytes 1179656 | tf_op jit(solution)/shard_map/ppermute | solution.py:177
  139.3 45.4 %collective-permute-start.1 = (bf16[32,12288]{1,0:T(8,128)(2,1)}, bf16[32,12288]{1,0:T(8,128)(2,1)S(1)}, u32[]{:S(2)}, u32[]{:S(2)}) collective-permute-start(bf16[32,12288]{1,0:T(8,128)(2,1)} %reduce-scatter.3.cloned.1.call-done), channel_id=1, source_target_pairs={{8,0},{16,8},{24,16},{9,1},{17,9},{25,17},{10,2},{18,10},{26,18},{... | collective-permute-start | bytes 2359304 | tf_op jit(solution)/shard_map/ppermute | solution.py:168
  143.3 44.6 %collective-permute-start.3 = (bf16[32,12288]{1,0:T(8,128)(2,1)}, bf16[32,12288]{1,0:T(8,128)(2,1)S(1)}, u32[]{:S(2)}, u32[]{:S(2)}) collective-permute-start(bf16[32,12288]{1,0:T(8,128)(2,1)} %reduce-scatter.5.cloned.1.call-done), channel_id=1, source_target_pairs={{0,8},{8,16},{16,24},{1,9},{9,17},{17,25},{2,10},{10,18},{18,26},{... | collective-permute-start | bytes 2359304 | tf_op jit(solution)/shard_map/ppermute | solution.py:168
Sparse Core Ops, SparseCore 0:
  50.6 26.1 reduce-scatter.2
  89.5 26.1 reduce-scatter.4

commit v14 on v9

--- a/solution.py
+++ b/solution.py
@@ -79,7 +79,7 @@
     rows, width = section_in.shape[2:]
     blocks, block = w_in.shape[2:4]
     per = blocks // sections
-    per_step = math.gcd(per, 8)
+    per_step = math.gcd(per, 12)
     turns = per // per_step
     piece = block // n_dp
     whole = pl.BlockSpec((None, None, rows, width), lambda i, *_: (relay, 0, 0, 0))

time: 174 us -> 172 us (0.989)
  the two profiles are of different devices: /device:TPU:16 before, /device:TPU:20 now
where the time goes in v14:
time: 172 us; the launch traced here: 171 us
  waiting for transfers between devices  89 us (52%)
  Pallas kernels  31 us (18%)
  starting transfers between devices  17.6 us (10%)
  other arithmetic  15 us (9%)
  between operations  14.2 us (8%)
  local copies, waits for them, and re-layouts  4.09 us (2%)
    ppermute x6, waiting for transfers between devices, flip_bit(): lax.ppermute(value, axis, [(i, i ^ bit) for i in range(lax.axis_size(axis...  51.5 us
    pallas_call x2, Pallas kernels, tick(): pl.pallas_call(functools.partial(tick_kernel, relay, per_step, n_mp, len(...  31 us
    ppermute x6, waiting for transfers between devices, rotate(): lax.ppermute(part, axis, [(i, (i + k) % n) for i in range(n)])  25.7 us
    ppermute x2, waiting for transfers between devices, from_behind(): return lax.ppermute(value, axis, route)  11.7 us
    ppermute x6, starting transfers between devices, rotate(): lax.ppermute(part, axis, [(i, (i + k) % n) for i in range(n)])  7.93 us
    ppermute x2, starting transfers between devices, from_behind(): return lax.ppermute(value, axis, route)  5.89 us
    ppermute x6, starting transfers between devices, flip_bit(): lax.ppermute(value, axis, [(i, i ^ bit) for i in range(lax.axis_size(axis...  3.73 us
    convert_element_type x1, other arithmetic, body(): sum1 = total(tie(b2, came0), hot2).astype(jnp.bfloat16)  3.66 us
  transfers between devices with their start and end apart: 16, of which 8 were waited for; matrix products, arithmetic and copies ran while one was open for 9% of the time, Pallas kernels for 9%

profile of v14, /device:TPU:20, one launch (start us, length us, event | category | flops | bytes accessed | tf_op | source)
XLA Modules:
  0.0 170.9 jit_solution(14420799734644773876)
XLA Ops:
  7.2 15.2 %tick0.1 = (bf16[4,2,24,32,128]{4,3,2,1,0:T(8,128)(2,1)}, bf16[4,2,24,32,128]{4,3,2,1,0:T(8,128)(2,1)}, bf16[4,2,24,32,128]{4,3,2,1,0:T(8,128)(2,1)}, bf16[4,2,2...) custom-call(s32[2]{0:T(128)} %bitcast.34, s32[1,2,96]{2,1,0:T(2,128)} %idx_in_ref.3, s32[1,2,96]{2,1,0:T(2,128)} %idx_out_ref.3, ...), custom_call_target="tpu_custom_call" | custom-call | flops 1006632960 | bytes 17301504 | tf_op jit(solution)/shard_map/tick0/pallas_call | solution.py:89
  22.6 3.5 %collective-permute-done.1 = bf16[4,2,24,32,128]{4,3,2,1,0:T(8,128)(2,1)S(1)} collective-permute-done((bf16[4,2,24,32,128]{4,3,2,1,0:T(8,128)(2,1)}, bf16[4,2,24,32,128]{4,3,2,1,0:T(8,128)(2,1)S(1)}, u32[]{:S(2)}, u32[]{:S(2)}) %collective-permute-start.1) | collective-permute-done | bytes 1572896 | tf_op jit(solution)/shard_map/ppermute | solution.py:129
  26.1 0.4 add_convert_fusion.3.refs_0_
  26.6 1.5 collective-permute-start.2
  28.1 15.8 %tick1.1 = (bf16[4,2,24,32,128]{4,3,2,1,0:T(8,128)(2,1)}, bf16[4,2,24,32,128]{4,3,2,1,0:T(8,128)(2,1)}, bf16[4,2,24,32,128]{4,3,2,1,0:T(8,128)(2,1)}, bf16[4,2,2...) custom-call(s32[2]{0:T(128)} %bitcast.35, s32[1,2,96]{2,1,0:T(2,128)} %idx_in_ref.3, s32[1,2,96]{2,1,0:T(2,128)} %idx_out_ref.3, ...), custom_call_target="tpu_custom_call" | custom-call | flops 1006632960 | bytes 17301504 | tf_op jit(solution)/shard_map/tick1/pallas_call | solution.py:89
  44.0 19.1 %collective-permute-done.2.refs_1_ = bf16[4,2,24,32,128]{4,3,2,1,0:T(8,128)(2,1)S(1)} collective-permute-done((bf16[4,2,24,32,128]{4,3,2,1,0:T(8,128)(2,1)S(1)}, bf16[4,2,24,32,128]{4,3,2,1,0:T(8,128)(2,1)S(1)}, u32[]{:S(2)}, u32[]{:S(2)}) %collective-permute-start.2) | collective-permute-done | bytes 1572896 | tf_op jit(solution)/shard_map/ppermute | solution.py:129
  63.1 1.2 copy-done
  64.4 0.5 collective-permute-start.8
  65.0 3.7 %add_convert_fusion.1 = bf16[4,2,24,32,128]{4,3,2,1,0:T(8,128)(2,1)} fusion(bf16[4,2,24,32,128]{4,3,2,1,0:T(8,128)(2,1)} %collective-permute-done.9, bf16[4,2,24,32,128]{4,3,2,1,0:T(8,128)(2,1)} %tie.3), kind=kLoop, calls=%fused_computation.2 | loop fusion | flops 3145728 | bytes 4718592 | tf_op jit(solution)/shard_map/convert_element_type | solution.py:169
  68.6 1.5 collective-permute-start.10
  70.1 2.0 %add_convert_fusion.2 = bf16[4,2,24,32,128]{4,3,2,1,0:T(8,128)(2,1)S(1)} fusion(bf16[4,2,24,32,128]{4,3,2,1,0:T(8,128)(2,1)S(1)} %copy-done.1, bf16[4,2,24,32,128]{4,3,2,1,0:T(8,128)(2,1)} %collective-permute-done.4, bf16[4,2,24,32,128]{4,3,2,1,0:T(8,128)(2,1)S(1)} %copy-done.3), kind=kLoop, calls=%fused_computation.3 | loop fusion | flops 4718592 | bytes 6291456 | tf_op jit(solution)/shard_map/convert_element_type | solution.py:172
  72.4 0.5 collective-permute-start.7
  72.9 3.5 %collective-permute-start.6 = (bf16[2,24,32,128]{3,2,1,0:T(8,128)(2,1)S(1)}, bf16[2,24,32,128]{3,2,1,0:T(8,128)(2,1)S(1)}, u32[]{:S(2)}, u32[]{:S(2)}) collective-permute-start(bf16[2,24,32,128]{3,2,1,0:T(8,128)(2,1)S(1)} %get-tuple-element.38), channel_id=1, source_target_pairs={{0,16},{8,24},{16,0},{24,8},{1,17},{9,25},{17,1},{25,9},{2,18},{10... | collective-permute-start | bytes 1179656 | tf_op jit(solution)/shard_map/ppermute | solution.py:144
  76.4 28.9 %collective-permute-done.10 = bf16[4,2,24,32,128]{4,3,2,1,0:T(8,128)(2,1)} collective-permute-done((bf16[4,2,24,32,128]{4,3,2,1,0:T(8,128)(2,1)}, bf16[4,2,24,32,128]{4,3,2,1,0:T(8,128)(2,1)}, u32[]{:S(2)}, u32[]{:S(2)}) %collective-permute-start.10) | collective-permute-done | bytes 1572896 | tf_op jit(solution)/shard_map/ppermute | solution.py:129
  105.3 2.5 %add_convert_fusion = bf16[4,2,24,32,128]{4,3,2,1,0:T(8,128)(2,1)S(1)} fusion(bf16[4,2,24,32,128]{4,3,2,1,0:T(8,128)(2,1)} %collective-permute-done.10, bf16[4,2,24,32,128]{4,3,2,1,0:T(8,128)(2,1)} %collective-permute-done.8, bf16[4,2,24,32,128]{4,3,2,1,0:T(8,128)(2,1)S(1)} %copy-done.4), kind=kLoop, calls=%fused_computation.1 | loop fusion | flops 4718592 | bytes 6291456 | tf_op jit(solution)/shard_map/convert_element_type | solution.py:175
  107.8 1.1 constant_dynamic-slice_fusion.4
  109.0 0.4 collective-permute-start.13
  109.4 3.5 %collective-permute-start.12 = (bf16[2,24,32,128]{3,2,1,0:T(8,128)(2,1)}, bf16[2,24,32,128]{3,2,1,0:T(8,128)(2,1)}, u32[]{:S(2)}, u32[]{:S(2)}) collective-permute-start(bf16[2,24,32,128]{3,2,1,0:T(8,128)(2,1)} %get-tuple-element.30), channel_id=1, source_target_pairs={{0,16},{8,24},{16,0},{24,8},{1,17},{9,25},{17,1},{25,9},{2,18},{10... | collective-permute-start | bytes 1179656 | tf_op jit(solution)/shard_map/ppermute | solution.py:144
  112.9 3.9 %collective-permute-start = (bf16[32,12288]{1,0:T(8,128)(2,1)}, bf16[32,12288]{1,0:T(8,128)(2,1)S(1)}, u32[]{:S(2)}, u32[]{:S(2)}) collective-permute-start(bf16[32,12288]{1,0:T(8,128)(2,1)} %reduce-scatter.3.cloned.1.call-done), channel_id=1, source_target_pairs={{8,0},{16,8},{24,16},{9,1},{17,9},{25,17},{10,2},{18,10},{26,18},{... | collective-permute-start | bytes 2359304 | tf_op jit(solution)/shard_map/ppermute | solution.py:135
  116.9 0.7 copy-done.7
  117.6 1.3 pad_maximum_fusion
  118.9 2.0 %collective-permute-start.3 = (bf16[32,12288]{1,0:T(8,128)(2,1)}, bf16[32,12288]{1,0:T(8,128)(2,1)S(1)}, u32[]{:S(2)}, u32[]{:S(2)}) collective-permute-start(bf16[32,12288]{1,0:T(8,128)(2,1)} %reduce-scatter.5.cloned.1.call-done), channel_id=1, source_target_pairs={{0,8},{8,16},{16,24},{1,9},{9,17},{17,25},{2,10},{10,18},{18,26},{... | collective-permute-start | bytes 2359304 | tf_op jit(solution)/shard_map/ppermute | solution.py:135
  120.9 0.4 constant_dynamic-slice_fusion.8
  121.3 13.3 %collective-permute-done.13 = bf16[2,24,32,128]{3,2,1,0:T(8,128)(2,1)} collective-permute-done((bf16[2,24,32,128]{3,2,1,0:T(8,128)(2,1)}, bf16[2,24,32,128]{3,2,1,0:T(8,128)(2,1)}, u32[]{:S(2)}, u32[]{:S(2)}) %collective-permute-start.13) | collective-permute-done | bytes 393248 | tf_op jit(solution)/shard_map/ppermute | solution.py:144
  134.6 10.0 %collective-permute-done.12 = bf16[2,24,32,128]{3,2,1,0:T(8,128)(2,1)} collective-permute-done((bf16[2,24,32,128]{3,2,1,0:T(8,128)(2,1)}, bf16[2,24,32,128]{3,2,1,0:T(8,128)(2,1)}, u32[]{:S(2)}, u32[]{:S(2)}) %collective-permute-start.12) | collective-permute-done | bytes 393248 | tf_op jit(solution)/shard_map/ppermute | solution.py:144
  144.6 2.4 %collective-permute-done.11 = bf16[2,24,32,128]{3,2,1,0:T(8,128)(2,1)} collective-permute-done((bf16[2,24,32,128]{3,2,1,0:T(8,128)(2,1)}, bf16[2,24,32,128]{3,2,1,0:T(8,128)(2,1)}, u32[]{:S(2)}, u32[]{:S(2)}) %collective-permute-start.11) | collective-permute-done | bytes 393248 | tf_op jit(solution)/shard_map/ppermute | solution.py:144
  147.0 1.4 pad_maximum_fusion.1
  148.4 0.3 constant_dynamic-slice_fusion.3
  148.9 2.2 %add_bitcast_fusion = f32[4,2,1,24,32,128]{5,4,3,2,1,0:T(8,128)} fusion(bf16[1,2,24,32,128]{4,3,2,1,0:T(8,128)(2,1)S(1)} %get-tuple-element.33, bf16[1,2,24,32,128]{4,3,2,1,0:T(8,128)(2,1)S(1)} %get-tuple-element.34, bf16[1,2,24,32,128]{4,3,2,1,0:T(8,128)(2,1)S(1)} %get-tuple-element.35, bf16[1,2,24,32,128]{4,3,2,1,0:T(8,128)(2,1)S(1)} %get-tuple-element.32, ...), kind=kLoop, calls=%fused_computation | loop fusion | flops 7864320 | bytes 6291456
  151.1 8.6 %collective-permute-done = bf16[32,12288]{1,0:T(8,128)(2,1)S(1)} collective-permute-done((bf16[32,12288]{1,0:T(8,128)(2,1)}, bf16[32,12288]{1,0:T(8,128)(2,1)S(1)}, u32[]{:S(2)}, u32[]{:S(2)}) %collective-permute-start) | collective-permute-done | bytes 786464 | tf_op jit(solution)/shard_map/ppermute | solution.py:135
  159.7 3.2 %collective-permute-done.3 = bf16[32,12288]{1,0:T(8,128)(2,1)S(1)} collective-permute-done((bf16[32,12288]{1,0:T(8,128)(2,1)}, bf16[32,12288]{1,0:T(8,128)(2,1)S(1)}, u32[]{:S(2)}, u32[]{:S(2)}) %collective-permute-start.3) | collective-permute-done | bytes 786464 | tf_op jit(solution)/shard_map/ppermute | solution.py:135
  162.8 1.3 maximum_bitcast_fusion
  (35 shorter events, 0.9 us)
Async XLA Ops:
  7.2 105.7 %reduce-scatter.3.cloned.1.call-start = ((), (), s32[]{:S(2)}) async-start(), calls=%async_computation.2 | async-start | bytes 2359296 | tf_op jit(solution)/shard_map/reduce_scatter | solution.py:160
  22.4 3.7 %copy-start.5 = (bf16[4,2,24,32,128]{4,3,2,1,0:T(8,128)(2,1)S(1)}, bf16[4,2,24,32,128]{4,3,2,1,0:T(8,128)(2,1)}, u32[]{:S(2)}) copy-start(bf16[4,2,24,32,128]{4,3,2,1,0:T(8,128)(2,1)} %get-tuple-element.13) | copy-start | bytes 4718596
  22.4 3.7 %collective-permute-start.1 = (bf16[4,2,24,32,128]{4,3,2,1,0:T(8,128)(2,1)}, bf16[4,2,24,32,128]{4,3,2,1,0:T(8,128)(2,1)S(1)}, u32[]{:S(2)}, u32[]{:S(2)}) collective-permute-start(bf16[4,2,24,32,128]{4,3,2,1,0:T(8,128)(2,1)} %get-tuple-element.14), channel_id=1, source_target_pairs={{0,2},{2,0},{4,6},{6,4},{1,3},{3,1},{5,7},{7,5},{8,10},{10,8},{12,... | collective-permute-start | bytes 4718600 | tf_op jit(solution)/shard_map/ppermute | solution.py:129
  22.5 96.4 %reduce-scatter.5.cloned.1.call-start = ((), (), s32[]{:S(2)}) async-start(), calls=%async_computation.3 | async-start | bytes 2359296 | tf_op jit(solution)/shard_map/reduce_scatter | solution.py:160
  26.6 1.6 copy-start.2
  26.6 36.5 %collective-permute-start.2 = (bf16[4,2,24,32,128]{4,3,2,1,0:T(8,128)(2,1)S(1)}, bf16[4,2,24,32,128]{4,3,2,1,0:T(8,128)(2,1)S(1)}, u32[]{:S(2)}, u32[]{:S(2)}) collective-permute-start(bf16[4,2,24,32,128]{4,3,2,1,0:T(8,128)(2,1)S(1)} %add_convert_fusion.3.refs_0_), channel_id=1, source_target_pairs={{0,4},{2,6},{4,0},{6,2},{1,5},{3,7},{5,1},{7,3},{8,12},{10,14},{12... | collective-permute-start | bytes 4718600 | tf_op jit(solution)/shard_map/ppermute | solution.py:129
  43.9 21.0 %collective-permute-start.9 = (bf16[4,2,24,32,128]{4,3,2,1,0:T(8,128)(2,1)}, bf16[4,2,24,32,128]{4,3,2,1,0:T(8,128)(2,1)}, u32[]{:S(2)}, u32[]{:S(2)}) collective-permute-start(bf16[4,2,24,32,128]{4,3,2,1,0:T(8,128)(2,1)} %get-tuple-element.21), channel_id=1, source_target_pairs={{0,2},{2,0},{4,6},{6,4},{1,3},{3,1},{5,7},{7,5},{8,10},{10,8},{12,... | collective-permute-start | bytes 4718600 | tf_op jit(solution)/shard_map/ppermute | solution.py:129
  63.1 1.3 copy-start
  64.4 5.7 %collective-permute-start.4 = (bf16[4,2,24,32,128]{4,3,2,1,0:T(8,128)(2,1)}, bf16[4,2,24,32,128]{4,3,2,1,0:T(8,128)(2,1)}, u32[]{:S(2)}, u32[]{:S(2)}) collective-permute-start(bf16[4,2,24,32,128]{4,3,2,1,0:T(8,128)(2,1)} %get-tuple-element.17), channel_id=1, source_target_pairs={{0,2},{2,0},{4,6},{6,4},{1,3},{3,1},{5,7},{7,5},{8,10},{10,8},{12,... | collective-permute-start | bytes 4718600 | tf_op jit(solution)/shard_map/ppermute | solution.py:129
  64.4 12.0 %collective-permute-start.8 = (bf16[4,2,24,32,128]{4,3,2,1,0:T(8,128)(2,1)}, bf16[4,2,24,32,128]{4,3,2,1,0:T(8,128)(2,1)}, u32[]{:S(2)}, u32[]{:S(2)}) collective-permute-start(bf16[4,2,24,32,128]{4,3,2,1,0:T(8,128)(2,1)} %get-tuple-element.19), channel_id=1, source_target_pairs={{0,2},{2,0},{4,6},{6,4},{1,3},{3,1},{5,7},{7,5},{8,10},{10,8},{12,... | collective-permute-start | bytes 4718600 | tf_op jit(solution)/shard_map/ppermute | solution.py:129
  64.9 5.2 %copy-start.1 = (bf16[4,2,24,32,128]{4,3,2,1,0:T(8,128)(2,1)S(1)}, bf16[4,2,24,32,128]{4,3,2,1,0:T(8,128)(2,1)}, u32[]{:S(2)}) copy-start(bf16[4,2,24,32,128]{4,3,2,1,0:T(8,128)(2,1)} %copy-done) | copy-start | bytes 4718596
  64.9 5.2 %copy-start.3 = (bf16[4,2,24,32,128]{4,3,2,1,0:T(8,128)(2,1)S(1)}, bf16[4,2,24,32,128]{4,3,2,1,0:T(8,128)(2,1)}, u32[]{:S(2)}) copy-start(bf16[4,2,24,32,128]{4,3,2,1,0:T(8,128)(2,1)} %get-tuple-element.16) | copy-start | bytes 4718596
  68.6 36.7 %collective-permute-start.10 = (bf16[4,2,24,32,128]{4,3,2,1,0:T(8,128)(2,1)}, bf16[4,2,24,32,128]{4,3,2,1,0:T(8,128)(2,1)}, u32[]{:S(2)}, u32[]{:S(2)}) collective-permute-start(bf16[4,2,24,32,128]{4,3,2,1,0:T(8,128)(2,1)} %add_convert_fusion.1), channel_id=1, source_target_pairs={{0,4},{2,6},{4,0},{6,2},{1,5},{3,7},{5,1},{7,3},{8,12},{10,14},{12... | collective-permute-start | bytes 4718600 | tf_op jit(solution)/shard_map/ppermute | solution.py:129
  72.1 33.2 %copy-start.4 = (bf16[4,2,24,32,128]{4,3,2,1,0:T(8,128)(2,1)S(1)}, bf16[4,2,24,32,128]{4,3,2,1,0:T(8,128)(2,1)}, u32[]{:S(2)}) copy-start(bf16[4,2,24,32,128]{4,3,2,1,0:T(8,128)(2,1)} %get-tuple-element.18) | copy-start | bytes 4718596
  72.4 40.5 %collective-permute-start.7 = (bf16[2,24,32,128]{3,2,1,0:T(8,128)(2,1)S(1)}, bf16[2,24,32,128]{3,2,1,0:T(8,128)(2,1)S(1)}, u32[]{:S(2)}, u32[]{:S(2)}) collective-permute-start(bf16[2,24,32,128]{3,2,1,0:T(8,128)(2,1)S(1)} %get-tuple-element.37), channel_id=1, source_target_pairs={{0,24},{8,0},{16,8},{24,16},{1,25},{9,1},{17,9},{25,17},{2,26},{10... | collective-permute-start | bytes 1179656 | tf_op jit(solution)/shard_map/ppermute | solution.py:144
  72.9 40.0 %collective-permute-start.6 = (bf16[2,24,32,128]{3,2,1,0:T(8,128)(2,1)S(1)}, bf16[2,24,32,128]{3,2,1,0:T(8,128)(2,1)S(1)}, u32[]{:S(2)}, u32[]{:S(2)}) collective-permute-start(bf16[2,24,32,128]{3,2,1,0:T(8,128)(2,1)S(1)} %get-tuple-element.38), channel_id=1, source_target_pairs={{0,16},{8,24},{16,0},{24,8},{1,17},{9,25},{17,1},{25,9},{2,18},{10... | collective-permute-start | bytes 1179656 | tf_op jit(solution)/shard_map/ppermute | solution.py:144
  76.4 40.4 %collective-permute-start.5 = (bf16[2,24,32,128]{3,2,1,0:T(8,128)(2,1)S(1)}, bf16[2,24,32,128]{3,2,1,0:T(8,128)(2,1)S(1)}, u32[]{:S(2)}, u32[]{:S(2)}) collective-permute-start(bf16[2,24,32,128]{3,2,1,0:T(8,128)(2,1)S(1)} %get-tuple-element.39), channel_id=1, source_target_pairs={{0,8},{8,16},{16,24},{24,0},{1,9},{9,17},{17,25},{25,1},{2,10},{10... | collective-permute-start | bytes 1179656 | tf_op jit(solution)/shard_map/ppermute | solution.py:144
  109.0 25.7 %collective-permute-start.13 = (bf16[2,24,32,128]{3,2,1,0:T(8,128)(2,1)}, bf16[2,24,32,128]{3,2,1,0:T(8,128)(2,1)}, u32[]{:S(2)}, u32[]{:S(2)}) collective-permute-start(bf16[2,24,32,128]{3,2,1,0:T(8,128)(2,1)} %get-tuple-element.29), channel_id=1, source_target_pairs={{0,24},{8,0},{16,8},{24,16},{1,25},{9,1},{17,9},{25,17},{2,26},{10... | collective-permute-start | bytes 1179656 | tf_op jit(solution)/shard_map/ppermute | solution.py:144
  109.4 35.2 %collective-permute-start.12 = (bf16[2,24,32,128]{3,2,1,0:T(8,128)(2,1)}, bf16[2,24,32,128]{3,2,1,0:T(8,128)(2,1)}, u32[]{:S(2)}, u32[]{:S(2)}) collective-permute-start(bf16[2,24,32,128]{3,2,1,0:T(8,128)(2,1)} %get-tuple-element.30), channel_id=1, source_target_pairs={{0,16},{8,24},{16,0},{24,8},{1,17},{9,25},{17,1},{25,9},{2,18},{10... | collective-permute-start | bytes 1179656 | tf_op jit(solution)/shard_map/ppermute | solution.py:144
  112.9 34.1 %collective-permute-start.11 = (bf16[2,24,32,128]{3,2,1,0:T(8,128)(2,1)}, bf16[2,24,32,128]{3,2,1,0:T(8,128)(2,1)}, u32[]{:S(2)}, u32[]{:S(2)}) collective-permute-start(bf16[2,24,32,128]{3,2,1,0:T(8,128)(2,1)} %get-tuple-element.31), channel_id=1, source_target_pairs={{0,8},{8,16},{16,24},{24,0},{1,9},{9,17},{17,25},{25,1},{2,10},{10... | collective-permute-start | bytes 1179656 | tf_op jit(solution)/shard_map/ppermute | solution.py:144
  112.9 3.9 %copy-start.6 = (bf16[2,24,32,128]{3,2,1,0:T(8,128)(2,1)}, bf16[2,24,32,128]{3,2,1,0:T(8,128)(2,1)S(1)}, u32[]{:S(2)}) copy-start(bf16[2,24,32,128]{3,2,1,0:T(8,128)(2,1)S(1)} %collective-permute-done.6) | copy-start | bytes 1179652
  112.9 46.8 %collective-permute-start = (bf16[32,12288]{1,0:T(8,128)(2,1)}, bf16[32,12288]{1,0:T(8,128)(2,1)S(1)}, u32[]{:S(2)}, u32[]{:S(2)}) collective-permute-start(bf16[32,12288]{1,0:T(8,128)(2,1)} %reduce-scatter.3.cloned.1.call-done), channel_id=1, source_target_pairs={{8,0},{16,8},{24,16},{9,1},{17,9},{25,17},{10,2},{18,10},{26,18},{... | collective-permute-start | bytes 2359304 | tf_op jit(solution)/shard_map/ppermute | solution.py:135
  116.8 0.7 copy-start.7
  118.9 43.9 %collective-permute-start.3 = (bf16[32,12288]{1,0:T(8,128)(2,1)}, bf16[32,12288]{1,0:T(8,128)(2,1)S(1)}, u32[]{:S(2)}, u32[]{:S(2)}) collective-permute-start(bf16[32,12288]{1,0:T(8,128)(2,1)} %reduce-scatter.5.cloned.1.call-done), channel_id=1, source_target_pairs={{0,8},{8,16},{16,24},{1,9},{9,17},{17,25},{2,10},{10,18},{18,26},{... | collective-permute-start | bytes 2359304 | tf_op jit(solution)/shard_map/ppermute | solution.py:135
Sparse Core Ops, SparseCore 0:
  22.7 26.2 reduce-scatter.2
  64.5 26.1 reduce-scatter.4

commit v15 on v14

--- a/solution.py
+++ b/solution.py
@@ -79,7 +79,7 @@
     rows, width = section_in.shape[2:]
     blocks, block = w_in.shape[2:4]
     per = blocks // sections
-    per_step = math.gcd(per, 12)
+    per_step = math.gcd(per, 24)
     turns = per // per_step
     piece = block // n_dp
     whole = pl.BlockSpec((None, None, rows, width), lambda i, *_: (relay, 0, 0, 0))

time: 172 us -> 170 us (0.988)
  Pallas kernels: 31 us -> 29.2 us
    pallas_call x2, Pallas kernels: 31 us -> 29.2 us  [tick(): pl.pallas_call(functools.partial(tick_kernel, relay, per_step, n_mp, len(...]
where the time goes in v15:
time: 170 us
  waiting for transfers between devices  89.9 us (53%)
  Pallas kernels  29.2 us (17%)
  starting transfers between devices  17.6 us (10%)
  other arithmetic  15 us (9%)
  between operations  14.2 us (8%)
  local copies, waits for them, and re-layouts  4.09 us (2%)
    ppermute x6, waiting for transfers between devices, flip_bit(): lax.ppermute(value, axis, [(i, i ^ bit) for i in range(lax.axis_size(axis...  52.5 us
    pallas_call x2, Pallas kernels, tick(): pl.pallas_call(functools.partial(tick_kernel, relay, per_step, n_mp, len(...  29.2 us
    ppermute x6, waiting for transfers between devices, rotate(): lax.ppermute(part, axis, [(i, (i + k) % n) for i in range(n)])  25.7 us
    ppermute x2, waiting for transfers between devices, from_behind(): return lax.ppermute(value, axis, route)  11.7 us
    ppermute x6, starting transfers between devices, rotate(): lax.ppermute(part, axis, [(i, (i + k) % n) for i in range(n)])  7.88 us
    ppermute x2, starting transfers between devices, from_behind(): return lax.ppermute(value, axis, route)  5.89 us
    ppermute x6, starting transfers between devices, flip_bit(): lax.ppermute(value, axis, [(i, i ^ bit) for i in range(lax.axis_size(axis...  3.72 us
    convert_element_type x1, other arithmetic, body(): sum1 = total(tie(b2, came0), hot2).astype(jnp.bfloat16)  3.66 us
  transfers between devices with their start and end apart: 16, of which 8 were waited for; matrix products, arithmetic and copies ran while one was open for 9% of the time, Pallas kernels for 9%

profile of v15, /device:TPU:20, one launch (start us, length us, event | category | flops | bytes accessed | tf_op | source)
XLA Modules:
  0.0 170.1 jit_solution(5463666502793973610)
XLA Ops:
  7.2 14.4 %tick0.1 = (bf16[4,2,24,32,128]{4,3,2,1,0:T(8,128)(2,1)}, bf16[4,2,24,32,128]{4,3,2,1,0:T(8,128)(2,1)}, bf16[4,2,24,32,128]{4,3,2,1,0:T(8,128)(2,1)}, bf16[4,2,2...) custom-call(s32[2]{0:T(128)} %bitcast.34, s32[1,2,96]{2,1,0:T(2,128)} %idx_in_ref.3, s32[1,2,96]{2,1,0:T(2,128)} %idx_out_ref.3, ...), custom_call_target="tpu_custom_call" | custom-call | flops 1006632960 | bytes 17301504 | tf_op jit(solution)/shard_map/tick0/pallas_call | solution.py:89
  21.8 3.5 %collective-permute-done.1 = bf16[4,2,24,32,128]{4,3,2,1,0:T(8,128)(2,1)S(1)} collective-permute-done((bf16[4,2,24,32,128]{4,3,2,1,0:T(8,128)(2,1)}, bf16[4,2,24,32,128]{4,3,2,1,0:T(8,128)(2,1)S(1)}, u32[]{:S(2)}, u32[]{:S(2)}) %collective-permute-start.1) | collective-permute-done | bytes 1572896 | tf_op jit(solution)/shard_map/ppermute | solution.py:129
  25.3 0.4 add_convert_fusion.3.refs_0_
  25.7 1.5 collective-permute-start.2
  27.3 14.9 %tick1.1 = (bf16[4,2,24,32,128]{4,3,2,1,0:T(8,128)(2,1)}, bf16[4,2,24,32,128]{4,3,2,1,0:T(8,128)(2,1)}, bf16[4,2,24,32,128]{4,3,2,1,0:T(8,128)(2,1)}, bf16[4,2,2...) custom-call(s32[2]{0:T(128)} %bitcast.35, s32[1,2,96]{2,1,0:T(2,128)} %idx_in_ref.3, s32[1,2,96]{2,1,0:T(2,128)} %idx_out_ref.3, ...), custom_call_target="tpu_custom_call" | custom-call | flops 1006632960 | bytes 17301504 | tf_op jit(solution)/shard_map/tick1/pallas_call | solution.py:89
  42.2 20.0 %collective-permute-done.2.refs_1_ = bf16[4,2,24,32,128]{4,3,2,1,0:T(8,128)(2,1)S(1)} collective-permute-done((bf16[4,2,24,32,128]{4,3,2,1,0:T(8,128)(2,1)S(1)}, bf16[4,2,24,32,128]{4,3,2,1,0:T(8,128)(2,1)S(1)}, u32[]{:S(2)}, u32[]{:S(2)}) %collective-permute-start.2) | collective-permute-done | bytes 1572896 | tf_op jit(solution)/shard_map/ppermute | solution.py:129
  62.3 1.2 copy-done
  63.6 0.5 collective-permute-start.8
  64.1 3.7 %add_convert_fusion.1 = bf16[4,2,24,32,128]{4,3,2,1,0:T(8,128)(2,1)} fusion(bf16[4,2,24,32,128]{4,3,2,1,0:T(8,128)(2,1)} %collective-permute-done.9, bf16[4,2,24,32,128]{4,3,2,1,0:T(8,128)(2,1)} %tie.3), kind=kLoop, calls=%fused_computation.2 | loop fusion | flops 3145728 | bytes 4718592 | tf_op jit(solution)/shard_map/convert_element_type | solution.py:169
  67.8 1.5 collective-permute-start.10
  69.3 2.0 %add_convert_fusion.2 = bf16[4,2,24,32,128]{4,3,2,1,0:T(8,128)(2,1)S(1)} fusion(bf16[4,2,24,32,128]{4,3,2,1,0:T(8,128)(2,1)S(1)} %copy-done.1, bf16[4,2,24,32,128]{4,3,2,1,0:T(8,128)(2,1)} %collective-permute-done.4, bf16[4,2,24,32,128]{4,3,2,1,0:T(8,128)(2,1)S(1)} %copy-done.3), kind=kLoop, calls=%fused_computation.3 | loop fusion | flops 4718592 | bytes 6291456 | tf_op jit(solution)/shard_map/convert_element_type | solution.py:172
  71.6 0.5 collective-permute-start.7
  72.1 3.4 %collective-permute-start.6 = (bf16[2,24,32,128]{3,2,1,0:T(8,128)(2,1)S(1)}, bf16[2,24,32,128]{3,2,1,0:T(8,128)(2,1)S(1)}, u32[]{:S(2)}, u32[]{:S(2)}) collective-permute-start(bf16[2,24,32,128]{3,2,1,0:T(8,128)(2,1)S(1)} %get-tuple-element.38), channel_id=1, source_target_pairs={{0,16},{8,24},{16,0},{24,8},{1,17},{9,25},{17,1},{25,9},{2,18},{10... | collective-permute-start | bytes 1179656 | tf_op jit(solution)/shard_map/ppermute | solution.py:144
  75.6 28.9 %collective-permute-done.10 = bf16[4,2,24,32,128]{4,3,2,1,0:T(8,128)(2,1)} collective-permute-done((bf16[4,2,24,32,128]{4,3,2,1,0:T(8,128)(2,1)}, bf16[4,2,24,32,128]{4,3,2,1,0:T(8,128)(2,1)}, u32[]{:S(2)}, u32[]{:S(2)}) %collective-permute-start.10) | collective-permute-done | bytes 1572896 | tf_op jit(solution)/shard_map/ppermute | solution.py:129
  104.5 2.5 %add_convert_fusion = bf16[4,2,24,32,128]{4,3,2,1,0:T(8,128)(2,1)S(1)} fusion(bf16[4,2,24,32,128]{4,3,2,1,0:T(8,128)(2,1)} %collective-permute-done.10, bf16[4,2,24,32,128]{4,3,2,1,0:T(8,128)(2,1)} %collective-permute-done.8, bf16[4,2,24,32,128]{4,3,2,1,0:T(8,128)(2,1)S(1)} %copy-done.4), kind=kLoop, calls=%fused_computation.1 | loop fusion | flops 4718592 | bytes 6291456 | tf_op jit(solution)/shard_map/convert_element_type | solution.py:175
  107.0 1.1 constant_dynamic-slice_fusion.4
  108.1 0.4 collective-permute-start.13
  108.6 3.5 %collective-permute-start.12 = (bf16[2,24,32,128]{3,2,1,0:T(8,128)(2,1)}, bf16[2,24,32,128]{3,2,1,0:T(8,128)(2,1)}, u32[]{:S(2)}, u32[]{:S(2)}) collective-permute-start(bf16[2,24,32,128]{3,2,1,0:T(8,128)(2,1)} %get-tuple-element.30), channel_id=1, source_target_pairs={{0,16},{8,24},{16,0},{24,8},{1,17},{9,25},{17,1},{25,9},{2,18},{10... | collective-permute-start | bytes 1179656 | tf_op jit(solution)/shard_map/ppermute | solution.py:144
  112.1 3.9 %collective-permute-start = (bf16[32,12288]{1,0:T(8,128)(2,1)}, bf16[32,12288]{1,0:T(8,128)(2,1)S(1)}, u32[]{:S(2)}, u32[]{:S(2)}) collective-permute-start(bf16[32,12288]{1,0:T(8,128)(2,1)} %reduce-scatter.3.cloned.1.call-done), channel_id=1, source_target_pairs={{8,0},{16,8},{24,16},{9,1},{17,9},{25,17},{10,2},{18,10},{26,18},{... | collective-permute-start | bytes 2359304 | tf_op jit(solution)/shard_map/ppermute | solution.py:135
  116.0 0.7 copy-done.7
  116.7 1.3 pad_maximum_fusion
  118.1 2.0 %collective-permute-start.3 = (bf16[32,12288]{1,0:T(8,128)(2,1)}, bf16[32,12288]{1,0:T(8,128)(2,1)S(1)}, u32[]{:S(2)}, u32[]{:S(2)}) collective-permute-start(bf16[32,12288]{1,0:T(8,128)(2,1)} %reduce-scatter.5.cloned.1.call-done), channel_id=1, source_target_pairs={{0,8},{8,16},{16,24},{1,9},{9,17},{17,25},{2,10},{10,18},{18,26},{... | collective-permute-start | bytes 2359304 | tf_op jit(solution)/shard_map/ppermute | solution.py:135
  120.1 0.4 constant_dynamic-slice_fusion.8
  120.4 13.3 %collective-permute-done.13 = bf16[2,24,32,128]{3,2,1,0:T(8,128)(2,1)} collective-permute-done((bf16[2,24,32,128]{3,2,1,0:T(8,128)(2,1)}, bf16[2,24,32,128]{3,2,1,0:T(8,128)(2,1)}, u32[]{:S(2)}, u32[]{:S(2)}) %collective-permute-start.13) | collective-permute-done | bytes 393248 | tf_op jit(solution)/shard_map/ppermute | solution.py:144
  133.8 10.0 %collective-permute-done.12 = bf16[2,24,32,128]{3,2,1,0:T(8,128)(2,1)} collective-permute-done((bf16[2,24,32,128]{3,2,1,0:T(8,128)(2,1)}, bf16[2,24,32,128]{3,2,1,0:T(8,128)(2,1)}, u32[]{:S(2)}, u32[]{:S(2)}) %collective-permute-start.12) | collective-permute-done | bytes 393248 | tf_op jit(solution)/shard_map/ppermute | solution.py:144
  143.8 2.3 %collective-permute-done.11 = bf16[2,24,32,128]{3,2,1,0:T(8,128)(2,1)} collective-permute-done((bf16[2,24,32,128]{3,2,1,0:T(8,128)(2,1)}, bf16[2,24,32,128]{3,2,1,0:T(8,128)(2,1)}, u32[]{:S(2)}, u32[]{:S(2)}) %collective-permute-start.11) | collective-permute-done | bytes 393248 | tf_op jit(solution)/shard_map/ppermute | solution.py:144
  146.1 1.4 pad_maximum_fusion.1
  147.5 0.3 constant_dynamic-slice_fusion.3
  148.0 2.2 %add_bitcast_fusion = f32[4,2,1,24,32,128]{5,4,3,2,1,0:T(8,128)} fusion(bf16[1,2,24,32,128]{4,3,2,1,0:T(8,128)(2,1)S(1)} %get-tuple-element.33, bf16[1,2,24,32,128]{4,3,2,1,0:T(8,128)(2,1)S(1)} %get-tuple-element.34, bf16[1,2,24,32,128]{4,3,2,1,0:T(8,128)(2,1)S(1)} %get-tuple-element.35, bf16[1,2,24,32,128]{4,3,2,1,0:T(8,128)(2,1)S(1)} %get-tuple-element.32, ...), kind=kLoop, calls=%fused_computation | loop fusion | flops 7864320 | bytes 6291456
  150.2 8.6 %collective-permute-done = bf16[32,12288]{1,0:T(8,128)(2,1)S(1)} collective-permute-done((bf16[32,12288]{1,0:T(8,128)(2,1)}, bf16[32,12288]{1,0:T(8,128)(2,1)S(1)}, u32[]{:S(2)}, u32[]{:S(2)}) %collective-permute-start) | collective-permute-done | bytes 786464 | tf_op jit(solution)/shard_map/ppermute | solution.py:135
  158.8 3.2 %collective-permute-done.3 = bf16[32,12288]{1,0:T(8,128)(2,1)S(1)} collective-permute-done((bf16[32,12288]{1,0:T(8,128)(2,1)}, bf16[32,12288]{1,0:T(8,128)(2,1)S(1)}, u32[]{:S(2)}, u32[]{:S(2)}) %collective-permute-start.3) | collective-permute-done | bytes 786464 | tf_op jit(solution)/shard_map/ppermute | solution.py:135
  162.0 1.3 maximum_bitcast_fusion
  (35 shorter events, 0.9 us)
Async XLA Ops:
  7.2 104.9 %reduce-scatter.3.cloned.1.call-start = ((), (), s32[]{:S(2)}) async-start(), calls=%async_computation.2 | async-start | bytes 2359296 | tf_op jit(solution)/shard_map/reduce_scatter | solution.py:160
  21.6 3.7 %copy-start.5 = (bf16[4,2,24,32,128]{4,3,2,1,0:T(8,128)(2,1)S(1)}, bf16[4,2,24,32,128]{4,3,2,1,0:T(8,128)(2,1)}, u32[]{:S(2)}) copy-start(bf16[4,2,24,32,128]{4,3,2,1,0:T(8,128)(2,1)} %get-tuple-element.13) | copy-start | bytes 4718596
  21.6 3.7 %collective-permute-start.1 = (bf16[4,2,24,32,128]{4,3,2,1,0:T(8,128)(2,1)}, bf16[4,2,24,32,128]{4,3,2,1,0:T(8,128)(2,1)S(1)}, u32[]{:S(2)}, u32[]{:S(2)}) collective-permute-start(bf16[4,2,24,32,128]{4,3,2,1,0:T(8,128)(2,1)} %get-tuple-element.14), channel_id=1, source_target_pairs={{0,2},{2,0},{4,6},{6,4},{1,3},{3,1},{5,7},{7,5},{8,10},{10,8},{12,... | collective-permute-start | bytes 4718600 | tf_op jit(solution)/shard_map/ppermute | solution.py:129
  21.7 96.4 %reduce-scatter.5.cloned.1.call-start = ((), (), s32[]{:S(2)}) async-start(), calls=%async_computation.3 | async-start | bytes 2359296 | tf_op jit(solution)/shard_map/reduce_scatter | solution.py:160
  25.7 1.6 copy-start.2
  25.7 36.5 %collective-permute-start.2 = (bf16[4,2,24,32,128]{4,3,2,1,0:T(8,128)(2,1)S(1)}, bf16[4,2,24,32,128]{4,3,2,1,0:T(8,128)(2,1)S(1)}, u32[]{:S(2)}, u32[]{:S(2)}) collective-permute-start(bf16[4,2,24,32,128]{4,3,2,1,0:T(8,128)(2,1)S(1)} %add_convert_fusion.3.refs_0_), channel_id=1, source_target_pairs={{0,4},{2,6},{4,0},{6,2},{1,5},{3,7},{5,1},{7,3},{8,12},{10,14},{12... | collective-permute-start | bytes 4718600 | tf_op jit(solution)/shard_map/ppermute | solution.py:129
  42.2 21.9 %collective-permute-start.9 = (bf16[4,2,24,32,128]{4,3,2,1,0:T(8,128)(2,1)}, bf16[4,2,24,32,128]{4,3,2,1,0:T(8,128)(2,1)}, u32[]{:S(2)}, u32[]{:S(2)}) collective-permute-start(bf16[4,2,24,32,128]{4,3,2,1,0:T(8,128)(2,1)} %get-tuple-element.21), channel_id=1, source_target_pairs={{0,2},{2,0},{4,6},{6,4},{1,3},{3,1},{5,7},{7,5},{8,10},{10,8},{12,... | collective-permute-start | bytes 4718600 | tf_op jit(solution)/shard_map/ppermute | solution.py:129
  62.2 1.3 copy-start
  63.5 5.7 %collective-permute-start.4 = (bf16[4,2,24,32,128]{4,3,2,1,0:T(8,128)(2,1)}, bf16[4,2,24,32,128]{4,3,2,1,0:T(8,128)(2,1)}, u32[]{:S(2)}, u32[]{:S(2)}) collective-permute-start(bf16[4,2,24,32,128]{4,3,2,1,0:T(8,128)(2,1)} %get-tuple-element.17), channel_id=1, source_target_pairs={{0,2},{2,0},{4,6},{6,4},{1,3},{3,1},{5,7},{7,5},{8,10},{10,8},{12,... | collective-permute-start | bytes 4718600 | tf_op jit(solution)/shard_map/ppermute | solution.py:129
  63.6 12.0 %collective-permute-start.8 = (bf16[4,2,24,32,128]{4,3,2,1,0:T(8,128)(2,1)}, bf16[4,2,24,32,128]{4,3,2,1,0:T(8,128)(2,1)}, u32[]{:S(2)}, u32[]{:S(2)}) collective-permute-start(bf16[4,2,24,32,128]{4,3,2,1,0:T(8,128)(2,1)} %get-tuple-element.19), channel_id=1, source_target_pairs={{0,2},{2,0},{4,6},{6,4},{1,3},{3,1},{5,7},{7,5},{8,10},{10,8},{12,... | collective-permute-start | bytes 4718600 | tf_op jit(solution)/shard_map/ppermute | solution.py:129
  64.1 5.2 %copy-start.1 = (bf16[4,2,24,32,128]{4,3,2,1,0:T(8,128)(2,1)S(1)}, bf16[4,2,24,32,128]{4,3,2,1,0:T(8,128)(2,1)}, u32[]{:S(2)}) copy-start(bf16[4,2,24,32,128]{4,3,2,1,0:T(8,128)(2,1)} %copy-done) | copy-start | bytes 4718596
  64.1 5.2 %copy-start.3 = (bf16[4,2,24,32,128]{4,3,2,1,0:T(8,128)(2,1)S(1)}, bf16[4,2,24,32,128]{4,3,2,1,0:T(8,128)(2,1)}, u32[]{:S(2)}) copy-start(bf16[4,2,24,32,128]{4,3,2,1,0:T(8,128)(2,1)} %get-tuple-element.16) | copy-start | bytes 4718596
  67.8 36.7 %collective-permute-start.10 = (bf16[4,2,24,32,128]{4,3,2,1,0:T(8,128)(2,1)}, bf16[4,2,24,32,128]{4,3,2,1,0:T(8,128)(2,1)}, u32[]{:S(2)}, u32[]{:S(2)}) collective-permute-start(bf16[4,2,24,32,128]{4,3,2,1,0:T(8,128)(2,1)} %add_convert_fusion.1), channel_id=1, source_target_pairs={{0,4},{2,6},{4,0},{6,2},{1,5},{3,7},{5,1},{7,3},{8,12},{10,14},{12... | collective-permute-start | bytes 4718600 | tf_op jit(solution)/shard_map/ppermute | solution.py:129
  71.3 33.2 %copy-start.4 = (bf16[4,2,24,32,128]{4,3,2,1,0:T(8,128)(2,1)S(1)}, bf16[4,2,24,32,128]{4,3,2,1,0:T(8,128)(2,1)}, u32[]{:S(2)}) copy-start(bf16[4,2,24,32,128]{4,3,2,1,0:T(8,128)(2,1)} %get-tuple-element.18) | copy-start | bytes 4718596
  71.6 40.4 %collective-permute-start.7 = (bf16[2,24,32,128]{3,2,1,0:T(8,128)(2,1)S(1)}, bf16[2,24,32,128]{3,2,1,0:T(8,128)(2,1)S(1)}, u32[]{:S(2)}, u32[]{:S(2)}) collective-permute-start(bf16[2,24,32,128]{3,2,1,0:T(8,128)(2,1)S(1)} %get-tuple-element.37), channel_id=1, source_target_pairs={{0,24},{8,0},{16,8},{24,16},{1,25},{9,1},{17,9},{25,17},{2,26},{10... | collective-permute-start | bytes 1179656 | tf_op jit(solution)/shard_map/ppermute | solution.py:144
  72.1 39.9 %collective-permute-start.6 = (bf16[2,24,32,128]{3,2,1,0:T(8,128)(2,1)S(1)}, bf16[2,24,32,128]{3,2,1,0:T(8,128)(2,1)S(1)}, u32[]{:S(2)}, u32[]{:S(2)}) collective-permute-start(bf16[2,24,32,128]{3,2,1,0:T(8,128)(2,1)S(1)} %get-tuple-element.38), channel_id=1, source_target_pairs={{0,16},{8,24},{16,0},{24,8},{1,17},{9,25},{17,1},{25,9},{2,18},{10... | collective-permute-start | bytes 1179656 | tf_op jit(solution)/shard_map/ppermute | solution.py:144
  75.6 40.4 %collective-permute-start.5 = (bf16[2,24,32,128]{3,2,1,0:T(8,128)(2,1)S(1)}, bf16[2,24,32,128]{3,2,1,0:T(8,128)(2,1)S(1)}, u32[]{:S(2)}, u32[]{:S(2)}) collective-permute-start(bf16[2,24,32,128]{3,2,1,0:T(8,128)(2,1)S(1)} %get-tuple-element.39), channel_id=1, source_target_pairs={{0,8},{8,16},{16,24},{24,0},{1,9},{9,17},{17,25},{25,1},{2,10},{10... | collective-permute-start | bytes 1179656 | tf_op jit(solution)/shard_map/ppermute | solution.py:144
  108.1 25.7 %collective-permute-start.13 = (bf16[2,24,32,128]{3,2,1,0:T(8,128)(2,1)}, bf16[2,24,32,128]{3,2,1,0:T(8,128)(2,1)}, u32[]{:S(2)}, u32[]{:S(2)}) collective-permute-start(bf16[2,24,32,128]{3,2,1,0:T(8,128)(2,1)} %get-tuple-element.29), channel_id=1, source_target_pairs={{0,24},{8,0},{16,8},{24,16},{1,25},{9,1},{17,9},{25,17},{2,26},{10... | collective-permute-start | bytes 1179656 | tf_op jit(solution)/shard_map/ppermute | solution.py:144
  108.6 35.2 %collective-permute-start.12 = (bf16[2,24,32,128]{3,2,1,0:T(8,128)(2,1)}, bf16[2,24,32,128]{3,2,1,0:T(8,128)(2,1)}, u32[]{:S(2)}, u32[]{:S(2)}) collective-permute-start(bf16[2,24,32,128]{3,2,1,0:T(8,128)(2,1)} %get-tuple-element.30), channel_id=1, source_target_pairs={{0,16},{8,24},{16,0},{24,8},{1,17},{9,25},{17,1},{25,9},{2,18},{10... | collective-permute-start | bytes 1179656 | tf_op jit(solution)/shard_map/ppermute | solution.py:144
  112.0 34.1 %collective-permute-start.11 = (bf16[2,24,32,128]{3,2,1,0:T(8,128)(2,1)}, bf16[2,24,32,128]{3,2,1,0:T(8,128)(2,1)}, u32[]{:S(2)}, u32[]{:S(2)}) collective-permute-start(bf16[2,24,32,128]{3,2,1,0:T(8,128)(2,1)} %get-tuple-element.31), channel_id=1, source_target_pairs={{0,8},{8,16},{16,24},{24,0},{1,9},{9,17},{17,25},{25,1},{2,10},{10... | collective-permute-start | bytes 1179656 | tf_op jit(solution)/shard_map/ppermute | solution.py:144
  112.0 3.9 %copy-start.6 = (bf16[2,24,32,128]{3,2,1,0:T(8,128)(2,1)}, bf16[2,24,32,128]{3,2,1,0:T(8,128)(2,1)S(1)}, u32[]{:S(2)}) copy-start(bf16[2,24,32,128]{3,2,1,0:T(8,128)(2,1)S(1)} %collective-permute-done.6) | copy-start | bytes 1179652
  112.1 46.8 %collective-permute-start = (bf16[32,12288]{1,0:T(8,128)(2,1)}, bf16[32,12288]{1,0:T(8,128)(2,1)S(1)}, u32[]{:S(2)}, u32[]{:S(2)}) collective-permute-start(bf16[32,12288]{1,0:T(8,128)(2,1)} %reduce-scatter.3.cloned.1.call-done), channel_id=1, source_target_pairs={{8,0},{16,8},{24,16},{9,1},{17,9},{25,17},{10,2},{18,10},{26,18},{... | collective-permute-start | bytes 2359304 | tf_op jit(solution)/shard_map/ppermute | solution.py:135
  116.0 0.7 copy-start.7
  118.1 43.9 %collective-permute-start.3 = (bf16[32,12288]{1,0:T(8,128)(2,1)}, bf16[32,12288]{1,0:T(8,128)(2,1)S(1)}, u32[]{:S(2)}, u32[]{:S(2)}) collective-permute-start(bf16[32,12288]{1,0:T(8,128)(2,1)} %reduce-scatter.5.cloned.1.call-done), channel_id=1, source_target_pairs={{0,8},{8,16},{16,24},{1,9},{9,17},{17,25},{2,10},{10,18},{18,26},{... | collective-permute-start | bytes 2359304 | tf_op jit(solution)/shard_map/ppermute | solution.py:135
Sparse Core Ops, SparseCore 0:
  21.8 26.2 reduce-scatter.2
  63.6 26.1 reduce-scatter.4
